TPU v7x, 32 devices: a whole 2x2x4 slice. The times are simulated.
32 devices in a mesh: dp: 16 (over z, x, core), tensor: 2 (over y).
Axes of the slice: x: 2, y: 2, z: 4, core: 2. Of those that a mesh axis runs over, the one named last changes fastest.
Arguments:
- hidden: bfloat16 [64, 128, 768], P('dp'), may hold values from -6 to 6
- image: bfloat16 [64, 257, 1408], P('dp'), may hold values from -6 to 6
- segment_ids: int32 [64, 128], P('dp'), may hold values from 0 to 3, never falling along the last dimension, each value on 1 to 64 neighbouring positions
- cotangent: bfloat16 [64, 128, 768], P('dp'), may hold values from -6 to 6
- slot_block: int32 [2, 464], P('tensor'), may hold values from 0 to 463, as said below
- weight_master: float32 [2, 464, 128, 128], P('tensor', 'dp')
- moment_one: float32 [2, 464, 128, 128], P('tensor', 'dp')
- moment_two: float32 [2, 464, 128, 128], P('tensor', 'dp'), as said below
- left_stat: float32 [2, 464, 128, 128], P('tensor', 'dp'), as said below
- right_stat: float32 [2, 464, 128, 128], P('tensor', 'dp'), as said below
- left_basis: float32 [2, 464, 128, 128], P('tensor', 'dp'), as said below
- right_basis: float32 [2, 464, 128, 128], P('tensor', 'dp'), as said below
- norm_params: float32 [4, 2, 768], replicated, as said below
- norm_moment_one: float32 [4, 2, 768], replicated
- norm_moment_two: float32 [4, 2, 768], replicated, as said below
Outputs:
- output: bfloat16 [64, 128, 768], P('dp')
- input_grad: float32 [64, 128, 768], P('dp')
- weight_new: float32 [2, 464, 128, 128], P('tensor', 'dp')
- weight_copy: bfloat16 [2, 464, 128, 128], P('tensor', 'dp')
- moment_one_new: float32 [2, 464, 128, 128], P('tensor', 'dp')
- moment_two_new: float32 [2, 464, 128, 128], P('tensor', 'dp')
- left_stat_new: float32 [2, 464, 128, 128], P('tensor', 'dp')
- right_stat_new: float32 [2, 464, 128, 128], P('tensor', 'dp')
- left_basis_new: float32 [2, 464, 128, 128], P('tensor', 'dp')
- right_basis_new: float32 [2, 464, 128, 128], P('tensor', 'dp')
- norm_moment_one_new: float32 [4, 2, 768], replicated
- norm_moment_two_new: float32 [4, 2, 768], replicated
- norm_new: float32 [4, 2, 768], replicated
Inputs may be any that keep to these rules, and one draw needn't show every extreme that they name: `slot_block`: each row is a permutation of 0 to 463; numbers below 462 name blocks, the others spare slots. `left_basis`: every block is orthogonal. `right_basis`: every block is orthogonal. `left_stat`: every block is symmetric positive definite. `right_stat`: every block is symmetric positive definite. `moment_two`: every entry is positive. `norm_moment_two`: every entry is positive. `norm_params`: gains are positive.
All inputs are finite; a program needn't handle non-finite values.
Results may differ from a plain program's by a relative error of at most 0.034.
Values may be sent and summed in bfloat16 or wider, within the bound.
No kernel may reach another device: no remote copies, remote signals or barrier semaphores. Data moves between devices by JAX's collectives and lax.ppermute only.
A program may use at most 256 MiB of HBM per device.

v0:
```python
import jax
import jax.numpy as jnp
from jax import lax
from jax.sharding import PartitionSpec as P

HEADS = 12
FF = 3072
NQ = 32
STEP = 10


beta_first = 0.9
beta_second = 0.999
beta_stats = 0.95
adam_epsilon = 1e-08
norm_epsilon = 1e-06
matrix_rate = 0.03
matrix_decay = 0.05
norm_rate = 0.6
masked_score = -1000000000.0
highest = lax.Precision.HIGHEST


def matrix_shapes(width, image_width, hidden_units, tensor_count):
    half_width = width // tensor_count
    half_hidden = hidden_units // tensor_count
    return [
        (width, half_width),
        (width, half_width),
        (width, half_width),
        (half_width, width),
        (width, half_width),
        (image_width, half_width),
        (image_width, half_width),
        (half_width, width),
        (width, half_hidden),
        (half_hidden, width),
        (width, half_hidden),
        (half_hidden, width),
    ]


def unpack_blocks(blocks, shapes, block_side):
    matrices = []
    offset = 0
    for rows_count, cols_count in shapes:
        row_tiles = rows_count // block_side
        col_tiles = cols_count // block_side
        number = row_tiles * col_tiles
        portion = blocks[offset : offset + number].reshape(
            row_tiles, col_tiles, block_side, block_side
        )
        matrices.append(portion.transpose(0, 2, 1, 3).reshape(rows_count, cols_count))
        offset = offset + number
    return matrices


def layer_norm(resid_rows, gain, shift):
    center = resid_rows - jnp.mean(resid_rows, axis=-1, keepdims=True)
    variance = jnp.mean(center * center, axis=-1, keepdims=True)
    return center * lax.rsqrt(variance + norm_epsilon) * gain + shift


def first_norm(resid_rows, params):
    return layer_norm(resid_rows, params[0, 0], params[0, 1])


def second_norm(resid_rows, params):
    return layer_norm(resid_rows, params[1, 0], params[1, 1])


def last_norm(resid_rows, params):
    return jnp.concatenate(
        [
            layer_norm(resid_rows[:, :NQ], params[2, 0], params[2, 1]),
            layer_norm(resid_rows[:, NQ:], params[3, 0], params[3, 1]),
        ],
        axis=1,
    )


def gelu_exact(values):
    return jax.nn.gelu(values, approximate=False)


def dense(inputs, weight):
    return jnp.einsum("rsd,de->rse", inputs, weight, preferred_element_type=jnp.float32)


def dense_back(grads, weight):
    return jnp.einsum("rse,de->rsd", grads, weight, preferred_element_type=jnp.float32)


def block_grad(inputs, grads, block_side):
    row_count, seq_count, in_width = inputs.shape
    out_width = grads.shape[2]
    left_tiles = inputs.reshape(row_count, seq_count, in_width // block_side, block_side)
    right_tiles = grads.reshape(row_count, seq_count, out_width // block_side, block_side)
    tiles = jnp.einsum(
        "rsia,rsjb->ijab", left_tiles, right_tiles, preferred_element_type=jnp.float32
    )
    return tiles.reshape(-1, block_side, block_side)


def split_heads(array, heads):
    return array.reshape(array.shape[0], array.shape[1], heads, array.shape[2] // heads)


def masked_scores(queries, key_rows, allowed, heads, scale):
    scores = (
        jnp.einsum(
            "rqhd,rkhd->rhqk",
            split_heads(queries, heads),
            split_heads(key_rows, heads),
            preferred_element_type=jnp.float32,
        )
        * scale
    )
    if allowed is not None:
        scores = jnp.where(allowed, scores, masked_score)
    return scores


def attend(queries, key_rows, value_rows, allowed, heads, scale):
    scores = masked_scores(queries, key_rows, allowed, heads, scale)
    totals = jax.nn.logsumexp(scores, axis=-1)
    probs = jnp.exp(scores - totals[..., None]).astype(jnp.bfloat16)
    mixed = jnp.einsum(
        "rhqk,rkhd->rqhd", probs, split_heads(value_rows, heads), preferred_element_type=jnp.float32
    )
    return (mixed.reshape(queries.shape).astype(jnp.bfloat16), totals)


def attend_back(queries, key_rows, value_rows, allowed, heads, scale, totals, mixed_grad):
    scores = masked_scores(queries, key_rows, allowed, heads, scale)
    probs = jnp.exp(scores - totals[..., None])
    grad_heads = split_heads(mixed_grad, heads)
    value_grad = jnp.einsum(
        "rhqk,rqhd->rkhd",
        probs.astype(jnp.bfloat16),
        grad_heads,
        preferred_element_type=jnp.float32,
    )
    prob_grad = jnp.einsum(
        "rqhd,rkhd->rhqk",
        grad_heads,
        split_heads(value_rows, heads),
        preferred_element_type=jnp.float32,
    )
    score_grad = (
        probs * (prob_grad - jnp.sum(probs * prob_grad, axis=-1, keepdims=True)) * scale
    ).astype(jnp.bfloat16)
    query_grad = jnp.einsum(
        "rhqk,rkhd->rqhd",
        score_grad,
        split_heads(key_rows, heads),
        preferred_element_type=jnp.float32,
    )
    key_grad = jnp.einsum(
        "rhqk,rqhd->rkhd",
        score_grad,
        split_heads(queries, heads),
        preferred_element_type=jnp.float32,
    )
    return (
        query_grad.reshape(queries.shape).astype(jnp.bfloat16),
        key_grad.reshape(key_rows.shape).astype(jnp.bfloat16),
        value_grad.reshape(value_rows.shape).astype(jnp.bfloat16),
    )


def finish_branch(partial_sum, residual, normalize):
    total = lax.psum(partial_sum.astype(jnp.bfloat16), "tensor").astype(jnp.float32)
    summed = residual + total
    return (summed, normalize(summed))


def back_sum(partial_sum):
    return lax.psum(partial_sum.astype(jnp.bfloat16), "tensor").astype(jnp.float32)


def layer_rows(
    hidden, image, segment_ids, cotangent, weights, norm_params, heads_local, scale, block_side
):
    (
        self_query,
        self_key,
        self_value,
        self_out,
        cross_query,
        cross_key,
        cross_value,
        cross_out,
        query_up,
        query_down,
        text_up,
        text_down,
    ) = weights
    resid_input = hidden.astype(jnp.float32)
    allowed = (segment_ids[:, :, None] == segment_ids[:, None, :])[:, None]
    queries = dense(hidden, self_query).astype(jnp.bfloat16)
    key_rows = dense(hidden, self_key).astype(jnp.bfloat16)
    value_rows = dense(hidden, self_value).astype(jnp.bfloat16)
    mixed, self_totals = attend(queries, key_rows, value_rows, allowed, heads_local, scale)
    first_sum, first = finish_branch(
        dense(mixed, self_out), resid_input, lambda resid_rows: first_norm(resid_rows, norm_params)
    )
    learned = first[:, :NQ]
    learned_low = learned.astype(jnp.bfloat16)
    cross_queries = dense(learned_low, cross_query).astype(jnp.bfloat16)
    image_keys = dense(image, cross_key).astype(jnp.bfloat16)
    image_values = dense(image, cross_value).astype(jnp.bfloat16)
    looked, cross_totals = attend(cross_queries, image_keys, image_values, None, heads_local, scale)
    second_sum, second = finish_branch(
        dense(looked, cross_out), learned, lambda resid_rows: second_norm(resid_rows, norm_params)
    )
    middle_states = jnp.concatenate([second, first[:, NQ:]], axis=1)
    middle_low = middle_states.astype(jnp.bfloat16)
    query_before = dense(middle_low[:, :NQ], query_up)
    text_before = dense(middle_low[:, NQ:], text_up)
    query_hidden = gelu_exact(query_before).astype(jnp.bfloat16)
    text_hidden = gelu_exact(text_before).astype(jnp.bfloat16)
    forward_partial = jnp.concatenate(
        [dense(query_hidden, query_down), dense(text_hidden, text_down)], axis=1
    )
    third_sum, output_rows = finish_branch(
        forward_partial, middle_states, lambda resid_rows: last_norm(resid_rows, norm_params)
    )
    upstream = cotangent.astype(jnp.float32)
    _, third_pull = jax.vjp(last_norm, third_sum, norm_params)
    third_grad, norm_grad_three = third_pull(upstream)
    down_low = third_grad.astype(jnp.bfloat16)
    grad_query_down = block_grad(query_hidden, down_low[:, :NQ], block_side)
    grad_text_down = block_grad(text_hidden, down_low[:, NQ:], block_side)
    _, query_gelu_pull = jax.vjp(gelu_exact, query_before)
    _, text_gelu_pull = jax.vjp(gelu_exact, text_before)
    query_pre_grad = query_gelu_pull(dense_back(down_low[:, :NQ], query_down))[0].astype(
        jnp.bfloat16
    )
    text_pre_grad = text_gelu_pull(dense_back(down_low[:, NQ:], text_down))[0].astype(jnp.bfloat16)
    grad_query_up = block_grad(middle_low[:, :NQ], query_pre_grad, block_side)
    grad_text_up = block_grad(middle_low[:, NQ:], text_pre_grad, block_side)
    middle_partial = jnp.concatenate(
        [dense_back(query_pre_grad, query_up), dense_back(text_pre_grad, text_up)], axis=1
    )
    middle_grad = third_grad + back_sum(middle_partial)
    _, second_pull = jax.vjp(second_norm, second_sum, norm_params)
    second_grad, norm_grad_two = second_pull(middle_grad[:, :NQ])
    cross_out_low = second_grad.astype(jnp.bfloat16)
    grad_cross_out = block_grad(looked, cross_out_low, block_side)
    looked_grad = dense_back(cross_out_low, cross_out).astype(jnp.bfloat16)
    cross_query_back, image_key_back, image_value_back = attend_back(
        cross_queries, image_keys, image_values, None, heads_local, scale, cross_totals, looked_grad
    )
    grad_cross_query = block_grad(learned_low, cross_query_back, block_side)
    grad_cross_key = block_grad(image, image_key_back, block_side)
    grad_cross_value = block_grad(image, image_value_back, block_side)
    learned_grad = second_grad + back_sum(dense_back(cross_query_back, cross_query))
    first_grad_rows = jnp.concatenate([learned_grad, middle_grad[:, NQ:]], axis=1)
    _, first_pull = jax.vjp(first_norm, first_sum, norm_params)
    first_grad, norm_grad_one = first_pull(first_grad_rows)
    self_out_low = first_grad.astype(jnp.bfloat16)
    grad_self_out = block_grad(mixed, self_out_low, block_side)
    mixed_grad = dense_back(self_out_low, self_out).astype(jnp.bfloat16)
    self_query_back, self_key_back, self_value_back = attend_back(
        queries, key_rows, value_rows, allowed, heads_local, scale, self_totals, mixed_grad
    )
    grad_self_query = block_grad(hidden, self_query_back, block_side)
    grad_self_key = block_grad(hidden, self_key_back, block_side)
    grad_self_value = block_grad(hidden, self_value_back, block_side)
    input_partial = (
        dense_back(self_query_back, self_query)
        + dense_back(self_key_back, self_key)
        + dense_back(self_value_back, self_value)
    )
    input_grad = first_grad + back_sum(input_partial)
    packed = jnp.concatenate(
        [
            grad_self_query,
            grad_self_key,
            grad_self_value,
            grad_self_out,
            grad_cross_query,
            grad_cross_key,
            grad_cross_value,
            grad_cross_out,
            grad_query_up,
            grad_query_down,
            grad_text_up,
            grad_text_down,
        ],
        axis=0,
    )
    return (
        output_rows.astype(jnp.bfloat16),
        input_grad,
        packed,
        norm_grad_one + norm_grad_two + norm_grad_three,
    )


def times(left_matrix, right_matrix):
    return jnp.einsum("...ij,...jk->...ik", left_matrix, right_matrix, precision=highest)


def flipped(block_matrix):
    return jnp.swapaxes(block_matrix, -1, -2)


def orthonormal(columns):
    gram = times(flipped(columns), columns)
    factor = jnp.linalg.cholesky(gram)
    return lax.linalg.triangular_solve(
        factor, columns, left_side=False, lower=True, transpose_a=True
    )


def rotated_update(
    gradient, master, first_moment, second_moment, left_stats, right_stats, left_bases, right_bases
):
    rotated = times(times(flipped(left_bases), gradient), right_bases)
    first_new = beta_first * first_moment + (1 - beta_first) * rotated
    second_new = beta_second * second_moment + (1 - beta_second) * rotated * rotated
    step_rotated = (
        first_new
        / (1 - beta_first**STEP)
        / (jnp.sqrt(second_new / (1 - beta_second**STEP)) + adam_epsilon)
    )
    step_full = times(times(left_bases, step_rotated), flipped(right_bases))
    master_new = master - matrix_rate * (step_full + matrix_decay * master)
    left_new = beta_stats * left_stats + (1 - beta_stats) * times(gradient, flipped(gradient))
    right_new = beta_stats * right_stats + (1 - beta_stats) * times(flipped(gradient), gradient)
    return (
        master_new,
        first_new,
        second_new,
        left_new,
        right_new,
        orthonormal(times(left_new, left_bases)),
        orthonormal(times(right_new, right_bases)),
    )


def per_device(
    hidden,
    image,
    segment_ids,
    cotangent,
    slot_block,
    weight_master,
    moment_one,
    moment_two,
    left_stat,
    right_stat,
    left_basis,
    right_basis,
    norm_params,
    norm_moment_one,
    norm_moment_two,
):
    tensors = lax.axis_size("tensor")
    width = hidden.shape[2]
    image_width = image.shape[2]
    block_side = weight_master.shape[2]
    heads_local = HEADS // tensors
    scale = (width // HEADS) ** (-0.5)
    shapes = matrix_shapes(width, image_width, FF, tensors)
    block_count = sum(
        (rows_count // block_side * (cols_count // block_side) for rows_count, cols_count in shapes)
    )
    order = slot_block[0]
    slot_count = order.shape[0]
    gathered = lax.all_gather(weight_master[0].astype(jnp.bfloat16), "dp", axis=0, tiled=True)
    inverse = jnp.zeros_like(order).at[order].set(jnp.arange(slot_count, dtype=jnp.int32))
    natural = gathered[inverse[:block_count]]
    weights = unpack_blocks(natural, shapes, block_side)
    used_slot = (order < block_count)[:, None, None]
    safe_order = jnp.minimum(order, block_count - 1)
    owned = None
    out_rows, in_grad, packed, norm_part = layer_rows(
        hidden, image, segment_ids, cotangent, weights, norm_params, heads_local, scale, block_side
    )
    owned = lax.psum_scatter(
        jnp.where(used_slot, packed[safe_order], 0.0), "dp", scatter_dimension=0, tiled=True
    )
    norm_total = lax.psum(norm_part, "dp")
    updated = rotated_update(
        owned,
        weight_master[0],
        moment_one[0],
        moment_two[0],
        left_stat[0],
        right_stat[0],
        left_basis[0],
        right_basis[0],
    )
    (
        weight_new,
        moment_one_new,
        moment_two_new,
        left_stat_new,
        right_stat_new,
        left_basis_new,
        right_basis_new,
    ) = [array[None] for array in updated]
    norm_first = beta_first * norm_moment_one + (1 - beta_first) * norm_total
    norm_second = beta_second * norm_moment_two + (1 - beta_second) * norm_total * norm_total
    norm_new = norm_params - norm_rate * (norm_first / (1 - beta_first**STEP)) / (
        jnp.sqrt(norm_second / (1 - beta_second**STEP)) + adam_epsilon
    )
    return (
        out_rows,
        in_grad,
        weight_new,
        weight_new.astype(jnp.bfloat16),
        moment_one_new,
        moment_two_new,
        left_stat_new,
        right_stat_new,
        left_basis_new,
        right_basis_new,
        norm_first,
        norm_second,
        norm_new,
    )


def solution(mesh):
    in_specs = (
        P("dp", None, None),
        P("dp", None, None),
        P("dp", None),
        P("dp", None, None),
        P("tensor", None),
        P("tensor", "dp", None, None),
        P("tensor", "dp", None, None),
        P("tensor", "dp", None, None),
        P("tensor", "dp", None, None),
        P("tensor", "dp", None, None),
        P("tensor", "dp", None, None),
        P("tensor", "dp", None, None),
        P(),
        P(),
        P(),
    )
    out_specs = (
        P("dp", None, None),
        P("dp", None, None),
        P("tensor", "dp", None, None),
        P("tensor", "dp", None, None),
        P("tensor", "dp", None, None),
        P("tensor", "dp", None, None),
        P("tensor", "dp", None, None),
        P("tensor", "dp", None, None),
        P("tensor", "dp", None, None),
        P("tensor", "dp", None, None),
        P(),
        P(),
        P(),
    )
    return jax.shard_map(
        per_device, mesh=mesh, in_specs=in_specs, out_specs=out_specs, check_vma=False
    )
```

profile of v0, /device:TPU:0, one launch (start us, length us, event | category | flops | bytes accessed | tf_op | source)
XLA Modules:
  0.0 2225.1 jit_solution(1904844397807004387)
XLA Ops:
  14.4 116.4 %all-gather.2.cloned.1.call-done = bf16[464,128,128]{2,1,0:T(8,128)(2,1)} async-done(((bf16[29,128,128]{2,1,0:T(8,128)(2,1)}), bf16[464,128,128]{2,1,0:T(8,128)(2,1)}) %all-gather.2.cloned.1.call-update) | async-done | bytes 15204368 | tf_op jit(solution)/shard_map/all_gather | solution.py:373
  130.7 18.8 gather_fusion
  227.1 6.4 fusion.195
  247.4 6.0 reshape.604
  268.9 6.4 reshape.602
  284.2 6.1 multiply_convert_fusion
  311.0 19.9 all-reduce.21.cloned.1.call-done
  366.0 6.4 copy.339
  378.4 6.2 copy.342
  389.8 6.1 copy.345
  403.4 6.1 copy.348
  419.5 7.5 fusion.84
  432.3 7.7 convolution_convert_fusion.1
  548.9 23.4 %gather_fusion.1 = f32[464,128,128]{2,1,0:T(8,128)} fusion(f32[462,128,128]{2,1,0:T(8,128)} %constant_dynamic-update-slice_fusion, s32[1024]{0:T(1024)S(1)} %copy-done.98), kind=kCustom, calls=%fused_computation.1 | custom fusion | bytes 60819264 | tf_op jit(solution)/shard_map/gather | solution.py:384
  572.3 21.6 broadcast_select_fusion
  597.4 61.8 %psum.55 = f32[4,2,768]{2,1,0:T(2,128)S(1)} all-reduce(f32[4,2,768]{2,1,0:T(2,128)S(1)} %add_add_fusion.4), channel_id=1, replica_groups=mesh['dp'=16,'tensor'=2] {'dp'}, use_global_device_ids=true, to_apply=%region_41.44 | all-reduce | flops 6144 | bytes 49152 | tf_op jit(solution)/shard_map/psum | solution.py:386
  663.2 217.1 %reduce-scatter.2.cloned.1.call-done = f32[29,128,128]{2,1,0:T(8,128)} async-done(((f32[464,128,128]{2,1,0:T(8,128)}), f32[29,128,128]{2,1,0:T(8,128)}) %reduce-scatter.2.cloned.1.call-update) | async-done | bytes 1900560 | tf_op jit(solution)/shard_map/reduce_scatter | solution.py:383
  924.5 341.4 %custom-call.10 = f32[29,128,128]{2,1,0:T(8,128)} custom-call(f32[29,128,128]{2,1,0:T(8,128)} %fusion.17), custom_call_target="Cholesky" | custom-call | tf_op jit(solution)/shard_map/jit(cholesky)/cholesky | solution.py:312
  1266.0 6.5 fusion.201
  1279.1 341.6 %custom-call.8 = f32[29,128,128]{2,1,0:T(8,128)} custom-call(f32[29,128,128]{2,1,0:T(8,128)} %fusion.20), custom_call_target="Cholesky" | custom-call | tf_op jit(solution)/shard_map/jit(cholesky)/cholesky | solution.py:312
  1626.3 286.3 %custom-call.9 = f32[29,1,128,128]{2,3,1,0:T(8,128)} custom-call(f32[29,1,128,128]{3,2,1,0:T(8,128)} %get-tuple-element.132), custom_call_target="InvertDiagBlocksLowerTriangular" | custom-call | tf_op jit(solution)/shard_map/triangular_solve/custom-call.0 | solution.py:313
  1912.6 6.5 fusion.48
  1921.9 286.5 %custom-call.11 = f32[29,1,128,128]{2,3,1,0:T(8,128)} custom-call(f32[29,1,128,128]{3,2,1,0:T(8,128)} %get-tuple-element.131), custom_call_target="InvertDiagBlocksLowerTriangular" | custom-call | tf_op jit(solution)/shard_map/triangular_solve/custom-call.0 | solution.py:313
  2208.5 6.5 fusion.51
  (453 shorter events, 389.8 us)
Async XLA Ops:
  7.2 873.1 %copy-start = (f32[1,29,128,128]{3,2,1,0:T(8,128)S(1)}, f32[1,29,128,128]{3,2,1,0:T(8,128)}, u32[]{:S(2)}) copy-start(f32[1,29,128,128]{3,2,1,0:T(8,128)} %param.28) | copy-start | bytes 5701636
  7.2 6.4 copy-start.81
  7.2 7.0 copy-start.99
  7.2 123.5 %all-gather.2.cloned.1.call-start = ((), (), s32[]{:S(2)}) async-start(), calls=%async_computation.1 | async-start | bytes 16154624 | tf_op jit(solution)/shard_map/all_gather | solution.py:373
  10.0 203.0 %all-reduce.17.cloned.1.call-start = ((), (), s32[]{:S(2)}) async-start(), calls=%async_computation.2 | async-start | bytes 1572864 | tf_op jit(solution)/shard_map/psum | solution.py:173
  156.7 6.3 copy-start.33
  156.7 6.3 copy-start.3
  180.4 97.3 %all-reduce.19.cloned.1.call-start = ((), (), s32[]{:S(2)}) async-start(), calls=%async_computation.3 | async-start | bytes 393216 | tf_op jit(solution)/shard_map/psum | solution.py:173
  226.9 104.0 %all-reduce.21.cloned.1.call-start = ((), (), s32[]{:S(2)}) async-start(), calls=%async_computation.4 | async-start | bytes 1572864 | tf_op jit(solution)/shard_map/psum | solution.py:173
  283.5 8.0 copy-start.76
  284.2 6.1 copy-start.64
  296.3 113.2 %all-reduce.23.cloned.1.call-start = ((), (), s32[]{:S(2)}) async-start(), calls=%async_computation.5 | async-start | bytes 1572864 | tf_op jit(solution)/shard_map/psum | solution.py:179
  302.7 5.9 copy-start.101
  346.5 6.0 copy-start.63
  361.9 115.4 %all-reduce.25.cloned.1.call-start = ((), (), s32[]{:S(2)}) async-start(), calls=%async_computation.6 | async-start | bytes 393216 | tf_op jit(solution)/shard_map/psum | solution.py:179
  447.0 213.7 %all-reduce.27.cloned.1.call-start = ((), (), s32[]{:S(2)}) async-start(), calls=%async_computation.7 | async-start | bytes 1572864 | tf_op jit(solution)/shard_map/psum | solution.py:179
  505.5 374.7 %reduce-scatter.2.cloned.1.call-start = ((), (), s32[]{:S(2)}) async-start(), calls=%async_computation.8 | async-start | bytes 32309248 | tf_op jit(solution)/shard_map/reduce_scatter | solution.py:383
  529.3 8.1 slice-start
  531.5 5.9 slice-start.1
  537.4 6.0 slice-start.4
  548.9 23.4 %copy-start.103 = (pred[464]{0:T(512)(128)(4,1)S(1)}, pred[464]{0:T(512)(128)(4,1)}, u32[]{:S(2)}) copy-start(pred[464]{0:T(512)(128)(4,1)} %compare_reduce_fusion.2) | copy-start | bytes 1396
  594.0 65.2 %copy-start.82 = (f32[4,2,768]{2,1,0:T(2,128)S(1)}, f32[4,2,768]{2,1,0:T(2,128)}, u32[]{:S(2)}) copy-start(f32[4,2,768]{2,1,0:T(2,128)} %param.30) | copy-start | bytes 73732
  594.0 66.7 %copy-start.11 = (f32[4,128,768]{2,1,0:T(8,128)S(1)}, f32[4,128,768]{2,1,0:T(8,128)}, u32[]{:S(2)}) copy-start(f32[4,128,768]{2,1,0:T(8,128)} %copy-done.10) | copy-start | bytes 4718596
  1275.3 345.4 %copy-start.84 = (pred[128,128]{1,0:T(8,128)(4,1)S(1)}, pred[128,128]{1,0:T(8,128)(4,1)}, u32[]{:S(2)}) copy-start(pred[128,128]{1,0:T(8,128)(4,1)} %iota_compare_fusion.1) | copy-start | bytes 49156
  (96 other events, 234.7 us)
Sparse Core Ops, SparseCore 0:
  10.9 119.7 all-gather.1
  180.5 32.4 all-reduce.16
  227.0 22.3 all-reduce.18
  296.5 34.3 all-reduce.20
  362.0 34.3 all-reduce.22
  447.1 22.1 all-reduce.24
  505.7 34.1 all-reduce.26
  594.1 286.0 reduce-scatter.1
where the time goes:
time: 2240 us; the launch traced here: 2230 us
  other arithmetic  1340 us (60%)
  waiting for transfers between devices  355 us (16%)
  local copies, waits for them, and re-layouts  280 us (12%)
  matrix products  172 us (8%)
  blocking collectives  61.8 us (3%)
    another operation x5, other arithmetic, orthonormal(): factor = jnp.linalg.cholesky(gram)  687 us
    another operation x4, other arithmetic, orthonormal(): lax.linalg.triangular_solve(factor, columns, left_side=False, lower=True,...  576 us
    reduce_scatter x1, waiting for transfers between devices, per_device(): lax.psum_scatter(jnp.where(used_slot, packed[safe_order], 0.0), 'dp', sca...  217 us
    all_gather x1, waiting for transfers between devices, per_device(): lax.all_gather(weight_master[0].astype(jnp.bfloat16), 'dp', axis=0, tiled...  116 us
    psum x1, blocking collectives, per_device(): norm_total = lax.psum(norm_part, 'dp')  61.8 us
    unnamed x239, local copies, waits for them, and re-layouts  49.7 us
    transpose x12, local copies, waits for them, and re-layouts, block_grad(): jnp.einsum('rsia,rsjb->ijab', left_tiles, right_tiles, preferred_element_...  46.8 us
  transfers between devices with their start and end apart: 8, of which 4 were waited for; matrix products, arithmetic and copies ran while one was open for 12% of the time, Pallas kernels for 0%

commit v1 on v0

--- a/solution.py
+++ b/solution.py
@@ -1,6 +1,10 @@
+import functools
+
 import jax
 import jax.numpy as jnp
 from jax import lax
+from jax.experimental import pallas as pl
+from jax.experimental.pallas import tpu as pltpu
 from jax.sharding import PartitionSpec as P
 
 HEADS = 12
@@ -169,14 +173,22 @@
     )
 
 
+def tensor_sum(partial_sum):
+    mine = partial_sum.astype(jnp.bfloat16)
+    if lax.axis_size("tensor") != 2:
+        return lax.psum(mine, "tensor").astype(jnp.float32)
+    other = lax.ppermute(mine, "tensor", [(0, 1), (1, 0)])
+    return mine.astype(jnp.float32) + other.astype(jnp.float32)
+
+
 def finish_branch(partial_sum, residual, normalize):
-    total = lax.psum(partial_sum.astype(jnp.bfloat16), "tensor").astype(jnp.float32)
+    total = tensor_sum(partial_sum)
     summed = residual + total
     return (summed, normalize(summed))
 
 
 def back_sum(partial_sum):
-    return lax.psum(partial_sum.astype(jnp.bfloat16), "tensor").astype(jnp.float32)
+    return tensor_sum(partial_sum)
 
 
 def layer_rows(
@@ -307,12 +319,112 @@
     return jnp.swapaxes(block_matrix, -1, -2)
 
 
-def orthonormal(columns):
-    gram = times(flipped(columns), columns)
-    factor = jnp.linalg.cholesky(gram)
-    return lax.linalg.triangular_solve(
-        factor, columns, left_side=False, lower=True, transpose_a=True
-    )
+f32=jnp.float32; bf16=jnp.bfloat16
+
+def split3(a):
+    h=a.astype(bf16); r=a-h.astype(f32); m=r.astype(bf16); l=(r-m.astype(f32)).astype(bf16)
+    return h,m,l
+def split2(a):
+    h=a.astype(bf16); return h,(a-h.astype(f32)).astype(bf16)
+def mm(a,b,dims):
+    return lax.dot_general(a,b,(dims,((),())),preferred_element_type=f32)
+NN=((1,),(0,)); NT=((1,),(1,)); TN=((0,),(0,))
+def dot3(a,b,dims):
+    ah,al=split2(a); bh,bl=split2(b)
+    return mm(ah,bh,dims)+(mm(ah,bl,dims)+mm(al,bh,dims))
+def gram6(p):
+    h,m,l=split3(p)
+    hh=mm(h,h,TN); mmm=mm(m,m,TN); hm=mm(h,m,TN)+mm(h,l,TN)
+    return hh+(mmm+(hm+hm.T))
+
+PB=16
+def panel_steps(x, kb, g):
+    base=kb*PB
+    lane=lax.broadcasted_iota(jnp.int32,(1,8,128),2)
+    sub=lax.broadcasted_iota(jnp.int32,(1,8,128),1)
+    halves=[x[:,:8],x[:,8:]]
+    rinvs=[]
+    for s in range(PB):
+        k=base+s
+        hs=s//8; r=s%8
+        cur=halves[hs]
+        row=cur[:,r:r+1,:]
+        piv=cur[:,r:r+1,k:k+1]
+        rinv=1.0/piv
+        rinvs.append(rinv)
+        scaled=jnp.where(lane[:,:1]==k,1.0,row)*rinv
+        for h in range(hs,2):
+            y=halves[h]
+            col=jnp.broadcast_to(y[:,:,k:k+1],y.shape)
+            if h==hs:
+                low=(sub>r)
+                col=jnp.where(low,col,0.0)
+                y=jnp.where((lane==k)&(sub>r),0.0,y)
+                y=jnp.where((lane==k)&(sub==r),1.0,y)
+            else:
+                y=jnp.where(lane==k,0.0,y)
+            halves[h]=y-col*scaled
+    return jnp.concatenate(halves,axis=1), jnp.concatenate(rinvs,axis=1)
+
+def ortho_body(n_pad, n, g, s_ref,b_ref,q_ref,a_ref,p_ref,d_ref):
+    def first(i,c):
+        p=dot3(s_ref[i],b_ref[i],NN)
+        p_ref[i]=p
+        a_ref[i]=gram6(p)
+        return c
+    lax.fori_loop(0,n,first,0)
+    eye=(lax.broadcasted_iota(jnp.int32,(128,128),0)==lax.broadcasted_iota(jnp.int32,(128,128),1)).astype(f32)
+    for i in range(n,n_pad):
+        a_ref[i]=eye
+    lane=lax.broadcasted_iota(jnp.int32,(1,PB,128),2)
+    sub=lax.broadcasted_iota(jnp.int32,(1,PB,128),1)
+    for kb in range(128//PB):
+        base=kb*PB; end=base+PB
+        def group(gi,c):
+            i0=gi*g
+            x=a_ref[pl.ds(i0,g),base:end,:]
+            x,rinv=panel_steps(x,kb,g)
+            w=jnp.where((lane>=base)&(lane<end)&(lane-base>sub),0.0,x)
+            d_ref[pl.ds(i0,g),base:end,:]=jnp.broadcast_to(rinv,x.shape)
+            a_ref[pl.ds(i0,g),base:end,:]=w
+            if end<128:
+                u=jnp.where(lane>=end,x*rinv,0.0)
+                wh,wm,wl=split3(w); uh,um,ul=split3(u)
+                lhs=jnp.concatenate([uh,uh,um,uh,ul,um],axis=1)
+                rhs=jnp.concatenate([wh,wm,wh,wl,wh,wm],axis=1)
+                lane2=lax.broadcasted_iota(jnp.int32,(128-end,128),1)
+                inside=(lane2>=base)&(lane2<end)
+                for j in range(g):
+                    upd=mm(lhs[j],rhs[j],TN)
+                    old=a_ref[i0+j,end:,:]
+                    a_ref[i0+j,end:,:]=jnp.where(inside,0.0,old)-upd[end:,:]
+            return c
+        lax.fori_loop(0,n_pad//g,group,0)
+    ii=lax.broadcasted_iota(jnp.int32,(128,128),0); jj=lax.broadcasted_iota(jnp.int32,(128,128),1)
+    def last(i,c):
+        inv=jnp.where(ii>=jj,a_ref[i],0.0)*jnp.sqrt(d_ref[i])
+        q_ref[i]=dot3(p_ref[i],inv,NT)
+        return c
+    lax.fori_loop(0,n,last,0)
+
+def ortho(s,b,g=29):
+    n=s.shape[0]; n_pad=-(-n//g)*g
+    return pl.pallas_call(
+        functools.partial(ortho_body,n_pad,n,g),
+        out_shape=jax.ShapeDtypeStruct(s.shape,f32),
+        in_specs=[pl.BlockSpec(memory_space=pltpu.VMEM)]*2,
+        out_specs=pl.BlockSpec(memory_space=pltpu.VMEM),
+        scratch_shapes=[pltpu.VMEM((n_pad,128,128),f32),pltpu.VMEM((n,128,128),f32),pltpu.VMEM((n_pad,128,128),f32)],
+        compiler_params=pltpu.CompilerParams(vmem_limit_bytes=50*1024*1024),
+    )(s,b)
+
+
+def orthonormal_pair(left_new, left_bases, right_new, right_bases):
+    count = left_new.shape[0]
+    both = ortho(
+        jnp.concatenate([left_new, right_new]), jnp.concatenate([left_bases, right_bases]), count
+    )
+    return both[:count], both[count:]
 
 
 def rotated_update(
@@ -336,8 +448,7 @@
         second_new,
         left_new,
         right_new,
-        orthonormal(times(left_new, left_bases)),
-        orthonormal(times(right_new, right_bases)),
+        *orthonormal_pair(left_new, left_bases, right_new, right_bases),
     )
 
 
@@ -381,8 +492,11 @@
         hidden, image, segment_ids, cotangent, weights, norm_params, heads_local, scale, block_side
     )
     owned = lax.psum_scatter(
-        jnp.where(used_slot, packed[safe_order], 0.0), "dp", scatter_dimension=0, tiled=True
-    )
+        jnp.where(used_slot, packed.astype(jnp.bfloat16)[safe_order], 0.0),
+        "dp",
+        scatter_dimension=0,
+        tiled=True,
+    ).astype(jnp.float32)
     norm_total = lax.psum(norm_part, "dp")
     updated = rotated_update(
         owned,

time: 2240 us -> 787 us (0.35)
  other arithmetic: 1340 us -> 66.6 us
  waiting for transfers between devices: 355 us -> 194 us
  Pallas kernels: 0 us -> 88.6 us
  matrix products: 172 us -> 117 us
  local copies, waits for them, and re-layouts: 280 us -> 225 us
    another operation x9 -> x0, other arithmetic: 1260 us -> none  [the longest x5 687 us: orthonormal(): factor = jnp.linalg.cholesky(gram)]
    reduce_scatter x1, waiting for transfers between devices: 217 us -> 77.9 us  [per_device(): lax.psum_scatter(jnp.where(used_slot, packed.astype(jnp.bfloat16)[safe_or...]
    pallas_call x0 -> x1, Pallas kernels: none -> 88.6 us  [ortho(): pl.pallas_call(functools.partial(ortho_body, n_pad, n, g), out_shape=jax....]
    dot_general x10 -> x6, matrix products: 38.4 us -> 14.3 us  [times(): jnp.einsum('...ij,...jk->...ik', left_matrix, right_matrix, precision=hig...]
    unnamed x239 -> x277, local copies, waits for them, and re-layouts: 49.7 us -> 37.5 us
  transfers between devices with their start and end apart: 8 -> 8, of which waited for: 4 -> 3; matrix products, arithmetic and copies ran while one was open for 12% -> 24% of each run, Pallas kernels for 0% -> 0%
where the time goes in v1:
time: 787 us; the launch traced here: 775 us
  local copies, waits for them, and re-layouts  225 us (29%)
  waiting for transfers between devices  194 us (25%)
  matrix products  117 us (15%)
  Pallas kernels  88.6 us (11%)
  other arithmetic  66.6 us (8%)
  blocking collectives  60 us (8%)
  between operations  16.1 us (2%)
    all_gather x1, waiting for transfers between devices, per_device(): lax.all_gather(weight_master[0].astype(jnp.bfloat16), 'dp', axis=0, tiled...  116 us
    pallas_call x1, Pallas kernels, ortho(): pl.pallas_call(functools.partial(ortho_body, n_pad, n, g), out_shape=jax....  88.6 us
    reduce_scatter x1, waiting for transfers between devices, per_device(): lax.psum_scatter(jnp.where(used_slot, packed.astype(jnp.bfloat16)[safe_or...  77.9 us
    psum x1, blocking collectives, per_device(): norm_total = lax.psum(norm_part, 'dp')  60 us
    unnamed x277, local copies, waits for them, and re-layouts  37.5 us
    dot_general x12, matrix products, block_grad(): jnp.einsum('rsia,rsjb->ijab', left_tiles, right_tiles, preferred_element_...  34.6 us
    reshape x11, local copies, waits for them, and re-layouts, unpack_blocks(): portion.transpose(0, 2, 1, 3).reshape(rows_count, cols_count)  32.4 us
    transpose x12, local copies, waits for them, and re-layouts, block_grad(): jnp.einsum('rsia,rsjb->ijab', left_tiles, right_tiles, preferred_element_...  28.9 us
  transfers between devices with their start and end apart: 8, of which 3 were waited for; matrix products, arithmetic and copies ran while one was open for 24% of the time, Pallas kernels for 0%

profile of v1, /device:TPU:0, one launch (start us, length us, event | category | flops | bytes accessed | tf_op | source)
XLA Modules:
  0.0 774.9 jit_solution(11194274556179611157)
XLA Ops:
  14.9 115.8 %all-gather.2.cloned.1.call-done = bf16[464,128,128]{2,1,0:T(8,128)(2,1)} async-done(((bf16[29,128,128]{2,1,0:T(8,128)(2,1)}), bf16[464,128,128]{2,1,0:T(8,128)(2,1)}) %all-gather.2.cloned.1.call-update) | async-done | bytes 15204368 | tf_op jit(solution)/shard_map/all_gather | solution.py:484
  130.7 18.9 %gather_fusion = bf16[462,128,128]{2,1,0:T(8,128)(2,1)} fusion(bf16[464,128,128]{2,1,0:T(8,128)(2,1)} %all-gather.2.cloned.1.call-done, s32[1024]{0:T(1024)S(1)} %pad_clamp_fusion.1), kind=kCustom, calls=%fused_computation | custom fusion | bytes 30279480 | tf_op jit(solution)/shard_map/gather | solution.py:486
  184.8 4.8 fusion.57
  205.3 18.5 %fusion.195 = (bf16[72,128,128]{2,1,0:T(8,128)(2,1)}, bf16[72,128,128]{2,1,0:T(8,128)(2,1)S(1)}, bf16[72,128,128]{2,1,0:T(8,128)(2,1)}, bf16[72,128,128]{2,1,0:T(8,128)(2,1)}) fusion(bf16[462,128,128]{2,1,0:T(8,128)(2,1)} %gather_fusion), kind=kLoop, calls=%fused_computation.366 | loop fusion | bytes 18874368 | tf_op jit(solution)/shard_map/slice | solution.py:54
  227.0 5.4 reshape.597
  232.5 5.1 copy.454
  237.5 6.0 reshape.598
  243.5 4.9 copy.457
  248.5 5.4 reshape.595
  253.9 5.1 copy.456
  258.9 6.0 reshape.596
  273.3 6.1 multiply_convert_fusion
  294.3 5.6 reshape.538
  321.8 5.0 add_convert_fusion
  353.5 4.5 fusion.9
  381.5 7.5 fusion.77
  391.1 7.7 convolution_convert_fusion.1
  409.6 5.3 fusion.43
  417.2 5.3 fusion.46
  472.2 18.8 %gather_fusion.1 = bf16[464,128,128]{2,1,0:T(8,128)(2,1)} fusion(bf16[462,128,128]{2,1,0:T(8,128)(2,1)} %constant_dynamic-update-slice_fusion, s32[1024]{0:T(1024)S(1)} %copy-done.128), kind=kCustom, calls=%fused_computation.1 | custom fusion | bytes 30410560 | tf_op jit(solution)/shard_map/gather | solution.py:495
  491.1 11.4 %broadcast_select_fusion = bf16[464,128,128]{2,1,0:T(8,128)(2,1)} fusion(bf16[464,128,128]{2,1,0:T(8,128)(2,1)} %gather_fusion.1, pred[464]{0:T(512)(128)(4,1)S(1)} %copy-done.131), kind=kLoop, calls=%fused_computation.5 | loop fusion | flops 7602176 | bytes 30409168 | tf_op jit(solution)/shard_map/jit(_where)/select_n | solution.py:495
  512.0 60.0 %psum.7 = f32[4,2,768]{2,1,0:T(2,128)S(1)} all-reduce(f32[4,2,768]{2,1,0:T(2,128)S(1)} %add_add_fusion.10), channel_id=1, replica_groups=mesh['dp'=16,'tensor'=2] {'dp'}, use_global_device_ids=true, to_apply=%region_33.34 | all-reduce | flops 6144 | bytes 49152 | tf_op jit(solution)/shard_map/psum | solution.py:500
  576.3 77.9 %reduce-scatter.2.cloned.1.call-done = bf16[29,128,128]{2,1,0:T(8,128)(2,1)} async-done(((bf16[464,128,128]{2,1,0:T(8,128)(2,1)}), bf16[29,128,128]{2,1,0:T(8,128)(2,1)}) %reduce-scatter.2.cloned.1.call-update) | async-done | bytes 950288 | tf_op jit(solution)/shard_map/reduce_scatter | solution.py:494
  676.6 88.6 %shard_map.246 = f32[58,128,128]{2,1,0:T(8,128)S(1)} custom-call(f32[58,128,128]{2,1,0:T(8,128)} %pad_maximum_fusion.s_ref, f32[58,128,128]{2,1,0:T(8,128)} %pad_maximum_fusion.1.b_ref), custom_call_target="tpu_custom_call" | custom-call | tf_op jit(solution)/shard_map/pallas_call | solution.py:412
  (466 shorter events, 259.2 us)
Async XLA Ops:
  7.2 6.3 copy-start.92
  7.2 7.0 copy-start.129
  7.2 123.5 %all-gather.2.cloned.1.call-start = ((), (), s32[]{:S(2)}) async-start(), calls=%async_computation.1 | async-start | bytes 16154624 | tf_op jit(solution)/shard_map/all_gather | solution.py:484
  9.9 644.3 %reduce-scatter.2.cloned.1.call-start = ((), (), s32[]{:S(2)}) async-start(), calls=%async_computation.2 | async-start | bytes 16154624 | tf_op jit(solution)/shard_map/reduce_scatter | solution.py:494
  14.2 183.4 %copy-start.97 = (f32[768]{0:T(1024)}, f32[768]{0:T(1024)S(1)}, u32[]{:S(2)}) copy-start(f32[768]{0:T(1024)S(1)} %get-tuple-element.38) | copy-start | bytes 9220
  156.5 4.5 copy-start.25
  156.5 4.5 copy-start.42
  159.5 6.2 copy-start.27
  171.2 24.1 %collective-permute-start = (bf16[4,128,768]{2,1,0:T(8,128)(2,1)}, bf16[4,128,768]{2,1,0:T(8,128)(2,1)}, u32[]{:S(2)}, u32[]{:S(2)}) collective-permute-start(bf16[4,128,768]{2,1,0:T(8,128)(2,1)} %convolution_convert_fusion.4), channel_id=1, source_target_pairs={{0,1},{1,0},{2,3},{3,2},{4,5},{5,4},{6,7},{7,6},{8,9},{9,8},{10,11... | collective-permute-start | bytes 2359304 | tf_op jit(solution)/shard_map/ppermute | solution.py:180
  202.5 21.2 %copy-start.50 = (bf16[4,32,6,64]{3,2,1,0:T(8,128)(2,1)}, bf16[4,32,6,64]{3,2,1,0:T(8,128)(2,1)S(1)}, u32[]{:S(2)}) copy-start(bf16[4,32,6,64]{3,2,1,0:T(8,128)(2,1)S(1)} %copy.181) | copy-start | bytes 294916
  204.8 61.6 %collective-permute-start.1 = (bf16[4,32,768]{2,1,0:T(8,128)(2,1)}, bf16[4,32,768]{2,1,0:T(8,128)(2,1)}, u32[]{:S(2)}, u32[]{:S(2)}) collective-permute-start(bf16[4,32,768]{2,1,0:T(8,128)(2,1)} %convolution_convert_fusion.17), channel_id=1, source_target_pairs={{0,1},{1,0},{2,3},{3,2},{4,5},{5,4},{6,7},{7,6},{8,9},{9,8},{10,11... | collective-permute-start | bytes 589832 | tf_op jit(solution)/shard_map/ppermute | solution.py:180
  272.5 8.0 %copy-start.79 = (f32[4,32,1536]{2,1,0:T(8,128)}, f32[4,32,1536]{2,1,0:T(8,128)S(1)}, u32[]{:S(2)}) copy-start(f32[4,32,1536]{2,1,0:T(8,128)S(1)} %get-tuple-element.90) | copy-start | bytes 2359300
  273.3 6.1 copy-start.58
  285.4 19.5 %collective-permute-start.2 = (bf16[4,128,768]{2,1,0:T(8,128)(2,1)}, bf16[4,128,768]{2,1,0:T(8,128)(2,1)}, u32[]{:S(2)}, u32[]{:S(2)}) collective-permute-start(bf16[4,128,768]{2,1,0:T(8,128)(2,1)} %pad_maximum_fusion.4), channel_id=1, source_target_pairs={{0,1},{1,0},{2,3},{3,2},{4,5},{5,4},{6,7},{7,6},{8,9},{9,8},{10,11... | collective-permute-start | bytes 2359304 | tf_op jit(solution)/shard_map/ppermute | solution.py:180
  321.8 5.0 copy-start.57
  329.7 43.8 %collective-permute-start.3 = (bf16[4,128,768]{2,1,0:T(8,128)(2,1)}, bf16[4,128,768]{2,1,0:T(8,128)(2,1)}, u32[]{:S(2)}, u32[]{:S(2)}) collective-permute-start(bf16[4,128,768]{2,1,0:T(8,128)(2,1)} %pad_maximum_fusion.6), channel_id=1, source_target_pairs={{0,1},{1,0},{2,3},{3,2},{4,5},{5,4},{6,7},{7,6},{8,9},{9,8},{10,11... | collective-permute-start | bytes 2359304 | tf_op jit(solution)/shard_map/ppermute | solution.py:180
  391.1 10.6 %copy-start.66 = (bf16[4,32,768]{2,1,0:T(8,128)(2,1)S(1)}, bf16[4,32,768]{2,1,0:T(8,128)(2,1)}, u32[]{:S(2)}) copy-start(bf16[4,32,768]{2,1,0:T(8,128)(2,1)} %copy-done.65) | copy-start | bytes 589828
  404.8 26.0 %collective-permute-start.4 = (bf16[4,32,768]{2,1,0:T(8,128)(2,1)}, bf16[4,32,768]{2,1,0:T(8,128)(2,1)}, u32[]{:S(2)}, u32[]{:S(2)}) collective-permute-start(bf16[4,32,768]{2,1,0:T(8,128)(2,1)} %convolution_convert_fusion.13), channel_id=1, source_target_pairs={{0,1},{1,0},{2,3},{3,2},{4,5},{5,4},{6,7},{7,6},{8,9},{9,8},{10,11... | collective-permute-start | bytes 589832 | tf_op jit(solution)/shard_map/ppermute | solution.py:180
  472.2 18.8 %copy-start.131 = (pred[464]{0:T(512)(128)(4,1)S(1)}, pred[464]{0:T(512)(128)(4,1)}, u32[]{:S(2)}) copy-start(pred[464]{0:T(512)(128)(4,1)} %compare_reduce_fusion) | copy-start | bytes 1396
  506.9 66.6 %collective-permute-start.5 = (bf16[4,128,768]{2,1,0:T(8,128)(2,1)}, bf16[4,128,768]{2,1,0:T(8,128)(2,1)}, u32[]{:S(2)}, u32[]{:S(2)}) collective-permute-start(bf16[4,128,768]{2,1,0:T(8,128)(2,1)} %add_convert_fusion.1), channel_id=1, source_target_pairs={{0,1},{1,0},{2,3},{3,2},{4,5},{5,4},{6,7},{7,6},{8,9},{9,8},{10,11... | collective-permute-start | bytes 2359304 | tf_op jit(solution)/shard_map/ppermute | solution.py:180
  508.5 63.6 %copy-start.93 = (f32[4,2,768]{2,1,0:T(2,128)S(1)}, f32[4,2,768]{2,1,0:T(2,128)}, u32[]{:S(2)}) copy-start(f32[4,2,768]{2,1,0:T(2,128)} %param.27) | copy-start | bytes 73732
  510.8 62.7 %copy-start.5 = (f32[4,128,768]{2,1,0:T(8,128)S(1)}, f32[4,128,768]{2,1,0:T(8,128)}, u32[]{:S(2)}) copy-start(f32[4,128,768]{2,1,0:T(8,128)} %copy-done.4) | copy-start | bytes 4718596
  510.8 62.7 %copy-start.115 = (f32[4,128]{1,0:T(4,128)S(1)}, f32[4,128]{1,0:T(4,128)}, u32[]{:S(2)}) copy-start(f32[4,128]{1,0:T(4,128)} %copy-done.114) | copy-start | bytes 6148
  670.7 94.5 %copy-start.19 = (f32[29,128,128]{2,1,0:T(8,128)}, f32[29,128,128]{2,1,0:T(8,128)S(1)}, u32[]{:S(2)}) copy-start(f32[29,128,128]{2,1,0:T(8,128)S(1)} %bitcast_subtract_fusion) | copy-start | bytes 5701636
  (116 other events, 259.4 us)
Sparse Core Ops, SparseCore 0:
  10.9 119.7 all-gather.1
  502.6 151.5 reduce-scatter.1

commit v2 on v1

v2 whole, which is shorter than its diff:
```python
import functools

import jax
import jax.numpy as jnp
from jax import lax
from jax.experimental import pallas as pl
from jax.experimental.pallas import tpu as pltpu
from jax.sharding import PartitionSpec as P

HEADS = 12
FF = 3072
NQ = 32
STEP = 10


beta_first = 0.9
beta_second = 0.999
beta_stats = 0.95
adam_epsilon = 1e-08
norm_epsilon = 1e-06
matrix_rate = 0.03
matrix_decay = 0.05
norm_rate = 0.6
masked_score = -1000000000.0
highest = lax.Precision.HIGHEST


TILE = 128
PATCHES_PAD = 16
f32 = jnp.float32
bf16 = jnp.bfloat16
NN = ((1,), (0,))
NT = ((1,), (1,))
TN = ((0,), (0,))
VMEM_BYTES = 56 * 1024 * 1024


def mm(left, right, dims):
    return lax.dot_general(left, right, (dims, ((), ())), preferred_element_type=f32)


def vmem_specs(count):
    return [pl.BlockSpec(memory_space=pltpu.VMEM)] * count


def any_specs(count):
    return [pl.BlockSpec(memory_space=pl.ANY)] * count


def vmem_params():
    return pltpu.CompilerParams(vmem_limit_bytes=VMEM_BYTES)


def cost(flops, bytes_accessed, transcendentals=0):
    return pl.CostEstimate(
        flops=int(flops), bytes_accessed=int(bytes_accessed), transcendentals=int(transcendentals)
    )


def matrix_of(blocks_ref, row_first, row_count, col_first, col_count, col_total, base=0):
    rows = []
    for row in range(row_count):
        first = base + (row_first + row) * col_total + col_first
        rows.append(
            jnp.concatenate([blocks_ref[first + col] for col in range(col_count)], axis=1)
        )
    return jnp.concatenate(rows, axis=0)


def norm_forward(resid):
    center = resid - jnp.mean(resid, axis=-1, keepdims=True)
    inverse = lax.rsqrt(jnp.mean(center * center, axis=-1, keepdims=True) + norm_epsilon)
    return center * inverse, inverse


def norm_backward(resid, upstream, gain):
    unit, inverse = norm_forward(resid)
    scaled = upstream * gain
    mean_scaled = jnp.mean(scaled, axis=-1, keepdims=True)
    mean_product = jnp.mean(scaled * unit, axis=-1, keepdims=True)
    grad = inverse * (scaled - mean_scaled - unit * mean_product)
    gain_grad = jnp.sum(upstream * unit, axis=0, keepdims=True)
    shift_grad = jnp.sum(upstream, axis=0, keepdims=True)
    return grad, gain_grad, shift_grad


def head_pair(tile):
    low_half = lax.broadcasted_iota(jnp.int32, tile.shape, 1) < TILE // 2
    zero = jnp.zeros_like(tile)
    return jnp.concatenate(
        [jnp.where(low_half, tile, zero), jnp.where(low_half, zero, tile)], axis=0
    )


def side_by_side(stacked):
    half = stacked.shape[0] // 2
    return jnp.concatenate([stacked[:half], stacked[half:]], axis=1)


def pair_probs(queries, keys, allowed, scale):
    scores = mm(head_pair(queries), keys, NT) * scale
    scores = jnp.where(allowed, scores, masked_score)
    weights = jnp.exp(scores - jnp.max(scores, axis=-1, keepdims=True))
    return weights / jnp.sum(weights, axis=-1, keepdims=True)


def pair_mix(probs, values):
    count = probs.shape[0] // 2
    low_half = lax.broadcasted_iota(jnp.int32, (count, TILE), 1) < TILE // 2
    mixed = mm(probs.astype(bf16), values, NN)
    return jnp.where(low_half, mixed[:count], mixed[count:]).astype(bf16)


def pair_backward(queries, keys, values, probs, mixed_grad, scale):
    grad_pair = head_pair(mixed_grad)
    value_grad = mm(probs.astype(bf16), grad_pair, TN).astype(bf16)
    prob_grad = mm(grad_pair, values, NT)
    inner = jnp.sum(probs * prob_grad, axis=-1, keepdims=True)
    score_grad = (probs * (prob_grad - inner) * scale).astype(bf16)
    count = queries.shape[0]
    low_half = lax.broadcasted_iota(jnp.int32, (count, TILE), 1) < TILE // 2
    both = mm(score_grad, keys, NN)
    query_grad = jnp.where(low_half, both[:count], both[count:]).astype(bf16)
    key_grad = mm(score_grad, head_pair(queries), TN).astype(bf16)
    return query_grad, key_grad, value_grad


def load_blocks(source, first, count, target, semaphore):
    copy = pltpu.make_async_copy(source.at[pl.ds(first, count)], target, semaphore)
    copy.start()
    return copy


class Plan:
    def __init__(self, rows, seq, width, image_width, patches, heads, hidden_units):
        self.rows, self.seq, self.width = rows, seq, width
        self.image_width, self.heads, self.hidden = image_width, heads, hidden_units
        self.half = heads * (TILE // 2)
        self.patches = patches
        self.keys = -(-patches // PATCHES_PAD) * PATCHES_PAD
        self.wt, self.ht = width // TILE, self.half // TILE
        self.it, self.ft = image_width // TILE, hidden_units // TILE
        square, cross, feed = self.wt * self.ht, self.it * self.ht, self.wt * self.ft
        self.square, self.cross, self.feed = square, cross, feed
        self.self_first, self.self_count = 0, 4 * square
        self.cross_first, self.cross_count = 4 * square, 2 * square + 2 * cross
        self.query_first = self.cross_first + self.cross_count
        self.text_first = self.query_first + 2 * feed
        self.block_count = self.text_first + 2 * feed
        self.tokens = rows * seq
        self.learned = rows * NQ
        self.texts = rows * (seq - NQ)


def self_forward_body(plan, scale, nat, hidden, seg_row, seg_col, qkv, probs, mixed, part, w, sem):
    copy = load_blocks(nat, plan.self_first, plan.self_count, w, sem)
    copy.wait()
    for piece in range(3):
        matrix = matrix_of(w, 0, plan.wt, 0, plan.ht, plan.ht, piece * plan.square)
        qkv[piece] = mm(hidden[...], matrix, NN).astype(bf16)

    def one(row, carry):
        place = pl.ds(pl.multiple_of(row * plan.seq, plan.seq), plan.seq)
        allowed = seg_col[row] == seg_row[row]
        allowed = jnp.concatenate([allowed, allowed], axis=0)
        for tile in range(plan.ht):
            cols = slice(tile * TILE, (tile + 1) * TILE)
            found = pair_probs(qkv[0, place, cols], qkv[1, place, cols], allowed, scale)
            probs[row, tile] = found
            mixed[place, cols] = pair_mix(found, qkv[2, place, cols])
        return carry

    lax.fori_loop(0, plan.rows, one, 0)
    matrix = matrix_of(w, 0, plan.ht, 0, plan.wt, plan.wt, 3 * plan.square)
    part[...] = mm(mixed[...], matrix, NN).astype(bf16)


def self_forward(plan, scale, nat, hidden, seg_row, seg_col):
    tokens, half, width = plan.tokens, plan.half, plan.width
    return pl.pallas_call(
        functools.partial(self_forward_body, plan, scale),
        out_shape=(
            jax.ShapeDtypeStruct((3, tokens, half), bf16),
            jax.ShapeDtypeStruct((plan.rows, plan.ht, 2 * plan.seq, plan.seq), f32),
            jax.ShapeDtypeStruct((tokens, half), bf16),
            jax.ShapeDtypeStruct((tokens, width), bf16),
        ),
        in_specs=any_specs(1) + vmem_specs(3),
        out_specs=tuple(vmem_specs(4)),
        scratch_shapes=[
            pltpu.VMEM((plan.self_count, TILE, TILE), bf16),
            pltpu.SemaphoreType.DMA,
        ],
        compiler_params=vmem_params(),
        cost_estimate=cost(2 * tokens * width * half * 4, 8e6),
        name="self_forward",
    )(nat, hidden, seg_row, seg_col)


def image_body(plan, nat, image, keys, values, w, sem):
    copy = load_blocks(nat, plan.cross_first + plan.square, 2 * plan.cross, w, sem)
    copy.wait()
    for piece, target in ((0, keys), (1, values)):
        matrix = matrix_of(w, 0, plan.it, 0, plan.ht, plan.ht, piece * plan.cross)

        def one(row, carry):
            place = pl.ds(pl.multiple_of(row * plan.keys, plan.keys), plan.keys)
            target[place, :] = mm(image[place, :], matrix, NN).astype(bf16)
            return carry

        lax.fori_loop(0, plan.rows, one, 0)


def image_forward(plan, nat, image):
    total = plan.rows * plan.keys
    return pl.pallas_call(
        functools.partial(image_body, plan),
        out_shape=(jax.ShapeDtypeStruct((total, plan.half), bf16),) * 2,
        in_specs=any_specs(1) + vmem_specs(1),
        out_specs=tuple(vmem_specs(2)),
        scratch_shapes=[
            pltpu.VMEM((2 * plan.cross, TILE, TILE), bf16),
            pltpu.SemaphoreType.DMA,
        ],
        compiler_params=vmem_params(),
        cost_estimate=cost(4 * total * plan.image_width * plan.half, 8e6),
        name="image_forward",
    )(nat, image)


def cross_forward_body(
    plan, scale, nat, hidden, mine, other, params, image_keys, image_values,
    resid, first_query, first_text, low_query, low_text, queries, probs, mixed, part, w, sem,
):
    copy = load_blocks(nat, plan.cross_first, plan.cross_count, w, sem)
    gain, shift = params[0, 0:1], params[0, 1:2]
    text = plan.seq - NQ

    def one_norm(row, carry):
        place = pl.ds(pl.multiple_of(row * plan.seq, plan.seq), plan.seq)
        summed = hidden[place, :].astype(f32) + (
            mine[place, :].astype(f32) + other[place, :].astype(f32)
        )
        resid[place, :] = summed
        first = norm_forward(summed)[0] * gain + shift
        query_place = pl.ds(pl.multiple_of(row * NQ, NQ), NQ)
        text_place = pl.ds(pl.multiple_of(row * text, text), text)
        first_query[query_place, :] = first[:NQ]
        first_text[text_place, :] = first[NQ:]
        low_query[query_place, :] = first[:NQ].astype(bf16)
        low_text[text_place, :] = first[NQ:].astype(bf16)
        return carry

    lax.fori_loop(0, plan.rows, one_norm, 0)
    copy.wait()
    matrix = matrix_of(w, 0, plan.wt, 0, plan.ht, plan.ht)
    queries[...] = mm(low_query[...], matrix, NN).astype(bf16)
    allowed = lax.broadcasted_iota(jnp.int32, (2 * NQ, plan.keys), 1) < plan.patches

    def one(row, carry):
        query_place = pl.ds(pl.multiple_of(row * NQ, NQ), NQ)
        place = pl.ds(pl.multiple_of(row * plan.keys, plan.keys), plan.keys)
        for tile in range(plan.ht):
            cols = slice(tile * TILE, (tile + 1) * TILE)
            found = pair_probs(queries[query_place, cols], image_keys[place, cols], allowed, scale)
            probs[row, tile] = found
            mixed[query_place, cols] = pair_mix(found, image_values[place, cols])
        return carry

    lax.fori_loop(0, plan.rows, one, 0)
    matrix = matrix_of(w, 0, plan.ht, 0, plan.wt, plan.wt, plan.square + 2 * plan.cross)
    part[...] = mm(mixed[...], matrix, NN).astype(bf16)


def cross_forward(plan, scale, nat, hidden, mine, other, params, image_keys, image_values):
    learned, texts, width, half = plan.learned, plan.texts, plan.width, plan.half
    return pl.pallas_call(
        functools.partial(cross_forward_body, plan, scale),
        out_shape=(
            jax.ShapeDtypeStruct((plan.tokens, width), f32),
            jax.ShapeDtypeStruct((learned, width), f32),
            jax.ShapeDtypeStruct((texts, width), f32),
            jax.ShapeDtypeStruct((learned, width), bf16),
            jax.ShapeDtypeStruct((texts, width), bf16),
            jax.ShapeDtypeStruct((learned, half), bf16),
            jax.ShapeDtypeStruct((plan.rows, plan.ht, 2 * NQ, plan.keys), f32),
            jax.ShapeDtypeStruct((learned, half), bf16),
            jax.ShapeDtypeStruct((learned, width), bf16),
        ),
        in_specs=any_specs(1) + vmem_specs(6),
        out_specs=tuple(vmem_specs(9)),
        scratch_shapes=[
            pltpu.VMEM((plan.cross_count, TILE, TILE), bf16),
            pltpu.SemaphoreType.DMA,
        ],
        compiler_params=vmem_params(),
        cost_estimate=cost(4 * learned * width * half, 1.2e7),
        name="cross_forward",
    )(nat, hidden, mine, other, params, image_keys, image_values)


def gelu_parts(values):
    normal = 0.5 * (1.0 + lax.erf(values * 0.7071067811865476))
    density = 0.3989422804014327 * jnp.exp(-0.5 * values * values)
    return values * normal, normal + values * density


def feed_forward_tail(plan, states_low, w, gated, slope, part):
    def one_up(chunk, carry):
        matrix = matrix_of(w, 0, plan.wt, chunk * 2, 2, plan.ft)
        active, derivative = gelu_parts(mm(states_low[...], matrix, NN))
        cols = pl.ds(pl.multiple_of(chunk * 2 * TILE, 2 * TILE), 2 * TILE)
        gated[:, cols] = active.astype(bf16)
        slope[:, cols] = derivative
        return carry

    lax.fori_loop(0, plan.ft // 2, one_up, 0)

    def one_down(chunk, carry):
        matrix = matrix_of(w, 0, plan.ft, chunk * 2, 2, plan.wt, plan.feed)
        cols = pl.ds(pl.multiple_of(chunk * 2 * TILE, 2 * TILE), 2 * TILE)
        part[:, cols] = mm(gated[...], matrix, NN).astype(bf16)
        return carry

    lax.fori_loop(0, plan.wt // 2, one_down, 0)


def text_forward_body(plan, nat, low_text, gated, slope, part, w, sem):
    copy = load_blocks(nat, plan.text_first, 2 * plan.feed, w, sem)
    copy.wait()
    feed_forward_tail(plan, low_text, w, gated, slope, part)


def query_forward_body(
    plan, nat, first_query, mine, other, params, resid, second, low, gated, slope, part, w, sem
):
    copy = load_blocks(nat, plan.query_first, 2 * plan.feed, w, sem)
    summed = first_query[...] + (mine[...].astype(f32) + other[...].astype(f32))
    resid[...] = summed
    normed = norm_forward(summed)[0] * params[1, 0:1] + params[1, 1:2]
    second[...] = normed
    low[...] = normed.astype(bf16)
    copy.wait()
    feed_forward_tail(plan, low, w, gated, slope, part)


def feed_shapes(plan, count):
    return (
        jax.ShapeDtypeStruct((count, plan.hidden), bf16),
        jax.ShapeDtypeStruct((count, plan.hidden), f32),
        jax.ShapeDtypeStruct((count, plan.width), bf16),
    )


def feed_scratch(plan):
    return [pltpu.VMEM((2 * plan.feed, TILE, TILE), bf16), pltpu.SemaphoreType.DMA]


def text_forward(plan, nat, low_text):
    return pl.pallas_call(
        functools.partial(text_forward_body, plan),
        out_shape=feed_shapes(plan, plan.texts),
        in_specs=any_specs(1) + vmem_specs(1),
        out_specs=tuple(vmem_specs(3)),
        scratch_shapes=feed_scratch(plan),
        compiler_params=vmem_params(),
        cost_estimate=cost(4 * plan.texts * plan.width * plan.hidden, 1e7),
        name="text_forward",
    )(nat, low_text)


def query_forward(plan, nat, first_query, mine, other, params):
    count, width = plan.learned, plan.width
    return pl.pallas_call(
        functools.partial(query_forward_body, plan),
        out_shape=(
            jax.ShapeDtypeStruct((count, width), f32),
            jax.ShapeDtypeStruct((count, width), f32),
            jax.ShapeDtypeStruct((count, width), bf16),
        )
        + feed_shapes(plan, count),
        in_specs=any_specs(1) + vmem_specs(4),
        out_specs=tuple(vmem_specs(6)),
        scratch_shapes=feed_scratch(plan),
        compiler_params=vmem_params(),
        cost_estimate=cost(4 * count * width * plan.hidden, 8e6),
        name="query_forward",
    )(nat, first_query, mine, other, params)


def feed_backward_body(
    plan, first_block, which, nat, states, mine, other, upstream, params, slope,
    out, grad, grad_low, before_low, part, norm_grad, w, sem,
):
    copy = load_blocks(nat, first_block, 2 * plan.feed, w, sem)
    gain, shift = params[which, 0:1], params[which, 1:2]
    count = states.shape[0] // plan.rows
    norm_grad[...] = jnp.zeros_like(norm_grad)

    def one_norm(row, carry):
        place = pl.ds(pl.multiple_of(row * count, count), count)
        summed = states[place, :] + (mine[place, :].astype(f32) + other[place, :].astype(f32))
        out[place, :] = (norm_forward(summed)[0] * gain + shift).astype(bf16)
        found, gain_grad, shift_grad = norm_backward(
            summed, upstream[place, :].astype(f32), gain
        )
        grad[place, :] = found
        grad_low[place, :] = found.astype(bf16)
        norm_grad[0:1] += gain_grad
        norm_grad[1:2] += shift_grad
        return carry

    lax.fori_loop(0, plan.rows, one_norm, 0)
    copy.wait()

    def one_down(chunk, carry):
        matrix = matrix_of(w, chunk * 2, 2, 0, plan.wt, plan.wt, plan.feed)
        cols = pl.ds(pl.multiple_of(chunk * 2 * TILE, 2 * TILE), 2 * TILE)
        before_low[:, cols] = (mm(grad_low[...], matrix, NT) * slope[:, cols]).astype(bf16)
        return carry

    lax.fori_loop(0, plan.ft // 2, one_down, 0)

    def one_up(chunk, carry):
        matrix = matrix_of(w, chunk * 2, 2, 0, plan.ft, plan.ft)
        cols = pl.ds(pl.multiple_of(chunk * 2 * TILE, 2 * TILE), 2 * TILE)
        part[:, cols] = mm(before_low[...], matrix, NT).astype(bf16)
        return carry

    lax.fori_loop(0, plan.wt // 2, one_up, 0)


def feed_backward(plan, first_block, which, nat, states, mine, other, upstream, params, slope):
    count, width = states.shape
    return pl.pallas_call(
        functools.partial(feed_backward_body, plan, first_block, which),
        out_shape=(
            jax.ShapeDtypeStruct((count, width), bf16),
            jax.ShapeDtypeStruct((count, width), f32),
            jax.ShapeDtypeStruct((count, width), bf16),
            jax.ShapeDtypeStruct((count, plan.hidden), bf16),
            jax.ShapeDtypeStruct((count, width), bf16),
            jax.ShapeDtypeStruct((2, width), f32),
        ),
        in_specs=any_specs(1) + vmem_specs(6),
        out_specs=tuple(vmem_specs(6)),
        scratch_shapes=feed_scratch(plan),
        compiler_params=vmem_params(),
        cost_estimate=cost(4 * count * width * plan.hidden, 1e7),
        name="feed_backward",
    )(nat, states, mine, other, upstream, params, slope)


def cross_backward_body(
    plan, scale, nat, resid, third_grad, mine, other, params, queries, keys, values, probs,
    grad, grad_low, query_back, key_back, value_back, part, norm_grad, looked, w, sem,
):
    copy = load_blocks(nat, plan.cross_first, plan.cross_count, w, sem)
    upstream = third_grad[...] + (mine[...].astype(f32) + other[...].astype(f32))
    found, gain_grad, shift_grad = norm_backward(resid[...], upstream, params[1, 0:1])
    grad[...] = found
    grad_low[...] = found.astype(bf16)
    norm_grad[0:1] = gain_grad
    norm_grad[1:2] = shift_grad
    copy.wait()
    matrix = matrix_of(w, 0, plan.ht, 0, plan.wt, plan.wt, plan.square + 2 * plan.cross)
    looked[...] = mm(grad_low[...], matrix, NT).astype(bf16)

    def one(row, carry):
        query_place = pl.ds(pl.multiple_of(row * NQ, NQ), NQ)
        place = pl.ds(pl.multiple_of(row * plan.keys, plan.keys), plan.keys)
        for tile in range(plan.ht):
            cols = slice(tile * TILE, (tile + 1) * TILE)
            query_grad, key_grad, value_grad = pair_backward(
                queries[query_place, cols], keys[place, cols], values[place, cols],
                probs[row, tile], looked[query_place, cols], scale,
            )
            query_back[query_place, cols] = query_grad
            key_back[place, cols] = key_grad
            value_back[place, cols] = value_grad
        return carry

    lax.fori_loop(0, plan.rows, one, 0)
    matrix = matrix_of(w, 0, plan.wt, 0, plan.ht, plan.ht)
    part[...] = mm(query_back[...], matrix, NT).astype(bf16)


def cross_backward(
    plan, scale, nat, resid, third_grad, mine, other, params, queries, keys, values, probs
):
    learned, width, half = plan.learned, plan.width, plan.half
    return pl.pallas_call(
        functools.partial(cross_backward_body, plan, scale),
        out_shape=(
            jax.ShapeDtypeStruct((learned, width), f32),
            jax.ShapeDtypeStruct((learned, width), bf16),
            jax.ShapeDtypeStruct((learned, half), bf16),
            jax.ShapeDtypeStruct(keys.shape, bf16),
            jax.ShapeDtypeStruct(keys.shape, bf16),
            jax.ShapeDtypeStruct((learned, width), bf16),
            jax.ShapeDtypeStruct((2, width), f32),
        ),
        in_specs=any_specs(1) + vmem_specs(9),
        out_specs=tuple(vmem_specs(7)),
        scratch_shapes=[
            pltpu.VMEM((learned, half), bf16),
            pltpu.VMEM((plan.cross_count, TILE, TILE), bf16),
            pltpu.SemaphoreType.DMA,
        ],
        compiler_params=vmem_params(),
        cost_estimate=cost(8 * learned * width * half, 1e7),
        name="cross_backward",
    )(nat, resid, third_grad, mine, other, params, queries, keys, values, probs)


def self_backward_body(
    plan, scale, nat, resid, query_grad, query_mine, query_other, text_grad, text_mine,
    text_other, params, qkv, probs,
    grad, grad_low, back, part, norm_grad, mixed, w, sem,
):
    copy = load_blocks(nat, plan.self_first, plan.self_count, w, sem)
    text = plan.seq - NQ
    gain = params[0, 0:1]
    norm_grad[...] = jnp.zeros_like(norm_grad)

    def one_norm(row, carry):
        place = pl.ds(pl.multiple_of(row * plan.seq, plan.seq), plan.seq)
        query_place = pl.ds(pl.multiple_of(row * NQ, NQ), NQ)
        text_place = pl.ds(pl.multiple_of(row * text, text), text)
        upstream = jnp.concatenate(
            [
                query_grad[query_place, :]
                + (query_mine[query_place, :].astype(f32) + query_other[query_place, :].astype(f32)),
                text_grad[text_place, :]
                + (text_mine[text_place, :].astype(f32) + text_other[text_place, :].astype(f32)),
            ],
            axis=0,
        )
        found, gain_grad, shift_grad = norm_backward(resid[place, :], upstream, gain)
        grad[place, :] = found
        grad_low[place, :] = found.astype(bf16)
        norm_grad[0:1] += gain_grad
        norm_grad[1:2] += shift_grad
        return carry

    lax.fori_loop(0, plan.rows, one_norm, 0)
    copy.wait()
    matrix = matrix_of(w, 0, plan.ht, 0, plan.wt, plan.wt, 3 * plan.square)
    mixed[...] = mm(grad_low[...], matrix, NT).astype(bf16)

    def one(row, carry):
        place = pl.ds(pl.multiple_of(row * plan.seq, plan.seq), plan.seq)
        for tile in range(plan.ht):
            cols = slice(tile * TILE, (tile + 1) * TILE)
            found = pair_backward(
                qkv[0, place, cols], qkv[1, place, cols], qkv[2, place, cols],
                probs[row, tile], mixed[place, cols], scale,
            )
            for piece in range(3):
                first = piece * plan.half + tile * TILE
                back[place, first : first + TILE] = found[piece]
        return carry

    lax.fori_loop(0, plan.rows, one, 0)
    matrix = jnp.concatenate(
        [matrix_of(w, 0, plan.wt, 0, plan.ht, plan.ht, p * plan.square) for p in range(3)], axis=1
    )
    part[...] = mm(back[...], matrix, NT).astype(bf16)


def self_backward(
    plan, scale, nat, resid, query_grad, query_mine, query_other, text_grad, text_mine,
    text_other, params, qkv, probs,
):
    tokens, width, half = plan.tokens, plan.width, plan.half
    return pl.pallas_call(
        functools.partial(self_backward_body, plan, scale),
        out_shape=(
            jax.ShapeDtypeStruct((tokens, width), f32),
            jax.ShapeDtypeStruct((tokens, width), bf16),
            jax.ShapeDtypeStruct((tokens, 3 * half), bf16),
            jax.ShapeDtypeStruct((tokens, width), bf16),
            jax.ShapeDtypeStruct((2, width), f32),
        ),
        in_specs=any_specs(1) + vmem_specs(10),
        out_specs=tuple(vmem_specs(5)),
        scratch_shapes=[
            pltpu.VMEM((tokens, half), bf16),
            pltpu.VMEM((plan.self_count, TILE, TILE), bf16),
            pltpu.SemaphoreType.DMA,
        ],
        compiler_params=vmem_params(),
        cost_estimate=cost(8 * tokens * width * half, 1.2e7),
        name="self_backward",
    )(
        nat, resid, query_grad, query_mine, query_other, text_grad, text_mine, text_other,
        params, qkv, probs,
    )


def store_blocks(target, first, product, col_total):
    for row in range(product.shape[0] // TILE):
        for col in range(col_total):
            target[first + row * col_total + col] = product[
                row * TILE : (row + 1) * TILE, col * TILE : (col + 1) * TILE
            ].astype(bf16)


def grad_blocks_body(first_block, pairs, total, *refs):
    sources, target, staged, sems = refs[: len(refs) - 4], refs[-3], refs[-2], refs[-1]
    copies = []
    base = 0
    for number, (left_at, right_at, right_first, right_width, step) in enumerate(pairs):
        left, right = sources[left_at], sources[right_at]
        left_tiles, col_total = left.shape[1] // TILE, right_width // TILE

        def one(chunk, carry, base=base, left=left, right=right, step=step, col_total=col_total,
                right_first=right_first, right_width=right_width):
            cols = pl.ds(pl.multiple_of(chunk * step * TILE, step * TILE), step * TILE)
            product = mm(left[:, cols], right[:, right_first : right_first + right_width], TN)
            store_blocks(staged, base + chunk * step * col_total, product, col_total)
            return carry

        lax.fori_loop(0, left_tiles // step, one, 0)
        count = left_tiles * col_total
        copy = pltpu.make_async_copy(
            staged.at[pl.ds(base, count)],
            target.at[pl.ds(first_block + base, count)],
            sems.at[number],
        )
        copy.start()
        copies.append(copy)
        base += count
    for copy in copies:
        copy.wait()


def grad_blocks(buffer, first_block, sources, pairs, flops):
    total = sum(sources[a].shape[1] // TILE * (width // TILE) for a, _, _, width, _ in pairs)
    return pl.pallas_call(
        functools.partial(grad_blocks_body, first_block, pairs, total),
        out_shape=jax.ShapeDtypeStruct(buffer.shape, buffer.dtype),
        in_specs=vmem_specs(len(sources)) + any_specs(1),
        out_specs=any_specs(1)[0],
        scratch_shapes=[
            pltpu.VMEM((total, TILE, TILE), bf16),
            pltpu.SemaphoreType.DMA((len(pairs),)),
        ],
        input_output_aliases={len(sources): 0},
        compiler_params=vmem_params(),
        cost_estimate=cost(flops, 1e7),
        name="grad_blocks",
    )(*sources, buffer)


def swap_tensor(part):
    if lax.axis_size("tensor") != 2:
        total = lax.psum(part.astype(f32), "tensor")
        return (total - part.astype(f32)).astype(bf16)
    return lax.ppermute(part, "tensor", [(0, 1), (1, 0)])


def layer_rows(
    hidden, image, segment_ids, cotangent, nat, norm_params, heads_local, scale, slot_count
):
    rows, seq, width = hidden.shape
    plan = Plan(
        rows, seq, width, image.shape[2], image.shape[1], heads_local, FF // lax.axis_size("tensor")
    )
    tokens, learned, texts, half = plan.tokens, plan.learned, plan.texts, plan.half
    flat_hidden = hidden.reshape(tokens, width)
    flat_image = jnp.pad(image, ((0, 0), (0, plan.keys - plan.patches), (0, 0))).reshape(
        rows * plan.keys, plan.image_width
    )
    up_query = cotangent[:, :NQ].reshape(learned, width)
    up_text = cotangent[:, NQ:].reshape(texts, width)
    buffer = jnp.zeros((slot_count, TILE, TILE), bf16)

    qkv, self_probs, mixed, part_one = self_forward(
        plan, scale, nat, flat_hidden, segment_ids[:, None, :], segment_ids[:, :, None]
    )
    other_one = swap_tensor(part_one)
    image_keys, image_values = image_forward(plan, nat, flat_image)
    (
        first_sum, first_query, first_text, low_query, low_text, cross_queries, cross_probs,
        looked, part_two,
    ) = cross_forward(
        plan, scale, nat, flat_hidden, part_one, other_one, norm_params, image_keys, image_values
    )
    other_two = swap_tensor(part_two)
    text_gated, text_slope, part_text = text_forward(plan, nat, low_text)
    other_text = swap_tensor(part_text)
    second_sum, second, low_second, query_gated, query_slope, part_query = query_forward(
        plan, nat, first_query, part_two, other_two, norm_params
    )
    other_query = swap_tensor(part_query)
    out_text, third_text, third_text_low, before_text, part_four_text, norm_text = feed_backward(
        plan, plan.text_first, 3, nat, first_text, part_text, other_text, up_text, norm_params,
        text_slope,
    )
    other_four_text = swap_tensor(part_four_text)
    out_query, third_query, third_query_low, before_query, part_four_query, norm_query = (
        feed_backward(
            plan, plan.query_first, 2, nat, second, part_query, other_query, up_query, norm_params,
            query_slope,
        )
    )
    other_four_query = swap_tensor(part_four_query)
    feed_pairs = [(0, 1, 0, plan.hidden, 2), (2, 3, 0, width, 2)]
    buffer = grad_blocks(
        buffer, plan.text_first, [low_text, before_text, text_gated, third_text_low], feed_pairs,
        4 * texts * width * plan.hidden,
    )
    second_grad, cross_low, query_back, key_back, value_back, part_five, norm_second = (
        cross_backward(
            plan, scale, nat, second_sum, third_query, part_four_query, other_four_query,
            norm_params, cross_queries, image_keys, image_values, cross_probs,
        )
    )
    other_five = swap_tensor(part_five)
    buffer = grad_blocks(
        buffer, plan.query_first, [low_second, before_query, query_gated, third_query_low],
        feed_pairs, 4 * learned * width * plan.hidden,
    )
    buffer = grad_blocks(
        buffer, plan.cross_first,
        [low_query, query_back, flat_image, key_back, value_back, looked, cross_low],
        [(0, 1, 0, half, 2), (2, 3, 0, half, 1), (2, 4, 0, half, 1), (5, 6, 0, width, 1)],
        4 * rows * plan.keys * plan.image_width * half,
    )
    first_grad, self_low, self_back, part_six, norm_first = self_backward(
        plan, scale, nat, first_sum, second_grad, part_five, other_five, third_text,
        part_four_text, other_four_text, norm_params, qkv, self_probs,
    )
    other_six = swap_tensor(part_six)
    buffer = grad_blocks(
        buffer, plan.self_first, [flat_hidden, self_back, mixed, self_low],
        [(0, 1, 0, half, 2), (0, 1, half, half, 2), (0, 1, 2 * half, half, 2), (2, 3, 0, width, 1)],
        8 * tokens * width * half,
    )
    input_grad = first_grad + (part_six.astype(f32) + other_six.astype(f32))
    output_rows = jnp.concatenate(
        [out_query.reshape(rows, NQ, width), out_text.reshape(rows, seq - NQ, width)], axis=1
    )
    norm_part = jnp.stack([norm_first, norm_second, norm_query, norm_text])
    return (output_rows, input_grad.reshape(rows, seq, width), buffer, norm_part)


def times(left_matrix, right_matrix):
    return jnp.einsum("...ij,...jk->...ik", left_matrix, right_matrix, precision=highest)


def flipped(block_matrix):
    return jnp.swapaxes(block_matrix, -1, -2)


def split3(a):
    h=a.astype(bf16); r=a-h.astype(f32); m=r.astype(bf16); l=(r-m.astype(f32)).astype(bf16)
    return h,m,l
def split2(a):
    h=a.astype(bf16); return h,(a-h.astype(f32)).astype(bf16)
def dot3(a,b,dims):
    ah,al=split2(a); bh,bl=split2(b)
    return mm(ah,bh,dims)+(mm(ah,bl,dims)+mm(al,bh,dims))
def gram6(p):
    h,m,l=split3(p)
    hh=mm(h,h,TN); mmm=mm(m,m,TN); hm=mm(h,m,TN)+mm(h,l,TN)
    return hh+(mmm+(hm+hm.T))

PB=16
def panel_steps(x, kb, g):
    base=kb*PB
    lane=lax.broadcasted_iota(jnp.int32,(1,8,128),2)
    sub=lax.broadcasted_iota(jnp.int32,(1,8,128),1)
    halves=[x[:,:8],x[:,8:]]
    rinvs=[]
    for s in range(PB):
        k=base+s
        hs=s//8; r=s%8
        cur=halves[hs]
        row=cur[:,r:r+1,:]
        piv=cur[:,r:r+1,k:k+1]
        rinv=1.0/piv
        rinvs.append(rinv)
        scaled=jnp.where(lane[:,:1]==k,1.0,row)*rinv
        for h in range(hs,2):
            y=halves[h]
            col=jnp.broadcast_to(y[:,:,k:k+1],y.shape)
            if h==hs:
                low=(sub>r)
                col=jnp.where(low,col,0.0)
                y=jnp.where((lane==k)&(sub>r),0.0,y)
                y=jnp.where((lane==k)&(sub==r),1.0,y)
            else:
                y=jnp.where(lane==k,0.0,y)
            halves[h]=y-col*scaled
    return jnp.concatenate(halves,axis=1), jnp.concatenate(rinvs,axis=1)

def ortho_body(n_pad, n, g, s_ref,b_ref,q_ref,a_ref,p_ref,d_ref):
    def first(i,c):
        p=dot3(s_ref[i],b_ref[i],NN)
        p_ref[i]=p
        a_ref[i]=gram6(p)
        return c
    lax.fori_loop(0,n,first,0)
    eye=(lax.broadcasted_iota(jnp.int32,(128,128),0)==lax.broadcasted_iota(jnp.int32,(128,128),1)).astype(f32)
    for i in range(n,n_pad):
        a_ref[i]=eye
    lane=lax.broadcasted_iota(jnp.int32,(1,PB,128),2)
    sub=lax.broadcasted_iota(jnp.int32,(1,PB,128),1)
    for kb in range(128//PB):
        base=kb*PB; end=base+PB
        def group(gi,c):
            i0=gi*g
            x=a_ref[pl.ds(i0,g),base:end,:]
            x,rinv=panel_steps(x,kb,g)
            w=jnp.where((lane>=base)&(lane<end)&(lane-base>sub),0.0,x)
            d_ref[pl.ds(i0,g),base:end,:]=jnp.broadcast_to(rinv,x.shape)
            a_ref[pl.ds(i0,g),base:end,:]=w
            if end<128:
                u=jnp.where(lane>=end,x*rinv,0.0)
                wh,wm,wl=split3(w); uh,um,ul=split3(u)
                lhs=jnp.concatenate([uh,uh,um,uh,ul,um],axis=1)
                rhs=jnp.concatenate([wh,wm,wh,wl,wh,wm],axis=1)
                lane2=lax.broadcasted_iota(jnp.int32,(128-end,128),1)
                inside=(lane2>=base)&(lane2<end)
                for j in range(g):
                    upd=mm(lhs[j],rhs[j],TN)
                    old=a_ref[i0+j,end:,:]
                    a_ref[i0+j,end:,:]=jnp.where(inside,0.0,old)-upd[end:,:]
            return c
        lax.fori_loop(0,n_pad//g,group,0)
    ii=lax.broadcasted_iota(jnp.int32,(128,128),0); jj=lax.broadcasted_iota(jnp.int32,(128,128),1)
    def last(i,c):
        inv=jnp.where(ii>=jj,a_ref[i],0.0)*jnp.sqrt(d_ref[i])
        q_ref[i]=dot3(p_ref[i],inv,NT)
        return c
    lax.fori_loop(0,n,last,0)

def ortho(s,b,g=29):
    n=s.shape[0]; n_pad=-(-n//g)*g
    return pl.pallas_call(
        functools.partial(ortho_body,n_pad,n,g),
        out_shape=jax.ShapeDtypeStruct(s.shape,f32),
        in_specs=[pl.BlockSpec(memory_space=pltpu.VMEM)]*2,
        out_specs=pl.BlockSpec(memory_space=pltpu.VMEM),
        scratch_shapes=[pltpu.VMEM((n_pad,128,128),f32),pltpu.VMEM((n,128,128),f32),pltpu.VMEM((n_pad,128,128),f32)],
        compiler_params=pltpu.CompilerParams(vmem_limit_bytes=50*1024*1024),
    )(s,b)


def orthonormal_pair(left_new, left_bases, right_new, right_bases):
    count = left_new.shape[0]
    both = ortho(
        jnp.concatenate([left_new, right_new]), jnp.concatenate([left_bases, right_bases]), count
    )
    return both[:count], both[count:]


def rotated_update(
    gradient, master, first_moment, second_moment, left_stats, right_stats, left_bases, right_bases
):
    rotated = times(times(flipped(left_bases), gradient), right_bases)
    first_new = beta_first * first_moment + (1 - beta_first) * rotated
    second_new = beta_second * second_moment + (1 - beta_second) * rotated * rotated
    step_rotated = (
        first_new
        / (1 - beta_first**STEP)
        / (jnp.sqrt(second_new / (1 - beta_second**STEP)) + adam_epsilon)
    )
    step_full = times(times(left_bases, step_rotated), flipped(right_bases))
    master_new = master - matrix_rate * (step_full + matrix_decay * master)
    left_new = beta_stats * left_stats + (1 - beta_stats) * times(gradient, flipped(gradient))
    right_new = beta_stats * right_stats + (1 - beta_stats) * times(flipped(gradient), gradient)
    return (
        master_new,
        first_new,
        second_new,
        left_new,
        right_new,
        *orthonormal_pair(left_new, left_bases, right_new, right_bases),
    )


def per_device(
    hidden,
    image,
    segment_ids,
    cotangent,
    slot_block,
    weight_master,
    moment_one,
    moment_two,
    left_stat,
    right_stat,
    left_basis,
    right_basis,
    norm_params,
    norm_moment_one,
    norm_moment_two,
):
    tensors = lax.axis_size("tensor")
    width = hidden.shape[2]
    heads_local = HEADS // tensors
    scale = (width // HEADS) ** (-0.5)
    order = slot_block[0]
    slot_count = order.shape[0]
    gathered = lax.all_gather(weight_master[0].astype(jnp.bfloat16), "dp", axis=0, tiled=True)
    inverse = jnp.zeros_like(order).at[order].set(jnp.arange(slot_count, dtype=jnp.int32))
    natural = gathered[inverse]
    out_rows, in_grad, packed, norm_part = layer_rows(
        hidden, image, segment_ids, cotangent, natural, norm_params, heads_local, scale, slot_count
    )
    owned = lax.psum_scatter(
        packed[order], "dp", scatter_dimension=0, tiled=True
    ).astype(jnp.float32)
    norm_total = lax.psum(norm_part, "dp")
    updated = rotated_update(
        owned,
        weight_master[0],
        moment_one[0],
        moment_two[0],
        left_stat[0],
        right_stat[0],
        left_basis[0],
        right_basis[0],
    )
    (
        weight_new,
        moment_one_new,
        moment_two_new,
        left_stat_new,
        right_stat_new,
        left_basis_new,
        right_basis_new,
    ) = [array[None] for array in updated]
    norm_first = beta_first * norm_moment_one + (1 - beta_first) * norm_total
    norm_second = beta_second * norm_moment_two + (1 - beta_second) * norm_total * norm_total
    norm_new = norm_params - norm_rate * (norm_first / (1 - beta_first**STEP)) / (
        jnp.sqrt(norm_second / (1 - beta_second**STEP)) + adam_epsilon
    )
    return (
        out_rows,
        in_grad,
        weight_new,
        weight_new.astype(jnp.bfloat16),
        moment_one_new,
        moment_two_new,
        left_stat_new,
        right_stat_new,
        left_basis_new,
        right_basis_new,
        norm_first,
        norm_second,
        norm_new,
    )


def solution(mesh):
    in_specs = (
        P("dp", None, None),
        P("dp", None, None),
        P("dp", None),
        P("dp", None, None),
        P("tensor", None),
        P("tensor", "dp", None, None),
        P("tensor", "dp", None, None),
        P("tensor", "dp", None, None),
        P("tensor", "dp", None, None),
        P("tensor", "dp", None, None),
        P("tensor", "dp", None, None),
        P("tensor", "dp", None, None),
        P(),
        P(),
        P(),
    )
    out_specs = (
        P("dp", None, None),
        P("dp", None, None),
        P("tensor", "dp", None, None),
        P("tensor", "dp", None, None),
        P("tensor", "dp", None, None),
        P("tensor", "dp", None, None),
        P("tensor", "dp", None, None),
        P("tensor", "dp", None, None),
        P("tensor", "dp", None, None),
        P("tensor", "dp", None, None),
        P(),
        P(),
        P(),
    )
    return jax.shard_map(
        per_device, mesh=mesh, in_specs=in_specs, out_specs=out_specs, check_vma=False
    )
```

time: 787 us -> 618 us (0.79)
  local copies, waits for them, and re-layouts: 225 us -> 61.8 us
  Pallas kernels: 88.6 us -> 207 us
  matrix products: 117 us -> 14.3 us
  other arithmetic: 66.6 us -> 19.3 us
  waiting for transfers between devices: 194 us -> 221 us
    pallas_call x0 -> x13, Pallas kernels: none -> 118 us  [the longest x4 33.5 us: grad_blocks(): pl.pallas_call(functools.partial(grad_blocks_body, first_block, pairs, to...]
    dot_general x46 -> x0, matrix products: 103 us -> none  [the longest x12 34.6 us: block_grad(): jnp.einsum('rsia,rsjb->ijab', left_tiles, right_tiles, preferred_element_...]
    reshape x38 -> x0, local copies, waits for them, and re-layouts: 75.1 us -> none  [the longest x11 32.4 us: unpack_blocks(): portion.transpose(0, 2, 1, 3).reshape(rows_count, cols_count)]
    unnamed x277 -> x63, local copies, waits for them, and re-layouts: 37.5 us -> 7.63 us
    transpose x12 -> x0, local copies, waits for them, and re-layouts: 28.9 us -> none  [block_grad(): jnp.einsum('rsia,rsjb->ijab', left_tiles, right_tiles, preferred_element_...]
    slice x7 -> x2, local copies, waits for them, and re-layouts: 30.4 us -> 1.55 us  [the longest x1 0.87 us: layer_rows(): up_text = cotangent[:, NQ:].reshape(texts, width)]
    ppermute x6 -> x8, waiting for transfers between devices: 0.62 us -> 22.6 us  [swap_tensor(): return lax.ppermute(part, 'tensor', [(0, 1), (1, 0)])]
    reduce_sum x19 -> x0, other arithmetic: 14.3 us -> none  [the longest x9 8.34 us: layer_norm(): return center * lax.rsqrt(variance + norm_epsilon) * gain + shift]
  transfers between devices with their start and end apart: 8 -> 10, of which waited for: 3 -> 4; matrix products, arithmetic and copies ran while one was open for 24% -> 4% of each run, Pallas kernels for 0% -> 12%
where the time goes in v2:
time: 618 us; the launch traced here: 607 us
  waiting for transfers between devices  221 us (36%)
  Pallas kernels  207 us (33%)
  local copies, waits for them, and re-layouts  61.8 us (10%)
  blocking collectives  59.7 us (10%)
  other arithmetic  19.3 us (3%)
  between operations  14.9 us (2%)
  matrix products  14.3 us (2%)
  starting transfers between devices  9.56 us (2%)
    all_gather x1, waiting for transfers between devices, per_device(): lax.all_gather(weight_master[0].astype(jnp.bfloat16), 'dp', axis=0, tiled...  117 us
    pallas_call x1, Pallas kernels, ortho(): pl.pallas_call(functools.partial(ortho_body, n_pad, n, g), out_shape=jax....  88.6 us
    reduce_scatter x1, waiting for transfers between devices, per_device(): lax.psum_scatter(packed[order], 'dp', scatter_dimension=0, tiled=True)  81.6 us
    psum x1, blocking collectives, per_device(): norm_total = lax.psum(norm_part, 'dp')  59.7 us
    pallas_call x4, Pallas kernels, grad_blocks(): pl.pallas_call(functools.partial(grad_blocks_body, first_block, pairs, to...  33.5 us
    ppermute x8, waiting for transfers between devices, swap_tensor(): return lax.ppermute(part, 'tensor', [(0, 1), (1, 0)])  22.6 us
    gather x1, local copies, waits for them, and re-layouts, per_device(): packed[order]  18.9 us
    gather x1, local copies, waits for them, and re-layouts, per_device(): natural = gathered[inverse]  18.9 us
  transfers between devices with their start and end apart: 10, of which 4 were waited for; matrix products, arithmetic and copies ran while one was open for 4% of the time, Pallas kernels for 12%

profile of v2, /device:TPU:0, one launch (start us, length us, event | category | flops | bytes accessed | tf_op | source)
XLA Modules:
  0.0 607.5 jit_solution(11734411635325954950)
XLA Ops:
  13.8 116.9 %all-gather.2.cloned.1.call-done = bf16[464,128,128]{2,1,0:T(8,128)(2,1)} async-done(((bf16[29,128,128]{2,1,0:T(8,128)(2,1)}), bf16[464,128,128]{2,1,0:T(8,128)(2,1)}) %all-gather.2.cloned.1.call-update) | async-done | bytes 15204368 | tf_op jit(solution)/shard_map/all_gather | solution.py:908
  130.7 18.9 %gather_fusion = bf16[464,128,128]{2,1,0:T(8,128)(2,1)} fusion(bf16[464,128,128]{2,1,0:T(8,128)(2,1)} %all-gather.2.cloned.1.call-done, s32[1024]{0:T(1024)S(1)} %pad_clamp_fusion.1), kind=kCustom, calls=%fused_computation | custom fusion | bytes 30410560 | tf_op jit(solution)/shard_map/gather | solution.py:910
  149.6 9.2 %self_forward.1 = (bf16[3,512,384]{2,1,0:T(8,128)(2,1)}, f32[4,3,256,128]{3,2,1,0:T(8,128)}, bf16[512,384]{1,0:T(8,128)(2,1)}, bf16[512,768]{1,0:T(8,128)(2,1)}) custom-call(bf16[464,128,128]{2,1,0:T(8,128)(2,1)} %gather_fusion, bf16[512,768]{1,0:T(8,128)(2,1)} %bitcast.81, s32[4,1,128]{2,1,0:T(1,128)} %bitcast.89, s32[4,128,1]{2,1,0:T(8,128)} %copy.37.seg_col), custom_call_target="tpu_custom_call" | custom-call | flops 1207959552 | bytes 8000000 | tf_op jit(solution)/shard_map/self_forward/pallas_call | solution.py:180
  162.5 9.2 %image_forward.1 = (bf16[1088,384]{1,0:T(8,128)(2,1)}, bf16[1088,384]{1,0:T(8,128)(2,1)}) custom-call(bf16[464,128,128]{2,1,0:T(8,128)(2,1)} %gather_fusion, bf16[1088,1408]{1,0:T(8,128)(2,1)} %bitcast.74), custom_call_target="tpu_custom_call" | custom-call | flops 2353004544 | bytes 8000000 | tf_op jit(solution)/shard_map/image_forward/pallas_call | solution.py:216
  171.7 7.0 %collective-permute-done.other = bf16[512,768]{1,0:T(8,128)(2,1)S(1)} collective-permute-done((bf16[512,768]{1,0:T(8,128)(2,1)}, bf16[512,768]{1,0:T(8,128)(2,1)S(1)}, u32[]{:S(2)}, u32[]{:S(2)}) %collective-permute-start) | collective-permute-done | bytes 786464 | tf_op jit(solution)/shard_map/ppermute | solution.py:660
  179.6 10.2 %cross_forward.1 = (f32[512,768]{1,0:T(8,128)}, f32[128,768]{1,0:T(8,128)}, f32[384,768]{1,0:T(8,128)}, bf16[128,768]{1,0:T(8,128)(2,1)}, bf16[384,768]{1,0:T(8,...) custom-call(bf16[464,128,128]{2,1,0:T(8,128)(2,1)} %gather_fusion, ...), custom_call_target="tpu_custom_call" | custom-call | flops 150994944 | bytes 12000000 | tf_op jit(solution)/shard_map/cross_forward/pallas_call | solution.py:277
  189.8 8.9 %text_forward.1 = (bf16[384,1536]{1,0:T(8,128)(2,1)}, f32[384,1536]{1,0:T(8,128)}, bf16[384,768]{1,0:T(8,128)(2,1)}) custom-call(bf16[464,128,128]{2,1,0:T(8,128)(2,1)} %gather_fusion, bf16[384,768]{1,0:T(8,128)(2,1)} %get-tuple-element.71.low_text.refs_0_), custom_call_target="tpu_custom_call" | custom-call | flops 1811939328 | bytes 10000000 | tf_op jit(solution)/shard_map/text_forward/pallas_call | solution.py:360
  202.4 15.5 %collective-permute-done.1.other = bf16[128,768]{1,0:T(8,128)(2,1)S(1)} collective-permute-done((bf16[128,768]{1,0:T(8,128)(2,1)S(1)}, bf16[128,768]{1,0:T(8,128)(2,1)S(1)}, u32[]{:S(2)}, u32[]{:S(2)}) %collective-permute-start.1) | collective-permute-done | bytes 196640 | tf_op jit(solution)/shard_map/ppermute | solution.py:660
  218.6 7.1 %query_forward.1 = (f32[128,768]{1,0:T(8,128)}, f32[128,768]{1,0:T(8,128)}, bf16[128,768]{1,0:T(8,128)(2,1)}, bf16[128,1536]{1,0:T(8,128)(2,1)}, f32[128,1536]{1,0:T(8,128)}, /*index=5*/bf16[128,768]{1,0:T(8,128)(2,1)}) custom-call(bf16[464,128,128]{2,1,0:T(8,128)(2,1)} %gather_fusion, f32[128,768]{1,0:T(8,128)} %get-tuple-element.64.first_query, ...), custom_call_target="tpu_custom_call" | custom-call | flops 603979776 | bytes 8000000 | tf_op jit(solution)/shard_map/query_forward/pallas_call | solution.py:374
  228.0 10.1 %feed_backward.3 = (bf16[384,768]{1,0:T(8,128)(2,1)}, f32[384,768]{1,0:T(8,128)}, bf16[384,768]{1,0:T(8,128)(2,1)}, bf16[384,1536]{1,0:T(8,128)(2,1)}, bf16[384,768]{1,0:T(8,128)(2,1)}, /*index=5*/f32[2,768]{1,0:T(2,128)}) custom-call(bf16[464,128,128]{2,1,0:T(8,128)(2,1)} %gather_fusion, f32[384,768]{1,0:T(8,128)} %get-tuple-element.70.states, ...), custom_call_target="tpu_custom_call" | custom-call | flops 1811939328 | bytes 10000000 | tf_op jit(solution)/shard_map/feed_backward/pallas_call | solution.py:435
  239.4 7.5 %feed_backward.2 = (bf16[128,768]{1,0:T(8,128)(2,1)}, f32[128,768]{1,0:T(8,128)}, bf16[128,768]{1,0:T(8,128)(2,1)}, bf16[128,1536]{1,0:T(8,128)(2,1)}, bf16[128,768]{1,0:T(8,128)(2,1)}, /*index=5*/f32[2,768]{1,0:T(2,128)}) custom-call(bf16[464,128,128]{2,1,0:T(8,128)(2,1)} %gather_fusion, f32[128,768]{1,0:T(8,128)} %get-tuple-element.66.states, ...), custom_call_target="tpu_custom_call" | custom-call | flops 603979776 | bytes 10000000 | tf_op jit(solution)/shard_map/feed_backward/pallas_call | solution.py:435
  248.5 9.2 %broadcast_in_dim.38.refs_4_ = bf16[464,128,128]{2,1,0:T(8,128)(2,1)} broadcast(bf16[]{:T(256)} %constant.16.clone.1), dimensions={} | broadcast | bytes 15204354 | tf_op jit(solution)/shard_map/broadcast_in_dim | solution.py:677
  257.7 8.1 %grad_blocks.4.refs_4_ = bf16[464,128,128]{2,1,0:T(8,128)(2,1)} custom-call(bf16[384,768]{1,0:T(8,128)(2,1)} %get-tuple-element.71.low_text.refs_0_, bf16[384,1536]{1,0:T(8,128)(2,1)} %get-tuple-element.102.refs_1_, bf16[384,1536]{1,0:T(8,128)(2,1)} %get-tuple-element.103.refs_2_, ...), custom_call_target="tpu_custom_call", output_to_operand_aliasing={{}: (4, {})} | custom-call | flops 1811939328 | bytes 10000000 | tf_op jit(solution)/shard_map/grad_blocks/pallas_call | solution.py:640
  265.9 5.6 grad_blocks.5.refs_7_
  272.2 10.8 %cross_backward.1 = (f32[128,768]{1,0:T(8,128)}, bf16[128,768]{1,0:T(8,128)(2,1)}, bf16[128,384]{1,0:T(8,128)(2,1)}, bf16[1088,384]{1,0:T(8,128)(2,1)}, bf16[108...) custom-call(bf16[464,128,128]{2,1,0:T(8,128)(2,1)} %gather_fusion, ...), custom_call_target="tpu_custom_call" | custom-call | flops 301989888 | bytes 10000000 | tf_op jit(solution)/shard_map/cross_backward/pallas_call | solution.py:492
  283.6 13.1 %grad_blocks.6.refs_4_ = bf16[464,128,128]{2,1,0:T(8,128)(2,1)} custom-call(bf16[128,768]{1,0:T(8,128)(2,1)} %get-tuple-element.92.refs_0_, bf16[128,384]{1,0:T(8,128)(2,1)} %get-tuple-element.93.refs_1_, bf16[1088,1408]{1,0:T(8,128)(2,1)} %bitcast.75, bf16[1088,384]{1,0:T(8,128)(2,1)} %get-tuple-element.94.refs_3_, ...), custom_call_target="tpu_custom_call", output_to_operand_aliasing={{}: (7, {})} | custom-call | flops 2353004544 | bytes 10000000 | tf_op jit(solution)/shard_map/grad_blocks/pallas_call | solution.py:640
  297.6 11.9 %self_backward.1 = (f32[512,768]{1,0:T(8,128)}, bf16[512,768]{1,0:T(8,128)(2,1)}, bf16[512,1152]{1,0:T(8,128)(2,1)}, bf16[512,768]{1,0:T(8,128)(2,1)}, f32[2,768]{1,0:T(2,128)}) custom-call(bf16[464,128,128]{2,1,0:T(8,128)(2,1)} %gather_fusion, f32[512,768]{1,0:T(8,128)} %get-tuple-element.75.resid, f32[128,768]{1,0:T(8,128)} %get-tuple-element.81.query_grad, ...), custom_call_target="tpu_custom_call" | custom-call | flops 1207959552 | bytes 12000000 | tf_op jit(solution)/shard_map/self_backward/pallas_call | solution.py:576
  309.5 6.7 %grad_blocks.7 = bf16[464,128,128]{2,1,0:T(8,128)(2,1)} custom-call(bf16[512,768]{1,0:T(8,128)(2,1)} %bitcast.83, bf16[512,1152]{1,0:T(8,128)(2,1)} %get-tuple-element.89.refs_1_, bf16[512,384]{1,0:T(8,128)(2,1)} %get-tuple-element.90.refs_2_, bf16[512,768]{1,0:T(8,128)(2,1)} %get-tuple-element.91.refs_3_, ...), custom_call_target="tpu_custom_call", output_to_operand_aliasing={{}: (4, {})} | custom-call | flops 1207959552 | bytes 10000000 | tf_op jit(solution)/shard_map/grad_blocks/pallas_call | solution.py:640
  316.2 18.9 %gather_fusion.1 = bf16[464,128,128]{2,1,0:T(8,128)(2,1)} fusion(bf16[464,128,128]{2,1,0:T(8,128)(2,1)} %grad_blocks.7, s32[1024]{0:T(1024)S(1)} %pad_clamp_fusion), kind=kCustom, calls=%fused_computation.1 | custom fusion | bytes 30410560 | tf_op jit(solution)/shard_map/gather | solution.py:915
  336.7 3.8 pad_maximum_fusion.1.b_ref
  341.4 59.7 %psum.7 = f32[4,2,768]{2,1,0:T(2,128)S(1)} all-reduce(f32[4,2,768]{2,1,0:T(2,128)S(1)} %pad_maximum_fusion.3), channel_id=1, replica_groups=mesh['dp'=16,'tensor'=2] {'dp'}, use_global_device_ids=true, to_apply=%region_2.3 | all-reduce | flops 6144 | bytes 49152 | tf_op jit(solution)/shard_map/psum | solution.py:917
  405.3 81.6 %reduce-scatter.2.cloned.1.call-done = bf16[29,128,128]{2,1,0:T(8,128)(2,1)} async-done(((bf16[464,128,128]{2,1,0:T(8,128)(2,1)}), bf16[29,128,128]{2,1,0:T(8,128)(2,1)}) %reduce-scatter.2.cloned.1.call-update) | async-done | bytes 950288 | tf_op jit(solution)/shard_map/reduce_scatter | solution.py:914
  499.2 4.0 bitcast_subtract_fusion
  509.2 88.6 %shard_map.246 = f32[58,128,128]{2,1,0:T(8,128)S(1)} custom-call(f32[58,128,128]{2,1,0:T(8,128)} %pad_maximum_fusion.s_ref, f32[58,128,128]{2,1,0:T(8,128)} %pad_maximum_fusion.1.b_ref), custom_call_target="tpu_custom_call" | custom-call | tf_op jit(solution)/shard_map/pallas_call | solution.py:842
  (104 shorter events, 50.1 us)
Async XLA Ops:
  7.2 123.5 %all-gather.2.cloned.1.call-start = ((), (), s32[]{:S(2)}) async-start(), calls=%async_computation.1 | async-start | bytes 16154624 | tf_op jit(solution)/shard_map/all_gather | solution.py:908
  9.9 477.0 %reduce-scatter.2.cloned.1.call-start = ((), (), s32[]{:S(2)}) async-start(), calls=%async_computation.2 | async-start | bytes 16154624 | tf_op jit(solution)/shard_map/reduce_scatter | solution.py:914
  149.6 10.7 %copy-start.7 = (bf16[4,257,1408]{2,0,1:T(4,128)(2,1)S(1)}, bf16[4,257,1408]{2,0,1:T(4,128)(2,1)}, u32[]{:S(2)}) copy-start(bf16[4,257,1408]{2,0,1:T(4,128)(2,1)} %param.16) | copy-start | bytes 8684548
  158.8 20.0 %collective-permute-start = (bf16[512,768]{1,0:T(8,128)(2,1)}, bf16[512,768]{1,0:T(8,128)(2,1)S(1)}, u32[]{:S(2)}, u32[]{:S(2)}) collective-permute-start(bf16[512,768]{1,0:T(8,128)(2,1)} %get-tuple-element.61.mine), channel_id=1, source_target_pairs={{0,1},{1,0},{2,3},{3,2},{4,5},{5,4},{6,7},{7,6},{8,9},{9,8},{10,11... | collective-permute-start | bytes 2359304 | tf_op jit(solution)/shard_map/ppermute | solution.py:660
  189.8 10.4 %copy-start.19 = (bf16[128,768]{1,0:T(8,128)(2,1)S(1)}, bf16[128,768]{1,0:T(8,128)(2,1)}, u32[]{:S(2)}) copy-start(bf16[128,768]{1,0:T(8,128)(2,1)} %get-tuple-element.65.mine) | copy-start | bytes 589828
  189.8 11.0 %copy-start.15 = (bf16[4,128,768]{2,1,0:T(8,128)(2,1)S(1)}, bf16[4,128,768]{2,1,0:T(8,128)(2,1)}, u32[]{:S(2)}) copy-start(bf16[4,128,768]{2,1,0:T(8,128)(2,1)} %param.18) | copy-start | bytes 2359300
  198.7 28.5 %collective-permute-start.3 = (bf16[384,768]{1,0:T(8,128)(2,1)}, bf16[384,768]{1,0:T(8,128)(2,1)S(1)}, u32[]{:S(2)}, u32[]{:S(2)}) collective-permute-start(bf16[384,768]{1,0:T(8,128)(2,1)} %get-tuple-element.72.mine), channel_id=1, source_target_pairs={{0,1},{1,0},{2,3},{3,2},{4,5},{5,4},{6,7},{7,6},{8,9},{9,8},{10,11... | collective-permute-start | bytes 1769480 | tf_op jit(solution)/shard_map/ppermute | solution.py:660
  200.3 17.6 %collective-permute-start.1 = (bf16[128,768]{1,0:T(8,128)(2,1)S(1)}, bf16[128,768]{1,0:T(8,128)(2,1)S(1)}, u32[]{:S(2)}, u32[]{:S(2)}) collective-permute-start(bf16[128,768]{1,0:T(8,128)(2,1)S(1)} %copy-done.19), channel_id=1, source_target_pairs={{0,1},{1,0},{2,3},{3,2},{4,5},{5,4},{6,7},{7,6},{8,9},{9,8},{10,11... | collective-permute-start | bytes 589832 | tf_op jit(solution)/shard_map/ppermute | solution.py:660
  225.6 13.1 %collective-permute-start.2 = (bf16[128,768]{1,0:T(8,128)(2,1)}, bf16[128,768]{1,0:T(8,128)(2,1)S(1)}, u32[]{:S(2)}, u32[]{:S(2)}) collective-permute-start(bf16[128,768]{1,0:T(8,128)(2,1)} %get-tuple-element.67.mine), channel_id=1, source_target_pairs={{0,1},{1,0},{2,3},{3,2},{4,5},{5,4},{6,7},{7,6},{8,9},{9,8},{10,11... | collective-permute-start | bytes 589832 | tf_op jit(solution)/shard_map/ppermute | solution.py:660
  238.1 58.6 %collective-permute-start.6 = (bf16[384,768]{1,0:T(8,128)(2,1)}, bf16[384,768]{1,0:T(8,128)(2,1)S(1)}, u32[]{:S(2)}, u32[]{:S(2)}) collective-permute-start(bf16[384,768]{1,0:T(8,128)(2,1)} %get-tuple-element.84.text_mine), channel_id=1, source_target_pairs={{0,1},{1,0},{2,3},{3,2},{4,5},{5,4},{6,7},{7,6},{8,9},{9,8},{10,11... | collective-permute-start | bytes 1769480 | tf_op jit(solution)/shard_map/ppermute | solution.py:660
  246.9 24.6 %collective-permute-start.4 = (bf16[128,768]{1,0:T(8,128)(2,1)}, bf16[128,768]{1,0:T(8,128)(2,1)S(1)}, u32[]{:S(2)}, u32[]{:S(2)}) collective-permute-start(bf16[128,768]{1,0:T(8,128)(2,1)} %get-tuple-element.78.mine), channel_id=1, source_target_pairs={{0,1},{1,0},{2,3},{3,2},{4,5},{5,4},{6,7},{7,6},{8,9},{9,8},{10,11... | collective-permute-start | bytes 589832 | tf_op jit(solution)/shard_map/ppermute | solution.py:660
  283.0 13.7 %collective-permute-start.5 = (bf16[128,768]{1,0:T(8,128)(2,1)}, bf16[128,768]{1,0:T(8,128)(2,1)S(1)}, u32[]{:S(2)}, u32[]{:S(2)}) collective-permute-start(bf16[128,768]{1,0:T(8,128)(2,1)} %get-tuple-element.82.query_mine), channel_id=1, source_target_pairs={{0,1},{1,0},{2,3},{3,2},{4,5},{5,4},{6,7},{7,6},{8,9},{9,8},{10,11... | collective-permute-start | bytes 589832 | tf_op jit(solution)/shard_map/ppermute | solution.py:660
  335.1 67.5 %collective-permute-start.7 = (bf16[512,768]{1,0:T(8,128)(2,1)}, bf16[512,768]{1,0:T(8,128)(2,1)}, u32[]{:S(2)}, u32[]{:S(2)}) collective-permute-start(bf16[512,768]{1,0:T(8,128)(2,1)} %get-tuple-element.88), channel_id=1, source_target_pairs={{0,1},{1,0},{2,3},{3,2},{4,5},{5,4},{6,7},{7,6},{8,9},{9,8},{10,11... | collective-permute-start | bytes 2359304 | tf_op jit(solution)/shard_map/ppermute | solution.py:660
  336.6 3.8 copy-start.18
  336.6 3.8 copy-start.24
  336.6 4.8 copy-start.26
  336.6 4.8 copy-start.27
  336.6 4.8 copy-start.28
  336.6 4.7 copy-start.29
  336.6 64.4 %copy-start.13 = (f32[4,2,768]{2,1,0:T(2,128)S(1)}, f32[4,2,768]{2,1,0:T(2,128)}, u32[]{:S(2)}) copy-start(f32[4,2,768]{2,1,0:T(2,128)} %params.11) | copy-start | bytes 73732
  340.4 62.1 %copy-start.12 = (f32[512,768]{1,0:T(8,128)S(1)}, f32[512,768]{1,0:T(8,128)}, u32[]{:S(2)}) copy-start(f32[512,768]{1,0:T(8,128)} %get-tuple-element.87) | copy-start | bytes 4718596
  499.2 4.1 copy-start
  499.2 4.1 copy-start.10
  503.3 94.5 %copy-start.2 = (f32[29,128,128]{2,1,0:T(8,128)}, f32[29,128,128]{2,1,0:T(8,128)S(1)}, u32[]{:S(2)}) copy-start(f32[29,128,128]{2,1,0:T(8,128)S(1)} %bitcast_subtract_fusion) | copy-start | bytes 5701636
  (17 other events, 28.8 us)
Sparse Core Ops, SparseCore 0:
  10.9 119.7 all-gather.1
  335.2 151.6 reduce-scatter.1

commit v3 on v2

--- a/solution.py
+++ b/solution.py
@@ -2,6 +2,7 @@
 
 import jax
 import jax.numpy as jnp
+import numpy as np
 from jax import lax
 from jax.experimental import pallas as pl
 from jax.experimental.pallas import tpu as pltpu
@@ -606,11 +607,33 @@
             ].astype(bf16)
 
 
-def grad_blocks_body(first_block, pairs, total, *refs):
-    sources, target, staged, sems = refs[: len(refs) - 4], refs[-3], refs[-2], refs[-1]
-    copies = []
+def send_block(source, position, targets, sem):
     base = 0
-    for number, (left_at, right_at, right_first, right_width, step) in enumerate(pairs):
+    for target in targets:
+        count = target.shape[0]
+
+        @pl.when((position >= base) & (position < base + count))
+        def _(base=base, target=target):
+            pltpu.make_async_copy(source, target.at[position - base], sem).start()
+
+        base += count
+
+
+def grad_blocks_body(first_block, pairs, source_count, target_count, spare, place, *refs):
+    sources, targets = refs[:source_count], refs[-3 - target_count : -3]
+    staged, blank, sem = refs[-3:]
+    base = 0
+    sent = 0
+    if spare is not None:
+        blank[...] = jnp.zeros_like(blank)
+
+        def one_spare(number, carry):
+            send_block(blank, place[spare[0] + number], targets, sem)
+            return carry
+
+        lax.fori_loop(0, spare[1], one_spare, 0)
+        sent += spare[1]
+    for left_at, right_at, right_first, right_width, step in pairs:
         left, right = sources[left_at], sources[right_at]
         left_tiles, col_total = left.shape[1] // TILE, right_width // TILE
 
@@ -618,39 +641,50 @@
                 right_first=right_first, right_width=right_width):
             cols = pl.ds(pl.multiple_of(chunk * step * TILE, step * TILE), step * TILE)
             product = mm(left[:, cols], right[:, right_first : right_first + right_width], TN)
-            store_blocks(staged, base + chunk * step * col_total, product, col_total)
+            first = base + chunk * step * col_total
+            store_blocks(staged, first, product, col_total)
+
+            def send(number, carry):
+                block = first + number
+                send_block(staged.at[block], place[first_block + block], targets, sem)
+                return carry
+
+            lax.fori_loop(0, step * col_total, send, 0)
             return carry
 
         lax.fori_loop(0, left_tiles // step, one, 0)
-        count = left_tiles * col_total
-        copy = pltpu.make_async_copy(
-            staged.at[pl.ds(base, count)],
-            target.at[pl.ds(first_block + base, count)],
-            sems.at[number],
-        )
-        copy.start()
-        copies.append(copy)
-        base += count
-    for copy in copies:
-        copy.wait()
-
-
-def grad_blocks(buffer, first_block, sources, pairs, flops):
+        base += left_tiles * col_total
+    sent += base
+    whole = staged.at[pl.ds(0, base)]
+    pltpu.make_async_copy(whole, whole, sem).wait()
+    for _ in range(sent - base):
+        pltpu.make_async_copy(blank, blank, sem).wait()
+
+
+def grad_blocks(buffers, place, first_block, sources, pairs, flops, spare=None):
     total = sum(sources[a].shape[1] // TILE * (width // TILE) for a, _, _, width, _ in pairs)
+    fresh = isinstance(buffers[0], jax.ShapeDtypeStruct)
+    given = [] if fresh else list(buffers)
+    aliases = {1 + len(sources) + number: number for number in range(len(given))}
     return pl.pallas_call(
-        functools.partial(grad_blocks_body, first_block, pairs, total),
-        out_shape=jax.ShapeDtypeStruct(buffer.shape, buffer.dtype),
-        in_specs=vmem_specs(len(sources)) + any_specs(1),
-        out_specs=any_specs(1)[0],
+        functools.partial(
+            grad_blocks_body, first_block, pairs, len(sources), len(buffers), spare
+        ),
+        out_shape=tuple(jax.ShapeDtypeStruct(b.shape, b.dtype) for b in buffers),
+        in_specs=[pl.BlockSpec(memory_space=pltpu.SMEM)]
+        + vmem_specs(len(sources))
+        + any_specs(len(given)),
+        out_specs=tuple(any_specs(len(buffers))),
         scratch_shapes=[
             pltpu.VMEM((total, TILE, TILE), bf16),
-            pltpu.SemaphoreType.DMA((len(pairs),)),
+            pltpu.VMEM((TILE, TILE), bf16),
+            pltpu.SemaphoreType.DMA,
         ],
-        input_output_aliases={len(sources): 0},
+        input_output_aliases=aliases,
         compiler_params=vmem_params(),
         cost_estimate=cost(flops, 1e7),
         name="grad_blocks",
-    )(*sources, buffer)
+    )(place, *sources, *given)
 
 
 def swap_tensor(part):
@@ -661,7 +695,7 @@
 
 
 def layer_rows(
-    hidden, image, segment_ids, cotangent, nat, norm_params, heads_local, scale, slot_count
+    hidden, image, segment_ids, cotangent, nat, norm_params, heads_local, scale, place, regions
 ):
     rows, seq, width = hidden.shape
     plan = Plan(
@@ -674,7 +708,7 @@
     )
     up_query = cotangent[:, :NQ].reshape(learned, width)
     up_text = cotangent[:, NQ:].reshape(texts, width)
-    buffer = jnp.zeros((slot_count, TILE, TILE), bf16)
+    buffers = [jax.ShapeDtypeStruct((count, TILE, TILE), bf16) for count in regions]
 
     qkv, self_probs, mixed, part_one = self_forward(
         plan, scale, nat, flat_hidden, segment_ids[:, None, :], segment_ids[:, :, None]
@@ -707,9 +741,10 @@
     )
     other_four_query = swap_tensor(part_four_query)
     feed_pairs = [(0, 1, 0, plan.hidden, 2), (2, 3, 0, width, 2)]
-    buffer = grad_blocks(
-        buffer, plan.text_first, [low_text, before_text, text_gated, third_text_low], feed_pairs,
+    buffers = grad_blocks(
+        buffers, place, plan.text_first, [low_text, before_text, text_gated, third_text_low], feed_pairs,
         4 * texts * width * plan.hidden,
+        spare=(plan.block_count, place.shape[0] - plan.block_count),
     )
     second_grad, cross_low, query_back, key_back, value_back, part_five, norm_second = (
         cross_backward(
@@ -718,12 +753,12 @@
         )
     )
     other_five = swap_tensor(part_five)
-    buffer = grad_blocks(
-        buffer, plan.query_first, [low_second, before_query, query_gated, third_query_low],
+    buffers = grad_blocks(
+        buffers, place, plan.query_first, [low_second, before_query, query_gated, third_query_low],
         feed_pairs, 4 * learned * width * plan.hidden,
     )
-    buffer = grad_blocks(
-        buffer, plan.cross_first,
+    buffers = grad_blocks(
+        buffers, place, plan.cross_first,
         [low_query, query_back, flat_image, key_back, value_back, looked, cross_low],
         [(0, 1, 0, half, 2), (2, 3, 0, half, 1), (2, 4, 0, half, 1), (5, 6, 0, width, 1)],
         4 * rows * plan.keys * plan.image_width * half,
@@ -733,8 +768,8 @@
         part_four_text, other_four_text, norm_params, qkv, self_probs,
     )
     other_six = swap_tensor(part_six)
-    buffer = grad_blocks(
-        buffer, plan.self_first, [flat_hidden, self_back, mixed, self_low],
+    buffers = grad_blocks(
+        buffers, place, plan.self_first, [flat_hidden, self_back, mixed, self_low],
         [(0, 1, 0, half, 2), (0, 1, half, half, 2), (0, 1, 2 * half, half, 2), (2, 3, 0, width, 1)],
         8 * tokens * width * half,
     )
@@ -743,7 +778,149 @@
         [out_query.reshape(rows, NQ, width), out_text.reshape(rows, seq - NQ, width)], axis=1
     )
     norm_part = jnp.stack([norm_first, norm_second, norm_query, norm_text])
-    return (output_rows, input_grad.reshape(rows, seq, width), buffer, norm_part)
+    return (output_rows, input_grad.reshape(rows, seq, width), buffers, norm_part)
+
+
+CHIP_RING = ((0, 0), (1, 0), (2, 0), (3, 0), (3, 1), (2, 1), (1, 1), (0, 1))
+RING = len(CHIP_RING)
+RING_DEVICES = 2 * RING
+
+
+def ring_index(position, core):
+    z, x = CHIP_RING[position % RING]
+    return (z * 2 + x) * 2 + core
+
+
+def direction_of(core):
+    return 1 - 2 * core
+
+
+RING_PAIRS = [
+    (ring_index(position, core), ring_index(position + direction_of(core), core))
+    for position in range(RING)
+    for core in range(2)
+]
+
+
+def ring_place(index):
+    return CHIP_RING.index((index // 4, index // 2 % 2)), index % 2
+
+
+CORE_PAIRS = [(index, index ^ 1) for index in range(RING_DEVICES)]
+
+
+def chain_parts(slots, chains):
+    cuts = [slots * number // chains for number in range(chains + 1)]
+    return [(first, last - first) for first, last in zip(cuts, cuts[1:])]
+
+
+def place_blocks_body(counts, first, ids, *refs):
+    sources, target, sem = refs[: len(counts)], refs[-2], refs[-1]
+    base = first
+    for source, count in zip(sources, counts):
+
+        def one(number, carry, base=base, source=source):
+            pltpu.make_async_copy(
+                source.at[number], target.at[ids[base + number]], sem
+            ).start()
+            return carry
+
+        lax.fori_loop(0, count, one, 0)
+        base += count
+    total = sum(counts)
+    pltpu.make_async_copy(
+        target.at[pl.ds(0, total)], target.at[pl.ds(0, total)], sem
+    ).wait()
+
+
+def place_blocks(ids, first, sources, target, shape):
+    counts = [source.shape[0] for source in sources]
+    operands = [ids, *sources]
+    specs = [pl.BlockSpec(memory_space=pltpu.SMEM)] + vmem_specs(len(sources))
+    aliases = {}
+    if target is not None:
+        operands.append(target)
+        specs += any_specs(1)
+        aliases = {len(operands) - 1: 0}
+    return pl.pallas_call(
+        functools.partial(place_blocks_body, counts, first),
+        out_shape=jax.ShapeDtypeStruct(shape, bf16),
+        in_specs=specs,
+        out_specs=any_specs(1)[0],
+        scratch_shapes=[pltpu.SemaphoreType.DMA],
+        input_output_aliases=aliases,
+        cost_estimate=cost(0, 4 * sum(counts) * TILE * TILE),
+        name="place_blocks",
+    )(*operands)
+
+
+def gather_ring(shard, order, chains=2):
+    slots = shard.shape[0]
+    parts = chain_parts(slots, chains)
+    table = np.zeros((RING_DEVICES, RING_DEVICES * slots), np.int32)
+    for index in range(RING_DEVICES):
+        position, core = ring_place(index)
+        found = []
+        for step in range(RING):
+            for side in (core, 1 - core):
+                owner = ring_index(position - direction_of(side) * step, side)
+                found += [owner * slots + slot for slot in range(slots)]
+        table[index] = found
+    ids = order[jnp.asarray(table)[lax.axis_index("dp")]]
+    shape = (order.shape[0], TILE, TILE)
+    other = lax.ppermute(shard, "dp", CORE_PAIRS)
+    held = [shard[first : first + count] for first, count in parts]
+    natural = None
+    waiting, first = [shard, other], 0
+    for step in range(1, RING):
+        held = [lax.ppermute(piece, "dp", RING_PAIRS) for piece in held]
+        if step > 1:
+            natural = place_blocks(ids, first, waiting, natural, shape)
+            held[0], natural = lax.optimization_barrier((held[0], natural))
+            waiting, first = [], step * 2 * slots
+        waiting = waiting + held + [lax.ppermute(piece, "dp", CORE_PAIRS) for piece in held]
+    return place_blocks(ids, first, waiting, natural, shape)
+
+
+def scatter_positions(slots):
+    table = np.zeros((RING_DEVICES, RING_DEVICES * slots), np.int32)
+    for index in range(RING_DEVICES):
+        position, core = ring_place(index)
+        for step in range(1, RING + 1):
+            for number, side in enumerate((1 - core, core)):
+                owner = ring_index(position - direction_of(side) * step, side)
+                base = (number * RING + step - 1) * slots
+                table[index, owner * slots : (owner + 1) * slots] = base + np.arange(slots)
+    return table
+
+
+def scatter_ring(early, late, own, slots, chains=2):
+    others = [lax.ppermute(early, "dp", CORE_PAIRS), lax.ppermute(late, "dp", CORE_PAIRS)]
+    early_steps = early.shape[0] // slots
+    parts = chain_parts(slots, chains)
+    held = [None] * chains
+    for step in range(1, RING + 1):
+        base = (step - 1) * slots
+        other, other_base = others[0], base
+        if step > early_steps:
+            other, other_base = others[1], base - early_steps * slots
+        for number, (first, count) in enumerate(parts):
+            summed = own[base + first : base + first + count].astype(f32) + other[
+                other_base + first : other_base + first + count
+            ].astype(f32)
+            if held[number] is not None:
+                summed = summed + held[number].astype(f32)
+            if step < RING:
+                summed = lax.ppermute(summed.astype(bf16), "dp", RING_PAIRS)
+            held[number] = summed
+    return jnp.concatenate(held, axis=0)
+
+
+def sum_small(values):
+    for bit in (1, 2, 4, 8):
+        pairs = [(index, index ^ bit) for index in range(RING_DEVICES)]
+        values = values + lax.ppermute(values, "dp", pairs)
+    return values
 
 
 def times(left_matrix, right_matrix):
@@ -905,16 +1082,29 @@
     scale = (width // HEADS) ** (-0.5)
     order = slot_block[0]
     slot_count = order.shape[0]
-    gathered = lax.all_gather(weight_master[0].astype(jnp.bfloat16), "dp", axis=0, tiled=True)
-    inverse = jnp.zeros_like(order).at[order].set(jnp.arange(slot_count, dtype=jnp.int32))
-    natural = gathered[inverse]
+    slots = weight_master.shape[1]
+    shard = weight_master[0].astype(bf16)
+    ring = lax.axis_size("dp") == RING_DEVICES
+    if ring:
+        natural = gather_ring(shard, order)
+        positions = jnp.asarray(scatter_positions(slots))[lax.axis_index("dp")]
+        regions = (2 * slots, (RING - 2) * slots, RING * slots)
+    else:
+        positions = jnp.arange(slot_count, dtype=jnp.int32)
+        gathered = lax.all_gather(shard, "dp", axis=0, tiled=True)
+        natural = gathered[jnp.zeros_like(order).at[order].set(positions)]
+        regions = (slot_count,)
+    place = jnp.zeros_like(order).at[order].set(positions)
     out_rows, in_grad, packed, norm_part = layer_rows(
-        hidden, image, segment_ids, cotangent, natural, norm_params, heads_local, scale, slot_count
-    )
-    owned = lax.psum_scatter(
-        packed[order], "dp", scatter_dimension=0, tiled=True
-    ).astype(jnp.float32)
-    norm_total = lax.psum(norm_part, "dp")
+        hidden, image, segment_ids, cotangent, natural, norm_params, heads_local, scale, place,
+        regions,
+    )
+    if ring:
+        owned = scatter_ring(*packed, slots)
+        norm_total = sum_small(norm_part)
+    else:
+        owned = lax.psum_scatter(packed[0], "dp", scatter_dimension=0, tiled=True).astype(f32)
+        norm_total = lax.psum(norm_part, "dp")
     updated = rotated_update(
         owned,
         weight_master[0],

time: 618 us -> 474 us (0.77); the launches traced: 607 us -> 470 us
  waiting for transfers between devices: 221 us -> 98.5 us
  blocking collectives: 59.7 us -> 0 us
  starting transfers between devices: 9.56 us -> 67 us
  local copies, waits for them, and re-layouts: 61.8 us -> 31.6 us
  Pallas kernels: 207 us -> 231 us
  between operations: 14.9 us -> 1.83 us
    all_gather x1 -> x0, waiting for transfers between devices: 117 us -> none  [per_device(): lax.all_gather(weight_master[0].astype(jnp.bfloat16), 'dp', axis=0, tiled...]
    reduce_scatter x1 -> x0, waiting for transfers between devices: 81.6 us -> none  [per_device(): lax.psum_scatter(packed[order], 'dp', scatter_dimension=0, tiled=True)]
    ppermute x0 -> x49, waiting for transfers between devices: none -> 76.4 us  [the longest x14 36.5 us: scatter_ring(): summed = lax.ppermute(summed.astype(bf16), 'dp', RING_PAIRS)]
    psum x1 -> x0, blocking collectives: 59.7 us -> none  [per_device(): norm_total = lax.psum(norm_part, 'dp')]
    ppermute x0 -> x49, starting transfers between devices: none -> 57.4 us  [the longest x14 25.2 us: gather_ring(): held = [lax.ppermute(piece, 'dp', RING_PAIRS) for piece in held]]
    gather x2 -> x1, local copies, waits for them, and re-layouts: 37.7 us -> 4.65 us  [gather_ring(): ids = order[jnp.asarray(table)[lax.axis_index('dp')]]]
    pallas_call x4 -> x11, Pallas kernels: 33.5 us -> 57 us  [the longest x4 36.5 us: grad_blocks(): pl.pallas_call(functools.partial(grad_blocks_body, first_block, pairs, le...]
    unnamed x63 -> x119, local copies, waits for them, and re-layouts: 7.63 us -> 15.6 us
  transfers between devices with their start and end apart: 10 -> 57, of which waited for: 4 -> 26; matrix products, arithmetic and copies ran while one was open for 4% -> 5% of each run, Pallas kernels for 12% -> 19%
where the time goes in v3:
time: 474 us; the launch traced here: 470 us
  Pallas kernels  231 us (49%)
  waiting for transfers between devices  98.5 us (21%)
  starting transfers between devices  67 us (14%)
  local copies, waits for them, and re-layouts  31.6 us (7%)
  matrix products  20.4 us (4%)
  other arithmetic  20.2 us (4%)
    pallas_call x1, Pallas kernels, ortho(): pl.pallas_call(functools.partial(ortho_body, n_pad, n, g), out_shape=jax....  88.9 us
    ppermute x14, waiting for transfers between devices, scatter_ring(): summed = lax.ppermute(summed.astype(bf16), 'dp', RING_PAIRS)  36.5 us
    pallas_call x4, Pallas kernels, grad_blocks(): pl.pallas_call(functools.partial(grad_blocks_body, first_block, pairs, le...  36.5 us
    ppermute x14, starting transfers between devices, gather_ring(): held = [lax.ppermute(piece, 'dp', RING_PAIRS) for piece in held]  25.2 us
    ppermute x14, starting transfers between devices, scatter_ring(): summed = lax.ppermute(summed.astype(bf16), 'dp', RING_PAIRS)  24.3 us
    ppermute x14, waiting for transfers between devices, gather_ring(): held = [lax.ppermute(piece, 'dp', RING_PAIRS) for piece in held]  23.2 us
    ppermute x8, waiting for transfers between devices, swap_tensor(): return lax.ppermute(part, 'tensor', [(0, 1), (1, 0)])  22.1 us
    pallas_call x7, Pallas kernels, place_blocks(): pl.pallas_call(functools.partial(place_blocks_body, counts, first), out_s...  20.5 us
  transfers between devices with their start and end apart: 57, of which 26 were waited for; matrix products, arithmetic and copies ran while one was open for 5% of the time, Pallas kernels for 19%

profile of v3, /device:TPU:0, one launch (start us, length us, event | category | flops | bytes accessed | tf_op | source)
XLA Modules:
  0.0 470.1 jit_solution(11654257560010299152)
XLA Ops:
  7.1 5.1 %collective-permute-done.3.refs_3_ = bf16[15,128,128]{2,1,0:T(8,128)(2,1)S(1)} collective-permute-done((bf16[15,128,128]{2,1,0:T(8,128)(2,1)S(1)}, bf16[15,128,128]{2,1,0:T(8,128)(2,1)S(1)}, u32[]{:S(2)}, u32[]{:S(2)}) %collective-permute-start.3) | collective-permute-done | bytes 491552 | tf_op jit(solution)/shard_map/ppermute | solution.py:876
  25.3 4.7 gather_fusion
  91.9 9.2 %self_forward.1 = (bf16[3,512,384]{2,1,0:T(8,128)(2,1)}, f32[4,3,256,128]{3,2,1,0:T(8,128)}, bf16[512,384]{1,0:T(8,128)(2,1)}, bf16[512,768]{1,0:T(8,128)(2,1)}) custom-call(bf16[464,128,128]{2,1,0:T(8,128)(2,1)} %place_blocks.13.nat, bf16[512,768]{1,0:T(8,128)(2,1)} %bitcast.82, s32[4,1,128]{2,1,0:T(1,128)} %bitcast.102, s32[4,128,1]{2,1,0:T(8,128)} %copy.47.seg_col), custom_call_target="tpu_custom_call" | custom-call | flops 1207959552 | bytes 8000000 | tf_op jit(solution)/shard_map/self_forward/pallas_call | solution.py:181
  105.0 9.2 %image_forward.1 = (bf16[1088,384]{1,0:T(8,128)(2,1)}, bf16[1088,384]{1,0:T(8,128)(2,1)}) custom-call(bf16[464,128,128]{2,1,0:T(8,128)(2,1)} %place_blocks.13.nat, bf16[1088,1408]{1,0:T(8,128)(2,1)} %bitcast.75), custom_call_target="tpu_custom_call" | custom-call | flops 2353004544 | bytes 8000000 | tf_op jit(solution)/shard_map/image_forward/pallas_call | solution.py:217
  114.2 6.8 %collective-permute-done.29.other = bf16[512,768]{1,0:T(8,128)(2,1)S(1)} collective-permute-done((bf16[512,768]{1,0:T(8,128)(2,1)}, bf16[512,768]{1,0:T(8,128)(2,1)S(1)}, u32[]{:S(2)}, u32[]{:S(2)}) %collective-permute-start.29) | collective-permute-done | bytes 786464 | tf_op jit(solution)/shard_map/ppermute | solution.py:694
  121.8 10.2 %cross_forward.1 = (f32[512,768]{1,0:T(8,128)}, f32[128,768]{1,0:T(8,128)}, f32[384,768]{1,0:T(8,128)}, bf16[128,768]{1,0:T(8,128)(2,1)}, bf16[384,768]{1,0:T(8,...) custom-call(bf16[464,128,128]{2,1,0:T(8,128)(2,1)} %place_blocks.13., ...), custom_call_target="tpu_custom_call" | custom-call | flops 150994944 | bytes 12000000 | tf_op jit(solution)/shard_map/cross_forward/pallas_call | solution.py:278
  132.0 8.9 %text_forward.1 = (bf16[384,1536]{1,0:T(8,128)(2,1)}, f32[384,1536]{1,0:T(8,128)}, bf16[384,768]{1,0:T(8,128)(2,1)}) custom-call(bf16[464,128,128]{2,1,0:T(8,128)(2,1)} %place_blocks.13.nat, bf16[384,768]{1,0:T(8,128)(2,1)} %get-tuple-element.107.low_text.refs_0_), custom_call_target="tpu_custom_call" | custom-call | flops 1811939328 | bytes 10000000 | tf_op jit(solution)/shard_map/text_forward/pallas_call | solution.py:361
  144.6 15.4 %collective-permute-done.30.other = bf16[128,768]{1,0:T(8,128)(2,1)S(1)} collective-permute-done((bf16[128,768]{1,0:T(8,128)(2,1)S(1)}, bf16[128,768]{1,0:T(8,128)(2,1)S(1)}, u32[]{:S(2)}, u32[]{:S(2)}) %collective-permute-start.30) | collective-permute-done | bytes 196640 | tf_op jit(solution)/shard_map/ppermute | solution.py:694
  160.6 7.1 %query_forward.1 = (f32[128,768]{1,0:T(8,128)}, f32[128,768]{1,0:T(8,128)}, bf16[128,768]{1,0:T(8,128)(2,1)}, bf16[128,1536]{1,0:T(8,128)(2,1)}, f32[128,1536]{1,0:T(8,128)}, /*index=5*/bf16[128,768]{1,0:T(8,128)(2,1)}) custom-call(bf16[464,128,128]{2,1,0:T(8,128)(2,1)} %place_blocks.13.nat, f32[128,768]{1,0:T(8,128)} %get-tuple-element.100.first_query, ...), custom_call_target="tpu_custom_call" | custom-call | flops 603979776 | bytes 8000000 | tf_op jit(solution)/shard_map/query_forward/pallas_call | solution.py:375
  170.2 10.1 %feed_backward.3 = (bf16[384,768]{1,0:T(8,128)(2,1)}, f32[384,768]{1,0:T(8,128)}, bf16[384,768]{1,0:T(8,128)(2,1)}, bf16[384,1536]{1,0:T(8,128)(2,1)}, bf16[384,768]{1,0:T(8,128)(2,1)}, /*index=5*/f32[2,768]{1,0:T(2,128)}) custom-call(bf16[464,128,128]{2,1,0:T(8,128)(2,1)} %place_blocks.13.nat, f32[384,768]{1,0:T(8,128)} %get-tuple-element.106.states, ...), custom_call_target="tpu_custom_call" | custom-call | flops 1811939328 | bytes 10000000 | tf_op jit(solution)/shard_map/feed_backward/pallas_call | solution.py:436
  186.1 7.5 %feed_backward.2 = (bf16[128,768]{1,0:T(8,128)(2,1)}, f32[128,768]{1,0:T(8,128)}, bf16[128,768]{1,0:T(8,128)(2,1)}, bf16[128,1536]{1,0:T(8,128)(2,1)}, bf16[128,768]{1,0:T(8,128)(2,1)}, /*index=5*/f32[2,768]{1,0:T(2,128)}) custom-call(bf16[464,128,128]{2,1,0:T(8,128)(2,1)} %place_blocks.13.nat, f32[128,768]{1,0:T(8,128)} %get-tuple-element.102.states, ...), custom_call_target="tpu_custom_call" | custom-call | flops 603979776 | bytes 10000000 | tf_op jit(solution)/shard_map/feed_backward/pallas_call | solution.py:436
  195.4 8.6 %grad_blocks.4 = (bf16[58,128,128]{2,1,0:T(8,128)(2,1)}, bf16[174,128,128]{2,1,0:T(8,128)(2,1)}, bf16[232,128,128]{2,1,0:T(8,128)(2,1)}) custom-call(s32[464]{0:T(512)} %scatter_custom_fusion.place, bf16[384,768]{1,0:T(8,128)(2,1)} %get-tuple-element.107.low_text.refs_0_, bf16[384,1536]{1,0:T(8,128)(2,1)} %get-tuple-element.138.refs_1_, ...), custom_call_target="tpu_custom_call" | custom-call | flops 1811939328 | bytes 10000000 | tf_op jit(solution)/shard_map/grad_blocks/pallas_call | solution.py:669
  204.0 6.6 %grad_blocks.5 = (bf16[58,128,128]{2,1,0:T(8,128)(2,1)}, bf16[174,128,128]{2,1,0:T(8,128)(2,1)}, bf16[232,128,128]{2,1,0:T(8,128)(2,1)}) custom-call(s32[464]{0:T(512)} %scatter_custom_fusion.place, bf16[128,768]{1,0:T(8,128)(2,1)} %get-tuple-element.134.refs_0_, ...), custom_call_target="tpu_custom_call", output_to_operand_aliasing={{0}: (5, {}), {1}: (6, {}), {2}: (7, {})} | custom-call | flops 603979776 | bytes 10000000 | tf_op jit(solution)/shard_map/grad_blocks/pallas_call | solution.py:669
  211.3 10.8 %cross_backward.1 = (f32[128,768]{1,0:T(8,128)}, bf16[128,768]{1,0:T(8,128)(2,1)}, bf16[128,384]{1,0:T(8,128)(2,1)}, bf16[1088,384]{1,0:T(8,128)(2,1)}, bf16[108...) custom-call(bf16[464,128,128]{2,1,0:T(8,128)(2,1)} %place_blocks.13.nat, ...), custom_call_target="tpu_custom_call" | custom-call | flops 301989888 | bytes 10000000 | tf_op jit(solution)/shard_map/cross_backward/pallas_call | solution.py:493
  222.5 14.1 %grad_blocks.6 = (bf16[58,128,128]{2,1,0:T(8,128)(2,1)}, bf16[174,128,128]{2,1,0:T(8,128)(2,1)}, bf16[232,128,128]{2,1,0:T(8,128)(2,1)}) custom-call(s32[464]{0:T(512)} %scatter_custom_fusion.place, bf16[128,768]{1,0:T(8,128)(2,1)} %get-tuple-element.128.refs_0_, ...), custom_call_target="tpu_custom_call", output_to_operand_aliasing={{0}: (8, {}), {1}: (9, {}), {2}: (10, {})} | custom-call | flops 2353004544 | bytes 10000000 | tf_op jit(solution)/shard_map/grad_blocks/pallas_call | solution.py:669
  237.5 11.9 %self_backward.1 = (f32[512,768]{1,0:T(8,128)}, bf16[512,768]{1,0:T(8,128)(2,1)}, bf16[512,1152]{1,0:T(8,128)(2,1)}, bf16[512,768]{1,0:T(8,128)(2,1)}, f32[2,768]{1,0:T(2,128)}) custom-call(bf16[464,128,128]{2,1,0:T(8,128)(2,1)} %place_blocks.13.nat, f32[512,768]{1,0:T(8,128)} %get-tuple-element.111.resid, f32[128,768]{1,0:T(8,128)} %get-tuple-element.117.query_grad, ...), custom_call_target="tpu_custom_call" | custom-call | flops 1207959552 | bytes 12000000 | tf_op jit(solution)/shard_map/self_backward/pallas_call | solution.py:577
  249.4 7.2 %grad_blocks.7 = (bf16[58,128,128]{2,1,0:T(8,128)(2,1)}, bf16[174,128,128]{2,1,0:T(8,128)(2,1)}, bf16[232,128,128]{2,1,0:T(8,128)(2,1)}) custom-call(s32[464]{0:T(512)} %scatter_custom_fusion.place, bf16[512,768]{1,0:T(8,128)(2,1)} %bitcast.84, ...), custom_call_target="tpu_custom_call", output_to_operand_aliasing={{0}: (5, {}), {1}: (6, {}), {2}: (7, {})} | custom-call | flops 1207959552 | bytes 10000000 | tf_op jit(solution)/shard_map/grad_blocks/pallas_call | solution.py:669
  257.2 11.7 %collective-permute-done.38 = bf16[58,128,128]{2,1,0:T(8,128)(2,1)S(1)} collective-permute-done((bf16[58,128,128]{2,1,0:T(8,128)(2,1)}, bf16[58,128,128]{2,1,0:T(8,128)(2,1)S(1)}, u32[]{:S(2)}, u32[]{:S(2)}) %collective-permute-start.38) | collective-permute-done | bytes 1900576 | tf_op jit(solution)/shard_map/ppermute | solution.py:898
  274.7 4.1 collective-permute-done.39
  330.6 5.0 %collective-permute-done.44 = bf16[14,128,128]{2,1,0:T(8,128)(2,1)S(1)} collective-permute-done((bf16[14,128,128]{2,1,0:T(8,128)(2,1)S(1)}, bf16[14,128,128]{2,1,0:T(8,128)(2,1)S(1)}, u32[]{:S(2)}, u32[]{:S(2)}) %collective-permute-start.44) | collective-permute-done | bytes 458784 | tf_op jit(solution)/shard_map/ppermute | solution.py:914
  345.9 5.1 %collective-permute-done.52 = bf16[15,128,128]{2,1,0:T(8,128)(2,1)S(1)} collective-permute-done((bf16[15,128,128]{2,1,0:T(8,128)(2,1)S(1)}, bf16[15,128,128]{2,1,0:T(8,128)(2,1)S(1)}, u32[]{:S(2)}, u32[]{:S(2)}) %collective-permute-start.52) | collective-permute-done | bytes 491552 | tf_op jit(solution)/shard_map/ppermute | solution.py:914
  360.0 4.3 bitcast_subtract_fusion
  367.2 4.1 bitcast_add_fusion.1
  378.6 88.9 %shard_map.264 = f32[58,128,128]{2,1,0:T(8,128)S(1)} custom-call(f32[58,128,128]{2,1,0:T(8,128)} %get-tuple-element.164.s_ref, f32[58,128,128]{2,1,0:T(8,128)} %get-tuple-element.165.b_ref), custom_call_target="tpu_custom_call" | custom-call | tf_op jit(solution)/shard_map/pallas_call | solution.py:1019
  (275 shorter events, 192.0 us)
Async XLA Ops:
  5.5 11.7 %collective-permute-start = (bf16[14,128,128]{2,1,0:T(8,128)(2,1)S(1)}, bf16[14,128,128]{2,1,0:T(8,128)(2,1)}, u32[]{:S(2)}, u32[]{:S(2)}) collective-permute-start(bf16[14,128,128]{2,1,0:T(8,128)(2,1)S(1)} %slice.154), channel_id=1, source_target_pairs={{0,8},{2,6},{8,16},{10,2},{16,24},{18,10},{24,28},{26,18},{28,20},... | collective-permute-start | bytes 1376264 | tf_op jit(solution)/shard_map/ppermute | solution.py:876
  7.1 22.8 %collective-permute-start.2 = (bf16[29,128,128]{2,1,0:T(8,128)(2,1)S(1)}, bf16[29,128,128]{2,1,0:T(8,128)(2,1)S(1)}, u32[]{:S(2)}, u32[]{:S(2)}) collective-permute-start(bf16[29,128,128]{2,1,0:T(8,128)(2,1)S(1)} %bitcast_convert_fusion.refs_0_), channel_id=1, source_target_pairs={{0,2},{2,0},{4,6},{6,4},{8,10},{10,8},{12,14},{14,12},{16,18},{18,... | collective-permute-start | bytes 2850824 | tf_op jit(solution)/shard_map/ppermute | solution.py:871
  17.2 12.8 %collective-permute-start.5 = (bf16[15,128,128]{2,1,0:T(8,128)(2,1)S(1)}, bf16[15,128,128]{2,1,0:T(8,128)(2,1)S(1)}, u32[]{:S(2)}, u32[]{:S(2)}) collective-permute-start(bf16[15,128,128]{2,1,0:T(8,128)(2,1)S(1)} %collective-permute-done.3.refs_3_), channel_id=1, source_target_pairs={{0,2},{2,0},{4,6},{6,4},{8,10},{10,8},{12,14},{14,12},{16,18},{18,... | collective-permute-start | bytes 1474568 | tf_op jit(solution)/shard_map/ppermute | solution.py:881
  17.7 18.0 %collective-permute-start.1 = (bf16[14,128,128]{2,1,0:T(8,128)(2,1)}, bf16[14,128,128]{2,1,0:T(8,128)(2,1)}, u32[]{:S(2)}, u32[]{:S(2)}) collective-permute-start(bf16[14,128,128]{2,1,0:T(8,128)(2,1)} %collective-permute-done.refs_2_), channel_id=1, source_target_pairs={{0,8},{2,6},{8,16},{10,2},{16,24},{18,10},{24,28},{26,18},{28,20},... | collective-permute-start | bytes 1376264 | tf_op jit(solution)/shard_map/ppermute | solution.py:876
  22.4 15.4 %collective-permute-start.11 = (bf16[15,128,128]{2,1,0:T(8,128)(2,1)S(1)}, bf16[15,128,128]{2,1,0:T(8,128)(2,1)}, u32[]{:S(2)}, u32[]{:S(2)}) collective-permute-start(bf16[15,128,128]{2,1,0:T(8,128)(2,1)S(1)} %collective-permute-done.7.refs_1_), channel_id=1, source_target_pairs={{0,8},{2,6},{8,16},{10,2},{16,24},{18,10},{24,28},{26,18},{28,20},... | collective-permute-start | bytes 1474568 | tf_op jit(solution)/shard_map/ppermute | solution.py:876
  25.2 14.2 %collective-permute-start.9 = (bf16[15,128,128]{2,1,0:T(8,128)(2,1)S(1)}, bf16[15,128,128]{2,1,0:T(8,128)(2,1)}, u32[]{:S(2)}, u32[]{:S(2)}) collective-permute-start(bf16[15,128,128]{2,1,0:T(8,128)(2,1)S(1)} %collective-permute-done.7.refs_1_), channel_id=1, source_target_pairs={{0,2},{2,0},{4,6},{6,4},{8,10},{10,8},{12,14},{14,12},{16,18},{18,... | collective-permute-start | bytes 1474568 | tf_op jit(solution)/shard_map/ppermute | solution.py:881
  37.8 12.4 %collective-permute-start.15 = (bf16[15,128,128]{2,1,0:T(8,128)(2,1)}, bf16[15,128,128]{2,1,0:T(8,128)(2,1)S(1)}, u32[]{:S(2)}, u32[]{:S(2)}) collective-permute-start(bf16[15,128,128]{2,1,0:T(8,128)(2,1)} %collective-permute-done.11.refs_1_), channel_id=1, source_target_pairs={{0,8},{2,6},{8,16},{10,2},{16,24},{18,10},{24,28},{26,18},{28,20},... | collective-permute-start | bytes 1474568 | tf_op jit(solution)/shard_map/ppermute | solution.py:876
  39.4 12.4 %collective-permute-start.13 = (bf16[15,128,128]{2,1,0:T(8,128)(2,1)}, bf16[15,128,128]{2,1,0:T(8,128)(2,1)S(1)}, u32[]{:S(2)}, u32[]{:S(2)}) collective-permute-start(bf16[15,128,128]{2,1,0:T(8,128)(2,1)} %collective-permute-done.11.refs_1_), channel_id=1, source_target_pairs={{0,2},{2,0},{4,6},{6,4},{8,10},{10,8},{12,14},{14,12},{16,18},{18,... | collective-permute-start | bytes 1474568 | tf_op jit(solution)/shard_map/ppermute | solution.py:881
  45.0 11.1 %collective-permute-start.10 = (bf16[14,128,128]{2,1,0:T(8,128)(2,1)S(1)}, bf16[14,128,128]{2,1,0:T(8,128)(2,1)S(1)}, u32[]{:S(2)}, u32[]{:S(2)}) collective-permute-start(bf16[14,128,128]{2,1,0:T(8,128)(2,1)S(1)} %collective-permute-done.6.refs_0_), channel_id=1, source_target_pairs={{0,8},{2,6},{8,16},{10,2},{16,24},{18,10},{24,28},{26,18},{28,20},... | collective-permute-start | bytes 1376264 | tf_op jit(solution)/shard_map/ppermute | solution.py:876
  51.8 11.0 %collective-permute-start.17 = (bf16[15,128,128]{2,1,0:T(8,128)(2,1)S(1)}, bf16[15,128,128]{2,1,0:T(8,128)(2,1)S(1)}, u32[]{:S(2)}, u32[]{:S(2)}) collective-permute-start(bf16[15,128,128]{2,1,0:T(8,128)(2,1)S(1)} %collective-permute-done.15.refs_1_), channel_id=1, source_target_pairs={{0,2},{2,0},{4,6},{6,4},{8,10},{10,8},{12,14},{14,12},{16,18},{18,... | collective-permute-start | bytes 1474568 | tf_op jit(solution)/shard_map/ppermute | solution.py:881
  61.9 11.0 %collective-permute-start.21 = (bf16[15,128,128]{2,1,0:T(8,128)(2,1)S(1)}, bf16[15,128,128]{2,1,0:T(8,128)(2,1)S(1)}, u32[]{:S(2)}, u32[]{:S(2)}) collective-permute-start(bf16[15,128,128]{2,1,0:T(8,128)(2,1)S(1)} %collective-permute-done.19.refs_1_), channel_id=1, source_target_pairs={{0,2},{2,0},{4,6},{6,4},{8,10},{10,8},{12,14},{14,12},{16,18},{18,... | collective-permute-start | bytes 1474568 | tf_op jit(solution)/shard_map/ppermute | solution.py:881
  101.1 19.8 %collective-permute-start.29 = (bf16[512,768]{1,0:T(8,128)(2,1)}, bf16[512,768]{1,0:T(8,128)(2,1)S(1)}, u32[]{:S(2)}, u32[]{:S(2)}) collective-permute-start(bf16[512,768]{1,0:T(8,128)(2,1)} %get-tuple-element.97.mine), channel_id=1, source_target_pairs={{0,1},{1,0},{2,3},{3,2},{4,5},{5,4},{6,7},{7,6},{8,9},{9,8},{10,11... | collective-permute-start | bytes 2359304 | tf_op jit(solution)/shard_map/ppermute | solution.py:694
  140.9 28.5 %collective-permute-start.32 = (bf16[384,768]{1,0:T(8,128)(2,1)}, bf16[384,768]{1,0:T(8,128)(2,1)S(1)}, u32[]{:S(2)}, u32[]{:S(2)}) collective-permute-start(bf16[384,768]{1,0:T(8,128)(2,1)} %get-tuple-element.108.mine), channel_id=1, source_target_pairs={{0,1},{1,0},{2,3},{3,2},{4,5},{5,4},{6,7},{7,6},{8,9},{9,8},{10,11... | collective-permute-start | bytes 1769480 | tf_op jit(solution)/shard_map/ppermute | solution.py:694
  144.2 15.7 %collective-permute-start.30 = (bf16[128,768]{1,0:T(8,128)(2,1)S(1)}, bf16[128,768]{1,0:T(8,128)(2,1)S(1)}, u32[]{:S(2)}, u32[]{:S(2)}) collective-permute-start(bf16[128,768]{1,0:T(8,128)(2,1)S(1)} %copy-done.49), channel_id=1, source_target_pairs={{0,1},{1,0},{2,3},{3,2},{4,5},{5,4},{6,7},{7,6},{8,9},{9,8},{10,11... | collective-permute-start | bytes 589832 | tf_op jit(solution)/shard_map/ppermute | solution.py:694
  167.6 17.8 %collective-permute-start.31 = (bf16[128,768]{1,0:T(8,128)(2,1)}, bf16[128,768]{1,0:T(8,128)(2,1)S(1)}, u32[]{:S(2)}, u32[]{:S(2)}) collective-permute-start(bf16[128,768]{1,0:T(8,128)(2,1)} %get-tuple-element.103.mine), channel_id=1, source_target_pairs={{0,1},{1,0},{2,3},{3,2},{4,5},{5,4},{6,7},{7,6},{8,9},{9,8},{10,11... | collective-permute-start | bytes 589832 | tf_op jit(solution)/shard_map/ppermute | solution.py:694
  180.3 56.3 %collective-permute-start.35 = (bf16[384,768]{1,0:T(8,128)(2,1)}, bf16[384,768]{1,0:T(8,128)(2,1)S(1)}, u32[]{:S(2)}, u32[]{:S(2)}) collective-permute-start(bf16[384,768]{1,0:T(8,128)(2,1)} %get-tuple-element.120.text_mine), channel_id=1, source_target_pairs={{0,1},{1,0},{2,3},{3,2},{4,5},{5,4},{6,7},{7,6},{8,9},{9,8},{10,11... | collective-permute-start | bytes 1769480 | tf_op jit(solution)/shard_map/ppermute | solution.py:694
  193.6 16.9 %collective-permute-start.33 = (bf16[128,768]{1,0:T(8,128)(2,1)}, bf16[128,768]{1,0:T(8,128)(2,1)S(1)}, u32[]{:S(2)}, u32[]{:S(2)}) collective-permute-start(bf16[128,768]{1,0:T(8,128)(2,1)} %get-tuple-element.114.mine), channel_id=1, source_target_pairs={{0,1},{1,0},{2,3},{3,2},{4,5},{5,4},{6,7},{7,6},{8,9},{9,8},{10,11... | collective-permute-start | bytes 589832 | tf_op jit(solution)/shard_map/ppermute | solution.py:694
  222.0 14.6 %collective-permute-start.34 = (bf16[128,768]{1,0:T(8,128)(2,1)}, bf16[128,768]{1,0:T(8,128)(2,1)S(1)}, u32[]{:S(2)}, u32[]{:S(2)}) collective-permute-start(bf16[128,768]{1,0:T(8,128)(2,1)} %get-tuple-element.118.query_mine), channel_id=1, source_target_pairs={{0,1},{1,0},{2,3},{3,2},{4,5},{5,4},{6,7},{7,6},{8,9},{9,8},{10,11... | collective-permute-start | bytes 589832 | tf_op jit(solution)/shard_map/ppermute | solution.py:694
  256.6 32.3 %collective-permute-start.37 = (bf16[174,128,128]{2,1,0:T(8,128)(2,1)}, bf16[174,128,128]{2,1,0:T(8,128)(2,1)S(1)}, u32[]{:S(2)}, u32[]{:S(2)}) collective-permute-start(bf16[174,128,128]{2,1,0:T(8,128)(2,1)} %get-tuple-element.151), channel_id=1, source_target_pairs={{0,2},{2,0},{4,6},{6,4},{8,10},{10,8},{12,14},{14,12},{16,18},{18,... | collective-permute-start | bytes 17104904 | tf_op jit(solution)/shard_map/ppermute | solution.py:898
  256.7 12.2 %collective-permute-start.38 = (bf16[58,128,128]{2,1,0:T(8,128)(2,1)}, bf16[58,128,128]{2,1,0:T(8,128)(2,1)S(1)}, u32[]{:S(2)}, u32[]{:S(2)}) collective-permute-start(bf16[58,128,128]{2,1,0:T(8,128)(2,1)} %get-tuple-element.152), channel_id=1, source_target_pairs={{0,2},{2,0},{4,6},{6,4},{8,10},{10,8},{12,14},{14,12},{16,18},{18,... | collective-permute-start | bytes 5701640 | tf_op jit(solution)/shard_map/ppermute | solution.py:898
  309.8 17.1 %collective-permute-start.43 = (bf16[14,128,128]{2,1,0:T(8,128)(2,1)S(1)}, bf16[14,128,128]{2,1,0:T(8,128)(2,1)S(1)}, u32[]{:S(2)}, u32[]{:S(2)}) collective-permute-start(bf16[14,128,128]{2,1,0:T(8,128)(2,1)S(1)} %add_convert_fusion.9), channel_id=1, source_target_pairs={{0,8},{2,6},{8,16},{10,2},{16,24},{18,10},{24,28},{26,18},{28,20},... | collective-permute-start | bytes 1376264 | tf_op jit(solution)/shard_map/ppermute | solution.py:914
  315.0 14.5 %collective-permute-start.50 = (bf16[15,128,128]{2,1,0:T(8,128)(2,1)S(1)}, bf16[15,128,128]{2,1,0:T(8,128)(2,1)S(1)}, u32[]{:S(2)}, u32[]{:S(2)}) collective-permute-start(bf16[15,128,128]{2,1,0:T(8,128)(2,1)S(1)} %add_convert_fusion.2), channel_id=1, source_target_pairs={{0,8},{2,6},{8,16},{10,2},{16,24},{18,10},{24,28},{26,18},{28,20},... | collective-permute-start | bytes 1474568 | tf_op jit(solution)/shard_map/ppermute | solution.py:914
  319.0 24.7 %collective-permute-start.36 = (bf16[512,768]{1,0:T(8,128)(2,1)S(1)}, bf16[512,768]{1,0:T(8,128)(2,1)S(1)}, u32[]{:S(2)}, u32[]{:S(2)}) collective-permute-start(bf16[512,768]{1,0:T(8,128)(2,1)S(1)} %copy-done.18), channel_id=1, source_target_pairs={{0,1},{1,0},{2,3},{3,2},{4,5},{5,4},{6,7},{7,6},{8,9},{9,8},{10,11... | collective-permute-start | bytes 2359304 | tf_op jit(solution)/shard_map/ppermute | solution.py:694
  329.8 11.1 %collective-permute-start.51 = (bf16[15,128,128]{2,1,0:T(8,128)(2,1)S(1)}, bf16[15,128,128]{2,1,0:T(8,128)(2,1)S(1)}, u32[]{:S(2)}, u32[]{:S(2)}) collective-permute-start(bf16[15,128,128]{2,1,0:T(8,128)(2,1)S(1)} %add_convert_fusion.1), channel_id=1, source_target_pairs={{0,8},{2,6},{8,16},{10,2},{16,24},{18,10},{24,28},{26,18},{28,20},... | collective-permute-start | bytes 1474568 | tf_op jit(solution)/shard_map/ppermute | solution.py:914
  (92 other events, 632.8 us)

commit v4 on v3

--- a/solution.py
+++ b/solution.py
@@ -23,7 +23,6 @@
 matrix_decay = 0.05
 norm_rate = 0.6
 masked_score = -1000000000.0
-highest = lax.Precision.HIGHEST
 
 
 TILE = 128
@@ -923,140 +922,288 @@
     return values
 
 
-def times(left_matrix, right_matrix):
-    return jnp.einsum("...ij,...jk->...ik", left_matrix, right_matrix, precision=highest)
-
-
-def flipped(block_matrix):
-    return jnp.swapaxes(block_matrix, -1, -2)
-
-
-def split3(a):
-    h=a.astype(bf16); r=a-h.astype(f32); m=r.astype(bf16); l=(r-m.astype(f32)).astype(bf16)
-    return h,m,l
-def split2(a):
-    h=a.astype(bf16); return h,(a-h.astype(f32)).astype(bf16)
-def dot3(a,b,dims):
-    ah,al=split2(a); bh,bl=split2(b)
-    return mm(ah,bh,dims)+(mm(ah,bl,dims)+mm(al,bh,dims))
-def gram6(p):
-    h,m,l=split3(p)
-    hh=mm(h,h,TN); mmm=mm(m,m,TN); hm=mm(h,m,TN)+mm(h,l,TN)
-    return hh+(mmm+(hm+hm.T))
-
-PB=16
-def panel_steps(x, kb, g):
-    base=kb*PB
-    lane=lax.broadcasted_iota(jnp.int32,(1,8,128),2)
-    sub=lax.broadcasted_iota(jnp.int32,(1,8,128),1)
-    halves=[x[:,:8],x[:,8:]]
-    rinvs=[]
-    for s in range(PB):
-        k=base+s
-        hs=s//8; r=s%8
-        cur=halves[hs]
-        row=cur[:,r:r+1,:]
-        piv=cur[:,r:r+1,k:k+1]
-        rinv=1.0/piv
-        rinvs.append(rinv)
-        scaled=jnp.where(lane[:,:1]==k,1.0,row)*rinv
-        for h in range(hs,2):
-            y=halves[h]
-            col=jnp.broadcast_to(y[:,:,k:k+1],y.shape)
-            if h==hs:
-                low=(sub>r)
-                col=jnp.where(low,col,0.0)
-                y=jnp.where((lane==k)&(sub>r),0.0,y)
-                y=jnp.where((lane==k)&(sub==r),1.0,y)
-            else:
-                y=jnp.where(lane==k,0.0,y)
-            halves[h]=y-col*scaled
-    return jnp.concatenate(halves,axis=1), jnp.concatenate(rinvs,axis=1)
-
-def ortho_body(n_pad, n, g, s_ref,b_ref,q_ref,a_ref,p_ref,d_ref):
-    def first(i,c):
-        p=dot3(s_ref[i],b_ref[i],NN)
-        p_ref[i]=p
-        a_ref[i]=gram6(p)
-        return c
-    lax.fori_loop(0,n,first,0)
-    eye=(lax.broadcasted_iota(jnp.int32,(128,128),0)==lax.broadcasted_iota(jnp.int32,(128,128),1)).astype(f32)
-    for i in range(n,n_pad):
-        a_ref[i]=eye
-    lane=lax.broadcasted_iota(jnp.int32,(1,PB,128),2)
-    sub=lax.broadcasted_iota(jnp.int32,(1,PB,128),1)
-    for kb in range(128//PB):
-        base=kb*PB; end=base+PB
-        def group(gi,c):
-            i0=gi*g
-            x=a_ref[pl.ds(i0,g),base:end,:]
-            x,rinv=panel_steps(x,kb,g)
-            w=jnp.where((lane>=base)&(lane<end)&(lane-base>sub),0.0,x)
-            d_ref[pl.ds(i0,g),base:end,:]=jnp.broadcast_to(rinv,x.shape)
-            a_ref[pl.ds(i0,g),base:end,:]=w
-            if end<128:
-                u=jnp.where(lane>=end,x*rinv,0.0)
-                wh,wm,wl=split3(w); uh,um,ul=split3(u)
-                lhs=jnp.concatenate([uh,uh,um,uh,ul,um],axis=1)
-                rhs=jnp.concatenate([wh,wm,wh,wl,wh,wm],axis=1)
-                lane2=lax.broadcasted_iota(jnp.int32,(128-end,128),1)
-                inside=(lane2>=base)&(lane2<end)
-                for j in range(g):
-                    upd=mm(lhs[j],rhs[j],TN)
-                    old=a_ref[i0+j,end:,:]
-                    a_ref[i0+j,end:,:]=jnp.where(inside,0.0,old)-upd[end:,:]
-            return c
-        lax.fori_loop(0,n_pad//g,group,0)
-    ii=lax.broadcasted_iota(jnp.int32,(128,128),0); jj=lax.broadcasted_iota(jnp.int32,(128,128),1)
-    def last(i,c):
-        inv=jnp.where(ii>=jj,a_ref[i],0.0)*jnp.sqrt(d_ref[i])
-        q_ref[i]=dot3(p_ref[i],inv,NT)
-        return c
-    lax.fori_loop(0,n,last,0)
-
-def ortho(s,b,g=29):
-    n=s.shape[0]; n_pad=-(-n//g)*g
+PANEL = 16
+PACK = TILE // PANEL
+
+
+def split_two(values):
+    high = values.astype(bf16)
+    return high, (values - high.astype(f32)).astype(bf16)
+
+
+def split_three(values):
+    high = values.astype(bf16)
+    rest = values - high.astype(f32)
+    middle = rest.astype(bf16)
+    return high, middle, (rest - middle.astype(f32)).astype(bf16)
+
+
+def join(axis, *pieces):
+    return jnp.concatenate(pieces, axis=axis)
+
+
+def fold(product):
+    return product[:, :TILE] + product[:, TILE:]
+
+
+def times_nn(left, right):
+    high, low = split_two(right)
+    row = join(1, high, low)
+    return fold(mm(join(1, *split_two(left)), join(0, row, row), NN))
+
+
+def times_precise(left, right):
+    lh, lm, ll = split_three(left)
+    rh, rm, rl = split_three(right)
+    both = mm(join(1, lh, lm), join(0, join(1, rh, rm), join(1, rm, rh)), NN)
+    return fold(both) + mm(join(1, lh, ll), join(0, rl, rh), NN)
+
+
+def diagonal_blocks(rows, base):
+    lane = lax.broadcasted_iota(jnp.int32, (PANEL, TILE), 1) // PANEL
+    packed = jnp.zeros((PANEL, TILE), f32)
+    for number in range(PACK):
+        piece = rows[number * PANEL : (number + 1) * PANEL]
+        shift = (number * PANEL - base) % TILE
+        if shift:
+            piece = pltpu.roll(piece, shift, 1)
+        packed = jnp.where(lane == number, piece, packed)
+    return packed
+
+
+def factor_inverses(packed):
+    groups = packed.shape[0] // PANEL
+    shape = packed.shape
+    lane = lax.broadcasted_iota(jnp.int32, shape, 1)
+    row = lax.broadcasted_iota(jnp.int32, shape, 0) % PANEL
+    col = lane % PANEL
+    first = lane - col
+
+    def spread(values, step):
+        picked = values.reshape(groups, PANEL, TILE)[:, step : step + 1]
+        return jnp.broadcast_to(picked, (groups, PANEL, TILE)).reshape(shape)
+
+    scale = jnp.zeros(shape, f32)
+    column = jnp.take_along_axis(packed, first, axis=1)
+    for step in range(PANEL):
+        pivot = spread(column, step)
+        inverse = reciprocal(pivot)
+        if step + 1 < PANEL:
+            following = jnp.take_along_axis(packed, first + (step + 1), axis=1)
+            following = following - column * (spread(column, step + 1) * inverse)
+        scaled = jnp.where(col == step, 1.0, spread(packed, step)) * inverse
+        kept = jnp.where(col == step, jnp.where(row > step, 0.0, 1.0), packed)
+        packed = jnp.where(
+            row > step, kept - column * scaled, jnp.where(row == step, kept, packed)
+        )
+        scale = jnp.where(row == step, lax.rsqrt(pivot), scale)
+        if step + 1 < PANEL:
+            column = following
+    return jnp.where(col <= row, packed * scale, 0.0)
+
+
+def reciprocal(values):
+    rough = pl.reciprocal(values, approx=True)
+    rough = rough * (2.0 - values * rough)
+    return rough * (2.0 - values * rough)
+
+
+def panel_products(solved, masked):
+    lh, lm, ll = split_three(masked)
+    rh, rm, rl = split_three(solved)
+    found = []
+    for number in range(PACK):
+        rows = slice(number * PANEL, (number + 1) * PANEL)
+        left = join(0, lh[rows], lh[rows], lm[rows], lh[rows], ll[rows], lm[rows])
+        right = join(0, rh[rows], rm[rows], rh[rows], rl[rows], rh[rows], rm[rows])
+        found.append(mm(left, right, TN))
+    return found
+
+
+def invert_factors(grams, inverses, count):
+    groups = count // PACK
+    lane = lax.broadcasted_iota(jnp.int32, (TILE, TILE), 1)
+    sub = lax.broadcasted_iota(jnp.int32, (TILE, TILE), 0)
+    same_block = lane // PANEL == sub // PANEL
+    for panel in range(TILE // PANEL):
+        base, end = panel * PANEL, (panel + 1) * PANEL
+        inside = (lane >= base) & (lane < end)
+        unit = (lane - base == sub % PANEL).astype(f32)
+        packed = []
+        for group in range(groups):
+            rows = grams[group * PACK : (group + 1) * PACK, base:end, :].reshape(TILE, TILE)
+            packed.append(diagonal_blocks(rows, base))
+        inverses[...] = factor_inverses(jnp.concatenate(packed, axis=0))
+
+        def one(first, width, base=base, end=end, inside=inside, unit=unit):
+            solved = []
+            for offset in range(width):
+                group = first + offset
+                place = pl.ds(pl.multiple_of(group * PANEL, PANEL), PANEL)
+                spread = jnp.where(
+                    same_block, jnp.concatenate([inverses[place, :]] * PACK, axis=0), 0.0
+                )
+                rows = grams[pl.ds(group * PACK, PACK), base:end, :].reshape(TILE, TILE)
+                solved.append(times_precise(spread, jnp.where(inside, unit, rows)))
+            for offset in range(width):
+                grams[pl.ds((first + offset) * PACK, PACK), base:end, :] = solved[offset].reshape(
+                    PACK, PANEL, TILE
+                )
+            if end == TILE:
+                return
+            for offset in range(width):
+                matrices = pl.ds((first + offset) * PACK, PACK)
+                old = grams[matrices, end:, :]
+                products = panel_products(
+                    solved[offset], jnp.where(lane >= end, solved[offset], 0.0)
+                )
+                products = jnp.stack([product[end:] for product in products])
+                grams[matrices, end:, :] = jnp.where(inside[None, end:], 0.0, old) - products
+
+        loop_groups(groups, GROUPS_AT_ONCE, one)
+
+
+GROUPS_AT_ONCE = 4
+
+
+def optimizer_slots(first, count, inputs, outputs, grams, products):
+    slots = products.shape[0] // 2
+    loaded = [[ref[first + offset] for ref in inputs] for offset in range(count)]
+    grad, weight, moment, square, left, right, left_base, right_base = map(list, zip(*loaded))
+    every = range(count)
+    turned_base = [left_base[n].T for n in every]
+    turned_grad = [grad[n].T for n in every]
+    turned_right = [right_base[n].T for n in every]
+    half = [times_nn(turned_base[n], grad[n]) for n in every]
+    left = [
+        beta_stats * left[n] + (1 - beta_stats) * times_nn(grad[n], turned_grad[n]) for n in every
+    ]
+    right = [
+        beta_stats * right[n] + (1 - beta_stats) * times_nn(turned_grad[n], grad[n])
+        for n in every
+    ]
+    rotated = [times_nn(half[n], right_base[n]) for n in every]
+    left_product = [times_nn(left[n], left_base[n]) for n in every]
+    right_product = [times_nn(right[n], right_base[n]) for n in every]
+    moment = [beta_first * moment[n] + (1 - beta_first) * rotated[n] for n in every]
+    square = [
+        beta_second * square[n] + (1 - beta_second) * rotated[n] * rotated[n] for n in every
+    ]
+    step = [
+        (moment[n] / (1 - beta_first**STEP))
+        / (jnp.sqrt(square[n] / (1 - beta_second**STEP)) + adam_epsilon)
+        for n in every
+    ]
+    half = [times_nn(left_base[n], step[n]) for n in every]
+    left_gram = [times_precise(left_product[n].T, left_product[n]) for n in every]
+    right_gram = [times_precise(right_product[n].T, right_product[n]) for n in every]
+    full = [times_nn(half[n], turned_right[n]) for n in every]
+    weight = [weight[n] - matrix_rate * (full[n] + matrix_decay * weight[n]) for n in every]
+    for n in every:
+        slot = first + n
+        values = (weight[n], weight[n].astype(bf16), moment[n], square[n], left[n], right[n])
+        for ref, value in zip(outputs, values):
+            ref[slot] = value
+        products[slot] = left_product[n]
+        products[slots + slot] = right_product[n]
+        grams[slot] = left_gram[n]
+        grams[slots + slot] = right_gram[n]
+
+
+def loop_groups(total, width, body):
+    def one(number, carry):
+        body(number * width, width)
+        return carry
+
+    lax.fori_loop(0, total // width, one, 0)
+    if total % width:
+        body(total - total % width, total % width)
+
+
+def optimizer_body(padded, *refs):
+    sources, targets = refs[:8], refs[8:16]
+    inputs, outputs = refs[16:24], refs[24:32]
+    grams, products, inverses, in_sems, out_sems = refs[32:]
+    slots = sources[0].shape[0]
+    lane = lax.broadcasted_iota(jnp.int32, (TILE, TILE), 1)
+    sub = lax.broadcasted_iota(jnp.int32, (TILE, TILE), 0)
+    cuts = [cut for cut in (0, SLOTS_AT_ONCE, 3 * SLOTS_AT_ONCE) if cut < slots] + [slots]
+    parts = [(first, last - first) for first, last in zip(cuts, cuts[1:])]
+    loads = [
+        [
+            pltpu.make_async_copy(
+                source.at[pl.ds(*part)], target.at[pl.ds(*part)], in_sems.at[number, index]
+            )
+            for index, (source, target) in enumerate(zip(sources, inputs))
+        ]
+        for number, part in enumerate(parts)
+    ]
+    for load in loads:
+        for copy in load:
+            copy.start()
+    for number in range(2 * slots, padded):
+        grams[number] = (lane == sub).astype(f32)
+    for load, (start, count) in zip(loads, parts):
+        for copy in load:
+            copy.wait()
+        loop_groups(
+            count,
+            min(SLOTS_AT_ONCE, count),
+            lambda first, width: optimizer_slots(
+                start + first, width, inputs, outputs, grams, products
+            ),
+        )
+    stores = [
+        pltpu.make_async_copy(staged, target, out_sems.at[index])
+        for index, (staged, target) in enumerate(zip(outputs, targets))
+    ]
+    for copy in stores[:6]:
+        copy.start()
+    invert_factors(grams, inverses, padded)
+
+    def finish(first, count):
+        found = []
+        for offset in range(count):
+            for side in range(2):
+                number = side * slots + first + offset
+                turned = jnp.where(sub >= lane, grams[number], 0.0).T
+                found.append(times_nn(products[number], turned))
+        for offset in range(count):
+            outputs[6][first + offset] = found[2 * offset]
+            outputs[7][first + offset] = found[2 * offset + 1]
+
+    loop_groups(slots, 4, finish)
+    for copy in stores[6:]:
+        copy.start()
+    for copy in stores:
+        copy.wait()
+
+
+SLOTS_AT_ONCE = 6
+
+
+def optimizer(*arrays):
+    shape = arrays[0].shape
+    slots = shape[0]
+    padded = -(-2 * slots // PACK) * PACK
+    kinds = [f32, bf16] + [f32] * 6
     return pl.pallas_call(
-        functools.partial(ortho_body,n_pad,n,g),
-        out_shape=jax.ShapeDtypeStruct(s.shape,f32),
-        in_specs=[pl.BlockSpec(memory_space=pltpu.VMEM)]*2,
-        out_specs=pl.BlockSpec(memory_space=pltpu.VMEM),
-        scratch_shapes=[pltpu.VMEM((n_pad,128,128),f32),pltpu.VMEM((n,128,128),f32),pltpu.VMEM((n_pad,128,128),f32)],
-        compiler_params=pltpu.CompilerParams(vmem_limit_bytes=50*1024*1024),
-    )(s,b)
-
-
-def orthonormal_pair(left_new, left_bases, right_new, right_bases):
-    count = left_new.shape[0]
-    both = ortho(
-        jnp.concatenate([left_new, right_new]), jnp.concatenate([left_bases, right_bases]), count
-    )
-    return both[:count], both[count:]
-
-
-def rotated_update(
-    gradient, master, first_moment, second_moment, left_stats, right_stats, left_bases, right_bases
-):
-    rotated = times(times(flipped(left_bases), gradient), right_bases)
-    first_new = beta_first * first_moment + (1 - beta_first) * rotated
-    second_new = beta_second * second_moment + (1 - beta_second) * rotated * rotated
-    step_rotated = (
-        first_new
-        / (1 - beta_first**STEP)
-        / (jnp.sqrt(second_new / (1 - beta_second**STEP)) + adam_epsilon)
-    )
-    step_full = times(times(left_bases, step_rotated), flipped(right_bases))
-    master_new = master - matrix_rate * (step_full + matrix_decay * master)
-    left_new = beta_stats * left_stats + (1 - beta_stats) * times(gradient, flipped(gradient))
-    right_new = beta_stats * right_stats + (1 - beta_stats) * times(flipped(gradient), gradient)
-    return (
-        master_new,
-        first_new,
-        second_new,
-        left_new,
-        right_new,
-        *orthonormal_pair(left_new, left_bases, right_new, right_bases),
-    )
+        functools.partial(optimizer_body, padded),
+        out_shape=tuple(jax.ShapeDtypeStruct(shape, kind) for kind in kinds),
+        in_specs=any_specs(8),
+        out_specs=tuple(any_specs(8)),
+        scratch_shapes=[pltpu.VMEM(shape, f32)] * 8
+        + [pltpu.VMEM(shape, kind) for kind in kinds]
+        + [
+            pltpu.VMEM((padded, TILE, TILE), f32),
+            pltpu.VMEM((2 * slots, TILE, TILE), f32),
+            pltpu.VMEM((padded // PACK * PANEL, TILE), f32),
+            pltpu.SemaphoreType.DMA((3, 8)),
+            pltpu.SemaphoreType.DMA((8,)),
+        ],
+        compiler_params=pltpu.CompilerParams(vmem_limit_bytes=60 * 1024 * 1024),
+        name="optimizer",
+    )(*arrays)
 
 
 def per_device(
@@ -1105,7 +1252,7 @@
     else:
         owned = lax.psum_scatter(packed[0], "dp", scatter_dimension=0, tiled=True).astype(f32)
         norm_total = lax.psum(norm_part, "dp")
-    updated = rotated_update(
+    updated = optimizer(
         owned,
         weight_master[0],
         moment_one[0],
@@ -1117,6 +1264,7 @@
     )
     (
         weight_new,
+        weight_copy,
         moment_one_new,
         moment_two_new,
         left_stat_new,
@@ -1133,7 +1281,7 @@
         out_rows,
         in_grad,
         weight_new,
-        weight_new.astype(jnp.bfloat16),
+        weight_copy,
         moment_one_new,
         moment_two_new,
         left_stat_new,

time: 474 us -> 390 us (0.82)
  Pallas kernels: 231 us -> 175 us
  matrix products: 20.4 us -> 0 us
  other arithmetic: 20.2 us -> 15.1 us
    pallas_call x1, Pallas kernels: 88.9 us -> 33.6 us  [optimizer(): pl.pallas_call(functools.partial(optimizer_body, padded), out_shape=tuple...]
    dot_general x6 -> x0, matrix products: 20.4 us -> none  [times(): jnp.einsum('...ij,...jk->...ik', left_matrix, right_matrix, precision=hig...]
    unnamed x119 -> x99, local copies, waits for them, and re-layouts: 15.6 us -> 15.2 us
  transfers between devices with their start and end apart: 57 -> 57, of which waited for: 26 -> 26; matrix products, arithmetic and copies ran while one was open for 5% -> 7% of each run, Pallas kernels for 19% -> 24%
where the time goes in v4:
time: 390 us; the launch traced here: 386 us
  Pallas kernels  175 us (45%)
  waiting for transfers between devices  98.5 us (25%)
  starting transfers between devices  67 us (17%)
  local copies, waits for them, and re-layouts  28.6 us (7%)
  other arithmetic  15.1 us (4%)
    ppermute x14, waiting for transfers between devices, scatter_ring(): summed = lax.ppermute(summed.astype(bf16), 'dp', RING_PAIRS)  37.1 us
    pallas_call x4, Pallas kernels, grad_blocks(): pl.pallas_call(functools.partial(grad_blocks_body, first_block, pairs, le...  36.5 us
    pallas_call x1, Pallas kernels, optimizer(): pl.pallas_call(functools.partial(optimizer_body, padded), out_shape=tuple...  33.6 us
    ppermute x14, starting transfers between devices, gather_ring(): held = [lax.ppermute(piece, 'dp', RING_PAIRS) for piece in held]  25.6 us
    ppermute x14, starting transfers between devices, scatter_ring(): summed = lax.ppermute(summed.astype(bf16), 'dp', RING_PAIRS)  23.5 us
    ppermute x14, waiting for transfers between devices, gather_ring(): held = [lax.ppermute(piece, 'dp', RING_PAIRS) for piece in held]  22.8 us
    ppermute x8, waiting for transfers between devices, swap_tensor(): return lax.ppermute(part, 'tensor', [(0, 1), (1, 0)])  22.2 us
    pallas_call x7, Pallas kernels, place_blocks(): pl.pallas_call(functools.partial(place_blocks_body, counts, first), out_s...  20.4 us
  transfers between devices with their start and end apart: 57, of which 26 were waited for; matrix products, arithmetic and copies ran while one was open for 7% of the time, Pallas kernels for 24%

profile of v4, /device:TPU:0, one launch (start us, length us, event | category | flops | bytes accessed | tf_op | source)
XLA Modules:
  0.0 386.2 jit_solution(10943958318378911439)
XLA Ops:
  7.1 5.1 %collective-permute-done.3.refs_3_ = bf16[15,128,128]{2,1,0:T(8,128)(2,1)S(1)} collective-permute-done((bf16[15,128,128]{2,1,0:T(8,128)(2,1)S(1)}, bf16[15,128,128]{2,1,0:T(8,128)(2,1)S(1)}, u32[]{:S(2)}, u32[]{:S(2)}) %collective-permute-start.3) | collective-permute-done | bytes 491552 | tf_op jit(solution)/shard_map/ppermute | solution.py:875
  25.3 4.7 %gather_fusion = s32[464]{0:T(512)} fusion(s32[464]{0:T(512)S(1)} %bitcast.37, s32[1024]{0:T(1024)S(1)} %pad_clamp_fusion), kind=kCustom, calls=%fused_computation | custom fusion | bytes 5568 | tf_op jit(solution)/shard_map/gather | solution.py:868
  31.7 3.9 %place_blocks.7.refs_4_ = bf16[464,128,128]{2,1,0:T(8,128)(2,1)} custom-call(s32[464]{0:T(512)} %gather_fusion, bf16[29,128,128]{2,1,0:T(8,128)(2,1)} %copy-done.2, bf16[29,128,128]{2,1,0:T(8,128)(2,1)} %copy-done.6, bf16[14,128,128]{2,1,0:T(8,128)(2,1)} %collective-permute-done.refs_2_, bf16[15,128,128]{2,1,0:T(8,128)(2,1)} %copy-done.13, ...), custom_call_target="tpu_custom_call" | custom-call | bytes 7602176 | tf_op jit(solution)/shard_map/place_blocks/pallas_call | solution.py:844
  91.8 9.2 %self_forward.1 = (bf16[3,512,384]{2,1,0:T(8,128)(2,1)}, f32[4,3,256,128]{3,2,1,0:T(8,128)}, bf16[512,384]{1,0:T(8,128)(2,1)}, bf16[512,768]{1,0:T(8,128)(2,1)}) custom-call(bf16[464,128,128]{2,1,0:T(8,128)(2,1)} %place_blocks.13.nat, bf16[512,768]{1,0:T(8,128)(2,1)} %bitcast.41, s32[4,1,128]{2,1,0:T(1,128)} %bitcast.67, s32[4,128,1]{2,1,0:T(8,128)} %copy.46.seg_col), custom_call_target="tpu_custom_call" | custom-call | flops 1207959552 | bytes 8000000 | tf_op jit(solution)/shard_map/self_forward/pallas_call | solution.py:180
  104.8 9.2 %image_forward.1 = (bf16[1088,384]{1,0:T(8,128)(2,1)}, bf16[1088,384]{1,0:T(8,128)(2,1)}) custom-call(bf16[464,128,128]{2,1,0:T(8,128)(2,1)} %place_blocks.13.nat, bf16[1088,1408]{1,0:T(8,128)(2,1)} %bitcast.38), custom_call_target="tpu_custom_call" | custom-call | flops 2353004544 | bytes 8000000 | tf_op jit(solution)/shard_map/image_forward/pallas_call | solution.py:216
  114.0 6.9 %collective-permute-done.29.other = bf16[512,768]{1,0:T(8,128)(2,1)S(1)} collective-permute-done((bf16[512,768]{1,0:T(8,128)(2,1)}, bf16[512,768]{1,0:T(8,128)(2,1)S(1)}, u32[]{:S(2)}, u32[]{:S(2)}) %collective-permute-start.29) | collective-permute-done | bytes 786464 | tf_op jit(solution)/shard_map/ppermute | solution.py:693
  121.8 10.2 %cross_forward.1 = (f32[512,768]{1,0:T(8,128)}, f32[128,768]{1,0:T(8,128)}, f32[384,768]{1,0:T(8,128)}, bf16[128,768]{1,0:T(8,128)(2,1)}, bf16[384,768]{1,0:T(8,...) custom-call(bf16[464,128,128]{2,1,0:T(8,128)(2,1)} %place_blocks.13., ...), custom_call_target="tpu_custom_call" | custom-call | flops 150994944 | bytes 12000000 | tf_op jit(solution)/shard_map/cross_forward/pallas_call | solution.py:277
  132.0 8.9 %text_forward.1 = (bf16[384,1536]{1,0:T(8,128)(2,1)}, f32[384,1536]{1,0:T(8,128)}, bf16[384,768]{1,0:T(8,128)(2,1)}) custom-call(bf16[464,128,128]{2,1,0:T(8,128)(2,1)} %place_blocks.13.nat, bf16[384,768]{1,0:T(8,128)(2,1)} %get-tuple-element.115.low_text.refs_0_), custom_call_target="tpu_custom_call" | custom-call | flops 1811939328 | bytes 10000000 | tf_op jit(solution)/shard_map/text_forward/pallas_call | solution.py:360
  144.5 15.3 %collective-permute-done.30.other = bf16[128,768]{1,0:T(8,128)(2,1)S(1)} collective-permute-done((bf16[128,768]{1,0:T(8,128)(2,1)S(1)}, bf16[128,768]{1,0:T(8,128)(2,1)S(1)}, u32[]{:S(2)}, u32[]{:S(2)}) %collective-permute-start.30) | collective-permute-done | bytes 196640 | tf_op jit(solution)/shard_map/ppermute | solution.py:693
  160.6 7.1 %query_forward.1 = (f32[128,768]{1,0:T(8,128)}, f32[128,768]{1,0:T(8,128)}, bf16[128,768]{1,0:T(8,128)(2,1)}, bf16[128,1536]{1,0:T(8,128)(2,1)}, f32[128,1536]{1,0:T(8,128)}, /*index=5*/bf16[128,768]{1,0:T(8,128)(2,1)}) custom-call(bf16[464,128,128]{2,1,0:T(8,128)(2,1)} %place_blocks.13.nat, f32[128,768]{1,0:T(8,128)} %get-tuple-element.108.first_query, ...), custom_call_target="tpu_custom_call" | custom-call | flops 603979776 | bytes 8000000 | tf_op jit(solution)/shard_map/query_forward/pallas_call | solution.py:374
  170.0 10.1 %feed_backward.3 = (bf16[384,768]{1,0:T(8,128)(2,1)}, f32[384,768]{1,0:T(8,128)}, bf16[384,768]{1,0:T(8,128)(2,1)}, bf16[384,1536]{1,0:T(8,128)(2,1)}, bf16[384,768]{1,0:T(8,128)(2,1)}, /*index=5*/f32[2,768]{1,0:T(2,128)}) custom-call(bf16[464,128,128]{2,1,0:T(8,128)(2,1)} %place_blocks.13.nat, f32[384,768]{1,0:T(8,128)} %get-tuple-element.114.states, ...), custom_call_target="tpu_custom_call" | custom-call | flops 1811939328 | bytes 10000000 | tf_op jit(solution)/shard_map/feed_backward/pallas_call | solution.py:435
  185.8 7.5 %feed_backward.2 = (bf16[128,768]{1,0:T(8,128)(2,1)}, f32[128,768]{1,0:T(8,128)}, bf16[128,768]{1,0:T(8,128)(2,1)}, bf16[128,1536]{1,0:T(8,128)(2,1)}, bf16[128,768]{1,0:T(8,128)(2,1)}, /*index=5*/f32[2,768]{1,0:T(2,128)}) custom-call(bf16[464,128,128]{2,1,0:T(8,128)(2,1)} %place_blocks.13.nat, f32[128,768]{1,0:T(8,128)} %get-tuple-element.110.states, ...), custom_call_target="tpu_custom_call" | custom-call | flops 603979776 | bytes 10000000 | tf_op jit(solution)/shard_map/feed_backward/pallas_call | solution.py:435
  194.9 8.6 %grad_blocks.4 = (bf16[58,128,128]{2,1,0:T(8,128)(2,1)}, bf16[174,128,128]{2,1,0:T(8,128)(2,1)}, bf16[232,128,128]{2,1,0:T(8,128)(2,1)}) custom-call(s32[464]{0:T(512)} %scatter_custom_fusion.place, bf16[384,768]{1,0:T(8,128)(2,1)} %get-tuple-element.115.low_text.refs_0_, bf16[384,1536]{1,0:T(8,128)(2,1)} %get-tuple-element.146.refs_1_, ...), custom_call_target="tpu_custom_call" | custom-call | flops 1811939328 | bytes 10000000 | tf_op jit(solution)/shard_map/grad_blocks/pallas_call | solution.py:668
  203.5 6.6 %grad_blocks.5 = (bf16[58,128,128]{2,1,0:T(8,128)(2,1)}, bf16[174,128,128]{2,1,0:T(8,128)(2,1)}, bf16[232,128,128]{2,1,0:T(8,128)(2,1)}) custom-call(s32[464]{0:T(512)} %scatter_custom_fusion.place, bf16[128,768]{1,0:T(8,128)(2,1)} %get-tuple-element.142.refs_0_, ...), custom_call_target="tpu_custom_call", output_to_operand_aliasing={{0}: (5, {}), {1}: (6, {}), {2}: (7, {})} | custom-call | flops 603979776 | bytes 10000000 | tf_op jit(solution)/shard_map/grad_blocks/pallas_call | solution.py:668
  210.8 10.8 %cross_backward.1 = (f32[128,768]{1,0:T(8,128)}, bf16[128,768]{1,0:T(8,128)(2,1)}, bf16[128,384]{1,0:T(8,128)(2,1)}, bf16[1088,384]{1,0:T(8,128)(2,1)}, bf16[108...) custom-call(bf16[464,128,128]{2,1,0:T(8,128)(2,1)} %place_blocks.13.nat, ...), custom_call_target="tpu_custom_call" | custom-call | flops 301989888 | bytes 10000000 | tf_op jit(solution)/shard_map/cross_backward/pallas_call | solution.py:492
  222.1 14.1 %grad_blocks.6 = (bf16[58,128,128]{2,1,0:T(8,128)(2,1)}, bf16[174,128,128]{2,1,0:T(8,128)(2,1)}, bf16[232,128,128]{2,1,0:T(8,128)(2,1)}) custom-call(s32[464]{0:T(512)} %scatter_custom_fusion.place, bf16[128,768]{1,0:T(8,128)(2,1)} %get-tuple-element.136.refs_0_, ...), custom_call_target="tpu_custom_call", output_to_operand_aliasing={{0}: (8, {}), {1}: (9, {}), {2}: (10, {})} | custom-call | flops 2353004544 | bytes 10000000 | tf_op jit(solution)/shard_map/grad_blocks/pallas_call | solution.py:668
  237.1 11.9 %self_backward.1 = (f32[512,768]{1,0:T(8,128)}, bf16[512,768]{1,0:T(8,128)(2,1)}, bf16[512,1152]{1,0:T(8,128)(2,1)}, bf16[512,768]{1,0:T(8,128)(2,1)}, f32[2,768]{1,0:T(2,128)}) custom-call(bf16[464,128,128]{2,1,0:T(8,128)(2,1)} %place_blocks.13.nat, f32[512,768]{1,0:T(8,128)} %get-tuple-element.119.resid, f32[128,768]{1,0:T(8,128)} %get-tuple-element.125.query_grad, ...), custom_call_target="tpu_custom_call" | custom-call | flops 1207959552 | bytes 12000000 | tf_op jit(solution)/shard_map/self_backward/pallas_call | solution.py:576
  249.0 7.2 %grad_blocks.7 = (bf16[58,128,128]{2,1,0:T(8,128)(2,1)}, bf16[174,128,128]{2,1,0:T(8,128)(2,1)}, bf16[232,128,128]{2,1,0:T(8,128)(2,1)}) custom-call(s32[464]{0:T(512)} %scatter_custom_fusion.place, bf16[512,768]{1,0:T(8,128)(2,1)} %bitcast.43, ...), custom_call_target="tpu_custom_call", output_to_operand_aliasing={{0}: (5, {}), {1}: (6, {}), {2}: (7, {})} | custom-call | flops 1207959552 | bytes 10000000 | tf_op jit(solution)/shard_map/grad_blocks/pallas_call | solution.py:668
  256.9 11.7 %collective-permute-done.38 = bf16[58,128,128]{2,1,0:T(8,128)(2,1)S(1)} collective-permute-done((bf16[58,128,128]{2,1,0:T(8,128)(2,1)}, bf16[58,128,128]{2,1,0:T(8,128)(2,1)S(1)}, u32[]{:S(2)}, u32[]{:S(2)}) %collective-permute-start.38) | collective-permute-done | bytes 1900576 | tf_op jit(solution)/shard_map/ppermute | solution.py:897
  274.4 4.0 %collective-permute-done.39 = bf16[14,128,128]{2,1,0:T(8,128)(2,1)S(1)} collective-permute-done((bf16[14,128,128]{2,1,0:T(8,128)(2,1)S(1)}, bf16[14,128,128]{2,1,0:T(8,128)(2,1)S(1)}, u32[]{:S(2)}, u32[]{:S(2)}) %collective-permute-start.39) | collective-permute-done | bytes 458784 | tf_op jit(solution)/shard_map/ppermute | solution.py:913
  310.8 3.8 collective-permute-done.49
  330.4 5.0 %collective-permute-done.44 = bf16[14,128,128]{2,1,0:T(8,128)(2,1)S(1)} collective-permute-done((bf16[14,128,128]{2,1,0:T(8,128)(2,1)S(1)}, bf16[14,128,128]{2,1,0:T(8,128)(2,1)S(1)}, u32[]{:S(2)}, u32[]{:S(2)}) %collective-permute-start.44) | collective-permute-done | bytes 458784 | tf_op jit(solution)/shard_map/ppermute | solution.py:913
  345.7 5.1 %collective-permute-done.52 = bf16[15,128,128]{2,1,0:T(8,128)(2,1)S(1)} collective-permute-done((bf16[15,128,128]{2,1,0:T(8,128)(2,1)S(1)}, bf16[15,128,128]{2,1,0:T(8,128)(2,1)S(1)}, u32[]{:S(2)}, u32[]{:S(2)}) %collective-permute-start.52) | collective-permute-done | bytes 491552 | tf_op jit(solution)/shard_map/ppermute | solution.py:913
  352.4 33.6 %optimizer.1 = (f32[29,128,128]{2,1,0:T(8,128)}, bf16[29,128,128]{2,1,0:T(8,128)(2,1)}, f32[29,128,128]{2,1,0:T(8,128)}, f32[29,128,128]{2,1,0:T(8,128)}, f32[29...) custom-call(f32[29,128,128]{2,1,0:T(8,128)} %pad_maximum_fusion.refs_0_, ...), custom_call_target="tpu_custom_call" | custom-call | tf_op jit(solution)/shard_map/optimizer/pallas_call | solution.py:1190
  (247 shorter events, 164.2 us)
Async XLA Ops:
  5.5 11.7 %collective-permute-start = (bf16[14,128,128]{2,1,0:T(8,128)(2,1)S(1)}, bf16[14,128,128]{2,1,0:T(8,128)(2,1)}, u32[]{:S(2)}, u32[]{:S(2)}) collective-permute-start(bf16[14,128,128]{2,1,0:T(8,128)(2,1)S(1)} %slice.146), channel_id=1, source_target_pairs={{0,8},{2,6},{8,16},{10,2},{16,24},{18,10},{24,28},{26,18},{28,20},... | collective-permute-start | bytes 1376264 | tf_op jit(solution)/shard_map/ppermute | solution.py:875
  7.1 22.8 %collective-permute-start.2 = (bf16[29,128,128]{2,1,0:T(8,128)(2,1)S(1)}, bf16[29,128,128]{2,1,0:T(8,128)(2,1)S(1)}, u32[]{:S(2)}, u32[]{:S(2)}) collective-permute-start(bf16[29,128,128]{2,1,0:T(8,128)(2,1)S(1)} %bitcast_convert_fusion.refs_0_), channel_id=1, source_target_pairs={{0,2},{2,0},{4,6},{6,4},{8,10},{10,8},{12,14},{14,12},{16,18},{18,... | collective-permute-start | bytes 2850824 | tf_op jit(solution)/shard_map/ppermute | solution.py:870
  17.2 12.8 %collective-permute-start.5 = (bf16[15,128,128]{2,1,0:T(8,128)(2,1)S(1)}, bf16[15,128,128]{2,1,0:T(8,128)(2,1)S(1)}, u32[]{:S(2)}, u32[]{:S(2)}) collective-permute-start(bf16[15,128,128]{2,1,0:T(8,128)(2,1)S(1)} %collective-permute-done.3.refs_3_), channel_id=1, source_target_pairs={{0,2},{2,0},{4,6},{6,4},{8,10},{10,8},{12,14},{14,12},{16,18},{18,... | collective-permute-start | bytes 1474568 | tf_op jit(solution)/shard_map/ppermute | solution.py:880
  17.7 17.9 %collective-permute-start.1 = (bf16[14,128,128]{2,1,0:T(8,128)(2,1)}, bf16[14,128,128]{2,1,0:T(8,128)(2,1)}, u32[]{:S(2)}, u32[]{:S(2)}) collective-permute-start(bf16[14,128,128]{2,1,0:T(8,128)(2,1)} %collective-permute-done.refs_2_), channel_id=1, source_target_pairs={{0,8},{2,6},{8,16},{10,2},{16,24},{18,10},{24,28},{26,18},{28,20},... | collective-permute-start | bytes 1376264 | tf_op jit(solution)/shard_map/ppermute | solution.py:875
  22.4 15.4 %collective-permute-start.11 = (bf16[15,128,128]{2,1,0:T(8,128)(2,1)S(1)}, bf16[15,128,128]{2,1,0:T(8,128)(2,1)}, u32[]{:S(2)}, u32[]{:S(2)}) collective-permute-start(bf16[15,128,128]{2,1,0:T(8,128)(2,1)S(1)} %collective-permute-done.7.refs_1_), channel_id=1, source_target_pairs={{0,8},{2,6},{8,16},{10,2},{16,24},{18,10},{24,28},{26,18},{28,20},... | collective-permute-start | bytes 1474568 | tf_op jit(solution)/shard_map/ppermute | solution.py:875
  25.2 14.2 %collective-permute-start.9 = (bf16[15,128,128]{2,1,0:T(8,128)(2,1)S(1)}, bf16[15,128,128]{2,1,0:T(8,128)(2,1)}, u32[]{:S(2)}, u32[]{:S(2)}) collective-permute-start(bf16[15,128,128]{2,1,0:T(8,128)(2,1)S(1)} %collective-permute-done.7.refs_1_), channel_id=1, source_target_pairs={{0,2},{2,0},{4,6},{6,4},{8,10},{10,8},{12,14},{14,12},{16,18},{18,... | collective-permute-start | bytes 1474568 | tf_op jit(solution)/shard_map/ppermute | solution.py:880
  37.8 12.3 %collective-permute-start.15 = (bf16[15,128,128]{2,1,0:T(8,128)(2,1)}, bf16[15,128,128]{2,1,0:T(8,128)(2,1)S(1)}, u32[]{:S(2)}, u32[]{:S(2)}) collective-permute-start(bf16[15,128,128]{2,1,0:T(8,128)(2,1)} %collective-permute-done.11.refs_1_), channel_id=1, source_target_pairs={{0,8},{2,6},{8,16},{10,2},{16,24},{18,10},{24,28},{26,18},{28,20},... | collective-permute-start | bytes 1474568 | tf_op jit(solution)/shard_map/ppermute | solution.py:875
  39.4 12.4 %collective-permute-start.13 = (bf16[15,128,128]{2,1,0:T(8,128)(2,1)}, bf16[15,128,128]{2,1,0:T(8,128)(2,1)S(1)}, u32[]{:S(2)}, u32[]{:S(2)}) collective-permute-start(bf16[15,128,128]{2,1,0:T(8,128)(2,1)} %collective-permute-done.11.refs_1_), channel_id=1, source_target_pairs={{0,2},{2,0},{4,6},{6,4},{8,10},{10,8},{12,14},{14,12},{16,18},{18,... | collective-permute-start | bytes 1474568 | tf_op jit(solution)/shard_map/ppermute | solution.py:880
  44.8 11.3 %collective-permute-start.10 = (bf16[14,128,128]{2,1,0:T(8,128)(2,1)S(1)}, bf16[14,128,128]{2,1,0:T(8,128)(2,1)S(1)}, u32[]{:S(2)}, u32[]{:S(2)}) collective-permute-start(bf16[14,128,128]{2,1,0:T(8,128)(2,1)S(1)} %collective-permute-done.6.refs_0_), channel_id=1, source_target_pairs={{0,8},{2,6},{8,16},{10,2},{16,24},{18,10},{24,28},{26,18},{28,20},... | collective-permute-start | bytes 1376264 | tf_op jit(solution)/shard_map/ppermute | solution.py:875
  51.7 11.0 %collective-permute-start.17 = (bf16[15,128,128]{2,1,0:T(8,128)(2,1)S(1)}, bf16[15,128,128]{2,1,0:T(8,128)(2,1)S(1)}, u32[]{:S(2)}, u32[]{:S(2)}) collective-permute-start(bf16[15,128,128]{2,1,0:T(8,128)(2,1)S(1)} %collective-permute-done.15.refs_1_), channel_id=1, source_target_pairs={{0,2},{2,0},{4,6},{6,4},{8,10},{10,8},{12,14},{14,12},{16,18},{18,... | collective-permute-start | bytes 1474568 | tf_op jit(solution)/shard_map/ppermute | solution.py:880
  101.0 19.8 %collective-permute-start.29 = (bf16[512,768]{1,0:T(8,128)(2,1)}, bf16[512,768]{1,0:T(8,128)(2,1)S(1)}, u32[]{:S(2)}, u32[]{:S(2)}) collective-permute-start(bf16[512,768]{1,0:T(8,128)(2,1)} %get-tuple-element.105.mine), channel_id=1, source_target_pairs={{0,1},{1,0},{2,3},{3,2},{4,5},{5,4},{6,7},{7,6},{8,9},{9,8},{10,11... | collective-permute-start | bytes 2359304 | tf_op jit(solution)/shard_map/ppermute | solution.py:693
  140.9 28.3 %collective-permute-start.32 = (bf16[384,768]{1,0:T(8,128)(2,1)}, bf16[384,768]{1,0:T(8,128)(2,1)S(1)}, u32[]{:S(2)}, u32[]{:S(2)}) collective-permute-start(bf16[384,768]{1,0:T(8,128)(2,1)} %get-tuple-element.116.mine), channel_id=1, source_target_pairs={{0,1},{1,0},{2,3},{3,2},{4,5},{5,4},{6,7},{7,6},{8,9},{9,8},{10,11... | collective-permute-start | bytes 1769480 | tf_op jit(solution)/shard_map/ppermute | solution.py:693
  144.0 15.9 %collective-permute-start.30 = (bf16[128,768]{1,0:T(8,128)(2,1)S(1)}, bf16[128,768]{1,0:T(8,128)(2,1)S(1)}, u32[]{:S(2)}, u32[]{:S(2)}) collective-permute-start(bf16[128,768]{1,0:T(8,128)(2,1)S(1)} %copy-done.39), channel_id=1, source_target_pairs={{0,1},{1,0},{2,3},{3,2},{4,5},{5,4},{6,7},{7,6},{8,9},{9,8},{10,11... | collective-permute-start | bytes 589832 | tf_op jit(solution)/shard_map/ppermute | solution.py:693
  167.6 17.5 %collective-permute-start.31 = (bf16[128,768]{1,0:T(8,128)(2,1)}, bf16[128,768]{1,0:T(8,128)(2,1)S(1)}, u32[]{:S(2)}, u32[]{:S(2)}) collective-permute-start(bf16[128,768]{1,0:T(8,128)(2,1)} %get-tuple-element.111.mine), channel_id=1, source_target_pairs={{0,1},{1,0},{2,3},{3,2},{4,5},{5,4},{6,7},{7,6},{8,9},{9,8},{10,11... | collective-permute-start | bytes 589832 | tf_op jit(solution)/shard_map/ppermute | solution.py:693
  180.1 56.1 %collective-permute-start.35 = (bf16[384,768]{1,0:T(8,128)(2,1)}, bf16[384,768]{1,0:T(8,128)(2,1)S(1)}, u32[]{:S(2)}, u32[]{:S(2)}) collective-permute-start(bf16[384,768]{1,0:T(8,128)(2,1)} %get-tuple-element.128.text_mine), channel_id=1, source_target_pairs={{0,1},{1,0},{2,3},{3,2},{4,5},{5,4},{6,7},{7,6},{8,9},{9,8},{10,11... | collective-permute-start | bytes 1769480 | tf_op jit(solution)/shard_map/ppermute | solution.py:693
  193.3 16.8 %collective-permute-start.33 = (bf16[128,768]{1,0:T(8,128)(2,1)}, bf16[128,768]{1,0:T(8,128)(2,1)S(1)}, u32[]{:S(2)}, u32[]{:S(2)}) collective-permute-start(bf16[128,768]{1,0:T(8,128)(2,1)} %get-tuple-element.122.mine), channel_id=1, source_target_pairs={{0,1},{1,0},{2,3},{3,2},{4,5},{5,4},{6,7},{7,6},{8,9},{9,8},{10,11... | collective-permute-start | bytes 589832 | tf_op jit(solution)/shard_map/ppermute | solution.py:693
  221.5 14.7 %collective-permute-start.34 = (bf16[128,768]{1,0:T(8,128)(2,1)}, bf16[128,768]{1,0:T(8,128)(2,1)S(1)}, u32[]{:S(2)}, u32[]{:S(2)}) collective-permute-start(bf16[128,768]{1,0:T(8,128)(2,1)} %get-tuple-element.126.query_mine), channel_id=1, source_target_pairs={{0,1},{1,0},{2,3},{3,2},{4,5},{5,4},{6,7},{7,6},{8,9},{9,8},{10,11... | collective-permute-start | bytes 589832 | tf_op jit(solution)/shard_map/ppermute | solution.py:693
  256.3 32.3 %collective-permute-start.37 = (bf16[174,128,128]{2,1,0:T(8,128)(2,1)}, bf16[174,128,128]{2,1,0:T(8,128)(2,1)S(1)}, u32[]{:S(2)}, u32[]{:S(2)}) collective-permute-start(bf16[174,128,128]{2,1,0:T(8,128)(2,1)} %get-tuple-element.159), channel_id=1, source_target_pairs={{0,2},{2,0},{4,6},{6,4},{8,10},{10,8},{12,14},{14,12},{16,18},{18,... | collective-permute-start | bytes 17104904 | tf_op jit(solution)/shard_map/ppermute | solution.py:897
  256.4 12.2 %collective-permute-start.38 = (bf16[58,128,128]{2,1,0:T(8,128)(2,1)}, bf16[58,128,128]{2,1,0:T(8,128)(2,1)S(1)}, u32[]{:S(2)}, u32[]{:S(2)}) collective-permute-start(bf16[58,128,128]{2,1,0:T(8,128)(2,1)} %get-tuple-element.160), channel_id=1, source_target_pairs={{0,2},{2,0},{4,6},{6,4},{8,10},{10,8},{12,14},{14,12},{16,18},{18,... | collective-permute-start | bytes 5701640 | tf_op jit(solution)/shard_map/ppermute | solution.py:897
  272.7 11.0 %collective-permute-start.46 = (bf16[15,128,128]{2,1,0:T(8,128)(2,1)S(1)}, bf16[15,128,128]{2,1,0:T(8,128)(2,1)S(1)}, u32[]{:S(2)}, u32[]{:S(2)}) collective-permute-start(bf16[15,128,128]{2,1,0:T(8,128)(2,1)S(1)} %add_convert_fusion.6), channel_id=1, source_target_pairs={{0,8},{2,6},{8,16},{10,2},{16,24},{18,10},{24,28},{26,18},{28,20},... | collective-permute-start | bytes 1474568 | tf_op jit(solution)/shard_map/ppermute | solution.py:913
  309.4 17.2 %collective-permute-start.43 = (bf16[14,128,128]{2,1,0:T(8,128)(2,1)S(1)}, bf16[14,128,128]{2,1,0:T(8,128)(2,1)S(1)}, u32[]{:S(2)}, u32[]{:S(2)}) collective-permute-start(bf16[14,128,128]{2,1,0:T(8,128)(2,1)S(1)} %add_convert_fusion.9), channel_id=1, source_target_pairs={{0,8},{2,6},{8,16},{10,2},{16,24},{18,10},{24,28},{26,18},{28,20},... | collective-permute-start | bytes 1376264 | tf_op jit(solution)/shard_map/ppermute | solution.py:913
  314.7 14.6 %collective-permute-start.50 = (bf16[15,128,128]{2,1,0:T(8,128)(2,1)S(1)}, bf16[15,128,128]{2,1,0:T(8,128)(2,1)S(1)}, u32[]{:S(2)}, u32[]{:S(2)}) collective-permute-start(bf16[15,128,128]{2,1,0:T(8,128)(2,1)S(1)} %add_convert_fusion.2), channel_id=1, source_target_pairs={{0,8},{2,6},{8,16},{10,2},{16,24},{18,10},{24,28},{26,18},{28,20},... | collective-permute-start | bytes 1474568 | tf_op jit(solution)/shard_map/ppermute | solution.py:913
  318.8 24.6 %collective-permute-start.36 = (bf16[512,768]{1,0:T(8,128)(2,1)S(1)}, bf16[512,768]{1,0:T(8,128)(2,1)S(1)}, u32[]{:S(2)}, u32[]{:S(2)}) collective-permute-start(bf16[512,768]{1,0:T(8,128)(2,1)S(1)} %copy-done.8), channel_id=1, source_target_pairs={{0,1},{1,0},{2,3},{3,2},{4,5},{5,4},{6,7},{7,6},{8,9},{9,8},{10,11... | collective-permute-start | bytes 2359304 | tf_op jit(solution)/shard_map/ppermute | solution.py:693
  329.6 11.0 %collective-permute-start.51 = (bf16[15,128,128]{2,1,0:T(8,128)(2,1)S(1)}, bf16[15,128,128]{2,1,0:T(8,128)(2,1)S(1)}, u32[]{:S(2)}, u32[]{:S(2)}) collective-permute-start(bf16[15,128,128]{2,1,0:T(8,128)(2,1)S(1)} %add_convert_fusion.1), channel_id=1, source_target_pairs={{0,8},{2,6},{8,16},{10,2},{16,24},{18,10},{24,28},{26,18},{28,20},... | collective-permute-start | bytes 1474568 | tf_op jit(solution)/shard_map/ppermute | solution.py:913
  (82 other events, 625.2 us)

commit v5 on v4

--- a/solution.py
+++ b/solution.py
@@ -32,7 +32,7 @@
 NN = ((1,), (0,))
 NT = ((1,), (1,))
 TN = ((0,), (0,))
-VMEM_BYTES = 56 * 1024 * 1024
+VMEM_BYTES = 10 * 1024 * 1024
 
 
 def mm(left, right, dims):
@@ -49,12 +49,24 @@
 
 def vmem_params():
     return pltpu.CompilerParams(vmem_limit_bytes=VMEM_BYTES)
+
+
+def held(shape, kind):
+    return pltpu.VMEM(shape, kind)
+
+
+def pin(*arrays):
+    return [pltpu.with_memory_space_constraint(array, pltpu.VMEM) for array in arrays]
 
 
 def cost(flops, bytes_accessed, transcendentals=0):
     return pl.CostEstimate(
         flops=int(flops), bytes_accessed=int(bytes_accessed), transcendentals=int(transcendentals)
     )
+
+
+def join(axis, *pieces):
+    return jnp.concatenate(pieces, axis=axis)
 
 
 def matrix_of(blocks_ref, row_first, row_count, col_first, col_count, col_total, base=0):
@@ -123,12 +135,6 @@
     query_grad = jnp.where(low_half, both[:count], both[count:]).astype(bf16)
     key_grad = mm(score_grad, head_pair(queries), TN).astype(bf16)
     return query_grad, key_grad, value_grad
-
-
-def load_blocks(source, first, count, target, semaphore):
-    copy = pltpu.make_async_copy(source.at[pl.ds(first, count)], target, semaphore)
-    copy.start()
-    return copy
 
 
 class Plan:
@@ -147,22 +153,23 @@
         self.query_first = self.cross_first + self.cross_count
         self.text_first = self.query_first + 2 * feed
         self.block_count = self.text_first + 2 * feed
+        self.self_out = 3 * square
+        self.image_first = self.cross_first + square
+        self.cross_out = self.image_first + 2 * cross
         self.tokens = rows * seq
         self.learned = rows * NQ
         self.texts = rows * (seq - NQ)
 
 
-def self_forward_body(plan, scale, nat, hidden, seg_row, seg_col, qkv, probs, mixed, part, w, sem):
-    copy = load_blocks(nat, plan.self_first, plan.self_count, w, sem)
-    copy.wait()
+def self_forward_body(plan, scale, nat, hidden, segments, qkv, probs, mixed, part):
     for piece in range(3):
-        matrix = matrix_of(w, 0, plan.wt, 0, plan.ht, plan.ht, piece * plan.square)
+        matrix = matrix_of(nat, 0, plan.wt, 0, plan.ht, plan.ht, piece * plan.square)
         qkv[piece] = mm(hidden[...], matrix, NN).astype(bf16)
 
     def one(row, carry):
         place = pl.ds(pl.multiple_of(row * plan.seq, plan.seq), plan.seq)
-        allowed = seg_col[row] == seg_row[row]
-        allowed = jnp.concatenate([allowed, allowed], axis=0)
+        along = jnp.broadcast_to(segments[row].astype(f32), (plan.seq, plan.seq))
+        allowed = jnp.concatenate([along.T, along.T], axis=0) == join(0, along, along)
         for tile in range(plan.ht):
             cols = slice(tile * TILE, (tile + 1) * TILE)
             found = pair_probs(qkv[0, place, cols], qkv[1, place, cols], allowed, scale)
@@ -171,37 +178,31 @@
         return carry
 
     lax.fori_loop(0, plan.rows, one, 0)
-    matrix = matrix_of(w, 0, plan.ht, 0, plan.wt, plan.wt, 3 * plan.square)
+    matrix = matrix_of(nat, 0, plan.ht, 0, plan.wt, plan.wt, plan.self_out)
     part[...] = mm(mixed[...], matrix, NN).astype(bf16)
 
 
-def self_forward(plan, scale, nat, hidden, seg_row, seg_col):
+def self_forward(plan, scale, nat, hidden, segments):
     tokens, half, width = plan.tokens, plan.half, plan.width
     return pl.pallas_call(
         functools.partial(self_forward_body, plan, scale),
         out_shape=(
-            jax.ShapeDtypeStruct((3, tokens, half), bf16),
-            jax.ShapeDtypeStruct((plan.rows, plan.ht, 2 * plan.seq, plan.seq), f32),
-            jax.ShapeDtypeStruct((tokens, half), bf16),
+            held((3, tokens, half), bf16),
+            held((plan.rows, plan.ht, 2 * plan.seq, plan.seq), f32),
+            held((tokens, half), bf16),
             jax.ShapeDtypeStruct((tokens, width), bf16),
         ),
-        in_specs=any_specs(1) + vmem_specs(3),
+        in_specs=vmem_specs(3),
         out_specs=tuple(vmem_specs(4)),
-        scratch_shapes=[
-            pltpu.VMEM((plan.self_count, TILE, TILE), bf16),
-            pltpu.SemaphoreType.DMA,
-        ],
         compiler_params=vmem_params(),
         cost_estimate=cost(2 * tokens * width * half * 4, 8e6),
         name="self_forward",
-    )(nat, hidden, seg_row, seg_col)
-
-
-def image_body(plan, nat, image, keys, values, w, sem):
-    copy = load_blocks(nat, plan.cross_first + plan.square, 2 * plan.cross, w, sem)
-    copy.wait()
+    )(*pin(nat, hidden), segments)
+
+
+def image_body(plan, nat, image, keys, values):
     for piece, target in ((0, keys), (1, values)):
-        matrix = matrix_of(w, 0, plan.it, 0, plan.ht, plan.ht, piece * plan.cross)
+        matrix = matrix_of(nat, 0, plan.it, 0, plan.ht, plan.ht, plan.image_first + piece * plan.cross)
 
         def one(row, carry):
             place = pl.ds(pl.multiple_of(row * plan.keys, plan.keys), plan.keys)
@@ -215,24 +216,19 @@
     total = plan.rows * plan.keys
     return pl.pallas_call(
         functools.partial(image_body, plan),
-        out_shape=(jax.ShapeDtypeStruct((total, plan.half), bf16),) * 2,
-        in_specs=any_specs(1) + vmem_specs(1),
+        out_shape=(held((total, plan.half), bf16),) * 2,
+        in_specs=vmem_specs(2),
         out_specs=tuple(vmem_specs(2)),
-        scratch_shapes=[
-            pltpu.VMEM((2 * plan.cross, TILE, TILE), bf16),
-            pltpu.SemaphoreType.DMA,
-        ],
         compiler_params=vmem_params(),
         cost_estimate=cost(4 * total * plan.image_width * plan.half, 8e6),
         name="image_forward",
-    )(nat, image)
+    )(*pin(nat, image))
 
 
 def cross_forward_body(
     plan, scale, nat, hidden, mine, other, params, image_keys, image_values,
-    resid, first_query, first_text, low_query, low_text, queries, probs, mixed, part, w, sem,
+    resid, first_query, first_text, low_query, low_text, queries, probs, mixed, part,
 ):
-    copy = load_blocks(nat, plan.cross_first, plan.cross_count, w, sem)
     gain, shift = params[0, 0:1], params[0, 1:2]
     text = plan.seq - NQ
 
@@ -252,8 +248,7 @@
         return carry
 
     lax.fori_loop(0, plan.rows, one_norm, 0)
-    copy.wait()
-    matrix = matrix_of(w, 0, plan.wt, 0, plan.ht, plan.ht)
+    matrix = matrix_of(nat, 0, plan.wt, 0, plan.ht, plan.ht, plan.cross_first)
     queries[...] = mm(low_query[...], matrix, NN).astype(bf16)
     allowed = lax.broadcasted_iota(jnp.int32, (2 * NQ, plan.keys), 1) < plan.patches
 
@@ -268,7 +263,7 @@
         return carry
 
     lax.fori_loop(0, plan.rows, one, 0)
-    matrix = matrix_of(w, 0, plan.ht, 0, plan.wt, plan.wt, plan.square + 2 * plan.cross)
+    matrix = matrix_of(nat, 0, plan.ht, 0, plan.wt, plan.wt, plan.cross_out)
     part[...] = mm(mixed[...], matrix, NN).astype(bf16)
 
 
@@ -277,26 +272,22 @@
     return pl.pallas_call(
         functools.partial(cross_forward_body, plan, scale),
         out_shape=(
-            jax.ShapeDtypeStruct((plan.tokens, width), f32),
-            jax.ShapeDtypeStruct((learned, width), f32),
-            jax.ShapeDtypeStruct((texts, width), f32),
-            jax.ShapeDtypeStruct((learned, width), bf16),
-            jax.ShapeDtypeStruct((texts, width), bf16),
-            jax.ShapeDtypeStruct((learned, half), bf16),
-            jax.ShapeDtypeStruct((plan.rows, plan.ht, 2 * NQ, plan.keys), f32),
-            jax.ShapeDtypeStruct((learned, half), bf16),
+            held((plan.tokens, width), f32),
+            held((learned, width), f32),
+            held((texts, width), f32),
+            held((learned, width), bf16),
+            held((texts, width), bf16),
+            held((learned, half), bf16),
+            held((plan.rows, plan.ht, 2 * NQ, plan.keys), f32),
+            held((learned, half), bf16),
             jax.ShapeDtypeStruct((learned, width), bf16),
         ),
-        in_specs=any_specs(1) + vmem_specs(6),
+        in_specs=vmem_specs(7),
         out_specs=tuple(vmem_specs(9)),
-        scratch_shapes=[
-            pltpu.VMEM((plan.cross_count, TILE, TILE), bf16),
-            pltpu.SemaphoreType.DMA,
-        ],
         compiler_params=vmem_params(),
         cost_estimate=cost(4 * learned * width * half, 1.2e7),
         name="cross_forward",
-    )(nat, hidden, mine, other, params, image_keys, image_values)
+    )(*pin(nat, hidden), mine, other, params, *pin(image_keys, image_values))
 
 
 def gelu_parts(values):
@@ -305,9 +296,9 @@
     return values * normal, normal + values * density
 
 
-def feed_forward_tail(plan, states_low, w, gated, slope, part):
+def feed_forward_tail(plan, first_block, nat, states_low, gated, slope, part):
     def one_up(chunk, carry):
-        matrix = matrix_of(w, 0, plan.wt, chunk * 2, 2, plan.ft)
+        matrix = matrix_of(nat, 0, plan.wt, chunk * 2, 2, plan.ft, first_block)
         active, derivative = gelu_parts(mm(states_low[...], matrix, NN))
         cols = pl.ds(pl.multiple_of(chunk * 2 * TILE, 2 * TILE), 2 * TILE)
         gated[:, cols] = active.astype(bf16)
@@ -317,7 +308,7 @@
     lax.fori_loop(0, plan.ft // 2, one_up, 0)
 
     def one_down(chunk, carry):
-        matrix = matrix_of(w, 0, plan.ft, chunk * 2, 2, plan.wt, plan.feed)
+        matrix = matrix_of(nat, 0, plan.ft, chunk * 2, 2, plan.wt, first_block + plan.feed)
         cols = pl.ds(pl.multiple_of(chunk * 2 * TILE, 2 * TILE), 2 * TILE)
         part[:, cols] = mm(gated[...], matrix, NN).astype(bf16)
         return carry
@@ -325,48 +316,39 @@
     lax.fori_loop(0, plan.wt // 2, one_down, 0)
 
 
-def text_forward_body(plan, nat, low_text, gated, slope, part, w, sem):
-    copy = load_blocks(nat, plan.text_first, 2 * plan.feed, w, sem)
-    copy.wait()
-    feed_forward_tail(plan, low_text, w, gated, slope, part)
+def text_forward_body(plan, nat, low_text, gated, slope, part):
+    feed_forward_tail(plan, plan.text_first, nat, low_text, gated, slope, part)
 
 
 def query_forward_body(
-    plan, nat, first_query, mine, other, params, resid, second, low, gated, slope, part, w, sem
+    plan, nat, first_query, mine, other, params, resid, second, low, gated, slope, part,
 ):
-    copy = load_blocks(nat, plan.query_first, 2 * plan.feed, w, sem)
     summed = first_query[...] + (mine[...].astype(f32) + other[...].astype(f32))
     resid[...] = summed
     normed = norm_forward(summed)[0] * params[1, 0:1] + params[1, 1:2]
     second[...] = normed
     low[...] = normed.astype(bf16)
-    copy.wait()
-    feed_forward_tail(plan, low, w, gated, slope, part)
+    feed_forward_tail(plan, plan.query_first, nat, low, gated, slope, part)
 
 
 def feed_shapes(plan, count):
     return (
-        jax.ShapeDtypeStruct((count, plan.hidden), bf16),
-        jax.ShapeDtypeStruct((count, plan.hidden), f32),
+        held((count, plan.hidden), bf16),
+        held((count, plan.hidden), f32),
         jax.ShapeDtypeStruct((count, plan.width), bf16),
     )
-
-
-def feed_scratch(plan):
-    return [pltpu.VMEM((2 * plan.feed, TILE, TILE), bf16), pltpu.SemaphoreType.DMA]
 
 
 def text_forward(plan, nat, low_text):
     return pl.pallas_call(
         functools.partial(text_forward_body, plan),
         out_shape=feed_shapes(plan, plan.texts),
-        in_specs=any_specs(1) + vmem_specs(1),
+        in_specs=vmem_specs(2),
         out_specs=tuple(vmem_specs(3)),
-        scratch_shapes=feed_scratch(plan),
         compiler_params=vmem_params(),
         cost_estimate=cost(4 * plan.texts * plan.width * plan.hidden, 1e7),
         name="text_forward",
-    )(nat, low_text)
+    )(*pin(nat, low_text))
 
 
 def query_forward(plan, nat, first_query, mine, other, params):
@@ -374,25 +356,23 @@
     return pl.pallas_call(
         functools.partial(query_forward_body, plan),
         out_shape=(
-            jax.ShapeDtypeStruct((count, width), f32),
-            jax.ShapeDtypeStruct((count, width), f32),
-            jax.ShapeDtypeStruct((count, width), bf16),
+            held((count, width), f32),
+            held((count, width), f32),
+            held((count, width), bf16),
         )
         + feed_shapes(plan, count),
-        in_specs=any_specs(1) + vmem_specs(4),
+        in_specs=vmem_specs(5),
         out_specs=tuple(vmem_specs(6)),
-        scratch_shapes=feed_scratch(plan),
         compiler_params=vmem_params(),
         cost_estimate=cost(4 * count * width * plan.hidden, 8e6),
         name="query_forward",
-    )(nat, first_query, mine, other, params)
+    )(*pin(nat, first_query), mine, other, params)
 
 
 def feed_backward_body(
-    plan, first_block, which, nat, states, mine, other, upstream, params, slope,
-    out, grad, grad_low, before_low, part, norm_grad, w, sem,
+    plan, first_block, first_token, which, nat, states, mine, other, upstream, params, slope,
+    out, grad, grad_low, before_low, part, norm_grad,
 ):
-    copy = load_blocks(nat, first_block, 2 * plan.feed, w, sem)
     gain, shift = params[which, 0:1], params[which, 1:2]
     count = states.shape[0] // plan.rows
     norm_grad[...] = jnp.zeros_like(norm_grad)
@@ -402,7 +382,7 @@
         summed = states[place, :] + (mine[place, :].astype(f32) + other[place, :].astype(f32))
         out[place, :] = (norm_forward(summed)[0] * gain + shift).astype(bf16)
         found, gain_grad, shift_grad = norm_backward(
-            summed, upstream[place, :].astype(f32), gain
+            summed, upstream[pl.ds(row * plan.seq + first_token, count), :].astype(f32), gain
         )
         grad[place, :] = found
         grad_low[place, :] = found.astype(bf16)
@@ -411,10 +391,9 @@
         return carry
 
     lax.fori_loop(0, plan.rows, one_norm, 0)
-    copy.wait()
 
     def one_down(chunk, carry):
-        matrix = matrix_of(w, chunk * 2, 2, 0, plan.wt, plan.wt, plan.feed)
+        matrix = matrix_of(nat, chunk * 2, 2, 0, plan.wt, plan.wt, first_block + plan.feed)
         cols = pl.ds(pl.multiple_of(chunk * 2 * TILE, 2 * TILE), 2 * TILE)
         before_low[:, cols] = (mm(grad_low[...], matrix, NT) * slope[:, cols]).astype(bf16)
         return carry
@@ -422,7 +401,7 @@
     lax.fori_loop(0, plan.ft // 2, one_down, 0)
 
     def one_up(chunk, carry):
-        matrix = matrix_of(w, chunk * 2, 2, 0, plan.ft, plan.ft)
+        matrix = matrix_of(nat, chunk * 2, 2, 0, plan.ft, plan.ft, first_block)
         cols = pl.ds(pl.multiple_of(chunk * 2 * TILE, 2 * TILE), 2 * TILE)
         part[:, cols] = mm(before_low[...], matrix, NT).astype(bf16)
         return carry
@@ -430,40 +409,37 @@
     lax.fori_loop(0, plan.wt // 2, one_up, 0)
 
 
-def feed_backward(plan, first_block, which, nat, states, mine, other, upstream, params, slope):
+def feed_backward(plan, first_block, first_token, which, nat, states, mine, other, upstream, params, slope):
     count, width = states.shape
     return pl.pallas_call(
-        functools.partial(feed_backward_body, plan, first_block, which),
+        functools.partial(feed_backward_body, plan, first_block, first_token, which),
         out_shape=(
             jax.ShapeDtypeStruct((count, width), bf16),
-            jax.ShapeDtypeStruct((count, width), f32),
-            jax.ShapeDtypeStruct((count, width), bf16),
-            jax.ShapeDtypeStruct((count, plan.hidden), bf16),
+            held((count, width), f32),
+            held((count, width), bf16),
+            held((count, plan.hidden), bf16),
             jax.ShapeDtypeStruct((count, width), bf16),
             jax.ShapeDtypeStruct((2, width), f32),
         ),
-        in_specs=any_specs(1) + vmem_specs(6),
+        in_specs=vmem_specs(7),
         out_specs=tuple(vmem_specs(6)),
-        scratch_shapes=feed_scratch(plan),
         compiler_params=vmem_params(),
         cost_estimate=cost(4 * count * width * plan.hidden, 1e7),
         name="feed_backward",
-    )(nat, states, mine, other, upstream, params, slope)
+    )(*pin(nat, states), mine, other, *pin(upstream), params, *pin(slope))
 
 
 def cross_backward_body(
     plan, scale, nat, resid, third_grad, mine, other, params, queries, keys, values, probs,
-    grad, grad_low, query_back, key_back, value_back, part, norm_grad, looked, w, sem,
+    grad, grad_low, query_back, key_back, value_back, part, norm_grad, looked,
 ):
-    copy = load_blocks(nat, plan.cross_first, plan.cross_count, w, sem)
     upstream = third_grad[...] + (mine[...].astype(f32) + other[...].astype(f32))
     found, gain_grad, shift_grad = norm_backward(resid[...], upstream, params[1, 0:1])
     grad[...] = found
     grad_low[...] = found.astype(bf16)
     norm_grad[0:1] = gain_grad
     norm_grad[1:2] = shift_grad
-    copy.wait()
-    matrix = matrix_of(w, 0, plan.ht, 0, plan.wt, plan.wt, plan.square + 2 * plan.cross)
+    matrix = matrix_of(nat, 0, plan.ht, 0, plan.wt, plan.wt, plan.cross_out)
     looked[...] = mm(grad_low[...], matrix, NT).astype(bf16)
 
     def one(row, carry):
@@ -481,7 +457,7 @@
         return carry
 
     lax.fori_loop(0, plan.rows, one, 0)
-    matrix = matrix_of(w, 0, plan.wt, 0, plan.ht, plan.ht)
+    matrix = matrix_of(nat, 0, plan.wt, 0, plan.ht, plan.ht, plan.cross_first)
     part[...] = mm(query_back[...], matrix, NT).astype(bf16)
 
 
@@ -492,33 +468,30 @@
     return pl.pallas_call(
         functools.partial(cross_backward_body, plan, scale),
         out_shape=(
-            jax.ShapeDtypeStruct((learned, width), f32),
-            jax.ShapeDtypeStruct((learned, width), bf16),
-            jax.ShapeDtypeStruct((learned, half), bf16),
-            jax.ShapeDtypeStruct(keys.shape, bf16),
-            jax.ShapeDtypeStruct(keys.shape, bf16),
+            held((learned, width), f32),
+            held((learned, width), bf16),
+            held((learned, half), bf16),
+            held(keys.shape, bf16),
+            held(keys.shape, bf16),
             jax.ShapeDtypeStruct((learned, width), bf16),
             jax.ShapeDtypeStruct((2, width), f32),
         ),
-        in_specs=any_specs(1) + vmem_specs(9),
+        in_specs=vmem_specs(10),
         out_specs=tuple(vmem_specs(7)),
         scratch_shapes=[
             pltpu.VMEM((learned, half), bf16),
-            pltpu.VMEM((plan.cross_count, TILE, TILE), bf16),
-            pltpu.SemaphoreType.DMA,
         ],
         compiler_params=vmem_params(),
         cost_estimate=cost(8 * learned * width * half, 1e7),
         name="cross_backward",
-    )(nat, resid, third_grad, mine, other, params, queries, keys, values, probs)
+    )(*pin(nat, resid, third_grad), mine, other, params, *pin(queries, keys, values, probs))
 
 
 def self_backward_body(
     plan, scale, nat, resid, query_grad, query_mine, query_other, text_grad, text_mine,
     text_other, params, qkv, probs,
-    grad, grad_low, back, part, norm_grad, mixed, w, sem,
+    grad, grad_low, back, part, norm_grad, mixed,
 ):
-    copy = load_blocks(nat, plan.self_first, plan.self_count, w, sem)
     text = plan.seq - NQ
     gain = params[0, 0:1]
     norm_grad[...] = jnp.zeros_like(norm_grad)
@@ -544,8 +517,7 @@
         return carry
 
     lax.fori_loop(0, plan.rows, one_norm, 0)
-    copy.wait()
-    matrix = matrix_of(w, 0, plan.ht, 0, plan.wt, plan.wt, 3 * plan.square)
+    matrix = matrix_of(nat, 0, plan.ht, 0, plan.wt, plan.wt, plan.self_out)
     mixed[...] = mm(grad_low[...], matrix, NT).astype(bf16)
 
     def one(row, carry):
@@ -563,7 +535,8 @@
 
     lax.fori_loop(0, plan.rows, one, 0)
     matrix = jnp.concatenate(
-        [matrix_of(w, 0, plan.wt, 0, plan.ht, plan.ht, p * plan.square) for p in range(3)], axis=1
+        [matrix_of(nat, 0, plan.wt, 0, plan.ht, plan.ht, p * plan.square) for p in range(3)],
+        axis=1,
     )
     part[...] = mm(back[...], matrix, NT).astype(bf16)
 
@@ -577,24 +550,22 @@
         functools.partial(self_backward_body, plan, scale),
         out_shape=(
             jax.ShapeDtypeStruct((tokens, width), f32),
-            jax.ShapeDtypeStruct((tokens, width), bf16),
-            jax.ShapeDtypeStruct((tokens, 3 * half), bf16),
+            held((tokens, width), bf16),
+            held((tokens, 3 * half), bf16),
             jax.ShapeDtypeStruct((tokens, width), bf16),
             jax.ShapeDtypeStruct((2, width), f32),
         ),
-        in_specs=any_specs(1) + vmem_specs(10),
+        in_specs=vmem_specs(11),
         out_specs=tuple(vmem_specs(5)),
         scratch_shapes=[
             pltpu.VMEM((tokens, half), bf16),
-            pltpu.VMEM((plan.self_count, TILE, TILE), bf16),
-            pltpu.SemaphoreType.DMA,
         ],
         compiler_params=vmem_params(),
         cost_estimate=cost(8 * tokens * width * half, 1.2e7),
         name="self_backward",
     )(
-        nat, resid, query_grad, query_mine, query_other, text_grad, text_mine, text_other,
-        params, qkv, probs,
+        *pin(nat, resid, query_grad), query_mine, query_other, *pin(text_grad), text_mine,
+        text_other, params, *pin(qkv, probs),
     )
 
 
@@ -669,11 +640,11 @@
         functools.partial(
             grad_blocks_body, first_block, pairs, len(sources), len(buffers), spare
         ),
-        out_shape=tuple(jax.ShapeDtypeStruct(b.shape, b.dtype) for b in buffers),
+        out_shape=tuple(pltpu.HBM(b.shape, b.dtype) for b in buffers),
         in_specs=[pl.BlockSpec(memory_space=pltpu.SMEM)]
         + vmem_specs(len(sources))
-        + any_specs(len(given)),
-        out_specs=tuple(any_specs(len(buffers))),
+        + [pl.BlockSpec(memory_space=pltpu.HBM)] * len(given),
+        out_specs=tuple([pl.BlockSpec(memory_space=pltpu.HBM)] * len(buffers)),
         scratch_shapes=[
             pltpu.VMEM((total, TILE, TILE), bf16),
             pltpu.VMEM((TILE, TILE), bf16),
@@ -683,7 +654,7 @@
         compiler_params=vmem_params(),
         cost_estimate=cost(flops, 1e7),
         name="grad_blocks",
-    )(place, *sources, *given)
+    )(place, *pin(*sources), *given)
 
 
 def swap_tensor(part):
@@ -694,23 +665,20 @@
 
 
 def layer_rows(
-    hidden, image, segment_ids, cotangent, nat, norm_params, heads_local, scale, place, regions
+    hidden, image, patches, segment_ids, cotangent, nat, norm_params, heads_local, scale, place, regions
 ):
     rows, seq, width = hidden.shape
     plan = Plan(
-        rows, seq, width, image.shape[2], image.shape[1], heads_local, FF // lax.axis_size("tensor")
+        rows, seq, width, image.shape[2], patches, heads_local, FF // lax.axis_size("tensor")
     )
     tokens, learned, texts, half = plan.tokens, plan.learned, plan.texts, plan.half
     flat_hidden = hidden.reshape(tokens, width)
-    flat_image = jnp.pad(image, ((0, 0), (0, plan.keys - plan.patches), (0, 0))).reshape(
-        rows * plan.keys, plan.image_width
-    )
-    up_query = cotangent[:, :NQ].reshape(learned, width)
-    up_text = cotangent[:, NQ:].reshape(texts, width)
+    flat_image = image.reshape(rows * plan.keys, plan.image_width)
+    flat_back = cotangent.reshape(tokens, width)
     buffers = [jax.ShapeDtypeStruct((count, TILE, TILE), bf16) for count in regions]
 
     qkv, self_probs, mixed, part_one = self_forward(
-        plan, scale, nat, flat_hidden, segment_ids[:, None, :], segment_ids[:, :, None]
+        plan, scale, nat, flat_hidden, segment_ids[:, None, :]
     )
     other_one = swap_tensor(part_one)
     image_keys, image_values = image_forward(plan, nat, flat_image)
@@ -728,13 +696,13 @@
     )
     other_query = swap_tensor(part_query)
     out_text, third_text, third_text_low, before_text, part_four_text, norm_text = feed_backward(
-        plan, plan.text_first, 3, nat, first_text, part_text, other_text, up_text, norm_params,
+        plan, plan.text_first, NQ, 3, nat, first_text, part_text, other_text, flat_back, norm_params,
         text_slope,
     )
     other_four_text = swap_tensor(part_four_text)
     out_query, third_query, third_query_low, before_query, part_four_query, norm_query = (
         feed_backward(
-            plan, plan.query_first, 2, nat, second, part_query, other_query, up_query, norm_params,
+            plan, plan.query_first, 0, 2, nat, second, part_query, other_query, flat_back, norm_params,
             query_slope,
         )
     )
@@ -835,27 +803,26 @@
 def place_blocks(ids, first, sources, target, shape):
     counts = [source.shape[0] for source in sources]
     operands = [ids, *sources]
-    specs = [pl.BlockSpec(memory_space=pltpu.SMEM)] + vmem_specs(len(sources))
+    specs = [pl.BlockSpec(memory_space=pltpu.SMEM)] + any_specs(len(sources))
     aliases = {}
     if target is not None:
-        operands.append(target)
-        specs += any_specs(1)
+        operands += pin(target)
+        specs += vmem_specs(1)
         aliases = {len(operands) - 1: 0}
     return pl.pallas_call(
         functools.partial(place_blocks_body, counts, first),
-        out_shape=jax.ShapeDtypeStruct(shape, bf16),
+        out_shape=held(shape, bf16),
         in_specs=specs,
-        out_specs=any_specs(1)[0],
+        out_specs=vmem_specs(1)[0],
         scratch_shapes=[pltpu.SemaphoreType.DMA],
         input_output_aliases=aliases,
+        compiler_params=pltpu.CompilerParams(vmem_limit_bytes=1024 * 1024),
         cost_estimate=cost(0, 4 * sum(counts) * TILE * TILE),
         name="place_blocks",
     )(*operands)
 
 
-def gather_ring(shard, order, chains=2):
-    slots = shard.shape[0]
-    parts = chain_parts(slots, chains)
+def gather_positions(slots):
     table = np.zeros((RING_DEVICES, RING_DEVICES * slots), np.int32)
     for index in range(RING_DEVICES):
         position, core = ring_place(index)
@@ -865,8 +832,42 @@
                 owner = ring_index(position - direction_of(side) * step, side)
                 found += [owner * slots + slot for slot in range(slots)]
         table[index] = found
-    ids = order[jnp.asarray(table)[lax.axis_index("dp")]]
-    shape = (order.shape[0], TILE, TILE)
+    return table
+
+
+def index_body(count, device, order, arrival, departure, ids, place):
+    me = device[0]
+
+    def one(number, carry):
+        ids[number] = order[arrival[me, number]]
+        place[order[number]] = departure[me, number]
+        return carry
+
+    lax.fori_loop(0, count, one, 0)
+
+
+def block_indices(order, slots):
+    count = order.shape[0]
+    smem = pl.BlockSpec(memory_space=pltpu.SMEM)
+    return pl.pallas_call(
+        functools.partial(index_body, count),
+        out_shape=(jax.ShapeDtypeStruct((count,), jnp.int32),) * 2,
+        in_specs=[smem] * 4,
+        out_specs=(smem, smem),
+        compiler_params=vmem_params(),
+        name="block_indices",
+    )(
+        lax.axis_index("dp").reshape(1),
+        order,
+        jnp.asarray(gather_positions(slots)),
+        jnp.asarray(scatter_positions(slots)),
+    )
+
+
+def gather_ring(shard, ids, chains=2):
+    slots = shard.shape[0]
+    parts = chain_parts(slots, chains)
+    shape = (ids.shape[0], TILE, TILE)
     other = lax.ppermute(shard, "dp", CORE_PAIRS)
     held = [shard[first : first + count] for first, count in parts]
     natural = None
@@ -936,10 +937,6 @@
     rest = values - high.astype(f32)
     middle = rest.astype(bf16)
     return high, middle, (rest - middle.astype(f32)).astype(bf16)
-
-
-def join(axis, *pieces):
-    return jnp.concatenate(pieces, axis=axis)
 
 
 def fold(product):
@@ -1232,19 +1229,22 @@
     slots = weight_master.shape[1]
     shard = weight_master[0].astype(bf16)
     ring = lax.axis_size("dp") == RING_DEVICES
+    patches = image.shape[1]
+    image = jnp.pad(image, ((0, 0), (0, -patches % PATCHES_PAD), (0, 0)))
     if ring:
-        natural = gather_ring(shard, order)
-        positions = jnp.asarray(scatter_positions(slots))[lax.axis_index("dp")]
+        ids, place = block_indices(order, slots)
+        ids, image = lax.optimization_barrier((ids, image))
+        natural = gather_ring(shard, ids)
         regions = (2 * slots, (RING - 2) * slots, RING * slots)
     else:
         positions = jnp.arange(slot_count, dtype=jnp.int32)
+        place = jnp.zeros_like(order).at[order].set(positions)
         gathered = lax.all_gather(shard, "dp", axis=0, tiled=True)
-        natural = gathered[jnp.zeros_like(order).at[order].set(positions)]
+        natural = gathered[place]
         regions = (slot_count,)
-    place = jnp.zeros_like(order).at[order].set(positions)
     out_rows, in_grad, packed, norm_part = layer_rows(
-        hidden, image, segment_ids, cotangent, natural, norm_params, heads_local, scale, place,
-        regions,
+        hidden, image, patches, segment_ids, cotangent, natural, norm_params, heads_local, scale,
+        place, regions,
     )
     if ring:
         owned = scatter_ring(*packed, slots)

time: 390 us -> 346 us (0.89)
  Pallas kernels: 175 us -> 144 us
  local copies, waits for them, and re-layouts: 28.6 us -> 4.27 us
  waiting for transfers between devices: 98.5 us -> 112 us
    unnamed x99 -> x24, local copies, waits for them, and re-layouts: 15.2 us -> 0.82 us
    pallas_call x4 -> x5, Pallas kernels: 33.8 us -> 23.7 us  [the longest x2 9.18 us: feed_backward(): pl.pallas_call(functools.partial(feed_backward_body, plan, first_block, f...]
    ppermute x8, waiting for transfers between devices: 22.2 us -> 29.5 us  [swap_tensor(): return lax.ppermute(part, 'tensor', [(0, 1), (1, 0)])]
    pallas_call x7, Pallas kernels: 20.4 us -> 26.3 us  [place_blocks(): pl.pallas_call(functools.partial(place_blocks_body, counts, first), out_s...]
    pallas_call x4, Pallas kernels: 36.5 us -> 31.3 us  [grad_blocks(): pl.pallas_call(functools.partial(grad_blocks_body, first_block, pairs, le...]
    pallas_call x1, Pallas kernels: 8.87 us -> 3.86 us  [text_forward(): pl.pallas_call(functools.partial(text_forward_body, plan), out_shape=feed...]
    pallas_call x1, Pallas kernels: 10.8 us -> 5.95 us  [cross_backward(): pl.pallas_call(functools.partial(cross_backward_body, plan, scale), out_s...]
    ppermute x14, waiting for transfers between devices: 22.8 us -> 27.6 us  [gather_ring(): held = [lax.ppermute(piece, 'dp', RING_PAIRS) for piece in held]]
  transfers between devices with their start and end apart: 57 -> 57, of which waited for: 26 -> 26; matrix products, arithmetic and copies ran while one was open for 7% -> 4% of each run, Pallas kernels for 24% -> 23%
where the time goes in v5:
time: 346 us; the launch traced here: 342 us
  Pallas kernels  144 us (42%)
  waiting for transfers between devices  112 us (32%)
  starting transfers between devices  65.8 us (19%)
  other arithmetic  14.4 us (4%)
  local copies, waits for them, and re-layouts  4.27 us (1%)
    ppermute x14, waiting for transfers between devices, scatter_ring(): summed = lax.ppermute(summed.astype(bf16), 'dp', RING_PAIRS)  37.3 us
    pallas_call x1, Pallas kernels, optimizer(): pl.pallas_call(functools.partial(optimizer_body, padded), out_shape=tuple...  34 us
    pallas_call x4, Pallas kernels, grad_blocks(): pl.pallas_call(functools.partial(grad_blocks_body, first_block, pairs, le...  31.3 us
    ppermute x8, waiting for transfers between devices, swap_tensor(): return lax.ppermute(part, 'tensor', [(0, 1), (1, 0)])  29.5 us
    ppermute x14, waiting for transfers between devices, gather_ring(): held = [lax.ppermute(piece, 'dp', RING_PAIRS) for piece in held]  27.6 us
    pallas_call x7, Pallas kernels, place_blocks(): pl.pallas_call(functools.partial(place_blocks_body, counts, first), out_s...  26.3 us
    ppermute x14, starting transfers between devices, gather_ring(): held = [lax.ppermute(piece, 'dp', RING_PAIRS) for piece in held]  25.2 us
    ppermute x14, starting transfers between devices, scatter_ring(): summed = lax.ppermute(summed.astype(bf16), 'dp', RING_PAIRS)  23.4 us
  transfers between devices with their start and end apart: 57, of which 26 were waited for; matrix products, arithmetic and copies ran while one was open for 4% of the time, Pallas kernels for 23%

profile of v5, /device:TPU:0, one launch (start us, length us, event | category | flops | bytes accessed | tf_op | source)
XLA Modules:
  0.0 341.9 jit_solution(8278556171129699095)
XLA Ops:
  7.1 5.1 %collective-permute-done.3.refs_3_ = bf16[15,128,128]{2,1,0:T(8,128)(2,1)S(1)} collective-permute-done((bf16[15,128,128]{2,1,0:T(8,128)(2,1)S(1)}, bf16[15,128,128]{2,1,0:T(8,128)(2,1)S(1)}, u32[]{:S(2)}, u32[]{:S(2)}) %collective-permute-start.3) | collective-permute-done | bytes 491552 | tf_op jit(solution)/shard_map/ppermute | solution.py:876
  28.4 6.9 %block_indices.1 = (s32[464]{0:T(512)S(1)}, s32[464]{0:T(512)S(1)}) custom-call(s32[1]{0:T(128)} %bitcast.device, s32[464]{0:T(512)S(1)} %bitcast.51, s32[16,464]{1,0:T(8,128)S(1)} %copy-done.5, s32[16,464]{1,0:T(8,128)S(1)} %copy-done.6), custom_call_target="tpu_custom_call" | custom-call | tf_op jit(solution)/shard_map/block_indices/pallas_call | solution.py:852
  35.4 5.9 %place_blocks.7.refs_4_ = bf16[464,128,128]{2,1,0:T(8,128)(2,1)S(1)} custom-call(s32[464]{0:T(512)S(1)} %get-tuple-element.98.ids, bf16[29,128,128]{2,1,0:T(8,128)(2,1)S(1)} %bitcast_convert_fusion.refs_0_, bf16[29,128,128]{2,1,0:T(8,128)(2,1)S(1)} %collective-permute-done.2.refs_1_, bf16[14,128,128]{2,1,0:T(8,128)(2,1)} %collective-permute-done.refs_2_, ...), custom_call_target="tpu_custom_call" | custom-call | bytes 7602176 | tf_op jit(solution)/shard_map/place_blocks/pallas_call | solution.py:812
  86.4 3.7 %place_blocks.12.refs_4_ = bf16[464,128,128]{2,1,0:T(8,128)(2,1)S(1)} custom-call(s32[464]{0:T(512)S(1)} %get-tuple-element.98.ids, bf16[14,128,128]{2,1,0:T(8,128)(2,1)S(1)} %collective-permute-done.18.refs_0_, bf16[15,128,128]{2,1,0:T(8,128)(2,1)S(1)} %collective-permute-done.23.refs_1_, ...), custom_call_target="tpu_custom_call", output_to_operand_aliasing={{}: (5, {})} | custom-call | bytes 3801088 | tf_op jit(solution)/shard_map/place_blocks/pallas_call | solution.py:812
  96.7 5.4 %self_forward.1 = (bf16[3,512,384]{2,1,0:T(8,128)(2,1)S(1)}, f32[4,3,256,128]{3,2,1,0:T(8,128)S(1)}, bf16[512,384]{1,0:T(8,128)(2,1)S(1)}, bf16[512,768]{1,0:T(8,128)(2,1)S(1)}) custom-call(bf16[464,128,128]{2,1,0:T(8,128)(2,1)S(1)} %place_blocks.13.nat, bf16[512,768]{1,0:T(8,128)(2,1)S(1)} %bitcast.31, s32[4,1,128]{2,1,0:T(1,128)S(1)} %bitcast.50), custom_call_target="tpu_custom_call" | custom-call | flops 1207959552 | bytes 8000000 | tf_op jit(solution)/shard_map/self_forward/pallas_call | solution.py:187
  104.0 4.9 %image_forward.1 = (bf16[1088,384]{1,0:T(8,128)(2,1)S(1)}, bf16[1088,384]{1,0:T(8,128)(2,1)S(1)}) custom-call(bf16[464,128,128]{2,1,0:T(8,128)(2,1)S(1)} %place_blocks.13.nat, bf16[1088,1408]{1,0:T(8,128)(2,1)S(1)} %bitcast.29), custom_call_target="tpu_custom_call" | custom-call | flops 2353004544 | bytes 8000000 | tf_op jit(solution)/shard_map/image_forward/pallas_call | solution.py:217
  108.9 12.8 %collective-permute-done.29.other = bf16[512,768]{1,0:T(8,128)(2,1)S(1)} collective-permute-done((bf16[512,768]{1,0:T(8,128)(2,1)S(1)}, bf16[512,768]{1,0:T(8,128)(2,1)S(1)}, u32[]{:S(2)}, u32[]{:S(2)}) %collective-permute-start.29) | collective-permute-done | bytes 786464 | tf_op jit(solution)/shard_map/ppermute | solution.py:664
  121.7 5.9 %cross_forward.1 = (f32[512,768]{1,0:T(8,128)S(1)}, f32[128,768]{1,0:T(8,128)S(1)}, f32[384,768]{1,0:T(8,128)S(1)}, bf16[128,768]{1,0:T(8,128)(2,1)S(1)}, bf16[3...) custom-call(bf16[464,128,128]{2,1,0:T(8,128)(2,1)S(1)} %place_blocks, ...), custom_call_target="tpu_custom_call" | custom-call | flops 150994944 | bytes 12000000 | tf_op jit(solution)/shard_map/cross_forward/pallas_call | solution.py:272
  127.6 3.9 %text_forward.1 = (bf16[384,1536]{1,0:T(8,128)(2,1)S(1)}, f32[384,1536]{1,0:T(8,128)S(1)}, bf16[384,768]{1,0:T(8,128)(2,1)S(1)}) custom-call(bf16[464,128,128]{2,1,0:T(8,128)(2,1)S(1)} %place_blocks.13.nat, bf16[384,768]{1,0:T(8,128)(2,1)S(1)} %get-tuple-element.122.low_text.refs_0_), custom_call_target="tpu_custom_call" | custom-call | flops 1811939328 | bytes 10000000 | tf_op jit(solution)/shard_map/text_forward/pallas_call | solution.py:343
  133.5 16.7 %collective-permute-done.30.other = bf16[128,768]{1,0:T(8,128)(2,1)S(1)} collective-permute-done((bf16[128,768]{1,0:T(8,128)(2,1)S(1)}, bf16[128,768]{1,0:T(8,128)(2,1)S(1)}, u32[]{:S(2)}, u32[]{:S(2)}) %collective-permute-start.30) | collective-permute-done | bytes 196640 | tf_op jit(solution)/shard_map/ppermute | solution.py:664
  154.6 5.1 %feed_backward.3 = (bf16[384,768]{1,0:T(8,128)(2,1)S(1)}, f32[384,768]{1,0:T(8,128)S(1)}, bf16[384,768]{1,0:T(8,128)(2,1)S(1)}, bf16[384,1536]{1,0:T(8,128)(2,1)...) custom-call(bf16[464,128,128]{2,1,0:T(8,128)(2,1)S(1)} %place_blocks.13.nat, ...), custom_call_target="tpu_custom_call" | custom-call | flops 1811939328 | bytes 10000000 | tf_op jit(solution)/shard_map/feed_backward/pallas_call | solution.py:414
  160.3 4.1 %feed_backward.2 = (bf16[128,768]{1,0:T(8,128)(2,1)S(1)}, f32[128,768]{1,0:T(8,128)S(1)}, bf16[128,768]{1,0:T(8,128)(2,1)S(1)}, bf16[128,1536]{1,0:T(8,128)(2,1)...) custom-call(bf16[464,128,128]{2,1,0:T(8,128)(2,1)S(1)} %place_blocks.13.nat, ...), custom_call_target="tpu_custom_call" | custom-call | flops 603979776 | bytes 10000000 | tf_op jit(solution)/shard_map/feed_backward/pallas_call | solution.py:414
  165.9 7.2 %grad_blocks.4 = (bf16[58,128,128]{2,1,0:T(8,128)(2,1)}, bf16[174,128,128]{2,1,0:T(8,128)(2,1)}, bf16[232,128,128]{2,1,0:T(8,128)(2,1)}) custom-call(s32[464]{0:T(512)S(1)} %get-tuple-element.140.place, bf16[384,768]{1,0:T(8,128)(2,1)S(1)} %get-tuple-element.122.low_text.refs_0_, bf16[384,1536]{1,0:T(8,128)(2,1)S(1)} %get-tuple-element.154.refs_1_, ...), custom_call_target="tpu_custom_call" | custom-call | flops 1811939328 | bytes 10000000 | tf_op jit(solution)/shard_map/grad_blocks/pallas_call | solution.py:639
  173.2 5.9 %grad_blocks.5 = (bf16[58,128,128]{2,1,0:T(8,128)(2,1)}, bf16[174,128,128]{2,1,0:T(8,128)(2,1)}, bf16[232,128,128]{2,1,0:T(8,128)(2,1)}) custom-call(s32[464]{0:T(512)S(1)} %get-tuple-element.140.place, bf16[128,768]{1,0:T(8,128)(2,1)S(1)} %get-tuple-element.150.refs_0_, ...), custom_call_target="tpu_custom_call", output_to_operand_aliasing={{0}: (5, {}), {1}: (6, {}), {2}: (7, {})} | custom-call | flops 603979776 | bytes 10000000 | tf_op jit(solution)/shard_map/grad_blocks/pallas_call | solution.py:639
  179.1 5.9 %cross_backward.1 = (f32[128,768]{1,0:T(8,128)S(1)}, bf16[128,768]{1,0:T(8,128)(2,1)S(1)}, bf16[128,384]{1,0:T(8,128)(2,1)S(1)}, bf16[1088,384]{1,0:T(8,128)(2,1...) custom-call(bf16[464,128,128]{2,1,0:T(8,128)(2,1)S(1)} %place_blocks.13.nat, ...), custom_call_target="tpu_custom_call" | custom-call | flops 301989888 | bytes 10000000 | tf_op jit(solution)/shard_map/cross_backward/pallas_call | solution.py:468
  185.6 12.2 %grad_blocks.6 = (bf16[58,128,128]{2,1,0:T(8,128)(2,1)}, bf16[174,128,128]{2,1,0:T(8,128)(2,1)}, bf16[232,128,128]{2,1,0:T(8,128)(2,1)}) custom-call(s32[464]{0:T(512)S(1)} %get-tuple-element.140.place, bf16[128,768]{1,0:T(8,128)(2,1)S(1)} %get-tuple-element.144.refs_0_, ...), custom_call_target="tpu_custom_call", output_to_operand_aliasing={{0}: (8, {}), {1}: (9, {}), {2}: (10, {})} | custom-call | flops 2353004544 | bytes 10000000 | tf_op jit(solution)/shard_map/grad_blocks/pallas_call | solution.py:639
  197.8 7.8 %self_backward.1 = (f32[512,768]{1,0:T(8,128)S(1)}, bf16[512,768]{1,0:T(8,128)(2,1)S(1)}, bf16[512,1152]{1,0:T(8,128)(2,1)S(1)}, bf16[512,768]{1,0:T(8,128)(2,1)S(1)}, f32[2,768]{1,0:T(2,128)S(1)}) custom-call(bf16[464,128,128]{2,1,0:T(8,128)(2,1)S(1)} %place_blocks.13.nat, f32[512,768]{1,0:T(8,128)S(1)} %get-tuple-element.126.resid, ...), custom_call_target="tpu_custom_call" | custom-call | flops 1207959552 | bytes 12000000 | tf_op jit(solution)/shard_map/self_backward/pallas_call | solution.py:549
  205.6 6.0 %grad_blocks.7 = (bf16[58,128,128]{2,1,0:T(8,128)(2,1)}, bf16[174,128,128]{2,1,0:T(8,128)(2,1)}, bf16[232,128,128]{2,1,0:T(8,128)(2,1)}) custom-call(s32[464]{0:T(512)S(1)} %get-tuple-element.140.place, bf16[512,768]{1,0:T(8,128)(2,1)S(1)} %bitcast.33, ...), custom_call_target="tpu_custom_call", output_to_operand_aliasing={{0}: (5, {}), {1}: (6, {}), {2}: (7, {})} | custom-call | flops 1207959552 | bytes 10000000 | tf_op jit(solution)/shard_map/grad_blocks/pallas_call | solution.py:639
  212.2 11.7 %collective-permute-done.38 = bf16[58,128,128]{2,1,0:T(8,128)(2,1)S(1)} collective-permute-done((bf16[58,128,128]{2,1,0:T(8,128)(2,1)}, bf16[58,128,128]{2,1,0:T(8,128)(2,1)S(1)}, u32[]{:S(2)}, u32[]{:S(2)}) %collective-permute-start.38) | collective-permute-done | bytes 1900576 | tf_op jit(solution)/shard_map/ppermute | solution.py:898
  229.7 4.1 %collective-permute-done.39 = bf16[14,128,128]{2,1,0:T(8,128)(2,1)S(1)} collective-permute-done((bf16[14,128,128]{2,1,0:T(8,128)(2,1)S(1)}, bf16[14,128,128]{2,1,0:T(8,128)(2,1)S(1)}, u32[]{:S(2)}, u32[]{:S(2)}) %collective-permute-start.39) | collective-permute-done | bytes 458784 | tf_op jit(solution)/shard_map/ppermute | solution.py:914
  275.5 3.8 %collective-permute-done.55 = f32[4,2,768]{2,1,0:T(2,128)S(1)} collective-permute-done((f32[4,2,768]{2,1,0:T(2,128)S(1)}, f32[4,2,768]{2,1,0:T(2,128)S(1)}, u32[]{:S(2)}, u32[]{:S(2)}) %collective-permute-start.55) | collective-permute-done | bytes 24608 | tf_op jit(solution)/shard_map/ppermute | solution.py:922
  285.7 5.0 %collective-permute-done.44 = bf16[14,128,128]{2,1,0:T(8,128)(2,1)S(1)} collective-permute-done((bf16[14,128,128]{2,1,0:T(8,128)(2,1)S(1)}, bf16[14,128,128]{2,1,0:T(8,128)(2,1)S(1)}, u32[]{:S(2)}, u32[]{:S(2)}) %collective-permute-start.44) | collective-permute-done | bytes 458784 | tf_op jit(solution)/shard_map/ppermute | solution.py:914
  301.0 5.1 %collective-permute-done.52 = bf16[15,128,128]{2,1,0:T(8,128)(2,1)S(1)} collective-permute-done((bf16[15,128,128]{2,1,0:T(8,128)(2,1)S(1)}, bf16[15,128,128]{2,1,0:T(8,128)(2,1)S(1)}, u32[]{:S(2)}, u32[]{:S(2)}) %collective-permute-start.52) | collective-permute-done | bytes 491552 | tf_op jit(solution)/shard_map/ppermute | solution.py:914
  307.7 34.0 %optimizer.1 = (f32[29,128,128]{2,1,0:T(8,128)}, bf16[29,128,128]{2,1,0:T(8,128)(2,1)}, f32[29,128,128]{2,1,0:T(8,128)}, f32[29,128,128]{2,1,0:T(8,128)}, f32[29...) custom-call(f32[29,128,128]{2,1,0:T(8,128)} %pad_maximum_fusion.refs_0_, ...), custom_call_target="tpu_custom_call" | custom-call | tf_op jit(solution)/shard_map/optimizer/pallas_call | solution.py:1187
  (165 shorter events, 151.5 us)
Async XLA Ops:
  5.4 29.9 %collective-permute-start.2 = (bf16[29,128,128]{2,1,0:T(8,128)(2,1)S(1)}, bf16[29,128,128]{2,1,0:T(8,128)(2,1)S(1)}, u32[]{:S(2)}, u32[]{:S(2)}) collective-permute-start(bf16[29,128,128]{2,1,0:T(8,128)(2,1)S(1)} %bitcast_convert_fusion.refs_0_), channel_id=1, source_target_pairs={{0,2},{2,0},{4,6},{6,4},{8,10},{10,8},{12,14},{14,12},{16,18},{18,... | collective-permute-start | bytes 2850824 | tf_op jit(solution)/shard_map/ppermute | solution.py:871
  5.5 11.7 %collective-permute-start = (bf16[14,128,128]{2,1,0:T(8,128)(2,1)S(1)}, bf16[14,128,128]{2,1,0:T(8,128)(2,1)}, u32[]{:S(2)}, u32[]{:S(2)}) collective-permute-start(bf16[14,128,128]{2,1,0:T(8,128)(2,1)S(1)} %slice.136), channel_id=1, source_target_pairs={{0,8},{2,6},{8,16},{10,2},{16,24},{18,10},{24,28},{26,18},{28,20},... | collective-permute-start | bytes 1376264 | tf_op jit(solution)/shard_map/ppermute | solution.py:876
  12.2 10.3 %collective-permute-start.7 = (bf16[15,128,128]{2,1,0:T(8,128)(2,1)S(1)}, bf16[15,128,128]{2,1,0:T(8,128)(2,1)}, u32[]{:S(2)}, u32[]{:S(2)}) collective-permute-start(bf16[15,128,128]{2,1,0:T(8,128)(2,1)S(1)} %collective-permute-done.3.refs_3_), channel_id=1, source_target_pairs={{0,8},{2,6},{8,16},{10,2},{16,24},{18,10},{24,28},{26,18},{28,20},... | collective-permute-start | bytes 1474568 | tf_op jit(solution)/shard_map/ppermute | solution.py:876
  14.3 21.1 %collective-permute-start.5 = (bf16[15,128,128]{2,1,0:T(8,128)(2,1)S(1)}, bf16[15,128,128]{2,1,0:T(8,128)(2,1)S(1)}, u32[]{:S(2)}, u32[]{:S(2)}) collective-permute-start(bf16[15,128,128]{2,1,0:T(8,128)(2,1)S(1)} %collective-permute-done.3.refs_3_), channel_id=1, source_target_pairs={{0,2},{2,0},{4,6},{6,4},{8,10},{10,8},{12,14},{14,12},{16,18},{18,... | collective-permute-start | bytes 1474568 | tf_op jit(solution)/shard_map/ppermute | solution.py:881
  17.2 24.1 %collective-permute-start.1 = (bf16[14,128,128]{2,1,0:T(8,128)(2,1)}, bf16[14,128,128]{2,1,0:T(8,128)(2,1)}, u32[]{:S(2)}, u32[]{:S(2)}) collective-permute-start(bf16[14,128,128]{2,1,0:T(8,128)(2,1)} %collective-permute-done.refs_2_), channel_id=1, source_target_pairs={{0,8},{2,6},{8,16},{10,2},{16,24},{18,10},{24,28},{26,18},{28,20},... | collective-permute-start | bytes 1376264 | tf_op jit(solution)/shard_map/ppermute | solution.py:876
  22.5 21.0 %collective-permute-start.11 = (bf16[15,128,128]{2,1,0:T(8,128)(2,1)}, bf16[15,128,128]{2,1,0:T(8,128)(2,1)S(1)}, u32[]{:S(2)}, u32[]{:S(2)}) collective-permute-start(bf16[15,128,128]{2,1,0:T(8,128)(2,1)} %collective-permute-done.7.refs_1_), channel_id=1, source_target_pairs={{0,8},{2,6},{8,16},{10,2},{16,24},{18,10},{24,28},{26,18},{28,20},... | collective-permute-start | bytes 1474568 | tf_op jit(solution)/shard_map/ppermute | solution.py:876
  25.3 19.7 %collective-permute-start.9 = (bf16[15,128,128]{2,1,0:T(8,128)(2,1)}, bf16[15,128,128]{2,1,0:T(8,128)(2,1)}, u32[]{:S(2)}, u32[]{:S(2)}) collective-permute-start(bf16[15,128,128]{2,1,0:T(8,128)(2,1)} %collective-permute-done.7.refs_1_), channel_id=1, source_target_pairs={{0,2},{2,0},{4,6},{6,4},{8,10},{10,8},{12,14},{14,12},{16,18},{18,... | collective-permute-start | bytes 1474568 | tf_op jit(solution)/shard_map/ppermute | solution.py:881
  43.5 12.4 %collective-permute-start.15 = (bf16[15,128,128]{2,1,0:T(8,128)(2,1)S(1)}, bf16[15,128,128]{2,1,0:T(8,128)(2,1)S(1)}, u32[]{:S(2)}, u32[]{:S(2)}) collective-permute-start(bf16[15,128,128]{2,1,0:T(8,128)(2,1)S(1)} %collective-permute-done.11.refs_1_), channel_id=1, source_target_pairs={{0,8},{2,6},{8,16},{10,2},{16,24},{18,10},{24,28},{26,18},{28,20},... | collective-permute-start | bytes 1474568 | tf_op jit(solution)/shard_map/ppermute | solution.py:876
  45.0 12.4 %collective-permute-start.13 = (bf16[15,128,128]{2,1,0:T(8,128)(2,1)S(1)}, bf16[15,128,128]{2,1,0:T(8,128)(2,1)S(1)}, u32[]{:S(2)}, u32[]{:S(2)}) collective-permute-start(bf16[15,128,128]{2,1,0:T(8,128)(2,1)S(1)} %collective-permute-done.11.refs_1_), channel_id=1, source_target_pairs={{0,2},{2,0},{4,6},{6,4},{8,10},{10,8},{12,14},{14,12},{16,18},{18,... | collective-permute-start | bytes 1474568 | tf_op jit(solution)/shard_map/ppermute | solution.py:881
  50.6 10.4 %collective-permute-start.10 = (bf16[14,128,128]{2,1,0:T(8,128)(2,1)S(1)}, bf16[14,128,128]{2,1,0:T(8,128)(2,1)S(1)}, u32[]{:S(2)}, u32[]{:S(2)}) collective-permute-start(bf16[14,128,128]{2,1,0:T(8,128)(2,1)S(1)} %collective-permute-done.6.refs_0_), channel_id=1, source_target_pairs={{0,8},{2,6},{8,16},{10,2},{16,24},{18,10},{24,28},{26,18},{28,20},... | collective-permute-start | bytes 1376264 | tf_op jit(solution)/shard_map/ppermute | solution.py:876
  102.0 19.7 %collective-permute-start.29 = (bf16[512,768]{1,0:T(8,128)(2,1)S(1)}, bf16[512,768]{1,0:T(8,128)(2,1)S(1)}, u32[]{:S(2)}, u32[]{:S(2)}) collective-permute-start(bf16[512,768]{1,0:T(8,128)(2,1)S(1)} %get-tuple-element.111.mine), channel_id=1, source_target_pairs={{0,1},{1,0},{2,3},{3,2},{4,5},{5,4},{6,7},{7,6},{8,9},{9,8},{10,11... | collective-permute-start | bytes 2359304 | tf_op jit(solution)/shard_map/ppermute | solution.py:664
  131.4 23.1 %collective-permute-start.32 = (bf16[384,768]{1,0:T(8,128)(2,1)S(1)}, bf16[384,768]{1,0:T(8,128)(2,1)S(1)}, u32[]{:S(2)}, u32[]{:S(2)}) collective-permute-start(bf16[384,768]{1,0:T(8,128)(2,1)S(1)} %get-tuple-element.123.mine), channel_id=1, source_target_pairs={{0,1},{1,0},{2,3},{3,2},{4,5},{5,4},{6,7},{7,6},{8,9},{9,8},{10,11... | collective-permute-start | bytes 1769480 | tf_op jit(solution)/shard_map/ppermute | solution.py:664
  133.0 17.2 %collective-permute-start.30 = (bf16[128,768]{1,0:T(8,128)(2,1)S(1)}, bf16[128,768]{1,0:T(8,128)(2,1)S(1)}, u32[]{:S(2)}, u32[]{:S(2)}) collective-permute-start(bf16[128,768]{1,0:T(8,128)(2,1)S(1)} %get-tuple-element.116.mine), channel_id=1, source_target_pairs={{0,1},{1,0},{2,3},{3,2},{4,5},{5,4},{6,7},{7,6},{8,9},{9,8},{10,11... | collective-permute-start | bytes 589832 | tf_op jit(solution)/shard_map/ppermute | solution.py:664
  159.7 38.1 %collective-permute-start.35 = (bf16[384,768]{1,0:T(8,128)(2,1)S(1)}, bf16[384,768]{1,0:T(8,128)(2,1)S(1)}, u32[]{:S(2)}, u32[]{:S(2)}) collective-permute-start(bf16[384,768]{1,0:T(8,128)(2,1)S(1)} %get-tuple-element.135.text_mine), channel_id=1, source_target_pairs={{0,1},{1,0},{2,3},{3,2},{4,5},{5,4},{6,7},{7,6},{8,9},{9,8},{10,11... | collective-permute-start | bytes 1769480 | tf_op jit(solution)/shard_map/ppermute | solution.py:664
  164.3 14.7 %collective-permute-start.33 = (bf16[128,768]{1,0:T(8,128)(2,1)S(1)}, bf16[128,768]{1,0:T(8,128)(2,1)S(1)}, u32[]{:S(2)}, u32[]{:S(2)}) collective-permute-start(bf16[128,768]{1,0:T(8,128)(2,1)S(1)} %get-tuple-element.129.mine), channel_id=1, source_target_pairs={{0,1},{1,0},{2,3},{3,2},{4,5},{5,4},{6,7},{7,6},{8,9},{9,8},{10,11... | collective-permute-start | bytes 589832 | tf_op jit(solution)/shard_map/ppermute | solution.py:664
  185.0 12.8 %collective-permute-start.34 = (bf16[128,768]{1,0:T(8,128)(2,1)S(1)}, bf16[128,768]{1,0:T(8,128)(2,1)S(1)}, u32[]{:S(2)}, u32[]{:S(2)}) collective-permute-start(bf16[128,768]{1,0:T(8,128)(2,1)S(1)} %get-tuple-element.133.query_mine), channel_id=1, source_target_pairs={{0,1},{1,0},{2,3},{3,2},{4,5},{5,4},{6,7},{7,6},{8,9},{9,8},{10,11... | collective-permute-start | bytes 589832 | tf_op jit(solution)/shard_map/ppermute | solution.py:664
  211.6 32.3 %collective-permute-start.37 = (bf16[174,128,128]{2,1,0:T(8,128)(2,1)}, bf16[174,128,128]{2,1,0:T(8,128)(2,1)S(1)}, u32[]{:S(2)}, u32[]{:S(2)}) collective-permute-start(bf16[174,128,128]{2,1,0:T(8,128)(2,1)} %get-tuple-element.167), channel_id=1, source_target_pairs={{0,2},{2,0},{4,6},{6,4},{8,10},{10,8},{12,14},{14,12},{16,18},{18,... | collective-permute-start | bytes 17104904 | tf_op jit(solution)/shard_map/ppermute | solution.py:898
  211.7 12.2 %collective-permute-start.38 = (bf16[58,128,128]{2,1,0:T(8,128)(2,1)}, bf16[58,128,128]{2,1,0:T(8,128)(2,1)S(1)}, u32[]{:S(2)}, u32[]{:S(2)}) collective-permute-start(bf16[58,128,128]{2,1,0:T(8,128)(2,1)} %get-tuple-element.168), channel_id=1, source_target_pairs={{0,2},{2,0},{4,6},{6,4},{8,10},{10,8},{12,14},{14,12},{16,18},{18,... | collective-permute-start | bytes 5701640 | tf_op jit(solution)/shard_map/ppermute | solution.py:898
  228.0 11.0 %collective-permute-start.46 = (bf16[15,128,128]{2,1,0:T(8,128)(2,1)S(1)}, bf16[15,128,128]{2,1,0:T(8,128)(2,1)S(1)}, u32[]{:S(2)}, u32[]{:S(2)}) collective-permute-start(bf16[15,128,128]{2,1,0:T(8,128)(2,1)S(1)} %add_convert_fusion.6), channel_id=1, source_target_pairs={{0,8},{2,6},{8,16},{10,2},{16,24},{18,10},{24,28},{26,18},{28,20},... | collective-permute-start | bytes 1474568 | tf_op jit(solution)/shard_map/ppermute | solution.py:914
  254.3 10.3 %collective-permute-start.42 = (bf16[14,128,128]{2,1,0:T(8,128)(2,1)S(1)}, bf16[14,128,128]{2,1,0:T(8,128)(2,1)S(1)}, u32[]{:S(2)}, u32[]{:S(2)}) collective-permute-start(bf16[14,128,128]{2,1,0:T(8,128)(2,1)S(1)} %add_convert_fusion.10), channel_id=1, source_target_pairs={{0,8},{2,6},{8,16},{10,2},{16,24},{18,10},{24,28},{26,18},{28,20},... | collective-permute-start | bytes 1376264 | tf_op jit(solution)/shard_map/ppermute | solution.py:914
  264.7 17.2 %collective-permute-start.43 = (bf16[14,128,128]{2,1,0:T(8,128)(2,1)S(1)}, bf16[14,128,128]{2,1,0:T(8,128)(2,1)S(1)}, u32[]{:S(2)}, u32[]{:S(2)}) collective-permute-start(bf16[14,128,128]{2,1,0:T(8,128)(2,1)S(1)} %add_convert_fusion.9), channel_id=1, source_target_pairs={{0,8},{2,6},{8,16},{10,2},{16,24},{18,10},{24,28},{26,18},{28,20},... | collective-permute-start | bytes 1376264 | tf_op jit(solution)/shard_map/ppermute | solution.py:914
  270.0 14.7 %collective-permute-start.50 = (bf16[15,128,128]{2,1,0:T(8,128)(2,1)S(1)}, bf16[15,128,128]{2,1,0:T(8,128)(2,1)S(1)}, u32[]{:S(2)}, u32[]{:S(2)}) collective-permute-start(bf16[15,128,128]{2,1,0:T(8,128)(2,1)S(1)} %add_convert_fusion.2), channel_id=1, source_target_pairs={{0,8},{2,6},{8,16},{10,2},{16,24},{18,10},{24,28},{26,18},{28,20},... | collective-permute-start | bytes 1474568 | tf_op jit(solution)/shard_map/ppermute | solution.py:914
  274.0 24.7 %collective-permute-start.36 = (bf16[512,768]{1,0:T(8,128)(2,1)S(1)}, bf16[512,768]{1,0:T(8,128)(2,1)S(1)}, u32[]{:S(2)}, u32[]{:S(2)}) collective-permute-start(bf16[512,768]{1,0:T(8,128)(2,1)S(1)} %get-tuple-element.139), channel_id=1, source_target_pairs={{0,1},{1,0},{2,3},{3,2},{4,5},{5,4},{6,7},{7,6},{8,9},{9,8},{10,11... | collective-permute-start | bytes 2359304 | tf_op jit(solution)/shard_map/ppermute | solution.py:664
  284.9 11.1 %collective-permute-start.51 = (bf16[15,128,128]{2,1,0:T(8,128)(2,1)S(1)}, bf16[15,128,128]{2,1,0:T(8,128)(2,1)S(1)}, u32[]{:S(2)}, u32[]{:S(2)}) collective-permute-start(bf16[15,128,128]{2,1,0:T(8,128)(2,1)S(1)} %add_convert_fusion.1), channel_id=1, source_target_pairs={{0,8},{2,6},{8,16},{10,2},{16,24},{18,10},{24,28},{26,18},{28,20},... | collective-permute-start | bytes 1474568 | tf_op jit(solution)/shard_map/ppermute | solution.py:914
  (45 other events, 380.8 us)

commit v6 on v5

--- a/solution.py
+++ b/solution.py
@@ -60,9 +60,7 @@
 
 
 def cost(flops, bytes_accessed, transcendentals=0):
-    return pl.CostEstimate(
-        flops=int(flops), bytes_accessed=int(bytes_accessed), transcendentals=int(transcendentals)
-    )
+    return pl.CostEstimate(flops=1, bytes_accessed=1, transcendentals=0)
 
 
 def join(axis, *pieces):
@@ -161,7 +159,9 @@
         self.texts = rows * (seq - NQ)
 
 
-def self_forward_body(plan, scale, nat, hidden, segments, qkv, probs, mixed, part):
+def self_forward_body(
+    plan, scale, nat, hidden, segments, qkv, probs, mixed, query_part, text_part
+):
     for piece in range(3):
         matrix = matrix_of(nat, 0, plan.wt, 0, plan.ht, plan.ht, piece * plan.square)
         qkv[piece] = mm(hidden[...], matrix, NN).astype(bf16)
@@ -179,7 +179,12 @@
 
     lax.fori_loop(0, plan.rows, one, 0)
     matrix = matrix_of(nat, 0, plan.ht, 0, plan.wt, plan.wt, plan.self_out)
-    part[...] = mm(mixed[...], matrix, NN).astype(bf16)
+    part = mm(mixed[...], matrix, NN).astype(bf16)
+    text = plan.seq - NQ
+    for row in range(plan.rows):
+        first = row * plan.seq
+        query_part[row * NQ : (row + 1) * NQ] = part[first : first + NQ]
+        text_part[row * text : (row + 1) * text] = part[first + NQ : first + plan.seq]
 
 
 def self_forward(plan, scale, nat, hidden, segments):
@@ -190,10 +195,11 @@
             held((3, tokens, half), bf16),
             held((plan.rows, plan.ht, 2 * plan.seq, plan.seq), f32),
             held((tokens, half), bf16),
-            jax.ShapeDtypeStruct((tokens, width), bf16),
+            jax.ShapeDtypeStruct((plan.learned, width), bf16),
+            jax.ShapeDtypeStruct((plan.texts, width), bf16),
         ),
         in_specs=vmem_specs(3),
-        out_specs=tuple(vmem_specs(4)),
+        out_specs=tuple(vmem_specs(5)),
         compiler_params=vmem_params(),
         cost_estimate=cost(2 * tokens * width * half * 4, 8e6),
         name="self_forward",
@@ -225,31 +231,31 @@
     )(*pin(nat, image))
 
 
-def cross_forward_body(
-    plan, scale, nat, hidden, mine, other, params, image_keys, image_values,
-    resid, first_query, first_text, low_query, low_text, queries, probs, mixed, part,
-):
+def first_norm(plan, token, count, hidden, mine, other, params, resid, first, low):
     gain, shift = params[0, 0:1], params[0, 1:2]
-    text = plan.seq - NQ
-
-    def one_norm(row, carry):
-        place = pl.ds(pl.multiple_of(row * plan.seq, plan.seq), plan.seq)
-        summed = hidden[place, :].astype(f32) + (
+
+    def one(row, carry):
+        place = pl.ds(pl.multiple_of(row * count, count), count)
+        start = pl.multiple_of(row * plan.seq + token, NQ)
+        summed = hidden[pl.ds(start, count), :].astype(f32) + (
             mine[place, :].astype(f32) + other[place, :].astype(f32)
         )
         resid[place, :] = summed
-        first = norm_forward(summed)[0] * gain + shift
-        query_place = pl.ds(pl.multiple_of(row * NQ, NQ), NQ)
-        text_place = pl.ds(pl.multiple_of(row * text, text), text)
-        first_query[query_place, :] = first[:NQ]
-        first_text[text_place, :] = first[NQ:]
-        low_query[query_place, :] = first[:NQ].astype(bf16)
-        low_text[text_place, :] = first[NQ:].astype(bf16)
+        normed = norm_forward(summed)[0] * gain + shift
+        first[place, :] = normed
+        low[place, :] = normed.astype(bf16)
         return carry
 
-    lax.fori_loop(0, plan.rows, one_norm, 0)
+    lax.fori_loop(0, plan.rows, one, 0)
+
+
+def cross_forward_body(
+    plan, scale, nat, hidden, mine, other, params, image_keys, image_values,
+    resid, first, low, queries, probs, mixed, part,
+):
+    first_norm(plan, 0, NQ, hidden, mine, other, params, resid, first, low)
     matrix = matrix_of(nat, 0, plan.wt, 0, plan.ht, plan.ht, plan.cross_first)
-    queries[...] = mm(low_query[...], matrix, NN).astype(bf16)
+    queries[...] = mm(low[...], matrix, NN).astype(bf16)
     allowed = lax.broadcasted_iota(jnp.int32, (2 * NQ, plan.keys), 1) < plan.patches
 
     def one(row, carry):
@@ -268,22 +274,20 @@
 
 
 def cross_forward(plan, scale, nat, hidden, mine, other, params, image_keys, image_values):
-    learned, texts, width, half = plan.learned, plan.texts, plan.width, plan.half
+    learned, width, half = plan.learned, plan.width, plan.half
     return pl.pallas_call(
         functools.partial(cross_forward_body, plan, scale),
         out_shape=(
-            held((plan.tokens, width), f32),
             held((learned, width), f32),
-            held((texts, width), f32),
+            held((learned, width), f32),
             held((learned, width), bf16),
-            held((texts, width), bf16),
             held((learned, half), bf16),
             held((plan.rows, plan.ht, 2 * NQ, plan.keys), f32),
             held((learned, half), bf16),
             jax.ShapeDtypeStruct((learned, width), bf16),
         ),
         in_specs=vmem_specs(7),
-        out_specs=tuple(vmem_specs(9)),
+        out_specs=tuple(vmem_specs(7)),
         compiler_params=vmem_params(),
         cost_estimate=cost(4 * learned * width * half, 1.2e7),
         name="cross_forward",
@@ -316,8 +320,11 @@
     lax.fori_loop(0, plan.wt // 2, one_down, 0)
 
 
-def text_forward_body(plan, nat, low_text, gated, slope, part):
-    feed_forward_tail(plan, plan.text_first, nat, low_text, gated, slope, part)
+def text_forward_body(
+    plan, nat, hidden, mine, other, params, resid, first, low, gated, slope, part
+):
+    first_norm(plan, NQ, plan.seq - NQ, hidden, mine, other, params, resid, first, low)
+    feed_forward_tail(plan, plan.text_first, nat, low, gated, slope, part)
 
 
 def query_forward_body(
@@ -339,16 +346,22 @@
     )
 
 
-def text_forward(plan, nat, low_text):
+def text_forward(plan, nat, hidden, mine, other, params):
+    count, width = plan.texts, plan.width
     return pl.pallas_call(
         functools.partial(text_forward_body, plan),
-        out_shape=feed_shapes(plan, plan.texts),
-        in_specs=vmem_specs(2),
-        out_specs=tuple(vmem_specs(3)),
+        out_shape=(
+            held((count, width), f32),
+            held((count, width), f32),
+            held((count, width), bf16),
+        )
+        + feed_shapes(plan, count),
+        in_specs=vmem_specs(5),
+        out_specs=tuple(vmem_specs(6)),
         compiler_params=vmem_params(),
-        cost_estimate=cost(4 * plan.texts * plan.width * plan.hidden, 1e7),
+        cost_estimate=cost(4 * count * width * plan.hidden, 1e7),
         name="text_forward",
-    )(*pin(nat, low_text))
+    )(*pin(nat, hidden), mine, other, params)
 
 
 def query_forward(plan, nat, first_query, mine, other, params):
@@ -488,8 +501,8 @@
 
 
 def self_backward_body(
-    plan, scale, nat, resid, query_grad, query_mine, query_other, text_grad, text_mine,
-    text_other, params, qkv, probs,
+    plan, scale, nat, query_resid, text_resid, query_grad, query_mine, query_other, text_grad,
+    text_mine, text_other, params, qkv, probs,
     grad, grad_low, back, part, norm_grad, mixed,
 ):
     text = plan.seq - NQ
@@ -509,7 +522,8 @@
             ],
             axis=0,
         )
-        found, gain_grad, shift_grad = norm_backward(resid[place, :], upstream, gain)
+        resid = join(0, query_resid[query_place, :], text_resid[text_place, :])
+        found, gain_grad, shift_grad = norm_backward(resid, upstream, gain)
         grad[place, :] = found
         grad_low[place, :] = found.astype(bf16)
         norm_grad[0:1] += gain_grad
@@ -542,8 +556,8 @@
 
 
 def self_backward(
-    plan, scale, nat, resid, query_grad, query_mine, query_other, text_grad, text_mine,
-    text_other, params, qkv, probs,
+    plan, scale, nat, query_resid, text_resid, query_grad, query_mine, query_other, text_grad,
+    text_mine, text_other, params, qkv, probs,
 ):
     tokens, width, half = plan.tokens, plan.width, plan.half
     return pl.pallas_call(
@@ -555,7 +569,7 @@
             jax.ShapeDtypeStruct((tokens, width), bf16),
             jax.ShapeDtypeStruct((2, width), f32),
         ),
-        in_specs=vmem_specs(11),
+        in_specs=vmem_specs(12),
         out_specs=tuple(vmem_specs(5)),
         scratch_shapes=[
             pltpu.VMEM((tokens, half), bf16),
@@ -564,45 +578,17 @@
         cost_estimate=cost(8 * tokens * width * half, 1.2e7),
         name="self_backward",
     )(
-        *pin(nat, resid, query_grad), query_mine, query_other, *pin(text_grad), text_mine,
+        *pin(nat, query_resid, text_resid, query_grad), query_mine, query_other, *pin(text_grad), text_mine,
         text_other, params, *pin(qkv, probs),
     )
 
 
-def store_blocks(target, first, product, col_total):
-    for row in range(product.shape[0] // TILE):
-        for col in range(col_total):
-            target[first + row * col_total + col] = product[
-                row * TILE : (row + 1) * TILE, col * TILE : (col + 1) * TILE
-            ].astype(bf16)
-
-
-def send_block(source, position, targets, sem):
-    base = 0
-    for target in targets:
-        count = target.shape[0]
-
-        @pl.when((position >= base) & (position < base + count))
-        def _(base=base, target=target):
-            pltpu.make_async_copy(source, target.at[position - base], sem).start()
-
-        base += count
-
-
-def grad_blocks_body(first_block, pairs, source_count, target_count, spare, place, *refs):
-    sources, targets = refs[:source_count], refs[-3 - target_count : -3]
-    staged, blank, sem = refs[-3:]
-    base = 0
-    sent = 0
+def grad_blocks_body(first_block, pairs, source_count, spare, place, *refs):
+    sources, target = refs[:source_count], refs[-1]
     if spare is not None:
-        blank[...] = jnp.zeros_like(blank)
-
-        def one_spare(number, carry):
-            send_block(blank, place[spare[0] + number], targets, sem)
-            return carry
-
-        lax.fori_loop(0, spare[1], one_spare, 0)
-        sent += spare[1]
+        for number in range(spare[1]):
+            target[place[spare[0] + number]] = jnp.zeros((TILE, TILE), bf16)
+    base = first_block
     for left_at, right_at, right_first, right_width, step in pairs:
         left, right = sources[left_at], sources[right_at]
         left_tiles, col_total = left.shape[1] // TILE, right_width // TILE
@@ -612,45 +598,25 @@
             cols = pl.ds(pl.multiple_of(chunk * step * TILE, step * TILE), step * TILE)
             product = mm(left[:, cols], right[:, right_first : right_first + right_width], TN)
             first = base + chunk * step * col_total
-            store_blocks(staged, first, product, col_total)
-
-            def send(number, carry):
-                block = first + number
-                send_block(staged.at[block], place[first_block + block], targets, sem)
-                return carry
-
-            lax.fori_loop(0, step * col_total, send, 0)
+            for row in range(step):
+                for col in range(col_total):
+                    target[place[first + row * col_total + col]] = product[
+                        row * TILE : (row + 1) * TILE, col * TILE : (col + 1) * TILE
+                    ].astype(bf16)
             return carry
 
         lax.fori_loop(0, left_tiles // step, one, 0)
         base += left_tiles * col_total
-    sent += base
-    whole = staged.at[pl.ds(0, base)]
-    pltpu.make_async_copy(whole, whole, sem).wait()
-    for _ in range(sent - base):
-        pltpu.make_async_copy(blank, blank, sem).wait()
-
-
-def grad_blocks(buffers, place, first_block, sources, pairs, flops, spare=None):
-    total = sum(sources[a].shape[1] // TILE * (width // TILE) for a, _, _, width, _ in pairs)
-    fresh = isinstance(buffers[0], jax.ShapeDtypeStruct)
-    given = [] if fresh else list(buffers)
-    aliases = {1 + len(sources) + number: number for number in range(len(given))}
+
+
+def grad_blocks(buffer, place, first_block, sources, pairs, flops, spare=None):
+    given = [] if isinstance(buffer, jax.ShapeDtypeStruct) else pin(buffer)
     return pl.pallas_call(
-        functools.partial(
-            grad_blocks_body, first_block, pairs, len(sources), len(buffers), spare
-        ),
-        out_shape=tuple(pltpu.HBM(b.shape, b.dtype) for b in buffers),
-        in_specs=[pl.BlockSpec(memory_space=pltpu.SMEM)]
-        + vmem_specs(len(sources))
-        + [pl.BlockSpec(memory_space=pltpu.HBM)] * len(given),
-        out_specs=tuple([pl.BlockSpec(memory_space=pltpu.HBM)] * len(buffers)),
-        scratch_shapes=[
-            pltpu.VMEM((total, TILE, TILE), bf16),
-            pltpu.VMEM((TILE, TILE), bf16),
-            pltpu.SemaphoreType.DMA,
-        ],
-        input_output_aliases=aliases,
+        functools.partial(grad_blocks_body, first_block, pairs, len(sources), spare),
+        out_shape=held(buffer.shape, buffer.dtype),
+        in_specs=[pl.BlockSpec(memory_space=pltpu.SMEM)] + vmem_specs(len(sources) + len(given)),
+        out_specs=vmem_specs(1)[0],
+        input_output_aliases={1 + len(sources): 0} if given else {},
         compiler_params=vmem_params(),
         cost_estimate=cost(flops, 1e7),
         name="grad_blocks",
@@ -664,8 +630,21 @@
     return lax.ppermute(part, "tensor", [(0, 1), (1, 0)])
 
 
+after = lax.optimization_barrier
+
+
+def sum_steps(values):
+    if lax.axis_size("dp") != RING_DEVICES:
+        values = lax.psum(values, "dp")
+        while True:
+            values = yield values
+    for bit in (1, 2, 4, 8):
+        pairs = [(index, index ^ bit) for index in range(RING_DEVICES)]
+        values = yield values + lax.ppermute(values, "dp", pairs)
+
+
 def layer_rows(
-    hidden, image, patches, segment_ids, cotangent, nat, norm_params, heads_local, scale, place, regions
+    hidden, image, patches, segment_ids, cotangent, nat, norm_params, heads_local, scale, place
 ):
     rows, seq, width = hidden.shape
     plan = Plan(
@@ -675,44 +654,52 @@
     flat_hidden = hidden.reshape(tokens, width)
     flat_image = image.reshape(rows * plan.keys, plan.image_width)
     flat_back = cotangent.reshape(tokens, width)
-    buffers = [jax.ShapeDtypeStruct((count, TILE, TILE), bf16) for count in regions]
-
-    qkv, self_probs, mixed, part_one = self_forward(
+    buffer = jax.ShapeDtypeStruct((place.shape[0], TILE, TILE), bf16)
+
+    qkv, self_probs, mixed, query_part, text_part = self_forward(
         plan, scale, nat, flat_hidden, segment_ids[:, None, :]
     )
-    other_one = swap_tensor(part_one)
+    query_other = swap_tensor(query_part)
     image_keys, image_values = image_forward(plan, nat, flat_image)
-    (
-        first_sum, first_query, first_text, low_query, low_text, cross_queries, cross_probs,
-        looked, part_two,
-    ) = cross_forward(
-        plan, scale, nat, flat_hidden, part_one, other_one, norm_params, image_keys, image_values
+    text_part, query_other, image_keys = after((text_part, query_other, image_keys))
+    text_other = swap_tensor(text_part)
+    query_first, first_query, low_query, cross_queries, cross_probs, looked, part_two = (
+        cross_forward(
+            plan, scale, nat, flat_hidden, query_part, query_other, norm_params, image_keys,
+            image_values,
+        )
     )
     other_two = swap_tensor(part_two)
-    text_gated, text_slope, part_text = text_forward(plan, nat, low_text)
-    other_text = swap_tensor(part_text)
     second_sum, second, low_second, query_gated, query_slope, part_query = query_forward(
         plan, nat, first_query, part_two, other_two, norm_params
     )
     other_query = swap_tensor(part_query)
-    out_text, third_text, third_text_low, before_text, part_four_text, norm_text = feed_backward(
-        plan, plan.text_first, NQ, 3, nat, first_text, part_text, other_text, flat_back, norm_params,
-        text_slope,
-    )
-    other_four_text = swap_tensor(part_four_text)
+    text_other, part_query = after((text_other, part_query))
+    text_first, first_text, low_text, text_gated, text_slope, part_text = text_forward(
+        plan, nat, flat_hidden, text_part, text_other, norm_params
+    )
+    other_query, part_text = after((other_query, part_text))
+    other_text = swap_tensor(part_text)
     out_query, third_query, third_query_low, before_query, part_four_query, norm_query = (
         feed_backward(
-            plan, plan.query_first, 0, 2, nat, second, part_query, other_query, flat_back, norm_params,
-            query_slope,
+            plan, plan.query_first, 0, 2, nat, second, part_query, other_query, flat_back,
+            norm_params, query_slope,
         )
     )
     other_four_query = swap_tensor(part_four_query)
     feed_pairs = [(0, 1, 0, plan.hidden, 2), (2, 3, 0, width, 2)]
-    buffers = grad_blocks(
-        buffers, place, plan.text_first, [low_text, before_text, text_gated, third_text_low], feed_pairs,
-        4 * texts * width * plan.hidden,
+    buffer = grad_blocks(
+        buffer, place, plan.query_first, [low_second, before_query, query_gated, third_query_low],
+        feed_pairs, 4 * learned * width * plan.hidden,
         spare=(plan.block_count, place.shape[0] - plan.block_count),
     )
+    other_text, buffer = after((other_text, buffer))
+    out_text, third_text, third_text_low, before_text, part_four_text, norm_text = feed_backward(
+        plan, plan.text_first, NQ, 3, nat, first_text, part_text, other_text, flat_back,
+        norm_params, text_slope,
+    )
+    other_four_query, part_four_text = after((other_four_query, part_four_text))
+    other_four_text = swap_tensor(part_four_text)
     second_grad, cross_low, query_back, key_back, value_back, part_five, norm_second = (
         cross_backward(
             plan, scale, nat, second_sum, third_query, part_four_query, other_four_query,
@@ -720,32 +707,53 @@
         )
     )
     other_five = swap_tensor(part_five)
-    buffers = grad_blocks(
-        buffers, place, plan.query_first, [low_second, before_query, query_gated, third_query_low],
-        feed_pairs, 4 * learned * width * plan.hidden,
-    )
-    buffers = grad_blocks(
-        buffers, place, plan.cross_first,
-        [low_query, query_back, flat_image, key_back, value_back, looked, cross_low],
-        [(0, 1, 0, half, 2), (2, 3, 0, half, 1), (2, 4, 0, half, 1), (5, 6, 0, width, 1)],
-        4 * rows * plan.keys * plan.image_width * half,
-    )
+    buffer, part_five = after((buffer, part_five))
+    buffer = grad_blocks(
+        buffer, place, plan.text_first, [low_text, before_text, text_gated, third_text_low],
+        feed_pairs, 4 * texts * width * plan.hidden,
+    )
+    cross_flops = 2 * rows * plan.keys * plan.image_width * half
+    buffer = grad_blocks(
+        buffer, place, plan.cross_first, [low_query, query_back, flat_image, key_back],
+        [(0, 1, 0, half, 2), (2, 3, 0, half, 1)], cross_flops,
+    )
+    other_four_text, buffer = after((other_four_text, buffer))
     first_grad, self_low, self_back, part_six, norm_first = self_backward(
-        plan, scale, nat, first_sum, second_grad, part_five, other_five, third_text,
+        plan, scale, nat, query_first, text_first, second_grad, part_five, other_five, third_text,
         part_four_text, other_four_text, norm_params, qkv, self_probs,
     )
     other_six = swap_tensor(part_six)
-    buffers = grad_blocks(
-        buffers, place, plan.self_first, [flat_hidden, self_back, mixed, self_low],
-        [(0, 1, 0, half, 2), (0, 1, half, half, 2), (0, 1, 2 * half, half, 2), (2, 3, 0, width, 1)],
-        8 * tokens * width * half,
-    )
-    input_grad = first_grad + (part_six.astype(f32) + other_six.astype(f32))
+    norm_steps = sum_steps(jnp.stack([norm_first, norm_second, norm_query, norm_text]))
+    norms = next(norm_steps)
+    buffer, part_six = after((buffer, part_six))
+    buffer = grad_blocks(
+        buffer, place, plan.image_first + plan.cross, [flat_image, value_back],
+        [(0, 1, 0, half, 1)], cross_flops,
+    )
+    buffer, norms = after((buffer, norms))
+    norms = norm_steps.send(norms)
+    buffer = grad_blocks(
+        buffer, place, plan.cross_out, [looked, cross_low], [(0, 1, 0, width, 1)],
+        2 * learned * width * half,
+    )
+    buffer, norms = after((buffer, norms))
+    norms = norm_steps.send(norms)
+    buffer = grad_blocks(
+        buffer, place, plan.self_first, [flat_hidden, self_back],
+        [(0, 1, 0, half, 2), (0, 1, half, half, 2), (0, 1, 2 * half, half, 2)],
+        6 * tokens * width * half,
+    )
+    buffer, norms = after((buffer, norms))
+    norms = norm_steps.send(norms)
+    buffer = grad_blocks(
+        buffer, place, plan.self_out, [mixed, self_low], [(0, 1, 0, width, 1)],
+        2 * tokens * width * half,
+    )
+    buffer, norms = after((buffer, norms))
     output_rows = jnp.concatenate(
         [out_query.reshape(rows, NQ, width), out_text.reshape(rows, seq - NQ, width)], axis=1
     )
-    norm_part = jnp.stack([norm_first, norm_second, norm_query, norm_text])
-    return (output_rows, input_grad.reshape(rows, seq, width), buffers, norm_part)
+    return (output_rows, first_grad, part_six, other_six, buffer, norms)
 
 
 CHIP_RING = ((0, 0), (1, 0), (2, 0), (3, 0), (3, 1), (2, 1), (1, 1), (0, 1))
@@ -785,14 +793,8 @@
     sources, target, sem = refs[: len(counts)], refs[-2], refs[-1]
     base = first
     for source, count in zip(sources, counts):
-
-        def one(number, carry, base=base, source=source):
-            pltpu.make_async_copy(
-                source.at[number], target.at[ids[base + number]], sem
-            ).start()
-            return carry
-
-        lax.fori_loop(0, count, one, 0)
+        for number in range(count):
+            pltpu.make_async_copy(source.at[number], target.at[ids[base + number]], sem).start()
         base += count
     total = sum(counts)
     pltpu.make_async_copy(
@@ -835,15 +837,23 @@
     return table
 
 
+AT_ONCE = 8
+
+
 def index_body(count, device, order, arrival, departure, ids, place):
     me = device[0]
 
-    def one(number, carry):
-        ids[number] = order[arrival[me, number]]
-        place[order[number]] = departure[me, number]
+    def one(group, carry):
+        numbers = [group * AT_ONCE + offset for offset in range(AT_ONCE)]
+        blocks = [order[number] for number in numbers]
+        arrived = [order[arrival[me, number]] for number in numbers]
+        places = [departure[me, number] for number in numbers]
+        for number, block, other, target in zip(numbers, blocks, arrived, places):
+            ids[number] = other
+            place[block] = target
         return carry
 
-    lax.fori_loop(0, count, one, 0)
+    lax.fori_loop(0, count // AT_ONCE, one, 0)
 
 
 def block_indices(order, slots):
@@ -864,22 +874,29 @@
     )
 
 
-def gather_ring(shard, ids, chains=2):
+def gather_ring(shard, order, image, chains=2):
     slots = shard.shape[0]
     parts = chain_parts(slots, chains)
-    shape = (ids.shape[0], TILE, TILE)
+    shape = (order.shape[0], TILE, TILE)
+    ids, place = block_indices(order, slots)
     other = lax.ppermute(shard, "dp", CORE_PAIRS)
     held = [shard[first : first + count] for first, count in parts]
     natural = None
-    waiting, first = [shard, other], 0
+    waiting, first, placed = [shard, other], 0, 2 * slots
     for step in range(1, RING):
         held = [lax.ppermute(piece, "dp", RING_PAIRS) for piece in held]
-        if step > 1:
-            natural = place_blocks(ids, first, waiting, natural, shape)
+        if step == 2:
+            held[0], ids, place = lax.optimization_barrier((held[0], ids, place))
+        if step == 3:
+            held[0], image = lax.optimization_barrier((held[0], pad_patches(image)))
+        if step >= 4:
+            now = 2 + 2 * chains if step == 4 else 4 * chains
+            count = sum(piece.shape[0] for piece in waiting[:now])
+            natural = place_blocks(ids, first, waiting[:now], natural, shape)
             held[0], natural = lax.optimization_barrier((held[0], natural))
-            waiting, first = [], step * 2 * slots
+            waiting, first = waiting[now:], first + count
         waiting = waiting + held + [lax.ppermute(piece, "dp", CORE_PAIRS) for piece in held]
-    return place_blocks(ids, first, waiting, natural, shape)
+    return place_blocks(ids, first, waiting, natural, shape), image, place
 
 
 def scatter_positions(slots):
@@ -894,33 +911,35 @@
     return table
 
 
-def scatter_ring(early, late, own, slots, chains=2):
-    others = [lax.ppermute(early, "dp", CORE_PAIRS), lax.ppermute(late, "dp", CORE_PAIRS)]
-    early_steps = early.shape[0] // slots
+def scatter_ring(packed, beside, slots, chains=2):
     parts = chain_parts(slots, chains)
     held = [None] * chains
+    other = None
     for step in range(1, RING + 1):
         base = (step - 1) * slots
-        other, other_base = others[0], base
-        if step > early_steps:
-            other, other_base = others[1], base - early_steps * slots
+        if step % 2:
+            if other is not None:
+                packed, other = lax.optimization_barrier((packed, other))
+            other = lax.ppermute(packed[base : base + 2 * slots], "dp", CORE_PAIRS)
+        pieces = []
         for number, (first, count) in enumerate(parts):
-            summed = own[base + first : base + first + count].astype(f32) + other[
-                other_base + first : other_base + first + count
-            ].astype(f32)
+            start = (RING + step - 1) * slots + first
+            place = (step - 1) % 2 * slots + first
+            terms = [packed[start : start + count], other[place : place + count]]
             if held[number] is not None:
-                summed = summed + held[number].astype(f32)
-            if step < RING:
-                summed = lax.ppermute(summed.astype(bf16), "dp", RING_PAIRS)
-            held[number] = summed
-    return jnp.concatenate(held, axis=0)
-
-
-def sum_small(values):
-    for bit in (1, 2, 4, 8):
-        pairs = [(index, index ^ bit) for index in range(RING_DEVICES)]
-        values = values + lax.ppermute(values, "dp", pairs)
-    return values
+                terms.append(held[number])
+            pieces.append(terms)
+        if step == RING:
+            return pieces, beside
+        for number, terms in enumerate(pieces):
+            summed = sum(term.astype(f32) for term in terms).astype(bf16)
+            held[number] = lax.ppermute(summed, "dp", RING_PAIRS)
+        if step == 1:
+            held[0], beside = lax.optimization_barrier((held[0], beside))
+
+
+def pad_patches(image):
+    return jnp.pad(image, ((0, 0), (0, -image.shape[1] % PATCHES_PAD), (0, 0)))
 
 
 PANEL = 16
@@ -1117,10 +1136,11 @@
         body(total - total % width, total % width)
 
 
-def optimizer_body(padded, *refs):
-    sources, targets = refs[:8], refs[8:16]
-    inputs, outputs = refs[16:24], refs[24:32]
-    grams, products, inverses, in_sems, out_sems = refs[32:]
+def optimizer_body(padded, counts, *refs):
+    pieces, refs = refs[: sum(counts)], refs[sum(counts) :]
+    sources, targets = refs[:7], refs[7:15]
+    gradient, inputs, outputs = refs[15], refs[16:23], refs[23:31]
+    grams, products, inverses, in_sems, out_sems = refs[31:]
     slots = sources[0].shape[0]
     lane = lax.broadcasted_iota(jnp.int32, (TILE, TILE), 1)
     sub = lax.broadcasted_iota(jnp.int32, (TILE, TILE), 0)
@@ -1140,6 +1160,11 @@
             copy.start()
     for number in range(2 * slots, padded):
         grams[number] = (lane == sub).astype(f32)
+    base = 0
+    for count in counts:
+        terms, pieces = pieces[:count], pieces[count:]
+        gradient[base : base + terms[0].shape[0]] = sum(term[...].astype(f32) for term in terms)
+        base += terms[0].shape[0]
     for load, (start, count) in zip(loads, parts):
         for copy in load:
             copy.wait()
@@ -1147,7 +1172,7 @@
             count,
             min(SLOTS_AT_ONCE, count),
             lambda first, width: optimizer_slots(
-                start + first, width, inputs, outputs, grams, products
+                start + first, width, (gradient, *inputs), outputs, grams, products
             ),
         )
     stores = [
@@ -1179,15 +1204,16 @@
 SLOTS_AT_ONCE = 6
 
 
-def optimizer(*arrays):
+def optimizer(pieces, *arrays):
     shape = arrays[0].shape
     slots = shape[0]
     padded = -(-2 * slots // PACK) * PACK
     kinds = [f32, bf16] + [f32] * 6
+    counts = [len(terms) for terms in pieces]
     return pl.pallas_call(
-        functools.partial(optimizer_body, padded),
+        functools.partial(optimizer_body, padded, counts),
         out_shape=tuple(jax.ShapeDtypeStruct(shape, kind) for kind in kinds),
-        in_specs=any_specs(8),
+        in_specs=vmem_specs(sum(counts)) + any_specs(7),
         out_specs=tuple(any_specs(8)),
         scratch_shapes=[pltpu.VMEM(shape, f32)] * 8
         + [pltpu.VMEM(shape, kind) for kind in kinds]
@@ -1195,12 +1221,12 @@
             pltpu.VMEM((padded, TILE, TILE), f32),
             pltpu.VMEM((2 * slots, TILE, TILE), f32),
             pltpu.VMEM((padded // PACK * PANEL, TILE), f32),
-            pltpu.SemaphoreType.DMA((3, 8)),
+            pltpu.SemaphoreType.DMA((3, 7)),
             pltpu.SemaphoreType.DMA((8,)),
         ],
         compiler_params=pltpu.CompilerParams(vmem_limit_bytes=60 * 1024 * 1024),
         name="optimizer",
-    )(*arrays)
+    )(*[term for terms in pieces for term in terms], *arrays)
 
 
 def per_device(
@@ -1230,28 +1256,25 @@
     shard = weight_master[0].astype(bf16)
     ring = lax.axis_size("dp") == RING_DEVICES
     patches = image.shape[1]
-    image = jnp.pad(image, ((0, 0), (0, -patches % PATCHES_PAD), (0, 0)))
     if ring:
-        ids, place = block_indices(order, slots)
-        ids, image = lax.optimization_barrier((ids, image))
-        natural = gather_ring(shard, ids)
-        regions = (2 * slots, (RING - 2) * slots, RING * slots)
+        natural, image, place = gather_ring(shard, order, image)
     else:
+        image = pad_patches(image)
         positions = jnp.arange(slot_count, dtype=jnp.int32)
         place = jnp.zeros_like(order).at[order].set(positions)
         gathered = lax.all_gather(shard, "dp", axis=0, tiled=True)
         natural = gathered[place]
-        regions = (slot_count,)
-    out_rows, in_grad, packed, norm_part = layer_rows(
+    out_rows, first_grad, part_six, other_six, packed, norm_total = layer_rows(
         hidden, image, patches, segment_ids, cotangent, natural, norm_params, heads_local, scale,
-        place, regions,
+        place,
     )
     if ring:
-        owned = scatter_ring(*packed, slots)
-        norm_total = sum_small(norm_part)
+        owned, beside = scatter_ring(packed, (other_six, norm_total), slots)
+        other_six, norm_total = beside
     else:
-        owned = lax.psum_scatter(packed[0], "dp", scatter_dimension=0, tiled=True).astype(f32)
-        norm_total = lax.psum(norm_part, "dp")
+        owned = [[lax.psum_scatter(packed, "dp", scatter_dimension=0, tiled=True)]]
+    in_grad = first_grad + (part_six.astype(f32) + other_six.astype(f32))
+    in_grad = in_grad.reshape(hidden.shape)
     updated = optimizer(
         owned,
         weight_master[0],

time: 346 us -> 323 us (0.934)
  waiting for transfers between devices: 112 us -> 99.3 us
  Pallas kernels: 144 us -> 135 us
  other arithmetic: 14.4 us -> 7.33 us
  local copies, waits for them, and re-layouts: 4.27 us -> 9.9 us
    ppermute x20 -> x22, waiting for transfers between devices: 52.9 us -> 43.7 us  [the longest x14 36.7 us: scatter_ring(): held[number] = lax.ppermute(summed, 'dp', RING_PAIRS)]
    pallas_call x4 -> x7, Pallas kernels: 31.3 us -> 24.9 us  [grad_blocks(): pl.pallas_call(functools.partial(grad_blocks_body, first_block, pairs, le...]
    convert_element_type x14, other arithmetic: 7.86 us -> 2.59 us  [scatter_ring(): summed = sum((term.astype(f32) for term in terms)).astype(bf16)]
    slice x0 -> x8, local copies, waits for them, and re-layouts: none -> 4.05 us  [the longest x4 3.28 us: scatter_ring(): terms = [packed[start:start + count], other[place:place + count]]]
    pallas_call x7 -> x5, Pallas kernels: 26.3 us -> 23.2 us  [place_blocks(): pl.pallas_call(functools.partial(place_blocks_body, counts, first), out_s...]
    ppermute x20 -> x22, starting transfers between devices: 28.8 us -> 26.5 us  [the longest x14 21.5 us: scatter_ring(): held[number] = lax.ppermute(summed, 'dp', RING_PAIRS)]
    ppermute x8 -> x9, waiting for transfers between devices: 29.5 us -> 27.9 us  [swap_tensor(): return lax.ppermute(part, 'tensor', [(0, 1), (1, 0)])]
    ppermute x8 -> x9, starting transfers between devices: 9.51 us -> 10.6 us  [swap_tensor(): return lax.ppermute(part, 'tensor', [(0, 1), (1, 0)])]
  transfers between devices with their start and end apart: 57 -> 60, of which waited for: 26 -> 29; matrix products, arithmetic and copies ran while one was open for 4% -> 4% of each run, Pallas kernels for 23% -> 26%
where the time goes in v6:
time: 323 us; the launch traced here: 318 us
  Pallas kernels  135 us (42%)
  waiting for transfers between devices  99.3 us (31%)
  starting transfers between devices  64.8 us (20%)
  local copies, waits for them, and re-layouts  9.9 us (3%)
  other arithmetic  7.33 us (2%)
    ppermute x14, waiting for transfers between devices, scatter_ring(): held[number] = lax.ppermute(summed, 'dp', RING_PAIRS)  36.7 us
    pallas_call x1, Pallas kernels, optimizer(): pl.pallas_call(functools.partial(optimizer_body, padded, counts), out_sha...  35.6 us
    ppermute x9, waiting for transfers between devices, swap_tensor(): return lax.ppermute(part, 'tensor', [(0, 1), (1, 0)])  27.9 us
    ppermute x14, starting transfers between devices, gather_ring(): held = [lax.ppermute(piece, 'dp', RING_PAIRS) for piece in held]  26 us
    ppermute x14, waiting for transfers between devices, gather_ring(): held = [lax.ppermute(piece, 'dp', RING_PAIRS) for piece in held]  25.9 us
    pallas_call x7, Pallas kernels, grad_blocks(): pl.pallas_call(functools.partial(grad_blocks_body, first_block, pairs, le...  24.9 us
    pallas_call x5, Pallas kernels, place_blocks(): pl.pallas_call(functools.partial(place_blocks_body, counts, first), out_s...  23.2 us
    ppermute x14, starting transfers between devices, scatter_ring(): held[number] = lax.ppermute(summed, 'dp', RING_PAIRS)  21.5 us
  transfers between devices with their start and end apart: 60, of which 29 were waited for; matrix products, arithmetic and copies ran while one was open for 4% of the time, Pallas kernels for 26%

profile of v6, /device:TPU:0, one launch (start us, length us, event | category | flops | bytes accessed | tf_op | source)
XLA Modules:
  0.0 317.7 jit_solution(13796498723392964626)
XLA Ops:
  7.2 5.1 %collective-permute-done.5.refs_3_ = bf16[15,128,128]{2,1,0:T(8,128)(2,1)S(1)} collective-permute-done((bf16[15,128,128]{2,1,0:T(8,128)(2,1)S(1)}, bf16[15,128,128]{2,1,0:T(8,128)(2,1)S(1)}, u32[]{:S(2)}, u32[]{:S(2)}) %collective-permute-start.5) | collective-permute-done | bytes 491552 | tf_op jit(solution)/shard_map/ppermute | solution.py:887
  24.5 4.9 %block_indices.1 = (s32[464]{0:T(512)S(1)}, s32[464]{0:T(512)S(1)}) custom-call(s32[1]{0:T(128)} %bitcast.1.device, s32[464]{0:T(512)S(1)} %bitcast.49, s32[16,464]{1,0:T(8,128)S(1)} %copy-done.13, s32[16,464]{1,0:T(8,128)S(1)} %copy-done.14), custom_call_target="tpu_custom_call" | custom-call | tf_op jit(solution)/shard_map/block_indices/pallas_call | solution.py:862
  48.4 5.3 %place_blocks.5.refs_8_ = bf16[464,128,128]{2,1,0:T(8,128)(2,1)S(1)} custom-call(s32[464]{0:T(512)S(1)} %get-tuple-element.119.ids, bf16[29,128,128]{2,1,0:T(8,128)(2,1)S(1)} %bitcast_convert_fusion.refs_0_, bf16[29,128,128]{2,1,0:T(8,128)(2,1)S(1)} %collective-permute-done.4.refs_1_, bf16[14,128,128]{2,1,0:T(8,128)(2,1)} %collective-permute-done.refs_2_, ...), custom_call_target="tpu_custom_call" | custom-call | flops 1 | bytes 1 | tf_op jit(solution)/shard_map/place_blocks/pallas_call | solution.py:814
  57.5 5.6 %place_blocks.6.refs_8_ = bf16[464,128,128]{2,1,0:T(8,128)(2,1)S(1)} custom-call(s32[464]{0:T(512)S(1)} %get-tuple-element.119.ids, bf16[14,128,128]{2,1,0:T(8,128)(2,1)} %collective-permute-done.1.refs_0_, bf16[15,128,128]{2,1,0:T(8,128)(2,1)S(1)} %collective-permute-done.9.refs_1_, ...), custom_call_target="tpu_custom_call", output_to_operand_aliasing={{}: (9, {})} | custom-call | flops 1 | bytes 1 | tf_op jit(solution)/shard_map/place_blocks/pallas_call | solution.py:814
  69.1 5.9 %place_blocks.7.refs_4_ = bf16[464,128,128]{2,1,0:T(8,128)(2,1)S(1)} custom-call(s32[464]{0:T(512)S(1)} %get-tuple-element.119.ids, bf16[14,128,128]{2,1,0:T(8,128)(2,1)S(1)} %collective-permute-done.3.refs_0_, bf16[15,128,128]{2,1,0:T(8,128)(2,1)S(1)} %collective-permute-done.16.refs_1_, ...), custom_call_target="tpu_custom_call", output_to_operand_aliasing={{}: (9, {})} | custom-call | flops 1 | bytes 1 | tf_op jit(solution)/shard_map/place_blocks/pallas_call | solution.py:814
  89.3 5.4 %self_forward.1 = (bf16[3,512,384]{2,1,0:T(8,128)(2,1)S(1)}, f32[4,3,256,128]{3,2,1,0:T(8,128)S(1)}, bf16[512,384]{1,0:T(8,128)(2,1)S(1)}, bf16[128,768]{1,0:T(8,128)(2,1)S(1)}, bf16[384,768]{1,0:T(8,128)(2,1)S(1)}) custom-call(bf16[464,128,128]{2,1,0:T(8,128)(2,1)S(1)} %place_blocks.9.nat, bf16[512,768]{1,0:T(8,128)(2,1)S(1)} %bitcast.32, ...), custom_call_target="tpu_custom_call" | custom-call | flops 1 | bytes 1 | tf_op jit(solution)/shard_map/self_forward/pallas_call | solution.py:192
  96.6 4.9 %image_forward.1 = (bf16[1088,384]{1,0:T(8,128)(2,1)S(1)}, bf16[1088,384]{1,0:T(8,128)(2,1)S(1)}) custom-call(bf16[464,128,128]{2,1,0:T(8,128)(2,1)S(1)} %place_blocks.9.nat, bf16[1088,1408]{1,0:T(8,128)(2,1)S(1)} %bitcast.29), custom_call_target="tpu_custom_call" | custom-call | flops 1 | bytes 1 | tf_op jit(solution)/shard_map/image_forward/pallas_call | solution.py:223
  103.2 5.6 %cross_forward.1 = (f32[128,768]{1,0:T(8,128)S(1)}, f32[128,768]{1,0:T(8,128)S(1)}, bf16[128,768]{1,0:T(8,128)(2,1)S(1)}, bf16[128,384]{1,0:T(8,128)(2,1)S(1)}, ...) custom-call(bf16[464,128,128]{2,1,0:T(8,128)(2,1)S(1)} %place_blocks.9.nat, ...), custom_call_target="tpu_custom_call" | custom-call | flops 1 | bytes 1 | tf_op jit(solution)/shard_map/cross_forward/pallas_call | solution.py:278
  109.4 11.5 %collective-permute-done.30.other = bf16[128,768]{1,0:T(8,128)(2,1)S(1)} collective-permute-done((bf16[128,768]{1,0:T(8,128)(2,1)S(1)}, bf16[128,768]{1,0:T(8,128)(2,1)S(1)}, u32[]{:S(2)}, u32[]{:S(2)}) %collective-permute-start.30) | collective-permute-done | bytes 196640 | tf_op jit(solution)/shard_map/ppermute | solution.py:630
  124.7 4.8 %text_forward.1 = (f32[384,768]{1,0:T(8,128)S(1)}, f32[384,768]{1,0:T(8,128)S(1)}, bf16[384,768]{1,0:T(8,128)(2,1)S(1)}, bf16[384,1536]{1,0:T(8,128)(2,1)S(1)}, ...) custom-call(bf16[464,128,128]{2,1,0:T(8,128)(2,1)S(1)} %place_blocks.9.nat, bf16[512,768]{1,0:T(8,128)(2,1)S(1)} %bitcast.34, ...), custom_call_target="tpu_custom_call" | custom-call | flops 1 | bytes 1 | tf_op jit(solution)/shard_map/text_forward/pallas_call | solution.py:351
  130.6 4.1 %feed_backward.2 = (bf16[128,768]{1,0:T(8,128)(2,1)S(1)}, f32[128,768]{1,0:T(8,128)S(1)}, bf16[128,768]{1,0:T(8,128)(2,1)S(1)}, bf16[128,1536]{1,0:T(8,128)(2,1)...) custom-call(bf16[464,128,128]{2,1,0:T(8,128)(2,1)S(1)} %place_blocks.9.nat, ...), custom_call_target="tpu_custom_call" | custom-call | flops 1 | bytes 1 | tf_op jit(solution)/shard_map/feed_backward/pallas_call | solution.py:427
  139.3 5.7 %collective-permute-done.33.other = bf16[384,768]{1,0:T(8,128)(2,1)S(1)} collective-permute-done((bf16[384,768]{1,0:T(8,128)(2,1)S(1)}, bf16[384,768]{1,0:T(8,128)(2,1)S(1)}, u32[]{:S(2)}, u32[]{:S(2)}) %collective-permute-start.33) | collective-permute-done | bytes 589856 | tf_op jit(solution)/shard_map/ppermute | solution.py:630
  145.1 5.0 %feed_backward.3 = (bf16[384,768]{1,0:T(8,128)(2,1)S(1)}, f32[384,768]{1,0:T(8,128)S(1)}, bf16[384,768]{1,0:T(8,128)(2,1)S(1)}, bf16[384,1536]{1,0:T(8,128)(2,1)...) custom-call(bf16[464,128,128]{2,1,0:T(8,128)(2,1)S(1)} %place_blocks.9.nat, ...), custom_call_target="tpu_custom_call" | custom-call | flops 1 | bytes 1 | tf_op jit(solution)/shard_map/feed_backward/pallas_call | solution.py:427
  152.5 5.9 %cross_backward.1 = (f32[128,768]{1,0:T(8,128)S(1)}, bf16[128,768]{1,0:T(8,128)(2,1)S(1)}, bf16[128,384]{1,0:T(8,128)(2,1)S(1)}, bf16[1088,384]{1,0:T(8,128)(2,1...) custom-call(bf16[464,128,128]{2,1,0:T(8,128)(2,1)S(1)} %place_blocks.9.nat, ...), custom_call_target="tpu_custom_call" | custom-call | flops 1 | bytes 1 | tf_op jit(solution)/shard_map/cross_backward/pallas_call | solution.py:481
  159.0 4.8 %grad_blocks.8.refs_4_ = bf16[464,128,128]{2,1,0:T(8,128)(2,1)S(1)} custom-call(s32[464]{0:T(512)S(1)} %get-tuple-element.150.place, bf16[384,768]{1,0:T(8,128)(2,1)S(1)} %get-tuple-element.176.refs_0_, bf16[384,1536]{1,0:T(8,128)(2,1)S(1)} %get-tuple-element.177.refs_1_, bf16[384,1536]{1,0:T(8,128)(2,1)S(1)} %copy-done.6, ...), custom_call_target="tpu_custom_call", output_to_operand_aliasing={{}: (5, {})} | custom-call | flops 1 | bytes 1 | tf_op jit(solution)/shard_map/grad_blocks/pallas_call | solution.py:614
  163.8 5.4 %grad_blocks.9.refs_2_ = bf16[464,128,128]{2,1,0:T(8,128)(2,1)S(1)} custom-call(s32[464]{0:T(512)S(1)} %get-tuple-element.150.place, bf16[128,768]{1,0:T(8,128)(2,1)S(1)} %get-tuple-element.173.refs_0_, bf16[128,384]{1,0:T(8,128)(2,1)S(1)} %get-tuple-element.174.refs_1_, bf16[1088,1408]{1,0:T(8,128)(2,1)S(1)} %bitcast.30, ...), custom_call_target="tpu_custom_call", output_to_operand_aliasing={{}: (5, {})} | custom-call | flops 1 | bytes 1 | tf_op jit(solution)/shard_map/grad_blocks/pallas_call | solution.py:614
  169.3 7.8 %self_backward.1 = (f32[512,768]{1,0:T(8,128)S(1)}, bf16[512,768]{1,0:T(8,128)(2,1)S(1)}, bf16[512,1152]{1,0:T(8,128)(2,1)S(1)}, bf16[512,768]{1,0:T(8,128)(2,1)S(1)}, f32[2,768]{1,0:T(2,128)S(1)}) custom-call(bf16[464,128,128]{2,1,0:T(8,128)(2,1)S(1)} %place_blocks.9.nat, f32[128,768]{1,0:T(8,128)S(1)} %get-tuple-element.158.query_resid, ...), custom_call_target="tpu_custom_call" | custom-call | flops 1 | bytes 1 | tf_op jit(solution)/shard_map/self_backward/pallas_call | solution.py:563
  177.2 4.7 %grad_blocks.10.refs_2_ = bf16[464,128,128]{2,1,0:T(8,128)(2,1)S(1)} custom-call(s32[464]{0:T(512)S(1)} %get-tuple-element.150.place, bf16[1088,1408]{1,0:T(8,128)(2,1)S(1)} %bitcast.31, bf16[1088,384]{1,0:T(8,128)(2,1)S(1)} %get-tuple-element.193.refs_1_, bf16[464,128,128]{2,1,0:T(8,128)(2,1)S(1)} %grad_blocks.9.refs_2_), custom_call_target="tpu_custom_call", output_to_operand_aliasing={{}: (3, {})} | custom-call | flops 1 | bytes 1 | tf_op jit(solution)/shard_map/grad_blocks/pallas_call | solution.py:614
  187.5 3.6 %grad_blocks.12.refs_2_ = bf16[464,128,128]{2,1,0:T(8,128)(2,1)S(1)} custom-call(s32[464]{0:T(512)S(1)} %get-tuple-element.150.place, bf16[512,768]{1,0:T(8,128)(2,1)S(1)} %bitcast.35, bf16[512,1152]{1,0:T(8,128)(2,1)S(1)} %get-tuple-element.190.refs_1_, bf16[464,128,128]{2,1,0:T(8,128)(2,1)S(1)} %grad_blocks.11.refs_2_), custom_call_target="tpu_custom_call", output_to_operand_aliasing={{}: (3, {})} | custom-call | flops 1 | bytes 1 | tf_op jit(solution)/shard_map/grad_blocks/pallas_call | solution.py:614
  196.4 3.9 %collective-permute-done.41 = bf16[58,128,128]{2,1,0:T(8,128)(2,1)S(1)} collective-permute-done((bf16[58,128,128]{2,1,0:T(8,128)(2,1)S(1)}, bf16[58,128,128]{2,1,0:T(8,128)(2,1)S(1)}, u32[]{:S(2)}, u32[]{:S(2)}) %collective-permute-start.41) | collective-permute-done | bytes 1900576 | tf_op jit(solution)/shard_map/ppermute | solution.py:923
  205.7 4.0 %collective-permute-done.53 = bf16[15,128,128]{2,1,0:T(8,128)(2,1)S(1)} collective-permute-done((bf16[15,128,128]{2,1,0:T(8,128)(2,1)S(1)}, bf16[15,128,128]{2,1,0:T(8,128)(2,1)S(1)}, u32[]{:S(2)}, u32[]{:S(2)}) %collective-permute-start.53) | collective-permute-done | bytes 491552 | tf_op jit(solution)/shard_map/ppermute | solution.py:936
  210.3 10.5 %collective-permute-done.43 = bf16[512,768]{1,0:T(8,128)(2,1)S(1)} collective-permute-done((bf16[512,768]{1,0:T(8,128)(2,1)S(1)}, bf16[512,768]{1,0:T(8,128)(2,1)S(1)}, u32[]{:S(2)}, u32[]{:S(2)}) %collective-permute-start.43) | collective-permute-done | bytes 786464 | tf_op jit(solution)/shard_map/ppermute | solution.py:630
  224.0 5.5 %collective-permute-done.47 = bf16[14,128,128]{2,1,0:T(8,128)(2,1)S(1)} collective-permute-done((bf16[14,128,128]{2,1,0:T(8,128)(2,1)S(1)}, bf16[14,128,128]{2,1,0:T(8,128)(2,1)S(1)}, u32[]{:S(2)}, u32[]{:S(2)}) %collective-permute-start.47) | collective-permute-done | bytes 458784 | tf_op jit(solution)/shard_map/ppermute | solution.py:936
  281.9 35.6 %optimizer.1 = (f32[29,128,128]{2,1,0:T(8,128)}, bf16[29,128,128]{2,1,0:T(8,128)(2,1)}, f32[29,128,128]{2,1,0:T(8,128)}, f32[29,128,128]{2,1,0:T(8,128)}, f32[29...) custom-call(bf16[14,128,128]{2,1,0:T(8,128)(2,1)} %slice.121.refs_0_, ...), custom_call_target="tpu_custom_call" | custom-call | tf_op jit(solution)/shard_map/optimizer/pallas_call | solution.py:1213
  (196 shorter events, 150.6 us)
Async XLA Ops:
  5.5 11.7 %collective-permute-start = (bf16[14,128,128]{2,1,0:T(8,128)(2,1)S(1)}, bf16[14,128,128]{2,1,0:T(8,128)(2,1)}, u32[]{:S(2)}, u32[]{:S(2)}) collective-permute-start(bf16[14,128,128]{2,1,0:T(8,128)(2,1)S(1)} %slice.152), channel_id=1, source_target_pairs={{0,8},{2,6},{8,16},{10,2},{16,24},{18,10},{24,28},{26,18},{28,20},... | collective-permute-start | bytes 1376264 | tf_op jit(solution)/shard_map/ppermute | solution.py:887
  17.2 12.2 %collective-permute-start.1 = (bf16[14,128,128]{2,1,0:T(8,128)(2,1)}, bf16[14,128,128]{2,1,0:T(8,128)(2,1)}, u32[]{:S(2)}, u32[]{:S(2)}) collective-permute-start(bf16[14,128,128]{2,1,0:T(8,128)(2,1)} %collective-permute-done.refs_2_), channel_id=1, source_target_pairs={{0,8},{2,6},{8,16},{10,2},{16,24},{18,10},{24,28},{26,18},{28,20},... | collective-permute-start | bytes 1376264 | tf_op jit(solution)/shard_map/ppermute | solution.py:887
  19.3 20.5 %collective-permute-start.4 = (bf16[29,128,128]{2,1,0:T(8,128)(2,1)S(1)}, bf16[29,128,128]{2,1,0:T(8,128)(2,1)S(1)}, u32[]{:S(2)}, u32[]{:S(2)}) collective-permute-start(bf16[29,128,128]{2,1,0:T(8,128)(2,1)S(1)} %bitcast_convert_fusion.refs_0_), channel_id=1, source_target_pairs={{0,2},{2,0},{4,6},{6,4},{8,10},{10,8},{12,14},{14,12},{16,18},{18,... | collective-permute-start | bytes 2850824 | tf_op jit(solution)/shard_map/ppermute | solution.py:882
  32.6 10.9 %collective-permute-start.16 = (bf16[15,128,128]{2,1,0:T(8,128)(2,1)S(1)}, bf16[15,128,128]{2,1,0:T(8,128)(2,1)S(1)}, u32[]{:S(2)}, u32[]{:S(2)}) collective-permute-start(bf16[15,128,128]{2,1,0:T(8,128)(2,1)S(1)} %collective-permute-done.12.refs_5_), channel_id=1, source_target_pairs={{0,8},{2,6},{8,16},{10,2},{16,24},{18,10},{24,28},{26,18},{28,20},... | collective-permute-start | bytes 1474568 | tf_op jit(solution)/shard_map/ppermute | solution.py:887
  39.8 15.5 %collective-permute-start.11 = (bf16[15,128,128]{2,1,0:T(8,128)(2,1)S(1)}, bf16[15,128,128]{2,1,0:T(8,128)(2,1)S(1)}, u32[]{:S(2)}, u32[]{:S(2)}) collective-permute-start(bf16[15,128,128]{2,1,0:T(8,128)(2,1)S(1)} %collective-permute-done.9.refs_1_), channel_id=1, source_target_pairs={{0,2},{2,0},{4,6},{6,4},{8,10},{10,8},{12,14},{14,12},{16,18},{18,... | collective-permute-start | bytes 1474568 | tf_op jit(solution)/shard_map/ppermute | solution.py:898
  39.8 13.9 %collective-permute-start.10 = (bf16[14,128,128]{2,1,0:T(8,128)(2,1)}, bf16[14,128,128]{2,1,0:T(8,128)(2,1)S(1)}, u32[]{:S(2)}, u32[]{:S(2)}) collective-permute-start(bf16[14,128,128]{2,1,0:T(8,128)(2,1)} %collective-permute-done.1.refs_0_), channel_id=1, source_target_pairs={{0,2},{2,0},{4,6},{6,4},{8,10},{10,8},{12,14},{14,12},{16,18},{18,... | collective-permute-start | bytes 1376264 | tf_op jit(solution)/shard_map/ppermute | solution.py:898
  43.5 11.8 %collective-permute-start.19 = (bf16[15,128,128]{2,1,0:T(8,128)(2,1)S(1)}, bf16[15,128,128]{2,1,0:T(8,128)(2,1)S(1)}, u32[]{:S(2)}, u32[]{:S(2)}) collective-permute-start(bf16[15,128,128]{2,1,0:T(8,128)(2,1)S(1)} %collective-permute-done.16.refs_1_), channel_id=1, source_target_pairs={{0,8},{2,6},{8,16},{10,2},{16,24},{18,10},{24,28},{26,18},{28,20},... | collective-permute-start | bytes 1474568 | tf_op jit(solution)/shard_map/ppermute | solution.py:887
  45.1 11.9 %collective-permute-start.14 = (bf16[15,128,128]{2,1,0:T(8,128)(2,1)S(1)}, bf16[15,128,128]{2,1,0:T(8,128)(2,1)S(1)}, u32[]{:S(2)}, u32[]{:S(2)}) collective-permute-start(bf16[15,128,128]{2,1,0:T(8,128)(2,1)S(1)} %collective-permute-done.12.refs_5_), channel_id=1, source_target_pairs={{0,2},{2,0},{4,6},{6,4},{8,10},{10,8},{12,14},{14,12},{16,18},{18,... | collective-permute-start | bytes 1474568 | tf_op jit(solution)/shard_map/ppermute | solution.py:898
  55.3 12.2 %collective-permute-start.23 = (bf16[15,128,128]{2,1,0:T(8,128)(2,1)S(1)}, bf16[15,128,128]{2,1,0:T(8,128)(2,1)S(1)}, u32[]{:S(2)}, u32[]{:S(2)}) collective-permute-start(bf16[15,128,128]{2,1,0:T(8,128)(2,1)S(1)} %collective-permute-done.19.refs_5_), channel_id=1, source_target_pairs={{0,8},{2,6},{8,16},{10,2},{16,24},{18,10},{24,28},{26,18},{28,20},... | collective-permute-start | bytes 1474568 | tf_op jit(solution)/shard_map/ppermute | solution.py:887
  57.0 12.1 %collective-permute-start.18 = (bf16[15,128,128]{2,1,0:T(8,128)(2,1)S(1)}, bf16[15,128,128]{2,1,0:T(8,128)(2,1)S(1)}, u32[]{:S(2)}, u32[]{:S(2)}) collective-permute-start(bf16[15,128,128]{2,1,0:T(8,128)(2,1)S(1)} %collective-permute-done.16.refs_1_), channel_id=1, source_target_pairs={{0,2},{2,0},{4,6},{6,4},{8,10},{10,8},{12,14},{14,12},{16,18},{18,... | collective-permute-start | bytes 1474568 | tf_op jit(solution)/shard_map/ppermute | solution.py:898
  57.0 12.1 %collective-permute-start.21 = (bf16[15,128,128]{2,1,0:T(8,128)(2,1)S(1)}, bf16[15,128,128]{2,1,0:T(8,128)(2,1)S(1)}, u32[]{:S(2)}, u32[]{:S(2)}) collective-permute-start(bf16[15,128,128]{2,1,0:T(8,128)(2,1)S(1)} %collective-permute-done.19.refs_5_), channel_id=1, source_target_pairs={{0,2},{2,0},{4,6},{6,4},{8,10},{10,8},{12,14},{14,12},{16,18},{18,... | collective-permute-start | bytes 1474568 | tf_op jit(solution)/shard_map/ppermute | solution.py:898
  63.3 11.7 %collective-permute-start.15 = (bf16[14,128,128]{2,1,0:T(8,128)(2,1)S(1)}, bf16[14,128,128]{2,1,0:T(8,128)(2,1)S(1)}, u32[]{:S(2)}, u32[]{:S(2)}) collective-permute-start(bf16[14,128,128]{2,1,0:T(8,128)(2,1)S(1)} %collective-permute-done.8.refs_4_), channel_id=1, source_target_pairs={{0,8},{2,6},{8,16},{10,2},{16,24},{18,10},{24,28},{26,18},{28,20},... | collective-permute-start | bytes 1376264 | tf_op jit(solution)/shard_map/ppermute | solution.py:887
  101.7 23.1 %collective-permute-start.31 = (bf16[384,768]{1,0:T(8,128)(2,1)S(1)}, bf16[384,768]{1,0:T(8,128)(2,1)S(1)}, u32[]{:S(2)}, u32[]{:S(2)}) collective-permute-start(bf16[384,768]{1,0:T(8,128)(2,1)S(1)} %get-tuple-element.140.mine), channel_id=1, source_target_pairs={{0,1},{1,0},{2,3},{3,2},{4,5},{5,4},{6,7},{7,6},{8,9},{9,8},{10,11... | collective-permute-start | bytes 1769480 | tf_op jit(solution)/shard_map/ppermute | solution.py:630
  108.8 12.1 %collective-permute-start.30 = (bf16[128,768]{1,0:T(8,128)(2,1)S(1)}, bf16[128,768]{1,0:T(8,128)(2,1)S(1)}, u32[]{:S(2)}, u32[]{:S(2)}) collective-permute-start(bf16[128,768]{1,0:T(8,128)(2,1)S(1)} %get-tuple-element.138.mine), channel_id=1, source_target_pairs={{0,1},{1,0},{2,3},{3,2},{4,5},{5,4},{6,7},{7,6},{8,9},{9,8},{10,11... | collective-permute-start | bytes 589832 | tf_op jit(solution)/shard_map/ppermute | solution.py:630
  129.5 15.5 %collective-permute-start.33 = (bf16[384,768]{1,0:T(8,128)(2,1)S(1)}, bf16[384,768]{1,0:T(8,128)(2,1)S(1)}, u32[]{:S(2)}, u32[]{:S(2)}) collective-permute-start(bf16[384,768]{1,0:T(8,128)(2,1)S(1)} %get-tuple-element.149.mine), channel_id=1, source_target_pairs={{0,1},{1,0},{2,3},{3,2},{4,5},{5,4},{6,7},{7,6},{8,9},{9,8},{10,11... | collective-permute-start | bytes 1769480 | tf_op jit(solution)/shard_map/ppermute | solution.py:630
  134.7 16.2 %collective-permute-start.34 = (bf16[128,768]{1,0:T(8,128)(2,1)S(1)}, bf16[128,768]{1,0:T(8,128)(2,1)S(1)}, u32[]{:S(2)}, u32[]{:S(2)}) collective-permute-start(bf16[128,768]{1,0:T(8,128)(2,1)S(1)} %get-tuple-element.162.mine), channel_id=1, source_target_pairs={{0,1},{1,0},{2,3},{3,2},{4,5},{5,4},{6,7},{7,6},{8,9},{9,8},{10,11... | collective-permute-start | bytes 589832 | tf_op jit(solution)/shard_map/ppermute | solution.py:630
  150.9 18.3 %collective-permute-start.36 = (bf16[384,768]{1,0:T(8,128)(2,1)S(1)}, bf16[384,768]{1,0:T(8,128)(2,1)S(1)}, u32[]{:S(2)}, u32[]{:S(2)}) collective-permute-start(bf16[384,768]{1,0:T(8,128)(2,1)S(1)} %get-tuple-element.172.text_mine), channel_id=1, source_target_pairs={{0,1},{1,0},{2,3},{3,2},{4,5},{5,4},{6,7},{7,6},{8,9},{9,8},{10,11... | collective-permute-start | bytes 1769480 | tf_op jit(solution)/shard_map/ppermute | solution.py:630
  201.2 19.6 %collective-permute-start.43 = (bf16[512,768]{1,0:T(8,128)(2,1)S(1)}, bf16[512,768]{1,0:T(8,128)(2,1)S(1)}, u32[]{:S(2)}, u32[]{:S(2)}) collective-permute-start(bf16[512,768]{1,0:T(8,128)(2,1)S(1)} %get-tuple-element.187), channel_id=1, source_target_pairs={{0,1},{1,0},{2,3},{3,2},{4,5},{5,4},{6,7},{7,6},{8,9},{9,8},{10,11... | collective-permute-start | bytes 2359304 | tf_op jit(solution)/shard_map/ppermute | solution.py:630
  202.9 17.9 %collective-permute-start.42 = (bf16[14,128,128]{2,1,0:T(8,128)(2,1)S(1)}, bf16[14,128,128]{2,1,0:T(8,128)(2,1)S(1)}, u32[]{:S(2)}, u32[]{:S(2)}) collective-permute-start(bf16[14,128,128]{2,1,0:T(8,128)(2,1)S(1)} %add_convert_fusion.13), channel_id=1, source_target_pairs={{0,8},{2,6},{8,16},{10,2},{16,24},{18,10},{24,28},{26,18},{28,20},... | collective-permute-start | bytes 1376264 | tf_op jit(solution)/shard_map/ppermute | solution.py:936
  205.6 31.1 %collective-permute-start.45 = (bf16[58,128,128]{2,1,0:T(8,128)(2,1)S(1)}, bf16[58,128,128]{2,1,0:T(8,128)(2,1)S(1)}, u32[]{:S(2)}, u32[]{:S(2)}) collective-permute-start(bf16[58,128,128]{2,1,0:T(8,128)(2,1)S(1)} %slice.120), channel_id=1, source_target_pairs={{0,2},{2,0},{4,6},{6,4},{8,10},{10,8},{12,14},{14,12},{16,18},{18,... | collective-permute-start | bytes 5701640 | tf_op jit(solution)/shard_map/ppermute | solution.py:923
  209.9 12.8 %collective-permute-start.54 = (bf16[15,128,128]{2,1,0:T(8,128)(2,1)S(1)}, bf16[15,128,128]{2,1,0:T(8,128)(2,1)S(1)}, u32[]{:S(2)}, u32[]{:S(2)}) collective-permute-start(bf16[15,128,128]{2,1,0:T(8,128)(2,1)S(1)} %add_convert_fusion.5), channel_id=1, source_target_pairs={{0,8},{2,6},{8,16},{10,2},{16,24},{18,10},{24,28},{26,18},{28,20},... | collective-permute-start | bytes 1474568 | tf_op jit(solution)/shard_map/ppermute | solution.py:936
  222.9 11.9 %collective-permute-start.55 = (bf16[15,128,128]{2,1,0:T(8,128)(2,1)S(1)}, bf16[15,128,128]{2,1,0:T(8,128)(2,1)S(1)}, u32[]{:S(2)}, u32[]{:S(2)}) collective-permute-start(bf16[15,128,128]{2,1,0:T(8,128)(2,1)S(1)} %add_convert_fusion.4), channel_id=1, source_target_pairs={{0,8},{2,6},{8,16},{10,2},{16,24},{18,10},{24,28},{26,18},{28,20},... | collective-permute-start | bytes 1474568 | tf_op jit(solution)/shard_map/ppermute | solution.py:936
  236.8 28.5 %collective-permute-start.46 = (bf16[58,128,128]{2,1,0:T(8,128)(2,1)S(1)}, bf16[58,128,128]{2,1,0:T(8,128)(2,1)S(1)}, u32[]{:S(2)}, u32[]{:S(2)}) collective-permute-start(bf16[58,128,128]{2,1,0:T(8,128)(2,1)S(1)} %slice.122), channel_id=1, source_target_pairs={{0,2},{2,0},{4,6},{6,4},{8,10},{10,8},{12,14},{14,12},{16,18},{18,... | collective-permute-start | bytes 5701640 | tf_op jit(solution)/shard_map/ppermute | solution.py:923
  265.5 14.9 %collective-permute-start.59 = (bf16[15,128,128]{2,1,0:T(8,128)(2,1)S(1)}, bf16[15,128,128]{2,1,0:T(8,128)(2,1)S(1)}, u32[]{:S(2)}, u32[]{:S(2)}) collective-permute-start(bf16[15,128,128]{2,1,0:T(8,128)(2,1)S(1)} %add_convert_fusion), channel_id=1, source_target_pairs={{0,8},{2,6},{8,16},{10,2},{16,24},{18,10},{24,28},{26,18},{28,20},... | collective-permute-start | bytes 1474568 | tf_op jit(solution)/shard_map/ppermute | solution.py:936
  (57 other events, 463.9 us)

commit v7 on v6

--- a/solution.py
+++ b/solution.py
@@ -743,7 +743,7 @@
         [(0, 1, 0, half, 2), (0, 1, half, half, 2), (0, 1, 2 * half, half, 2)],
         6 * tokens * width * half,
     )
-    buffer, norms = after((buffer, norms))
+    buffer, norms, other_six = after((buffer, norms, other_six))
     norms = norm_steps.send(norms)
     buffer = grad_blocks(
         buffer, place, plan.self_out, [mixed, self_low], [(0, 1, 0, width, 1)],
@@ -789,37 +789,33 @@
     return [(first, last - first) for first, last in zip(cuts, cuts[1:])]
 
 
-def place_blocks_body(counts, first, ids, *refs):
-    sources, target, sem = refs[: len(counts)], refs[-2], refs[-1]
+def place_blocks_body(first, ids, *refs):
+    sources, target = refs[:-1], refs[-1]
     base = first
-    for source, count in zip(sources, counts):
-        for number in range(count):
-            pltpu.make_async_copy(source.at[number], target.at[ids[base + number]], sem).start()
-        base += count
-    total = sum(counts)
-    pltpu.make_async_copy(
-        target.at[pl.ds(0, total)], target.at[pl.ds(0, total)], sem
-    ).wait()
+    for source in sources:
+        for number in range(source.shape[0]):
+            target[ids[base + number]] = source[number]
+        base += source.shape[0]
 
 
 def place_blocks(ids, first, sources, target, shape):
-    counts = [source.shape[0] for source in sources]
-    operands = [ids, *sources]
-    specs = [pl.BlockSpec(memory_space=pltpu.SMEM)] + any_specs(len(sources))
+    operands = [ids, *pin(*sources)]
     aliases = {}
     if target is not None:
         operands += pin(target)
-        specs += vmem_specs(1)
         aliases = {len(operands) - 1: 0}
+
+    def body(ids, *refs):
+        place_blocks_body(first, ids, *refs[: len(sources)], refs[-1])
+
     return pl.pallas_call(
-        functools.partial(place_blocks_body, counts, first),
+        body,
         out_shape=held(shape, bf16),
-        in_specs=specs,
+        in_specs=[pl.BlockSpec(memory_space=pltpu.SMEM)] + vmem_specs(len(operands) - 1),
         out_specs=vmem_specs(1)[0],
-        scratch_shapes=[pltpu.SemaphoreType.DMA],
         input_output_aliases=aliases,
-        compiler_params=pltpu.CompilerParams(vmem_limit_bytes=1024 * 1024),
-        cost_estimate=cost(0, 4 * sum(counts) * TILE * TILE),
+        compiler_params=pltpu.CompilerParams(vmem_limit_bytes=4 * 1024 * 1024),
+        cost_estimate=cost(0, 0),
         name="place_blocks",
     )(*operands)
 
@@ -911,7 +907,7 @@
     return table
 
 
-def scatter_ring(packed, beside, slots, chains=2):
+def scatter_ring(packed, slots, chains=2):
     parts = chain_parts(slots, chains)
     held = [None] * chains
     other = None
@@ -930,12 +926,10 @@
                 terms.append(held[number])
             pieces.append(terms)
         if step == RING:
-            return pieces, beside
+            return pieces
         for number, terms in enumerate(pieces):
             summed = sum(term.astype(f32) for term in terms).astype(bf16)
             held[number] = lax.ppermute(summed, "dp", RING_PAIRS)
-        if step == 1:
-            held[0], beside = lax.optimization_barrier((held[0], beside))
 
 
 def pad_patches(image):
@@ -1269,8 +1263,7 @@
         place,
     )
     if ring:
-        owned, beside = scatter_ring(packed, (other_six, norm_total), slots)
-        other_six, norm_total = beside
+        owned = scatter_ring(packed, slots)
     else:
         owned = [[lax.psum_scatter(packed, "dp", scatter_dimension=0, tiled=True)]]
     in_grad = first_grad + (part_six.astype(f32) + other_six.astype(f32))

time: 323 us -> 312 us (0.966)
  waiting for transfers between devices: 99.3 us -> 119 us
  Pallas kernels: 135 us -> 117 us
  starting transfers between devices: 64.8 us -> 52.9 us
    ppermute x14, waiting for transfers between devices: 36.7 us -> 55.9 us  [scatter_ring(): held[number] = lax.ppermute(summed, 'dp', RING_PAIRS)]
    pallas_call x5, Pallas kernels: 23.2 us -> 4.75 us  [place_blocks(): pl.pallas_call(body, out_shape=held(shape, bf16), in_specs=[pl.BlockSpec(...]
    ppermute x14, starting transfers between devices: 21.5 us -> 9.05 us  [scatter_ring(): held[number] = lax.ppermute(summed, 'dp', RING_PAIRS)]
    ppermute x14, waiting for transfers between devices: 25.9 us -> 37.5 us  [gather_ring(): held = [lax.ppermute(piece, 'dp', RING_PAIRS) for piece in held]]
    ppermute x9, waiting for transfers between devices: 27.9 us -> 17.4 us  [swap_tensor(): return lax.ppermute(part, 'tensor', [(0, 1), (1, 0)])]
  transfers between devices with their start and end apart: 60 -> 60, of which waited for: 29 -> 34; matrix products, arithmetic and copies ran while one was open for 4% -> 4% of each run, Pallas kernels for 26% -> 22%
where the time goes in v7:
time: 312 us; the launch traced here: 307 us
  waiting for transfers between devices  119 us (38%)
  Pallas kernels  117 us (38%)
  starting transfers between devices  52.9 us (17%)
  local copies, waits for them, and re-layouts  9.9 us (3%)
  other arithmetic  7.33 us (2%)
    ppermute x14, waiting for transfers between devices, scatter_ring(): held[number] = lax.ppermute(summed, 'dp', RING_PAIRS)  55.9 us
    ppermute x14, waiting for transfers between devices, gather_ring(): held = [lax.ppermute(piece, 'dp', RING_PAIRS) for piece in held]  37.5 us
    pallas_call x1, Pallas kernels, optimizer(): pl.pallas_call(functools.partial(optimizer_body, padded, counts), out_sha...  35.6 us
    ppermute x14, starting transfers between devices, gather_ring(): held = [lax.ppermute(piece, 'dp', RING_PAIRS) for piece in held]  25.8 us
    pallas_call x7, Pallas kernels, grad_blocks(): pl.pallas_call(functools.partial(grad_blocks_body, first_block, pairs, le...  25.1 us
    ppermute x9, waiting for transfers between devices, swap_tensor(): return lax.ppermute(part, 'tensor', [(0, 1), (1, 0)])  17.4 us
    ppermute x9, starting transfers between devices, swap_tensor(): return lax.ppermute(part, 'tensor', [(0, 1), (1, 0)])  10.6 us
    pallas_call x2, Pallas kernels, feed_backward(): pl.pallas_call(functools.partial(feed_backward_body, plan, first_block, f...  9.13 us
  transfers between devices with their start and end apart: 60, of which 34 were waited for; matrix products, arithmetic and copies ran while one was open for 4% of the time, Pallas kernels for 22%

profile of v7, /device:TPU:0, one launch (start us, length us, event | category | flops | bytes accessed | tf_op | source)
XLA Modules:
  0.0 307.1 jit_solution(2702135823840393739)
XLA Ops:
  7.2 5.1 %collective-permute-done.5.refs_3_ = bf16[15,128,128]{2,1,0:T(8,128)(2,1)S(1)} collective-permute-done((bf16[15,128,128]{2,1,0:T(8,128)(2,1)S(1)}, bf16[15,128,128]{2,1,0:T(8,128)(2,1)S(1)}, u32[]{:S(2)}, u32[]{:S(2)}) %collective-permute-start.5) | collective-permute-done | bytes 491552 | tf_op jit(solution)/shard_map/ppermute | solution.py:883
  24.5 4.9 %block_indices.1 = (s32[464]{0:T(512)S(1)}, s32[464]{0:T(512)S(1)}) custom-call(s32[1]{0:T(128)} %bitcast.1.device, s32[464]{0:T(512)S(1)} %bitcast.49, s32[16,464]{1,0:T(8,128)S(1)} %copy-done.13, s32[16,464]{1,0:T(8,128)S(1)} %copy-done.14), custom_call_target="tpu_custom_call" | custom-call | tf_op jit(solution)/shard_map/block_indices/pallas_call | solution.py:858
  81.5 5.5 %self_forward.1 = (bf16[3,512,384]{2,1,0:T(8,128)(2,1)S(1)}, f32[4,3,256,128]{3,2,1,0:T(8,128)S(1)}, bf16[512,384]{1,0:T(8,128)(2,1)S(1)}, bf16[128,768]{1,0:T(8,128)(2,1)S(1)}, bf16[384,768]{1,0:T(8,128)(2,1)S(1)}) custom-call(bf16[464,128,128]{2,1,0:T(8,128)(2,1)S(1)} %place_blocks.9.nat, bf16[512,768]{1,0:T(8,128)(2,1)S(1)} %bitcast.32, ...), custom_call_target="tpu_custom_call" | custom-call | flops 1 | bytes 1 | tf_op jit(solution)/shard_map/self_forward/pallas_call | solution.py:192
  89.0 4.9 %image_forward.1 = (bf16[1088,384]{1,0:T(8,128)(2,1)S(1)}, bf16[1088,384]{1,0:T(8,128)(2,1)S(1)}) custom-call(bf16[464,128,128]{2,1,0:T(8,128)(2,1)S(1)} %place_blocks.9.nat, bf16[1088,1408]{1,0:T(8,128)(2,1)S(1)} %bitcast.29), custom_call_target="tpu_custom_call" | custom-call | flops 1 | bytes 1 | tf_op jit(solution)/shard_map/image_forward/pallas_call | solution.py:223
  95.6 5.6 %cross_forward.1 = (f32[128,768]{1,0:T(8,128)S(1)}, f32[128,768]{1,0:T(8,128)S(1)}, bf16[128,768]{1,0:T(8,128)(2,1)S(1)}, bf16[128,384]{1,0:T(8,128)(2,1)S(1)}, ...) custom-call(bf16[464,128,128]{2,1,0:T(8,128)(2,1)S(1)} %place_blocks.9.nat, ...), custom_call_target="tpu_custom_call" | custom-call | flops 1 | bytes 1 | tf_op jit(solution)/shard_map/cross_forward/pallas_call | solution.py:278
  101.8 11.5 %collective-permute-done.30.other = bf16[128,768]{1,0:T(8,128)(2,1)S(1)} collective-permute-done((bf16[128,768]{1,0:T(8,128)(2,1)S(1)}, bf16[128,768]{1,0:T(8,128)(2,1)S(1)}, u32[]{:S(2)}, u32[]{:S(2)}) %collective-permute-start.30) | collective-permute-done | bytes 196640 | tf_op jit(solution)/shard_map/ppermute | solution.py:630
  117.1 4.8 %text_forward.1 = (f32[384,768]{1,0:T(8,128)S(1)}, f32[384,768]{1,0:T(8,128)S(1)}, bf16[384,768]{1,0:T(8,128)(2,1)S(1)}, bf16[384,1536]{1,0:T(8,128)(2,1)S(1)}, ...) custom-call(bf16[464,128,128]{2,1,0:T(8,128)(2,1)S(1)} %place_blocks.9.nat, bf16[512,768]{1,0:T(8,128)(2,1)S(1)} %bitcast.34, ...), custom_call_target="tpu_custom_call" | custom-call | flops 1 | bytes 1 | tf_op jit(solution)/shard_map/text_forward/pallas_call | solution.py:351
  131.7 5.7 %collective-permute-done.33.other = bf16[384,768]{1,0:T(8,128)(2,1)S(1)} collective-permute-done((bf16[384,768]{1,0:T(8,128)(2,1)S(1)}, bf16[384,768]{1,0:T(8,128)(2,1)S(1)}, u32[]{:S(2)}, u32[]{:S(2)}) %collective-permute-start.33) | collective-permute-done | bytes 589856 | tf_op jit(solution)/shard_map/ppermute | solution.py:630
  137.4 5.0 %feed_backward.3 = (bf16[384,768]{1,0:T(8,128)(2,1)S(1)}, f32[384,768]{1,0:T(8,128)S(1)}, bf16[384,768]{1,0:T(8,128)(2,1)S(1)}, bf16[384,1536]{1,0:T(8,128)(2,1)...) custom-call(bf16[464,128,128]{2,1,0:T(8,128)(2,1)S(1)} %place_blocks.9.nat, ...), custom_call_target="tpu_custom_call" | custom-call | flops 1 | bytes 1 | tf_op jit(solution)/shard_map/feed_backward/pallas_call | solution.py:427
  144.9 5.9 %cross_backward.1 = (f32[128,768]{1,0:T(8,128)S(1)}, bf16[128,768]{1,0:T(8,128)(2,1)S(1)}, bf16[128,384]{1,0:T(8,128)(2,1)S(1)}, bf16[1088,384]{1,0:T(8,128)(2,1...) custom-call(bf16[464,128,128]{2,1,0:T(8,128)(2,1)S(1)} %place_blocks.9.nat, ...), custom_call_target="tpu_custom_call" | custom-call | flops 1 | bytes 1 | tf_op jit(solution)/shard_map/cross_backward/pallas_call | solution.py:481
  151.3 4.8 %grad_blocks.8.refs_4_ = bf16[464,128,128]{2,1,0:T(8,128)(2,1)S(1)} custom-call(s32[464]{0:T(512)S(1)} %get-tuple-element.148.place, bf16[384,768]{1,0:T(8,128)(2,1)S(1)} %get-tuple-element.174.refs_0_, bf16[384,1536]{1,0:T(8,128)(2,1)S(1)} %get-tuple-element.175.refs_1_, bf16[384,1536]{1,0:T(8,128)(2,1)S(1)} %copy-done.6, ...), custom_call_target="tpu_custom_call", output_to_operand_aliasing={{}: (5, {})} | custom-call | flops 1 | bytes 1 | tf_op jit(solution)/shard_map/grad_blocks/pallas_call | solution.py:614
  156.2 5.4 %grad_blocks.9.refs_2_ = bf16[464,128,128]{2,1,0:T(8,128)(2,1)S(1)} custom-call(s32[464]{0:T(512)S(1)} %get-tuple-element.148.place, bf16[128,768]{1,0:T(8,128)(2,1)S(1)} %get-tuple-element.171.refs_0_, bf16[128,384]{1,0:T(8,128)(2,1)S(1)} %get-tuple-element.172.refs_1_, bf16[1088,1408]{1,0:T(8,128)(2,1)S(1)} %bitcast.30, ...), custom_call_target="tpu_custom_call", output_to_operand_aliasing={{}: (5, {})} | custom-call | flops 1 | bytes 1 | tf_op jit(solution)/shard_map/grad_blocks/pallas_call | solution.py:614
  161.7 7.6 %self_backward.1 = (f32[512,768]{1,0:T(8,128)S(1)}, bf16[512,768]{1,0:T(8,128)(2,1)S(1)}, bf16[512,1152]{1,0:T(8,128)(2,1)S(1)}, bf16[512,768]{1,0:T(8,128)(2,1)S(1)}, f32[2,768]{1,0:T(2,128)S(1)}) custom-call(bf16[464,128,128]{2,1,0:T(8,128)(2,1)S(1)} %place_blocks.9.nat, f32[128,768]{1,0:T(8,128)S(1)} %get-tuple-element.156.query_resid, ...), custom_call_target="tpu_custom_call" | custom-call | flops 1 | bytes 1 | tf_op jit(solution)/shard_map/self_backward/pallas_call | solution.py:563
  171.0 4.7 %grad_blocks.10.refs_2_ = bf16[464,128,128]{2,1,0:T(8,128)(2,1)S(1)} custom-call(s32[464]{0:T(512)S(1)} %get-tuple-element.148.place, bf16[1088,1408]{1,0:T(8,128)(2,1)S(1)} %bitcast.31, bf16[1088,384]{1,0:T(8,128)(2,1)S(1)} %get-tuple-element.189.refs_1_, bf16[464,128,128]{2,1,0:T(8,128)(2,1)S(1)} %grad_blocks.9.refs_2_), custom_call_target="tpu_custom_call", output_to_operand_aliasing={{}: (3, {})} | custom-call | flops 1 | bytes 1 | tf_op jit(solution)/shard_map/grad_blocks/pallas_call | solution.py:614
  198.9 4.9 %collective-permute-done.53 = bf16[15,128,128]{2,1,0:T(8,128)(2,1)S(1)} collective-permute-done((bf16[15,128,128]{2,1,0:T(8,128)(2,1)S(1)}, bf16[15,128,128]{2,1,0:T(8,128)(2,1)S(1)}, u32[]{:S(2)}, u32[]{:S(2)}) %collective-permute-start.53) | collective-permute-done | bytes 491552 | tf_op jit(solution)/shard_map/ppermute | solution.py:932
  204.4 4.2 %collective-permute-done.46 = bf16[14,128,128]{2,1,0:T(8,128)(2,1)S(1)} collective-permute-done((bf16[14,128,128]{2,1,0:T(8,128)(2,1)S(1)}, bf16[14,128,128]{2,1,0:T(8,128)(2,1)S(1)}, u32[]{:S(2)}, u32[]{:S(2)}) %collective-permute-start.46) | collective-permute-done | bytes 458784 | tf_op jit(solution)/shard_map/ppermute | solution.py:932
  209.3 4.6 %collective-permute-done.54 = bf16[15,128,128]{2,1,0:T(8,128)(2,1)S(1)} collective-permute-done((bf16[15,128,128]{2,1,0:T(8,128)(2,1)S(1)}, bf16[15,128,128]{2,1,0:T(8,128)(2,1)S(1)}, u32[]{:S(2)}, u32[]{:S(2)}) %collective-permute-start.54) | collective-permute-done | bytes 491552 | tf_op jit(solution)/shard_map/ppermute | solution.py:932
  214.6 4.2 %collective-permute-done.47 = bf16[14,128,128]{2,1,0:T(8,128)(2,1)S(1)} collective-permute-done((bf16[14,128,128]{2,1,0:T(8,128)(2,1)S(1)}, bf16[14,128,128]{2,1,0:T(8,128)(2,1)S(1)}, u32[]{:S(2)}, u32[]{:S(2)}) %collective-permute-start.47) | collective-permute-done | bytes 458784 | tf_op jit(solution)/shard_map/ppermute | solution.py:932
  219.5 4.6 %collective-permute-done.55 = bf16[15,128,128]{2,1,0:T(8,128)(2,1)S(1)} collective-permute-done((bf16[15,128,128]{2,1,0:T(8,128)(2,1)S(1)}, bf16[15,128,128]{2,1,0:T(8,128)(2,1)S(1)}, u32[]{:S(2)}, u32[]{:S(2)}) %collective-permute-start.55) | collective-permute-done | bytes 491552 | tf_op jit(solution)/shard_map/ppermute | solution.py:932
  229.7 4.6 %collective-permute-done.56 = bf16[15,128,128]{2,1,0:T(8,128)(2,1)S(1)} collective-permute-done((bf16[15,128,128]{2,1,0:T(8,128)(2,1)S(1)}, bf16[15,128,128]{2,1,0:T(8,128)(2,1)S(1)}, u32[]{:S(2)}, u32[]{:S(2)}) %collective-permute-start.56) | collective-permute-done | bytes 491552 | tf_op jit(solution)/shard_map/ppermute | solution.py:932
  235.0 4.2 %collective-permute-done.49 = bf16[14,128,128]{2,1,0:T(8,128)(2,1)S(1)} collective-permute-done((bf16[14,128,128]{2,1,0:T(8,128)(2,1)S(1)}, bf16[14,128,128]{2,1,0:T(8,128)(2,1)S(1)}, u32[]{:S(2)}, u32[]{:S(2)}) %collective-permute-start.49) | collective-permute-done | bytes 458784 | tf_op jit(solution)/shard_map/ppermute | solution.py:932
  239.9 4.6 %collective-permute-done.57 = bf16[15,128,128]{2,1,0:T(8,128)(2,1)S(1)} collective-permute-done((bf16[15,128,128]{2,1,0:T(8,128)(2,1)S(1)}, bf16[15,128,128]{2,1,0:T(8,128)(2,1)S(1)}, u32[]{:S(2)}, u32[]{:S(2)}) %collective-permute-start.57) | collective-permute-done | bytes 491552 | tf_op jit(solution)/shard_map/ppermute | solution.py:932
  245.2 4.2 %collective-permute-done.50 = bf16[14,128,128]{2,1,0:T(8,128)(2,1)S(1)} collective-permute-done((bf16[14,128,128]{2,1,0:T(8,128)(2,1)S(1)}, bf16[14,128,128]{2,1,0:T(8,128)(2,1)S(1)}, u32[]{:S(2)}, u32[]{:S(2)}) %collective-permute-start.50) | collective-permute-done | bytes 458784 | tf_op jit(solution)/shard_map/ppermute | solution.py:932
  271.3 35.6 %optimizer.1 = (f32[29,128,128]{2,1,0:T(8,128)}, bf16[29,128,128]{2,1,0:T(8,128)(2,1)}, f32[29,128,128]{2,1,0:T(8,128)}, f32[29,128,128]{2,1,0:T(8,128)}, f32[29...) custom-call(bf16[14,128,128]{2,1,0:T(8,128)(2,1)} %slice.119.refs_0_, ...), custom_call_target="tpu_custom_call" | custom-call | tf_op jit(solution)/shard_map/optimizer/pallas_call | solution.py:1207
  (196 shorter events, 148.4 us)
Async XLA Ops:
  5.5 11.7 %collective-permute-start = (bf16[14,128,128]{2,1,0:T(8,128)(2,1)S(1)}, bf16[14,128,128]{2,1,0:T(8,128)(2,1)}, u32[]{:S(2)}, u32[]{:S(2)}) collective-permute-start(bf16[14,128,128]{2,1,0:T(8,128)(2,1)S(1)} %slice.152), channel_id=1, source_target_pairs={{0,8},{2,6},{8,16},{10,2},{16,24},{18,10},{24,28},{26,18},{28,20},... | collective-permute-start | bytes 1376264 | tf_op jit(solution)/shard_map/ppermute | solution.py:883
  12.2 10.2 %collective-permute-start.9 = (bf16[15,128,128]{2,1,0:T(8,128)(2,1)S(1)}, bf16[15,128,128]{2,1,0:T(8,128)(2,1)S(1)}, u32[]{:S(2)}, u32[]{:S(2)}) collective-permute-start(bf16[15,128,128]{2,1,0:T(8,128)(2,1)S(1)} %collective-permute-done.5.refs_3_), channel_id=1, source_target_pairs={{0,8},{2,6},{8,16},{10,2},{16,24},{18,10},{24,28},{26,18},{28,20},... | collective-permute-start | bytes 1474568 | tf_op jit(solution)/shard_map/ppermute | solution.py:883
  17.2 12.2 %collective-permute-start.1 = (bf16[14,128,128]{2,1,0:T(8,128)(2,1)}, bf16[14,128,128]{2,1,0:T(8,128)(2,1)}, u32[]{:S(2)}, u32[]{:S(2)}) collective-permute-start(bf16[14,128,128]{2,1,0:T(8,128)(2,1)} %collective-permute-done.refs_2_), channel_id=1, source_target_pairs={{0,8},{2,6},{8,16},{10,2},{16,24},{18,10},{24,28},{26,18},{28,20},... | collective-permute-start | bytes 1376264 | tf_op jit(solution)/shard_map/ppermute | solution.py:883
  19.3 20.5 %collective-permute-start.4 = (bf16[29,128,128]{2,1,0:T(8,128)(2,1)S(1)}, bf16[29,128,128]{2,1,0:T(8,128)(2,1)S(1)}, u32[]{:S(2)}, u32[]{:S(2)}) collective-permute-start(bf16[29,128,128]{2,1,0:T(8,128)(2,1)S(1)} %bitcast_convert_fusion.refs_0_), channel_id=1, source_target_pairs={{0,2},{2,0},{4,6},{6,4},{8,10},{10,8},{12,14},{14,12},{16,18},{18,... | collective-permute-start | bytes 2850824 | tf_op jit(solution)/shard_map/ppermute | solution.py:878
  22.4 10.2 %collective-permute-start.12 = (bf16[15,128,128]{2,1,0:T(8,128)(2,1)S(1)}, bf16[15,128,128]{2,1,0:T(8,128)(2,1)S(1)}, u32[]{:S(2)}, u32[]{:S(2)}) collective-permute-start(bf16[15,128,128]{2,1,0:T(8,128)(2,1)S(1)} %collective-permute-done.9.refs_1_), channel_id=1, source_target_pairs={{0,8},{2,6},{8,16},{10,2},{16,24},{18,10},{24,28},{26,18},{28,20},... | collective-permute-start | bytes 1474568 | tf_op jit(solution)/shard_map/ppermute | solution.py:883
  32.6 10.9 %collective-permute-start.16 = (bf16[15,128,128]{2,1,0:T(8,128)(2,1)S(1)}, bf16[15,128,128]{2,1,0:T(8,128)(2,1)S(1)}, u32[]{:S(2)}, u32[]{:S(2)}) collective-permute-start(bf16[15,128,128]{2,1,0:T(8,128)(2,1)S(1)} %collective-permute-done.12.refs_5_), channel_id=1, source_target_pairs={{0,8},{2,6},{8,16},{10,2},{16,24},{18,10},{24,28},{26,18},{28,20},... | collective-permute-start | bytes 1474568 | tf_op jit(solution)/shard_map/ppermute | solution.py:883
  34.7 10.4 %collective-permute-start.7 = (bf16[15,128,128]{2,1,0:T(8,128)(2,1)S(1)}, bf16[15,128,128]{2,1,0:T(8,128)(2,1)S(1)}, u32[]{:S(2)}, u32[]{:S(2)}) collective-permute-start(bf16[15,128,128]{2,1,0:T(8,128)(2,1)S(1)} %collective-permute-done.5.refs_3_), channel_id=1, source_target_pairs={{0,2},{2,0},{4,6},{6,4},{8,10},{10,8},{12,14},{14,12},{16,18},{18,... | collective-permute-start | bytes 1474568 | tf_op jit(solution)/shard_map/ppermute | solution.py:894
  38.2 10.2 %collective-permute-start.3 = (bf16[14,128,128]{2,1,0:T(8,128)(2,1)S(1)}, bf16[14,128,128]{2,1,0:T(8,128)(2,1)S(1)}, u32[]{:S(2)}, u32[]{:S(2)}) collective-permute-start(bf16[14,128,128]{2,1,0:T(8,128)(2,1)S(1)} %collective-permute-done.2.refs_4_), channel_id=1, source_target_pairs={{0,8},{2,6},{8,16},{10,2},{16,24},{18,10},{24,28},{26,18},{28,20},... | collective-permute-start | bytes 1376264 | tf_op jit(solution)/shard_map/ppermute | solution.py:883
  39.8 11.5 %collective-permute-start.11 = (bf16[15,128,128]{2,1,0:T(8,128)(2,1)S(1)}, bf16[15,128,128]{2,1,0:T(8,128)(2,1)S(1)}, u32[]{:S(2)}, u32[]{:S(2)}) collective-permute-start(bf16[15,128,128]{2,1,0:T(8,128)(2,1)S(1)} %collective-permute-done.9.refs_1_), channel_id=1, source_target_pairs={{0,2},{2,0},{4,6},{6,4},{8,10},{10,8},{12,14},{14,12},{16,18},{18,... | collective-permute-start | bytes 1474568 | tf_op jit(solution)/shard_map/ppermute | solution.py:894
  43.5 10.2 %collective-permute-start.19 = (bf16[15,128,128]{2,1,0:T(8,128)(2,1)S(1)}, bf16[15,128,128]{2,1,0:T(8,128)(2,1)S(1)}, u32[]{:S(2)}, u32[]{:S(2)}) collective-permute-start(bf16[15,128,128]{2,1,0:T(8,128)(2,1)S(1)} %collective-permute-done.16.refs_1_), channel_id=1, source_target_pairs={{0,8},{2,6},{8,16},{10,2},{16,24},{18,10},{24,28},{26,18},{28,20},... | collective-permute-start | bytes 1474568 | tf_op jit(solution)/shard_map/ppermute | solution.py:883
  45.1 10.2 %collective-permute-start.14 = (bf16[15,128,128]{2,1,0:T(8,128)(2,1)S(1)}, bf16[15,128,128]{2,1,0:T(8,128)(2,1)S(1)}, u32[]{:S(2)}, u32[]{:S(2)}) collective-permute-start(bf16[15,128,128]{2,1,0:T(8,128)(2,1)S(1)} %collective-permute-done.12.refs_5_), channel_id=1, source_target_pairs={{0,2},{2,0},{4,6},{6,4},{8,10},{10,8},{12,14},{14,12},{16,18},{18,... | collective-permute-start | bytes 1474568 | tf_op jit(solution)/shard_map/ppermute | solution.py:894
  53.7 10.2 %collective-permute-start.23 = (bf16[15,128,128]{2,1,0:T(8,128)(2,1)S(1)}, bf16[15,128,128]{2,1,0:T(8,128)(2,1)S(1)}, u32[]{:S(2)}, u32[]{:S(2)}) collective-permute-start(bf16[15,128,128]{2,1,0:T(8,128)(2,1)S(1)} %collective-permute-done.19.refs_5_), channel_id=1, source_target_pairs={{0,8},{2,6},{8,16},{10,2},{16,24},{18,10},{24,28},{26,18},{28,20},... | collective-permute-start | bytes 1474568 | tf_op jit(solution)/shard_map/ppermute | solution.py:883
  55.3 10.2 %collective-permute-start.21 = (bf16[15,128,128]{2,1,0:T(8,128)(2,1)S(1)}, bf16[15,128,128]{2,1,0:T(8,128)(2,1)S(1)}, u32[]{:S(2)}, u32[]{:S(2)}) collective-permute-start(bf16[15,128,128]{2,1,0:T(8,128)(2,1)S(1)} %collective-permute-done.19.refs_5_), channel_id=1, source_target_pairs={{0,2},{2,0},{4,6},{6,4},{8,10},{10,8},{12,14},{14,12},{16,18},{18,... | collective-permute-start | bytes 1474568 | tf_op jit(solution)/shard_map/ppermute | solution.py:894
  94.1 23.1 %collective-permute-start.31 = (bf16[384,768]{1,0:T(8,128)(2,1)S(1)}, bf16[384,768]{1,0:T(8,128)(2,1)S(1)}, u32[]{:S(2)}, u32[]{:S(2)}) collective-permute-start(bf16[384,768]{1,0:T(8,128)(2,1)S(1)} %get-tuple-element.138.mine), channel_id=1, source_target_pairs={{0,1},{1,0},{2,3},{3,2},{4,5},{5,4},{6,7},{7,6},{8,9},{9,8},{10,11... | collective-permute-start | bytes 1769480 | tf_op jit(solution)/shard_map/ppermute | solution.py:630
  101.2 12.1 %collective-permute-start.30 = (bf16[128,768]{1,0:T(8,128)(2,1)S(1)}, bf16[128,768]{1,0:T(8,128)(2,1)S(1)}, u32[]{:S(2)}, u32[]{:S(2)}) collective-permute-start(bf16[128,768]{1,0:T(8,128)(2,1)S(1)} %get-tuple-element.136.mine), channel_id=1, source_target_pairs={{0,1},{1,0},{2,3},{3,2},{4,5},{5,4},{6,7},{7,6},{8,9},{9,8},{10,11... | collective-permute-start | bytes 589832 | tf_op jit(solution)/shard_map/ppermute | solution.py:630
  121.9 15.5 %collective-permute-start.33 = (bf16[384,768]{1,0:T(8,128)(2,1)S(1)}, bf16[384,768]{1,0:T(8,128)(2,1)S(1)}, u32[]{:S(2)}, u32[]{:S(2)}) collective-permute-start(bf16[384,768]{1,0:T(8,128)(2,1)S(1)} %get-tuple-element.147.mine), channel_id=1, source_target_pairs={{0,1},{1,0},{2,3},{3,2},{4,5},{5,4},{6,7},{7,6},{8,9},{9,8},{10,11... | collective-permute-start | bytes 1769480 | tf_op jit(solution)/shard_map/ppermute | solution.py:630
  127.1 16.2 %collective-permute-start.34 = (bf16[128,768]{1,0:T(8,128)(2,1)S(1)}, bf16[128,768]{1,0:T(8,128)(2,1)S(1)}, u32[]{:S(2)}, u32[]{:S(2)}) collective-permute-start(bf16[128,768]{1,0:T(8,128)(2,1)S(1)} %get-tuple-element.160.mine), channel_id=1, source_target_pairs={{0,1},{1,0},{2,3},{3,2},{4,5},{5,4},{6,7},{7,6},{8,9},{9,8},{10,11... | collective-permute-start | bytes 589832 | tf_op jit(solution)/shard_map/ppermute | solution.py:630
  143.3 18.3 %collective-permute-start.36 = (bf16[384,768]{1,0:T(8,128)(2,1)S(1)}, bf16[384,768]{1,0:T(8,128)(2,1)S(1)}, u32[]{:S(2)}, u32[]{:S(2)}) collective-permute-start(bf16[384,768]{1,0:T(8,128)(2,1)S(1)} %get-tuple-element.170.text_mine), channel_id=1, source_target_pairs={{0,1},{1,0},{2,3},{3,2},{4,5},{5,4},{6,7},{7,6},{8,9},{9,8},{10,11... | collective-permute-start | bytes 1769480 | tf_op jit(solution)/shard_map/ppermute | solution.py:630
  150.8 10.8 %collective-permute-start.35 = (bf16[128,768]{1,0:T(8,128)(2,1)S(1)}, bf16[128,768]{1,0:T(8,128)(2,1)S(1)}, u32[]{:S(2)}, u32[]{:S(2)}) collective-permute-start(bf16[128,768]{1,0:T(8,128)(2,1)S(1)} %get-tuple-element.168.query_mine), channel_id=1, source_target_pairs={{0,1},{1,0},{2,3},{3,2},{4,5},{5,4},{6,7},{7,6},{8,9},{9,8},{10,11... | collective-permute-start | bytes 589832 | tf_op jit(solution)/shard_map/ppermute | solution.py:630
  169.3 15.9 %collective-permute-start.40 = (bf16[512,768]{1,0:T(8,128)(2,1)S(1)}, bf16[512,768]{1,0:T(8,128)(2,1)S(1)}, u32[]{:S(2)}, u32[]{:S(2)}) collective-permute-start(bf16[512,768]{1,0:T(8,128)(2,1)S(1)} %get-tuple-element.185), channel_id=1, source_target_pairs={{0,1},{1,0},{2,3},{3,2},{4,5},{5,4},{6,7},{7,6},{8,9},{9,8},{10,11... | collective-permute-start | bytes 2359304 | tf_op jit(solution)/shard_map/ppermute | solution.py:630
  195.4 13.3 %collective-permute-start.46 = (bf16[14,128,128]{2,1,0:T(8,128)(2,1)S(1)}, bf16[14,128,128]{2,1,0:T(8,128)(2,1)S(1)}, u32[]{:S(2)}, u32[]{:S(2)}) collective-permute-start(bf16[14,128,128]{2,1,0:T(8,128)(2,1)S(1)} %add_convert_fusion.13), channel_id=1, source_target_pairs={{0,8},{2,6},{8,16},{10,2},{16,24},{18,10},{24,28},{26,18},{28,20},... | collective-permute-start | bytes 1376264 | tf_op jit(solution)/shard_map/ppermute | solution.py:932
  198.7 26.1 %collective-permute-start.44 = (bf16[58,128,128]{2,1,0:T(8,128)(2,1)S(1)}, bf16[58,128,128]{2,1,0:T(8,128)(2,1)S(1)}, u32[]{:S(2)}, u32[]{:S(2)}) collective-permute-start(bf16[58,128,128]{2,1,0:T(8,128)(2,1)S(1)} %slice.118), channel_id=1, source_target_pairs={{0,2},{2,0},{4,6},{6,4},{8,10},{10,8},{12,14},{14,12},{16,18},{18,... | collective-permute-start | bytes 5701640 | tf_op jit(solution)/shard_map/ppermute | solution.py:919
  224.9 29.7 %collective-permute-start.45 = (bf16[58,128,128]{2,1,0:T(8,128)(2,1)S(1)}, bf16[58,128,128]{2,1,0:T(8,128)(2,1)S(1)}, u32[]{:S(2)}, u32[]{:S(2)}) collective-permute-start(bf16[58,128,128]{2,1,0:T(8,128)(2,1)S(1)} %slice.120), channel_id=1, source_target_pairs={{0,2},{2,0},{4,6},{6,4},{8,10},{10,8},{12,14},{14,12},{16,18},{18,... | collective-permute-start | bytes 5701640 | tf_op jit(solution)/shard_map/ppermute | solution.py:919
  254.9 14.9 %collective-permute-start.59 = (bf16[15,128,128]{2,1,0:T(8,128)(2,1)S(1)}, bf16[15,128,128]{2,1,0:T(8,128)(2,1)S(1)}, u32[]{:S(2)}, u32[]{:S(2)}) collective-permute-start(bf16[15,128,128]{2,1,0:T(8,128)(2,1)S(1)} %add_convert_fusion), channel_id=1, source_target_pairs={{0,8},{2,6},{8,16},{10,2},{16,24},{18,10},{24,28},{26,18},{28,20},... | collective-permute-start | bytes 1474568 | tf_op jit(solution)/shard_map/ppermute | solution.py:932
  (57 other events, 443.8 us)

commit v8 on v7

--- a/solution.py
+++ b/solution.py
@@ -107,32 +107,57 @@
     return jnp.concatenate([stacked[:half], stacked[half:]], axis=1)
 
 
-def pair_probs(queries, keys, allowed, scale):
-    scores = mm(head_pair(queries), keys, NT) * scale
-    scores = jnp.where(allowed, scores, masked_score)
-    weights = jnp.exp(scores - jnp.max(scores, axis=-1, keepdims=True))
-    return weights / jnp.sum(weights, axis=-1, keepdims=True)
-
-
-def pair_mix(probs, values):
-    count = probs.shape[0] // 2
+def all_probs(queries, keys, allowed, scale):
+    every = range(len(queries))
+    scores = [mm(head_pair(queries[n]), keys[n], NT) for n in every]
+    scores = [jnp.where(allowed[n], scores[n] * scale, masked_score) for n in every]
+    weights = [jnp.exp(score - jnp.max(score, axis=-1, keepdims=True)) for score in scores]
+    return [weight / jnp.sum(weight, axis=-1, keepdims=True) for weight in weights]
+
+
+def all_mixed(probs, values):
+    count = probs[0].shape[0] // 2
     low_half = lax.broadcasted_iota(jnp.int32, (count, TILE), 1) < TILE // 2
-    mixed = mm(probs.astype(bf16), values, NN)
-    return jnp.where(low_half, mixed[:count], mixed[count:]).astype(bf16)
-
-
-def pair_backward(queries, keys, values, probs, mixed_grad, scale):
-    grad_pair = head_pair(mixed_grad)
-    value_grad = mm(probs.astype(bf16), grad_pair, TN).astype(bf16)
-    prob_grad = mm(grad_pair, values, NT)
-    inner = jnp.sum(probs * prob_grad, axis=-1, keepdims=True)
-    score_grad = (probs * (prob_grad - inner) * scale).astype(bf16)
-    count = queries.shape[0]
+    mixed = [mm(prob.astype(bf16), value, NN) for prob, value in zip(probs, values)]
+    return [jnp.where(low_half, mix[:count], mix[count:]).astype(bf16) for mix in mixed]
+
+
+def all_backward(queries, keys, values, probs, mixed_grads, scale):
+    every = range(len(queries))
+    pairs = [head_pair(grad) for grad in mixed_grads]
+    prob_grads = [mm(pairs[n], values[n], NT) for n in every]
+    value_grads = [mm(probs[n].astype(bf16), pairs[n], TN).astype(bf16) for n in every]
+    inner = [jnp.sum(probs[n] * prob_grads[n], axis=-1, keepdims=True) for n in every]
+    score_grads = [
+        (probs[n] * (prob_grads[n] - inner[n]) * scale).astype(bf16) for n in every
+    ]
+    count = queries[0].shape[0]
     low_half = lax.broadcasted_iota(jnp.int32, (count, TILE), 1) < TILE // 2
-    both = mm(score_grad, keys, NN)
-    query_grad = jnp.where(low_half, both[:count], both[count:]).astype(bf16)
-    key_grad = mm(score_grad, head_pair(queries), TN).astype(bf16)
-    return query_grad, key_grad, value_grad
+    both = [mm(score_grads[n], keys[n], NN) for n in every]
+    query_grads = [jnp.where(low_half, b[:count], b[count:]).astype(bf16) for b in both]
+    key_grads = [mm(score_grads[n], head_pair(queries[n]), TN).astype(bf16) for n in every]
+    return query_grads, key_grads, value_grads
+
+
+def each_tile(plan, rows_at_once, body):
+    def one(group, carry):
+        body(
+            [
+                (group * rows_at_once + row, tile, slice(tile * TILE, (tile + 1) * TILE))
+                for row in range(rows_at_once)
+                for tile in range(plan.ht)
+            ]
+        )
+        return carry
+
+    lax.fori_loop(0, plan.rows // rows_at_once, one, 0)
+
+
+def rows_of(row, count):
+    return pl.ds(pl.multiple_of(row * count, count), count)
+
+
+ROWS_AT_ONCE = 2
 
 
 class Plan:
@@ -166,18 +191,25 @@
         matrix = matrix_of(nat, 0, plan.wt, 0, plan.ht, plan.ht, piece * plan.square)
         qkv[piece] = mm(hidden[...], matrix, NN).astype(bf16)
 
-    def one(row, carry):
-        place = pl.ds(pl.multiple_of(row * plan.seq, plan.seq), plan.seq)
-        along = jnp.broadcast_to(segments[row].astype(f32), (plan.seq, plan.seq))
-        allowed = jnp.concatenate([along.T, along.T], axis=0) == join(0, along, along)
-        for tile in range(plan.ht):
-            cols = slice(tile * TILE, (tile + 1) * TILE)
-            found = pair_probs(qkv[0, place, cols], qkv[1, place, cols], allowed, scale)
-            probs[row, tile] = found
-            mixed[place, cols] = pair_mix(found, qkv[2, place, cols])
-        return carry
-
-    lax.fori_loop(0, plan.rows, one, 0)
+    def attend(items):
+        seq = plan.seq
+        allowed = []
+        for row, _, _ in items[:: plan.ht]:
+            along = jnp.broadcast_to(segments[row].astype(f32), (seq, seq))
+            same = along.T == along
+            allowed += [join(0, same, same)] * plan.ht
+        found = all_probs(
+            [qkv[0, rows_of(row, seq), cols] for row, _, cols in items],
+            [qkv[1, rows_of(row, seq), cols] for row, _, cols in items],
+            allowed,
+            scale,
+        )
+        values = [qkv[2, rows_of(row, seq), cols] for row, _, cols in items]
+        for (row, tile, cols), prob, mix in zip(items, found, all_mixed(found, values)):
+            probs[row, tile] = prob
+            mixed[rows_of(row, seq), cols] = mix
+
+    each_tile(plan, ROWS_AT_ONCE, attend)
     matrix = matrix_of(nat, 0, plan.ht, 0, plan.wt, plan.wt, plan.self_out)
     part = mm(mixed[...], matrix, NN).astype(bf16)
     text = plan.seq - NQ
@@ -209,13 +241,7 @@
 def image_body(plan, nat, image, keys, values):
     for piece, target in ((0, keys), (1, values)):
         matrix = matrix_of(nat, 0, plan.it, 0, plan.ht, plan.ht, plan.image_first + piece * plan.cross)
-
-        def one(row, carry):
-            place = pl.ds(pl.multiple_of(row * plan.keys, plan.keys), plan.keys)
-            target[place, :] = mm(image[place, :], matrix, NN).astype(bf16)
-            return carry
-
-        lax.fori_loop(0, plan.rows, one, 0)
+        target[...] = mm(image[...], matrix, NN).astype(bf16)
 
 
 def image_forward(plan, nat, image):
@@ -258,17 +284,19 @@
     queries[...] = mm(low[...], matrix, NN).astype(bf16)
     allowed = lax.broadcasted_iota(jnp.int32, (2 * NQ, plan.keys), 1) < plan.patches
 
-    def one(row, carry):
-        query_place = pl.ds(pl.multiple_of(row * NQ, NQ), NQ)
-        place = pl.ds(pl.multiple_of(row * plan.keys, plan.keys), plan.keys)
-        for tile in range(plan.ht):
-            cols = slice(tile * TILE, (tile + 1) * TILE)
-            found = pair_probs(queries[query_place, cols], image_keys[place, cols], allowed, scale)
-            probs[row, tile] = found
-            mixed[query_place, cols] = pair_mix(found, image_values[place, cols])
-        return carry
-
-    lax.fori_loop(0, plan.rows, one, 0)
+    def attend(items):
+        found = all_probs(
+            [queries[rows_of(row, NQ), cols] for row, _, cols in items],
+            [image_keys[rows_of(row, plan.keys), cols] for row, _, cols in items],
+            [allowed] * len(items),
+            scale,
+        )
+        values = [image_values[rows_of(row, plan.keys), cols] for row, _, cols in items]
+        for (row, tile, cols), prob, mix in zip(items, found, all_mixed(found, values)):
+            probs[row, tile] = prob
+            mixed[rows_of(row, NQ), cols] = mix
+
+    each_tile(plan, plan.rows, attend)
     matrix = matrix_of(nat, 0, plan.ht, 0, plan.wt, plan.wt, plan.cross_out)
     part[...] = mm(mixed[...], matrix, NN).astype(bf16)
 
@@ -455,21 +483,21 @@
     matrix = matrix_of(nat, 0, plan.ht, 0, plan.wt, plan.wt, plan.cross_out)
     looked[...] = mm(grad_low[...], matrix, NT).astype(bf16)
 
-    def one(row, carry):
-        query_place = pl.ds(pl.multiple_of(row * NQ, NQ), NQ)
-        place = pl.ds(pl.multiple_of(row * plan.keys, plan.keys), plan.keys)
-        for tile in range(plan.ht):
-            cols = slice(tile * TILE, (tile + 1) * TILE)
-            query_grad, key_grad, value_grad = pair_backward(
-                queries[query_place, cols], keys[place, cols], values[place, cols],
-                probs[row, tile], looked[query_place, cols], scale,
-            )
-            query_back[query_place, cols] = query_grad
-            key_back[place, cols] = key_grad
-            value_back[place, cols] = value_grad
-        return carry
-
-    lax.fori_loop(0, plan.rows, one, 0)
+    def back(items):
+        found = all_backward(
+            [queries[rows_of(row, NQ), cols] for row, _, cols in items],
+            [keys[rows_of(row, plan.keys), cols] for row, _, cols in items],
+            [values[rows_of(row, plan.keys), cols] for row, _, cols in items],
+            [probs[row, tile] for row, tile, _ in items],
+            [looked[rows_of(row, NQ), cols] for row, _, cols in items],
+            scale,
+        )
+        for (row, _, cols), query_grad, key_grad, value_grad in zip(items, *found):
+            query_back[rows_of(row, NQ), cols] = query_grad
+            key_back[rows_of(row, plan.keys), cols] = key_grad
+            value_back[rows_of(row, plan.keys), cols] = value_grad
+
+    each_tile(plan, plan.rows, back)
     matrix = matrix_of(nat, 0, plan.wt, 0, plan.ht, plan.ht, plan.cross_first)
     part[...] = mm(query_back[...], matrix, NT).astype(bf16)
 
@@ -534,20 +562,20 @@
     matrix = matrix_of(nat, 0, plan.ht, 0, plan.wt, plan.wt, plan.self_out)
     mixed[...] = mm(grad_low[...], matrix, NT).astype(bf16)
 
-    def one(row, carry):
-        place = pl.ds(pl.multiple_of(row * plan.seq, plan.seq), plan.seq)
-        for tile in range(plan.ht):
-            cols = slice(tile * TILE, (tile + 1) * TILE)
-            found = pair_backward(
-                qkv[0, place, cols], qkv[1, place, cols], qkv[2, place, cols],
-                probs[row, tile], mixed[place, cols], scale,
-            )
+    def back_rows(items):
+        seq = plan.seq
+        found = all_backward(
+            *[[qkv[piece, rows_of(row, seq), cols] for row, _, cols in items] for piece in range(3)],
+            [probs[row, tile] for row, tile, _ in items],
+            [mixed[rows_of(row, seq), cols] for row, _, cols in items],
+            scale,
+        )
+        for number, (row, tile, _) in enumerate(items):
             for piece in range(3):
                 first = piece * plan.half + tile * TILE
-                back[place, first : first + TILE] = found[piece]
-        return carry
-
-    lax.fori_loop(0, plan.rows, one, 0)
+                back[rows_of(row, seq), first : first + TILE] = found[piece][number]
+
+    each_tile(plan, ROWS_AT_ONCE, back_rows)
     matrix = jnp.concatenate(
         [matrix_of(nat, 0, plan.wt, 0, plan.ht, plan.ht, p * plan.square) for p in range(3)],
         axis=1,
@@ -687,7 +715,7 @@
         )
     )
     other_four_query = swap_tensor(part_four_query)
-    feed_pairs = [(0, 1, 0, plan.hidden, 2), (2, 3, 0, width, 2)]
+    feed_pairs = [(0, 1, 0, plan.hidden, 6), (2, 3, 0, width, 6)]
     buffer = grad_blocks(
         buffer, place, plan.query_first, [low_second, before_query, query_gated, third_query_low],
         feed_pairs, 4 * learned * width * plan.hidden,
@@ -715,7 +743,7 @@
     cross_flops = 2 * rows * plan.keys * plan.image_width * half
     buffer = grad_blocks(
         buffer, place, plan.cross_first, [low_query, query_back, flat_image, key_back],
-        [(0, 1, 0, half, 2), (2, 3, 0, half, 1)], cross_flops,
+        [(0, 1, 0, half, 6), (2, 3, 0, half, 11)], cross_flops,
     )
     other_four_text, buffer = after((other_four_text, buffer))
     first_grad, self_low, self_back, part_six, norm_first = self_backward(
@@ -728,25 +756,25 @@
     buffer, part_six = after((buffer, part_six))
     buffer = grad_blocks(
         buffer, place, plan.image_first + plan.cross, [flat_image, value_back],
-        [(0, 1, 0, half, 1)], cross_flops,
+        [(0, 1, 0, half, 11)], cross_flops,
     )
     buffer, norms = after((buffer, norms))
     norms = norm_steps.send(norms)
     buffer = grad_blocks(
-        buffer, place, plan.cross_out, [looked, cross_low], [(0, 1, 0, width, 1)],
+        buffer, place, plan.cross_out, [looked, cross_low], [(0, 1, 0, width, 3)],
         2 * learned * width * half,
     )
     buffer, norms = after((buffer, norms))
     norms = norm_steps.send(norms)
     buffer = grad_blocks(
         buffer, place, plan.self_first, [flat_hidden, self_back],
-        [(0, 1, 0, half, 2), (0, 1, half, half, 2), (0, 1, 2 * half, half, 2)],
+        [(0, 1, 0, half, 6), (0, 1, half, half, 6), (0, 1, 2 * half, half, 6)],
         6 * tokens * width * half,
     )
     buffer, norms, other_six = after((buffer, norms, other_six))
     norms = norm_steps.send(norms)
     buffer = grad_blocks(
-        buffer, place, plan.self_out, [mixed, self_low], [(0, 1, 0, width, 1)],
+        buffer, place, plan.self_out, [mixed, self_low], [(0, 1, 0, width, 3)],
         2 * tokens * width * half,
     )
     buffer, norms = after((buffer, norms))

time: 312 us -> 301 us (0.965)
  Pallas kernels: 117 us -> 94.1 us
  starting transfers between devices: 52.9 us -> 66.1 us
    ppermute x14, starting transfers between devices: 9.05 us -> 22.9 us  [scatter_ring(): held[number] = lax.ppermute(summed, 'dp', RING_PAIRS)]
    ppermute x14, waiting for transfers between devices: 55.9 us -> 42.3 us  [scatter_ring(): held[number] = lax.ppermute(summed, 'dp', RING_PAIRS)]
    ppermute x9, waiting for transfers between devices: 17.4 us -> 29.3 us  [swap_tensor(): return lax.ppermute(part, 'tensor', [(0, 1), (1, 0)])]
    pallas_call x7, Pallas kernels: 25.1 us -> 15.4 us  [grad_blocks(): pl.pallas_call(functools.partial(grad_blocks_body, first_block, pairs, le...]
    pallas_call x1, Pallas kernels: 5.93 us -> 2.33 us  [cross_backward(): pl.pallas_call(functools.partial(cross_backward_body, plan, scale), out_s...]
    pallas_call x1, Pallas kernels: 5.64 us -> 2.15 us  [cross_forward(): pl.pallas_call(functools.partial(cross_forward_body, plan, scale), out_sh...]
  transfers between devices with their start and end apart: 60 -> 60, of which waited for: 34 -> 38; matrix products, arithmetic and copies ran while one was open for 4% -> 4% of each run, Pallas kernels for 22% -> 17%
where the time goes in v8:
time: 301 us; the launch traced here: 297 us
  waiting for transfers between devices  118 us (39%)
  Pallas kernels  94.1 us (31%)
  starting transfers between devices  66.1 us (22%)
  local copies, waits for them, and re-layouts  9.9 us (3%)
  other arithmetic  7.32 us (2%)
    ppermute x14, waiting for transfers between devices, scatter_ring(): held[number] = lax.ppermute(summed, 'dp', RING_PAIRS)  42.3 us
    ppermute x14, waiting for transfers between devices, gather_ring(): held = [lax.ppermute(piece, 'dp', RING_PAIRS) for piece in held]  37.2 us
    pallas_call x1, Pallas kernels, optimizer(): pl.pallas_call(functools.partial(optimizer_body, padded, counts), out_sha...  35.5 us
    ppermute x9, waiting for transfers between devices, swap_tensor(): return lax.ppermute(part, 'tensor', [(0, 1), (1, 0)])  29.3 us
    ppermute x14, starting transfers between devices, gather_ring(): held = [lax.ppermute(piece, 'dp', RING_PAIRS) for piece in held]  26.1 us
    ppermute x14, starting transfers between devices, scatter_ring(): held[number] = lax.ppermute(summed, 'dp', RING_PAIRS)  22.9 us
    pallas_call x7, Pallas kernels, grad_blocks(): pl.pallas_call(functools.partial(grad_blocks_body, first_block, pairs, le...  15.4 us
    ppermute x9, starting transfers between devices, swap_tensor(): return lax.ppermute(part, 'tensor', [(0, 1), (1, 0)])  9.86 us
  transfers between devices with their start and end apart: 60, of which 38 were waited for; matrix products, arithmetic and copies ran while one was open for 4% of the time, Pallas kernels for 17%

profile of v8, /device:TPU:0, one launch (start us, length us, event | category | flops | bytes accessed | tf_op | source)
XLA Modules:
  0.0 296.7 jit_solution(13981665204424538885)
XLA Ops:
  2.4 3.1 %collective-permute-start.5 = (bf16[15,128,128]{2,1,0:T(8,128)(2,1)S(1)}, bf16[15,128,128]{2,1,0:T(8,128)(2,1)S(1)}, u32[]{:S(2)}, u32[]{:S(2)}) collective-permute-start(bf16[15,128,128]{2,1,0:T(8,128)(2,1)S(1)} %slice.153), channel_id=1, source_target_pairs={{0,8},{2,6},{8,16},{10,2},{16,24},{18,10},{24,28},{26,18},{28,20},... | collective-permute-start | bytes 1474568 | tf_op jit(solution)/shard_map/ppermute | solution.py:911
  7.2 5.1 %collective-permute-done.5.refs_3_ = bf16[15,128,128]{2,1,0:T(8,128)(2,1)S(1)} collective-permute-done((bf16[15,128,128]{2,1,0:T(8,128)(2,1)S(1)}, bf16[15,128,128]{2,1,0:T(8,128)(2,1)S(1)}, u32[]{:S(2)}, u32[]{:S(2)}) %collective-permute-start.5) | collective-permute-done | bytes 491552 | tf_op jit(solution)/shard_map/ppermute | solution.py:911
  24.5 4.9 %block_indices.1 = (s32[464]{0:T(512)S(1)}, s32[464]{0:T(512)S(1)}) custom-call(s32[1]{0:T(128)} %bitcast.1.device, s32[464]{0:T(512)S(1)} %bitcast.49, s32[16,464]{1,0:T(8,128)S(1)} %copy-done.13, s32[16,464]{1,0:T(8,128)S(1)} %copy-done.14), custom_call_target="tpu_custom_call" | custom-call | tf_op jit(solution)/shard_map/block_indices/pallas_call | solution.py:886
  40.3 3.2 %collective-permute-done.16.refs_1_ = bf16[15,128,128]{2,1,0:T(8,128)(2,1)S(1)} collective-permute-done((bf16[15,128,128]{2,1,0:T(8,128)(2,1)S(1)}, bf16[15,128,128]{2,1,0:T(8,128)(2,1)S(1)}, u32[]{:S(2)}, u32[]{:S(2)}) %collective-permute-start.16) | collective-permute-done | bytes 491552 | tf_op jit(solution)/shard_map/ppermute | solution.py:911
  45.1 3.3 %collective-permute-done.3.refs_0_ = bf16[14,128,128]{2,1,0:T(8,128)(2,1)S(1)} collective-permute-done((bf16[14,128,128]{2,1,0:T(8,128)(2,1)S(1)}, bf16[14,128,128]{2,1,0:T(8,128)(2,1)S(1)}, u32[]{:S(2)}, u32[]{:S(2)}) %collective-permute-start.3) | collective-permute-done | bytes 458784 | tf_op jit(solution)/shard_map/ppermute | solution.py:911
  60.2 3.7 %collective-permute-done.23.refs_1_ = bf16[15,128,128]{2,1,0:T(8,128)(2,1)S(1)} collective-permute-done((bf16[15,128,128]{2,1,0:T(8,128)(2,1)S(1)}, bf16[15,128,128]{2,1,0:T(8,128)(2,1)S(1)}, u32[]{:S(2)}, u32[]{:S(2)}) %collective-permute-start.23) | collective-permute-done | bytes 491552 | tf_op jit(solution)/shard_map/ppermute | solution.py:911
  70.6 3.4 %collective-permute-done.26.refs_1_ = bf16[15,128,128]{2,1,0:T(8,128)(2,1)S(1)} collective-permute-done((bf16[15,128,128]{2,1,0:T(8,128)(2,1)S(1)}, bf16[15,128,128]{2,1,0:T(8,128)(2,1)S(1)}, u32[]{:S(2)}, u32[]{:S(2)}) %collective-permute-start.26) | collective-permute-done | bytes 491552 | tf_op jit(solution)/shard_map/ppermute | solution.py:911
  74.8 4.2 %collective-permute-done.22.refs_0_ = bf16[14,128,128]{2,1,0:T(8,128)(2,1)S(1)} collective-permute-done((bf16[14,128,128]{2,1,0:T(8,128)(2,1)S(1)}, bf16[14,128,128]{2,1,0:T(8,128)(2,1)S(1)}, u32[]{:S(2)}, u32[]{:S(2)}) %collective-permute-start.22) | collective-permute-done | bytes 458784 | tf_op jit(solution)/shard_map/ppermute | solution.py:911
  81.5 3.5 %self_forward.1 = (bf16[3,512,384]{2,1,0:T(8,128)(2,1)S(1)}, f32[4,3,256,128]{3,2,1,0:T(8,128)S(1)}, bf16[512,384]{1,0:T(8,128)(2,1)S(1)}, bf16[128,768]{1,0:T(8,128)(2,1)S(1)}, bf16[384,768]{1,0:T(8,128)(2,1)S(1)}) custom-call(bf16[464,128,128]{2,1,0:T(8,128)(2,1)S(1)} %place_blocks.9.nat, bf16[512,768]{1,0:T(8,128)(2,1)S(1)} %bitcast.32, ...), custom_call_target="tpu_custom_call" | custom-call | flops 1 | bytes 1 | tf_op jit(solution)/shard_map/self_forward/pallas_call | solution.py:224
  87.0 3.5 %image_forward.1 = (bf16[1088,384]{1,0:T(8,128)(2,1)S(1)}, bf16[1088,384]{1,0:T(8,128)(2,1)S(1)}) custom-call(bf16[464,128,128]{2,1,0:T(8,128)(2,1)S(1)} %place_blocks.9.nat, bf16[1088,1408]{1,0:T(8,128)(2,1)S(1)} %bitcast.29), custom_call_target="tpu_custom_call" | custom-call | flops 1 | bytes 1 | tf_op jit(solution)/shard_map/image_forward/pallas_call | solution.py:249
  96.3 14.5 %collective-permute-done.30.other = bf16[128,768]{1,0:T(8,128)(2,1)S(1)} collective-permute-done((bf16[128,768]{1,0:T(8,128)(2,1)S(1)}, bf16[128,768]{1,0:T(8,128)(2,1)S(1)}, u32[]{:S(2)}, u32[]{:S(2)}) %collective-permute-start.30) | collective-permute-done | bytes 196640 | tf_op jit(solution)/shard_map/ppermute | solution.py:658
  115.1 4.8 %text_forward.1 = (f32[384,768]{1,0:T(8,128)S(1)}, f32[384,768]{1,0:T(8,128)S(1)}, bf16[384,768]{1,0:T(8,128)(2,1)S(1)}, bf16[384,1536]{1,0:T(8,128)(2,1)S(1)}, ...) custom-call(bf16[464,128,128]{2,1,0:T(8,128)(2,1)S(1)} %place_blocks.9.nat, bf16[512,768]{1,0:T(8,128)(2,1)S(1)} %bitcast.34, ...), custom_call_target="tpu_custom_call" | custom-call | flops 1 | bytes 1 | tf_op jit(solution)/shard_map/text_forward/pallas_call | solution.py:379
  120.8 4.1 %feed_backward.2 = (bf16[128,768]{1,0:T(8,128)(2,1)S(1)}, f32[128,768]{1,0:T(8,128)S(1)}, bf16[128,768]{1,0:T(8,128)(2,1)S(1)}, bf16[128,1536]{1,0:T(8,128)(2,1)...) custom-call(bf16[464,128,128]{2,1,0:T(8,128)(2,1)S(1)} %place_blocks.9.nat, ...), custom_call_target="tpu_custom_call" | custom-call | flops 1 | bytes 1 | tf_op jit(solution)/shard_map/feed_backward/pallas_call | solution.py:455
  128.6 6.8 %collective-permute-done.33.other = bf16[384,768]{1,0:T(8,128)(2,1)S(1)} collective-permute-done((bf16[384,768]{1,0:T(8,128)(2,1)S(1)}, bf16[384,768]{1,0:T(8,128)(2,1)S(1)}, u32[]{:S(2)}, u32[]{:S(2)}) %collective-permute-start.33) | collective-permute-done | bytes 589856 | tf_op jit(solution)/shard_map/ppermute | solution.py:658
  135.4 5.6 %feed_backward.3 = (bf16[384,768]{1,0:T(8,128)(2,1)S(1)}, f32[384,768]{1,0:T(8,128)S(1)}, bf16[384,768]{1,0:T(8,128)(2,1)S(1)}, bf16[384,1536]{1,0:T(8,128)(2,1)...) custom-call(bf16[464,128,128]{2,1,0:T(8,128)(2,1)S(1)} %place_blocks.9.nat, ...), custom_call_target="tpu_custom_call" | custom-call | flops 1 | bytes 1 | tf_op jit(solution)/shard_map/feed_backward/pallas_call | solution.py:455
  146.3 3.7 %grad_blocks.8.refs_4_ = bf16[464,128,128]{2,1,0:T(8,128)(2,1)S(1)} custom-call(s32[464]{0:T(512)S(1)} %get-tuple-element.148.place, bf16[384,768]{1,0:T(8,128)(2,1)S(1)} %get-tuple-element.174.refs_0_, bf16[384,1536]{1,0:T(8,128)(2,1)S(1)} %get-tuple-element.175.refs_1_, bf16[384,1536]{1,0:T(8,128)(2,1)S(1)} %copy-done.6, ...), custom_call_target="tpu_custom_call", output_to_operand_aliasing={{}: (5, {})} | custom-call | flops 1 | bytes 1 | tf_op jit(solution)/shard_map/grad_blocks/pallas_call | solution.py:642
  156.4 4.9 %self_backward.1 = (f32[512,768]{1,0:T(8,128)S(1)}, bf16[512,768]{1,0:T(8,128)(2,1)S(1)}, bf16[512,1152]{1,0:T(8,128)(2,1)S(1)}, bf16[512,768]{1,0:T(8,128)(2,1)S(1)}, f32[2,768]{1,0:T(2,128)S(1)}) custom-call(bf16[464,128,128]{2,1,0:T(8,128)(2,1)S(1)} %place_blocks.9.nat, f32[128,768]{1,0:T(8,128)S(1)} %get-tuple-element.156.query_resid, ...), custom_call_target="tpu_custom_call" | custom-call | flops 1 | bytes 1 | tf_op jit(solution)/shard_map/self_backward/pallas_call | solution.py:591
  180.0 3.9 %collective-permute-done.42 = bf16[58,128,128]{2,1,0:T(8,128)(2,1)S(1)} collective-permute-done((bf16[58,128,128]{2,1,0:T(8,128)(2,1)S(1)}, bf16[58,128,128]{2,1,0:T(8,128)(2,1)S(1)}, u32[]{:S(2)}, u32[]{:S(2)}) %collective-permute-start.42) | collective-permute-done | bytes 1900576 | tf_op jit(solution)/shard_map/ppermute | solution.py:947
  188.5 4.9 %collective-permute-done.53 = bf16[15,128,128]{2,1,0:T(8,128)(2,1)S(1)} collective-permute-done((bf16[15,128,128]{2,1,0:T(8,128)(2,1)S(1)}, bf16[15,128,128]{2,1,0:T(8,128)(2,1)S(1)}, u32[]{:S(2)}, u32[]{:S(2)}) %collective-permute-start.53) | collective-permute-done | bytes 491552 | tf_op jit(solution)/shard_map/ppermute | solution.py:960
  200.1 3.4 %collective-permute-done.54 = bf16[15,128,128]{2,1,0:T(8,128)(2,1)S(1)} collective-permute-done((bf16[15,128,128]{2,1,0:T(8,128)(2,1)S(1)}, bf16[15,128,128]{2,1,0:T(8,128)(2,1)S(1)}, u32[]{:S(2)}, u32[]{:S(2)}) %collective-permute-start.54) | collective-permute-done | bytes 491552 | tf_op jit(solution)/shard_map/ppermute | solution.py:960
  210.3 3.4 %collective-permute-done.55 = bf16[15,128,128]{2,1,0:T(8,128)(2,1)S(1)} collective-permute-done((bf16[15,128,128]{2,1,0:T(8,128)(2,1)S(1)}, bf16[15,128,128]{2,1,0:T(8,128)(2,1)S(1)}, u32[]{:S(2)}, u32[]{:S(2)}) %collective-permute-start.55) | collective-permute-done | bytes 491552 | tf_op jit(solution)/shard_map/ppermute | solution.py:960
  220.5 3.4 %collective-permute-done.56 = bf16[15,128,128]{2,1,0:T(8,128)(2,1)S(1)} collective-permute-done((bf16[15,128,128]{2,1,0:T(8,128)(2,1)S(1)}, bf16[15,128,128]{2,1,0:T(8,128)(2,1)S(1)}, u32[]{:S(2)}, u32[]{:S(2)}) %collective-permute-start.56) | collective-permute-done | bytes 491552 | tf_op jit(solution)/shard_map/ppermute | solution.py:960
  230.7 3.4 %collective-permute-done.57 = bf16[15,128,128]{2,1,0:T(8,128)(2,1)S(1)} collective-permute-done((bf16[15,128,128]{2,1,0:T(8,128)(2,1)S(1)}, bf16[15,128,128]{2,1,0:T(8,128)(2,1)S(1)}, u32[]{:S(2)}, u32[]{:S(2)}) %collective-permute-start.57) | collective-permute-done | bytes 491552 | tf_op jit(solution)/shard_map/ppermute | solution.py:960
  260.9 35.5 %optimizer.1 = (f32[29,128,128]{2,1,0:T(8,128)}, bf16[29,128,128]{2,1,0:T(8,128)(2,1)}, f32[29,128,128]{2,1,0:T(8,128)}, f32[29,128,128]{2,1,0:T(8,128)}, f32[29...) custom-call(bf16[14,128,128]{2,1,0:T(8,128)(2,1)} %slice.119.refs_0_, ...), custom_call_target="tpu_custom_call" | custom-call | tf_op jit(solution)/shard_map/optimizer/pallas_call | solution.py:1235
  (196 shorter events, 155.0 us)
Async XLA Ops:
  5.5 11.7 %collective-permute-start = (bf16[14,128,128]{2,1,0:T(8,128)(2,1)S(1)}, bf16[14,128,128]{2,1,0:T(8,128)(2,1)}, u32[]{:S(2)}, u32[]{:S(2)}) collective-permute-start(bf16[14,128,128]{2,1,0:T(8,128)(2,1)S(1)} %slice.152), channel_id=1, source_target_pairs={{0,8},{2,6},{8,16},{10,2},{16,24},{18,10},{24,28},{26,18},{28,20},... | collective-permute-start | bytes 1376264 | tf_op jit(solution)/shard_map/ppermute | solution.py:911
  12.2 10.2 %collective-permute-start.9 = (bf16[15,128,128]{2,1,0:T(8,128)(2,1)S(1)}, bf16[15,128,128]{2,1,0:T(8,128)(2,1)S(1)}, u32[]{:S(2)}, u32[]{:S(2)}) collective-permute-start(bf16[15,128,128]{2,1,0:T(8,128)(2,1)S(1)} %collective-permute-done.5.refs_3_), channel_id=1, source_target_pairs={{0,8},{2,6},{8,16},{10,2},{16,24},{18,10},{24,28},{26,18},{28,20},... | collective-permute-start | bytes 1474568 | tf_op jit(solution)/shard_map/ppermute | solution.py:911
  17.2 12.2 %collective-permute-start.1 = (bf16[14,128,128]{2,1,0:T(8,128)(2,1)}, bf16[14,128,128]{2,1,0:T(8,128)(2,1)}, u32[]{:S(2)}, u32[]{:S(2)}) collective-permute-start(bf16[14,128,128]{2,1,0:T(8,128)(2,1)} %collective-permute-done.refs_2_), channel_id=1, source_target_pairs={{0,8},{2,6},{8,16},{10,2},{16,24},{18,10},{24,28},{26,18},{28,20},... | collective-permute-start | bytes 1376264 | tf_op jit(solution)/shard_map/ppermute | solution.py:911
  19.3 20.5 %collective-permute-start.4 = (bf16[29,128,128]{2,1,0:T(8,128)(2,1)S(1)}, bf16[29,128,128]{2,1,0:T(8,128)(2,1)S(1)}, u32[]{:S(2)}, u32[]{:S(2)}) collective-permute-start(bf16[29,128,128]{2,1,0:T(8,128)(2,1)S(1)} %bitcast_convert_fusion.refs_0_), channel_id=1, source_target_pairs={{0,2},{2,0},{4,6},{6,4},{8,10},{10,8},{12,14},{14,12},{16,18},{18,... | collective-permute-start | bytes 2850824 | tf_op jit(solution)/shard_map/ppermute | solution.py:906
  22.4 10.2 %collective-permute-start.12 = (bf16[15,128,128]{2,1,0:T(8,128)(2,1)S(1)}, bf16[15,128,128]{2,1,0:T(8,128)(2,1)S(1)}, u32[]{:S(2)}, u32[]{:S(2)}) collective-permute-start(bf16[15,128,128]{2,1,0:T(8,128)(2,1)S(1)} %collective-permute-done.9.refs_1_), channel_id=1, source_target_pairs={{0,8},{2,6},{8,16},{10,2},{16,24},{18,10},{24,28},{26,18},{28,20},... | collective-permute-start | bytes 1474568 | tf_op jit(solution)/shard_map/ppermute | solution.py:911
  32.6 10.9 %collective-permute-start.16 = (bf16[15,128,128]{2,1,0:T(8,128)(2,1)S(1)}, bf16[15,128,128]{2,1,0:T(8,128)(2,1)S(1)}, u32[]{:S(2)}, u32[]{:S(2)}) collective-permute-start(bf16[15,128,128]{2,1,0:T(8,128)(2,1)S(1)} %collective-permute-done.12.refs_5_), channel_id=1, source_target_pairs={{0,8},{2,6},{8,16},{10,2},{16,24},{18,10},{24,28},{26,18},{28,20},... | collective-permute-start | bytes 1474568 | tf_op jit(solution)/shard_map/ppermute | solution.py:911
  34.7 10.4 %collective-permute-start.7 = (bf16[15,128,128]{2,1,0:T(8,128)(2,1)S(1)}, bf16[15,128,128]{2,1,0:T(8,128)(2,1)S(1)}, u32[]{:S(2)}, u32[]{:S(2)}) collective-permute-start(bf16[15,128,128]{2,1,0:T(8,128)(2,1)S(1)} %collective-permute-done.5.refs_3_), channel_id=1, source_target_pairs={{0,2},{2,0},{4,6},{6,4},{8,10},{10,8},{12,14},{14,12},{16,18},{18,... | collective-permute-start | bytes 1474568 | tf_op jit(solution)/shard_map/ppermute | solution.py:922
  38.2 10.2 %collective-permute-start.3 = (bf16[14,128,128]{2,1,0:T(8,128)(2,1)S(1)}, bf16[14,128,128]{2,1,0:T(8,128)(2,1)S(1)}, u32[]{:S(2)}, u32[]{:S(2)}) collective-permute-start(bf16[14,128,128]{2,1,0:T(8,128)(2,1)S(1)} %collective-permute-done.2.refs_4_), channel_id=1, source_target_pairs={{0,8},{2,6},{8,16},{10,2},{16,24},{18,10},{24,28},{26,18},{28,20},... | collective-permute-start | bytes 1376264 | tf_op jit(solution)/shard_map/ppermute | solution.py:911
  39.8 11.5 %collective-permute-start.11 = (bf16[15,128,128]{2,1,0:T(8,128)(2,1)S(1)}, bf16[15,128,128]{2,1,0:T(8,128)(2,1)S(1)}, u32[]{:S(2)}, u32[]{:S(2)}) collective-permute-start(bf16[15,128,128]{2,1,0:T(8,128)(2,1)S(1)} %collective-permute-done.9.refs_1_), channel_id=1, source_target_pairs={{0,2},{2,0},{4,6},{6,4},{8,10},{10,8},{12,14},{14,12},{16,18},{18,... | collective-permute-start | bytes 1474568 | tf_op jit(solution)/shard_map/ppermute | solution.py:922
  43.5 10.2 %collective-permute-start.19 = (bf16[15,128,128]{2,1,0:T(8,128)(2,1)S(1)}, bf16[15,128,128]{2,1,0:T(8,128)(2,1)S(1)}, u32[]{:S(2)}, u32[]{:S(2)}) collective-permute-start(bf16[15,128,128]{2,1,0:T(8,128)(2,1)S(1)} %collective-permute-done.16.refs_1_), channel_id=1, source_target_pairs={{0,8},{2,6},{8,16},{10,2},{16,24},{18,10},{24,28},{26,18},{28,20},... | collective-permute-start | bytes 1474568 | tf_op jit(solution)/shard_map/ppermute | solution.py:911
  45.1 10.2 %collective-permute-start.14 = (bf16[15,128,128]{2,1,0:T(8,128)(2,1)S(1)}, bf16[15,128,128]{2,1,0:T(8,128)(2,1)S(1)}, u32[]{:S(2)}, u32[]{:S(2)}) collective-permute-start(bf16[15,128,128]{2,1,0:T(8,128)(2,1)S(1)} %collective-permute-done.12.refs_5_), channel_id=1, source_target_pairs={{0,2},{2,0},{4,6},{6,4},{8,10},{10,8},{12,14},{14,12},{16,18},{18,... | collective-permute-start | bytes 1474568 | tf_op jit(solution)/shard_map/ppermute | solution.py:922
  53.7 10.2 %collective-permute-start.23 = (bf16[15,128,128]{2,1,0:T(8,128)(2,1)S(1)}, bf16[15,128,128]{2,1,0:T(8,128)(2,1)S(1)}, u32[]{:S(2)}, u32[]{:S(2)}) collective-permute-start(bf16[15,128,128]{2,1,0:T(8,128)(2,1)S(1)} %collective-permute-done.19.refs_5_), channel_id=1, source_target_pairs={{0,8},{2,6},{8,16},{10,2},{16,24},{18,10},{24,28},{26,18},{28,20},... | collective-permute-start | bytes 1474568 | tf_op jit(solution)/shard_map/ppermute | solution.py:911
  55.3 10.2 %collective-permute-start.21 = (bf16[15,128,128]{2,1,0:T(8,128)(2,1)S(1)}, bf16[15,128,128]{2,1,0:T(8,128)(2,1)S(1)}, u32[]{:S(2)}, u32[]{:S(2)}) collective-permute-start(bf16[15,128,128]{2,1,0:T(8,128)(2,1)S(1)} %collective-permute-done.19.refs_5_), channel_id=1, source_target_pairs={{0,2},{2,0},{4,6},{6,4},{8,10},{10,8},{12,14},{14,12},{16,18},{18,... | collective-permute-start | bytes 1474568 | tf_op jit(solution)/shard_map/ppermute | solution.py:922
  92.1 23.1 %collective-permute-start.31 = (bf16[384,768]{1,0:T(8,128)(2,1)S(1)}, bf16[384,768]{1,0:T(8,128)(2,1)S(1)}, u32[]{:S(2)}, u32[]{:S(2)}) collective-permute-start(bf16[384,768]{1,0:T(8,128)(2,1)S(1)} %get-tuple-element.138.mine), channel_id=1, source_target_pairs={{0,1},{1,0},{2,3},{3,2},{4,5},{5,4},{6,7},{7,6},{8,9},{9,8},{10,11... | collective-permute-start | bytes 1769480 | tf_op jit(solution)/shard_map/ppermute | solution.py:658
  95.7 15.1 %collective-permute-start.30 = (bf16[128,768]{1,0:T(8,128)(2,1)S(1)}, bf16[128,768]{1,0:T(8,128)(2,1)S(1)}, u32[]{:S(2)}, u32[]{:S(2)}) collective-permute-start(bf16[128,768]{1,0:T(8,128)(2,1)S(1)} %get-tuple-element.136.mine), channel_id=1, source_target_pairs={{0,1},{1,0},{2,3},{3,2},{4,5},{5,4},{6,7},{7,6},{8,9},{9,8},{10,11... | collective-permute-start | bytes 589832 | tf_op jit(solution)/shard_map/ppermute | solution.py:658
  119.9 15.5 %collective-permute-start.33 = (bf16[384,768]{1,0:T(8,128)(2,1)S(1)}, bf16[384,768]{1,0:T(8,128)(2,1)S(1)}, u32[]{:S(2)}, u32[]{:S(2)}) collective-permute-start(bf16[384,768]{1,0:T(8,128)(2,1)S(1)} %get-tuple-element.147.mine), channel_id=1, source_target_pairs={{0,1},{1,0},{2,3},{3,2},{4,5},{5,4},{6,7},{7,6},{8,9},{9,8},{10,11... | collective-permute-start | bytes 1769480 | tf_op jit(solution)/shard_map/ppermute | solution.py:658
  124.9 16.9 %collective-permute-start.34 = (bf16[128,768]{1,0:T(8,128)(2,1)S(1)}, bf16[128,768]{1,0:T(8,128)(2,1)S(1)}, u32[]{:S(2)}, u32[]{:S(2)}) collective-permute-start(bf16[128,768]{1,0:T(8,128)(2,1)S(1)} %get-tuple-element.160.mine), channel_id=1, source_target_pairs={{0,1},{1,0},{2,3},{3,2},{4,5},{5,4},{6,7},{7,6},{8,9},{9,8},{10,11... | collective-permute-start | bytes 589832 | tf_op jit(solution)/shard_map/ppermute | solution.py:658
  141.8 12.4 %collective-permute-start.36 = (bf16[384,768]{1,0:T(8,128)(2,1)S(1)}, bf16[384,768]{1,0:T(8,128)(2,1)S(1)}, u32[]{:S(2)}, u32[]{:S(2)}) collective-permute-start(bf16[384,768]{1,0:T(8,128)(2,1)S(1)} %get-tuple-element.170.text_mine), channel_id=1, source_target_pairs={{0,1},{1,0},{2,3},{3,2},{4,5},{5,4},{6,7},{7,6},{8,9},{9,8},{10,11... | collective-permute-start | bytes 1769480 | tf_op jit(solution)/shard_map/ppermute | solution.py:658
  144.7 11.7 %collective-permute-start.35 = (bf16[128,768]{1,0:T(8,128)(2,1)S(1)}, bf16[128,768]{1,0:T(8,128)(2,1)S(1)}, u32[]{:S(2)}, u32[]{:S(2)}) collective-permute-start(bf16[128,768]{1,0:T(8,128)(2,1)S(1)} %get-tuple-element.168.query_mine), channel_id=1, source_target_pairs={{0,1},{1,0},{2,3},{3,2},{4,5},{5,4},{6,7},{7,6},{8,9},{9,8},{10,11... | collective-permute-start | bytes 589832 | tf_op jit(solution)/shard_map/ppermute | solution.py:658
  161.3 13.7 %collective-permute-start.40 = (bf16[512,768]{1,0:T(8,128)(2,1)S(1)}, bf16[512,768]{1,0:T(8,128)(2,1)S(1)}, u32[]{:S(2)}, u32[]{:S(2)}) collective-permute-start(bf16[512,768]{1,0:T(8,128)(2,1)S(1)} %get-tuple-element.185), channel_id=1, source_target_pairs={{0,1},{1,0},{2,3},{3,2},{4,5},{5,4},{6,7},{7,6},{8,9},{9,8},{10,11... | collective-permute-start | bytes 2359304 | tf_op jit(solution)/shard_map/ppermute | solution.py:658
  186.2 12.0 %collective-permute-start.46 = (bf16[14,128,128]{2,1,0:T(8,128)(2,1)S(1)}, bf16[14,128,128]{2,1,0:T(8,128)(2,1)S(1)}, u32[]{:S(2)}, u32[]{:S(2)}) collective-permute-start(bf16[14,128,128]{2,1,0:T(8,128)(2,1)S(1)} %add_convert_fusion.13), channel_id=1, source_target_pairs={{0,8},{2,6},{8,16},{10,2},{16,24},{18,10},{24,28},{26,18},{28,20},... | collective-permute-start | bytes 1376264 | tf_op jit(solution)/shard_map/ppermute | solution.py:960
  188.3 27.3 %collective-permute-start.44 = (bf16[58,128,128]{2,1,0:T(8,128)(2,1)S(1)}, bf16[58,128,128]{2,1,0:T(8,128)(2,1)S(1)}, u32[]{:S(2)}, u32[]{:S(2)}) collective-permute-start(bf16[58,128,128]{2,1,0:T(8,128)(2,1)S(1)} %slice.118), channel_id=1, source_target_pairs={{0,2},{2,0},{4,6},{6,4},{8,10},{10,8},{12,14},{14,12},{16,18},{18,... | collective-permute-start | bytes 5701640 | tf_op jit(solution)/shard_map/ppermute | solution.py:947
  215.7 28.6 %collective-permute-start.45 = (bf16[58,128,128]{2,1,0:T(8,128)(2,1)S(1)}, bf16[58,128,128]{2,1,0:T(8,128)(2,1)S(1)}, u32[]{:S(2)}, u32[]{:S(2)}) collective-permute-start(bf16[58,128,128]{2,1,0:T(8,128)(2,1)S(1)} %slice.120), channel_id=1, source_target_pairs={{0,2},{2,0},{4,6},{6,4},{8,10},{10,8},{12,14},{14,12},{16,18},{18,... | collective-permute-start | bytes 5701640 | tf_op jit(solution)/shard_map/ppermute | solution.py:947
  244.5 14.9 %collective-permute-start.59 = (bf16[15,128,128]{2,1,0:T(8,128)(2,1)S(1)}, bf16[15,128,128]{2,1,0:T(8,128)(2,1)S(1)}, u32[]{:S(2)}, u32[]{:S(2)}) collective-permute-start(bf16[15,128,128]{2,1,0:T(8,128)(2,1)S(1)} %add_convert_fusion), channel_id=1, source_target_pairs={{0,8},{2,6},{8,16},{10,2},{16,24},{18,10},{24,28},{26,18},{28,20},... | collective-permute-start | bytes 1474568 | tf_op jit(solution)/shard_map/ppermute | solution.py:960
  (57 other events, 441.2 us)

commit v9 on v8

--- a/solution.py
+++ b/solution.py
@@ -180,12 +180,13 @@
         self.image_first = self.cross_first + square
         self.cross_out = self.image_first + 2 * cross
         self.tokens = rows * seq
+        self.half_rows = rows // 2
         self.learned = rows * NQ
         self.texts = rows * (seq - NQ)
 
 
 def self_forward_body(
-    plan, scale, nat, hidden, segments, qkv, probs, mixed, query_part, text_part
+    plan, scale, nat, hidden, segments, qkv, probs, mixed, query_part, *text_parts
 ):
     for piece in range(3):
         matrix = matrix_of(nat, 0, plan.wt, 0, plan.ht, plan.ht, piece * plan.square)
@@ -216,7 +217,10 @@
     for row in range(plan.rows):
         first = row * plan.seq
         query_part[row * NQ : (row + 1) * NQ] = part[first : first + NQ]
-        text_part[row * text : (row + 1) * text] = part[first + NQ : first + plan.seq]
+        local = row % plan.half_rows
+        text_parts[row // plan.half_rows][local * text : (local + 1) * text] = part[
+            first + NQ : first + plan.seq
+        ]
 
 
 def self_forward(plan, scale, nat, hidden, segments):
@@ -228,10 +232,11 @@
             held((plan.rows, plan.ht, 2 * plan.seq, plan.seq), f32),
             held((tokens, half), bf16),
             jax.ShapeDtypeStruct((plan.learned, width), bf16),
-            jax.ShapeDtypeStruct((plan.texts, width), bf16),
+            jax.ShapeDtypeStruct((plan.texts // 2, width), bf16),
+            jax.ShapeDtypeStruct((plan.texts // 2, width), bf16),
         ),
         in_specs=vmem_specs(3),
-        out_specs=tuple(vmem_specs(5)),
+        out_specs=tuple(vmem_specs(6)),
         compiler_params=vmem_params(),
         cost_estimate=cost(2 * tokens * width * half * 4, 8e6),
         name="self_forward",
@@ -257,12 +262,12 @@
     )(*pin(nat, image))
 
 
-def first_norm(plan, token, count, hidden, mine, other, params, resid, first, low):
+def first_norm(plan, rows, token, count, hidden, mine, other, params, resid, first, low):
     gain, shift = params[0, 0:1], params[0, 1:2]
 
     def one(row, carry):
         place = pl.ds(pl.multiple_of(row * count, count), count)
-        start = pl.multiple_of(row * plan.seq + token, NQ)
+        start = pl.multiple_of((rows[0] + row) * plan.seq + token, NQ)
         summed = hidden[pl.ds(start, count), :].astype(f32) + (
             mine[place, :].astype(f32) + other[place, :].astype(f32)
         )
@@ -272,14 +277,14 @@
         low[place, :] = normed.astype(bf16)
         return carry
 
-    lax.fori_loop(0, plan.rows, one, 0)
+    lax.fori_loop(0, rows[1], one, 0)
 
 
 def cross_forward_body(
     plan, scale, nat, hidden, mine, other, params, image_keys, image_values,
     resid, first, low, queries, probs, mixed, part,
 ):
-    first_norm(plan, 0, NQ, hidden, mine, other, params, resid, first, low)
+    first_norm(plan, (0, plan.rows), 0, NQ, hidden, mine, other, params, resid, first, low)
     matrix = matrix_of(nat, 0, plan.wt, 0, plan.ht, plan.ht, plan.cross_first)
     queries[...] = mm(low[...], matrix, NN).astype(bf16)
     allowed = lax.broadcasted_iota(jnp.int32, (2 * NQ, plan.keys), 1) < plan.patches
@@ -349,9 +354,10 @@
 
 
 def text_forward_body(
-    plan, nat, hidden, mine, other, params, resid, first, low, gated, slope, part
+    plan, half, nat, hidden, mine, other, params, resid, first, low, gated, slope, part
 ):
-    first_norm(plan, NQ, plan.seq - NQ, hidden, mine, other, params, resid, first, low)
+    rows = (half * plan.half_rows, plan.half_rows)
+    first_norm(plan, rows, NQ, plan.seq - NQ, hidden, mine, other, params, resid, first, low)
     feed_forward_tail(plan, plan.text_first, nat, low, gated, slope, part)
 
 
@@ -374,10 +380,10 @@
     )
 
 
-def text_forward(plan, nat, hidden, mine, other, params):
-    count, width = plan.texts, plan.width
+def text_forward(plan, half, nat, hidden, mine, other, params):
+    count, width = plan.texts // 2, plan.width
     return pl.pallas_call(
-        functools.partial(text_forward_body, plan),
+        functools.partial(text_forward_body, plan, half),
         out_shape=(
             held((count, width), f32),
             held((count, width), f32),
@@ -411,19 +417,20 @@
 
 
 def feed_backward_body(
-    plan, first_block, first_token, which, nat, states, mine, other, upstream, params, slope,
+    plan, first_block, rows, first_token, which, nat, states, mine, other, upstream, params, slope,
     out, grad, grad_low, before_low, part, norm_grad,
 ):
     gain, shift = params[which, 0:1], params[which, 1:2]
-    count = states.shape[0] // plan.rows
+    count = states.shape[0] // rows[1]
     norm_grad[...] = jnp.zeros_like(norm_grad)
 
     def one_norm(row, carry):
         place = pl.ds(pl.multiple_of(row * count, count), count)
         summed = states[place, :] + (mine[place, :].astype(f32) + other[place, :].astype(f32))
         out[place, :] = (norm_forward(summed)[0] * gain + shift).astype(bf16)
+        start = pl.multiple_of((rows[0] + row) * plan.seq + first_token, NQ)
         found, gain_grad, shift_grad = norm_backward(
-            summed, upstream[pl.ds(row * plan.seq + first_token, count), :].astype(f32), gain
+            summed, upstream[pl.ds(start, count), :].astype(f32), gain
         )
         grad[place, :] = found
         grad_low[place, :] = found.astype(bf16)
@@ -431,7 +438,7 @@
         norm_grad[1:2] += shift_grad
         return carry
 
-    lax.fori_loop(0, plan.rows, one_norm, 0)
+    lax.fori_loop(0, rows[1], one_norm, 0)
 
     def one_down(chunk, carry):
         matrix = matrix_of(nat, chunk * 2, 2, 0, plan.wt, plan.wt, first_block + plan.feed)
@@ -450,10 +457,12 @@
     lax.fori_loop(0, plan.wt // 2, one_up, 0)
 
 
-def feed_backward(plan, first_block, first_token, which, nat, states, mine, other, upstream, params, slope):
+def feed_backward(
+    plan, first_block, rows, first_token, which, nat, states, mine, other, upstream, params, slope
+):
     count, width = states.shape
     return pl.pallas_call(
-        functools.partial(feed_backward_body, plan, first_block, first_token, which),
+        functools.partial(feed_backward_body, plan, first_block, rows, first_token, which),
         out_shape=(
             jax.ShapeDtypeStruct((count, width), bf16),
             held((count, width), f32),
@@ -529,36 +538,38 @@
 
 
 def self_backward_body(
-    plan, scale, nat, query_resid, text_resid, query_grad, query_mine, query_other, text_grad,
-    text_mine, text_other, params, qkv, probs,
-    grad, grad_low, back, part, norm_grad, mixed,
+    plan, scale, nat, query_resid, query_grad, query_mine, query_other, *refs
 ):
+    text_resids, text_grads, text_mines, text_others = refs[:2], refs[2:4], refs[4:6], refs[6:8]
+    params, qkv, probs, grad, grad_low, back, part, norm_grad, mixed = refs[8:]
     text = plan.seq - NQ
     gain = params[0, 0:1]
     norm_grad[...] = jnp.zeros_like(norm_grad)
 
-    def one_norm(row, carry):
-        place = pl.ds(pl.multiple_of(row * plan.seq, plan.seq), plan.seq)
-        query_place = pl.ds(pl.multiple_of(row * NQ, NQ), NQ)
-        text_place = pl.ds(pl.multiple_of(row * text, text), text)
-        upstream = jnp.concatenate(
-            [
+    for half in range(2):
+        text_grad, text_mine, text_other = text_grads[half], text_mines[half], text_others[half]
+
+        def one_norm(local, carry, half=half, text_grad=text_grad, text_mine=text_mine,
+                     text_other=text_other):
+            row = half * plan.half_rows + local
+            place, query_place = rows_of(row, plan.seq), rows_of(row, NQ)
+            text_place = rows_of(local, text)
+            upstream = join(
+                0,
                 query_grad[query_place, :]
                 + (query_mine[query_place, :].astype(f32) + query_other[query_place, :].astype(f32)),
                 text_grad[text_place, :]
                 + (text_mine[text_place, :].astype(f32) + text_other[text_place, :].astype(f32)),
-            ],
-            axis=0,
-        )
-        resid = join(0, query_resid[query_place, :], text_resid[text_place, :])
-        found, gain_grad, shift_grad = norm_backward(resid, upstream, gain)
-        grad[place, :] = found
-        grad_low[place, :] = found.astype(bf16)
-        norm_grad[0:1] += gain_grad
-        norm_grad[1:2] += shift_grad
-        return carry
-
-    lax.fori_loop(0, plan.rows, one_norm, 0)
+            )
+            resid = join(0, query_resid[query_place, :], text_resids[half][text_place, :])
+            found, gain_grad, shift_grad = norm_backward(resid, upstream, gain)
+            grad[place, :] = found
+            grad_low[place, :] = found.astype(bf16)
+            norm_grad[0:1] += gain_grad
+            norm_grad[1:2] += shift_grad
+            return carry
+
+        lax.fori_loop(0, plan.half_rows, one_norm, 0)
     matrix = matrix_of(nat, 0, plan.ht, 0, plan.wt, plan.wt, plan.self_out)
     mixed[...] = mm(grad_low[...], matrix, NT).astype(bf16)
 
@@ -584,8 +595,8 @@
 
 
 def self_backward(
-    plan, scale, nat, query_resid, text_resid, query_grad, query_mine, query_other, text_grad,
-    text_mine, text_other, params, qkv, probs,
+    plan, scale, nat, query_resid, text_resids, query_grad, query_mine, query_other, text_grads,
+    text_mines, text_others, params, qkv, probs,
 ):
     tokens, width, half = plan.tokens, plan.width, plan.half
     return pl.pallas_call(
@@ -597,7 +608,7 @@
             jax.ShapeDtypeStruct((tokens, width), bf16),
             jax.ShapeDtypeStruct((2, width), f32),
         ),
-        in_specs=vmem_specs(12),
+        in_specs=vmem_specs(16),
         out_specs=tuple(vmem_specs(5)),
         scratch_shapes=[
             pltpu.VMEM((tokens, half), bf16),
@@ -606,8 +617,8 @@
         cost_estimate=cost(8 * tokens * width * half, 1.2e7),
         name="self_backward",
     )(
-        *pin(nat, query_resid, text_resid, query_grad), query_mine, query_other, *pin(text_grad), text_mine,
-        text_other, params, *pin(qkv, probs),
+        *pin(nat, query_resid, query_grad), query_mine, query_other, *pin(*text_resids, *text_grads),
+        *text_mines, *text_others, params, *pin(qkv, probs),
     )
 
 
@@ -618,13 +629,14 @@
             target[place[spare[0] + number]] = jnp.zeros((TILE, TILE), bf16)
     base = first_block
     for left_at, right_at, right_first, right_width, step in pairs:
-        left, right = sources[left_at], sources[right_at]
-        left_tiles, col_total = left.shape[1] // TILE, right_width // TILE
-
-        def one(chunk, carry, base=base, left=left, right=right, step=step, col_total=col_total,
+        terms = [(sources[a], sources[b]) for a, b in zip(left_at, right_at)]
+        left_tiles, col_total = terms[0][0].shape[1] // TILE, right_width // TILE
+
+        def one(chunk, carry, base=base, terms=terms, step=step, col_total=col_total,
                 right_first=right_first, right_width=right_width):
             cols = pl.ds(pl.multiple_of(chunk * step * TILE, step * TILE), step * TILE)
-            product = mm(left[:, cols], right[:, right_first : right_first + right_width], TN)
+            right_cols = slice(right_first, right_first + right_width)
+            product = sum(mm(left[:, cols], right[:, right_cols], TN) for left, right in terms)
             first = base + chunk * step * col_total
             for row in range(step):
                 for col in range(col_total):
@@ -684,13 +696,13 @@
     flat_back = cotangent.reshape(tokens, width)
     buffer = jax.ShapeDtypeStruct((place.shape[0], TILE, TILE), bf16)
 
-    qkv, self_probs, mixed, query_part, text_part = self_forward(
+    qkv, self_probs, mixed, query_part, *text_parts = self_forward(
         plan, scale, nat, flat_hidden, segment_ids[:, None, :]
     )
     query_other = swap_tensor(query_part)
     image_keys, image_values = image_forward(plan, nat, flat_image)
-    text_part, query_other, image_keys = after((text_part, query_other, image_keys))
-    text_other = swap_tensor(text_part)
+    text_parts[0], query_other, image_keys = after((text_parts[0], query_other, image_keys))
+    text_others = [swap_tensor(text_parts[0]), None]
     query_first, first_query, low_query, cross_queries, cross_probs, looked, part_two = (
         cross_forward(
             plan, scale, nat, flat_hidden, query_part, query_other, norm_params, image_keys,
@@ -698,36 +710,56 @@
         )
     )
     other_two = swap_tensor(part_two)
+    text_parts[1], text_others[0], other_two = after((text_parts[1], text_others[0], other_two))
+    text_others[1] = swap_tensor(text_parts[1])
+    texts_out = [
+        text_forward(plan, 0, nat, flat_hidden, text_parts[0], text_others[0], norm_params), None
+    ]
+    other_text = [swap_tensor(texts_out[0][-1]), None]
+    other_two, _ = after((other_two, texts_out[0][-1]))
     second_sum, second, low_second, query_gated, query_slope, part_query = query_forward(
         plan, nat, first_query, part_two, other_two, norm_params
     )
     other_query = swap_tensor(part_query)
-    text_other, part_query = after((text_other, part_query))
-    text_first, first_text, low_text, text_gated, text_slope, part_text = text_forward(
-        plan, nat, flat_hidden, text_part, text_other, norm_params
-    )
-    other_query, part_text = after((other_query, part_text))
-    other_text = swap_tensor(part_text)
+    text_others[1], part_query = after((text_others[1], part_query))
+    texts_out[1] = text_forward(
+        plan, 1, nat, flat_hidden, text_parts[1], text_others[1], norm_params
+    )
+    other_text[1] = swap_tensor(texts_out[1][-1])
+    text_first, first_text, low_text, text_gated, text_slope, part_text = zip(*texts_out)
+
+    def text_backward(number):
+        return feed_backward(
+            plan, plan.text_first, (number * plan.half_rows, plan.half_rows), NQ, 3, nat,
+            first_text[number], part_text[number], other_text[number], flat_back, norm_params,
+            text_slope[number],
+        )
+
+    other_text[0], _ = after((other_text[0], part_text[1]))
+    texts_back = [text_backward(0), None]
+    other_four_text = [swap_tensor(texts_back[0][4]), None]
+    other_query, _ = after((other_query, texts_back[0][4]))
     out_query, third_query, third_query_low, before_query, part_four_query, norm_query = (
         feed_backward(
-            plan, plan.query_first, 0, 2, nat, second, part_query, other_query, flat_back,
-            norm_params, query_slope,
+            plan, plan.query_first, (0, rows), 0, 2, nat, second, part_query, other_query,
+            flat_back, norm_params, query_slope,
         )
     )
     other_four_query = swap_tensor(part_four_query)
-    feed_pairs = [(0, 1, 0, plan.hidden, 6), (2, 3, 0, width, 6)]
+    other_text[1], _ = after((other_text[1], part_four_query))
+    texts_back[1] = text_backward(1)
+    other_four_text[1] = swap_tensor(texts_back[1][4])
+    out_text, third_text, third_text_low, before_text, part_four_text, norm_text = zip(*texts_back)
+    feed_pairs = [((0,), (1,), 0, plan.hidden, 6), ((2,), (3,), 0, width, 6)]
+    before_query, _ = after((before_query, part_four_text[1]))
     buffer = grad_blocks(
         buffer, place, plan.query_first, [low_second, before_query, query_gated, third_query_low],
         feed_pairs, 4 * learned * width * plan.hidden,
         spare=(plan.block_count, place.shape[0] - plan.block_count),
     )
-    other_text, buffer = after((other_text, buffer))
-    out_text, third_text, third_text_low, before_text, part_four_text, norm_text = feed_backward(
-        plan, plan.text_first, NQ, 3, nat, first_text, part_text, other_text, flat_back,
-        norm_params, text_slope,
-    )
-    other_four_query, part_four_text = after((other_four_query, part_four_text))
-    other_four_text = swap_tensor(part_four_text)
+    other_four_query, other_four_text[0], buffer = after(
+        (other_four_query, other_four_text[0], buffer)
+    )
     second_grad, cross_low, query_back, key_back, value_back, part_five, norm_second = (
         cross_backward(
             plan, scale, nat, second_sum, third_query, part_four_query, other_four_query,
@@ -737,49 +769,54 @@
     other_five = swap_tensor(part_five)
     buffer, part_five = after((buffer, part_five))
     buffer = grad_blocks(
-        buffer, place, plan.text_first, [low_text, before_text, text_gated, third_text_low],
-        feed_pairs, 4 * texts * width * plan.hidden,
+        buffer, place, plan.text_first, [*low_text, *before_text, *text_gated, *third_text_low],
+        [((0, 1), (2, 3), 0, plan.hidden, 6), ((4, 5), (6, 7), 0, width, 6)],
+        4 * texts * width * plan.hidden,
     )
     cross_flops = 2 * rows * plan.keys * plan.image_width * half
     buffer = grad_blocks(
         buffer, place, plan.cross_first, [low_query, query_back, flat_image, key_back],
-        [(0, 1, 0, half, 6), (2, 3, 0, half, 11)], cross_flops,
-    )
-    other_four_text, buffer = after((other_four_text, buffer))
+        [((0,), (1,), 0, half, 6), ((2,), (3,), 0, half, 11)], cross_flops,
+    )
+    other_four_text[1], buffer = after((other_four_text[1], buffer))
     first_grad, self_low, self_back, part_six, norm_first = self_backward(
         plan, scale, nat, query_first, text_first, second_grad, part_five, other_five, third_text,
         part_four_text, other_four_text, norm_params, qkv, self_probs,
     )
     other_six = swap_tensor(part_six)
-    norm_steps = sum_steps(jnp.stack([norm_first, norm_second, norm_query, norm_text]))
+    norm_steps = sum_steps(jnp.stack([norm_first, norm_second, norm_query, norm_text[0] + norm_text[1]]))
     norms = next(norm_steps)
     buffer, part_six = after((buffer, part_six))
     buffer = grad_blocks(
         buffer, place, plan.image_first + plan.cross, [flat_image, value_back],
-        [(0, 1, 0, half, 11)], cross_flops,
+        [((0,), (1,), 0, half, 11)], cross_flops,
     )
     buffer, norms = after((buffer, norms))
     norms = norm_steps.send(norms)
     buffer = grad_blocks(
-        buffer, place, plan.cross_out, [looked, cross_low], [(0, 1, 0, width, 3)],
+        buffer, place, plan.cross_out, [looked, cross_low], [((0,), (1,), 0, width, 3)],
         2 * learned * width * half,
     )
     buffer, norms = after((buffer, norms))
     norms = norm_steps.send(norms)
     buffer = grad_blocks(
         buffer, place, plan.self_first, [flat_hidden, self_back],
-        [(0, 1, 0, half, 6), (0, 1, half, half, 6), (0, 1, 2 * half, half, 6)],
+        [((0,), (1,), 0, half, 6), ((0,), (1,), half, half, 6), ((0,), (1,), 2 * half, half, 6)],
         6 * tokens * width * half,
     )
-    buffer, norms, other_six = after((buffer, norms, other_six))
+    buffer, norms = after((buffer, norms))
     norms = norm_steps.send(norms)
     buffer = grad_blocks(
-        buffer, place, plan.self_out, [mixed, self_low], [(0, 1, 0, width, 3)],
+        buffer, place, plan.self_out, [mixed, self_low], [((0,), (1,), 0, width, 3)],
         2 * tokens * width * half,
     )
-    buffer, norms = after((buffer, norms))
+    buffer, norms, other_six = after((buffer, norms, other_six))
     output_rows = jnp.concatenate(
-        [out_query.reshape(rows, NQ, width), out_text.reshape(rows, seq - NQ, width)], axis=1
+        [
+            out_query.reshape(rows, NQ, width),
+            jnp.concatenate(out_text, axis=0).reshape(rows, seq - NQ, width),
+        ],
+        axis=1,
     )
     return (output_rows, first_grad, part_six, other_six, buffer, norms)
 
@@ -1101,7 +1138,7 @@
         loop_groups(groups, GROUPS_AT_ONCE, one)
 
 
-GROUPS_AT_ONCE = 4
+GROUPS_AT_ONCE = 8
 
 
 def optimizer_slots(first, count, inputs, outputs, grams, products):
@@ -1216,7 +1253,7 @@
             outputs[6][first + offset] = found[2 * offset]
             outputs[7][first + offset] = found[2 * offset + 1]
 
-    loop_groups(slots, 4, finish)
+    loop_groups(slots, 8, finish)
     for copy in stores[6:]:
         copy.start()
     for copy in stores:

time: 301 us -> 292 us (0.970)
  waiting for transfers between devices: 118 us -> 99.4 us
  starting transfers between devices: 66.1 us -> 72.3 us
    ppermute x9 -> x12, waiting for transfers between devices: 29.3 us -> 10.7 us  [swap_tensor(): return lax.ppermute(part, 'tensor', [(0, 1), (1, 0)])]
    ppermute x9 -> x12, starting transfers between devices: 9.86 us -> 16.3 us  [swap_tensor(): return lax.ppermute(part, 'tensor', [(0, 1), (1, 0)])]
    pallas_call x3 -> x5, Pallas kernels: 14.4 us -> 18.2 us  [the longest x3 11.6 us: feed_backward(): pl.pallas_call(functools.partial(feed_backward_body, plan, first_block, r...]
  transfers between devices with their start and end apart: 60 -> 63, of which waited for: 38 -> 36; matrix products, arithmetic and copies ran while one was open for 4% -> 4% of each run, Pallas kernels for 17% -> 19%
where the time goes in v9:
time: 292 us; the launch traced here: 288 us
  waiting for transfers between devices  99.4 us (34%)
  Pallas kernels  95.9 us (33%)
  starting transfers between devices  72.3 us (25%)
  local copies, waits for them, and re-layouts  10.8 us (4%)
  other arithmetic  7.37 us (3%)
    ppermute x14, waiting for transfers between devices, scatter_ring(): held[number] = lax.ppermute(summed, 'dp', RING_PAIRS)  42.5 us
    ppermute x14, waiting for transfers between devices, gather_ring(): held = [lax.ppermute(piece, 'dp', RING_PAIRS) for piece in held]  37.3 us
    pallas_call x1, Pallas kernels, optimizer(): pl.pallas_call(functools.partial(optimizer_body, padded, counts), out_sha...  32.9 us
    ppermute x14, starting transfers between devices, gather_ring(): held = [lax.ppermute(piece, 'dp', RING_PAIRS) for piece in held]  26 us
    ppermute x14, starting transfers between devices, scatter_ring(): held[number] = lax.ppermute(summed, 'dp', RING_PAIRS)  22.7 us
    ppermute x12, starting transfers between devices, swap_tensor(): return lax.ppermute(part, 'tensor', [(0, 1), (1, 0)])  16.3 us
    pallas_call x7, Pallas kernels, grad_blocks(): pl.pallas_call(functools.partial(grad_blocks_body, first_block, pairs, le...  15.9 us
    pallas_call x3, Pallas kernels, feed_backward(): pl.pallas_call(functools.partial(feed_backward_body, plan, first_block, r...  11.6 us
  transfers between devices with their start and end apart: 63, of which 36 were waited for; matrix products, arithmetic and copies ran while one was open for 4% of the time, Pallas kernels for 19%

profile of v9, /device:TPU:0, one launch (start us, length us, event | category | flops | bytes accessed | tf_op | source)
XLA Modules:
  0.0 287.5 jit_solution(17904089916742607793)
XLA Ops:
  7.2 5.1 %collective-permute-done.5.refs_3_ = bf16[15,128,128]{2,1,0:T(8,128)(2,1)S(1)} collective-permute-done((bf16[15,128,128]{2,1,0:T(8,128)(2,1)S(1)}, bf16[15,128,128]{2,1,0:T(8,128)(2,1)S(1)}, u32[]{:S(2)}, u32[]{:S(2)}) %collective-permute-start.5) | collective-permute-done | bytes 491552 | tf_op jit(solution)/shard_map/ppermute | solution.py:948
  24.5 4.9 %block_indices.1 = (s32[464]{0:T(512)S(1)}, s32[464]{0:T(512)S(1)}) custom-call(s32[1]{0:T(128)} %bitcast.1.device, s32[464]{0:T(512)S(1)} %bitcast.49, s32[16,464]{1,0:T(8,128)S(1)} %copy-done.17, s32[16,464]{1,0:T(8,128)S(1)} %copy-done.18), custom_call_target="tpu_custom_call" | custom-call | tf_op jit(solution)/shard_map/block_indices/pallas_call | solution.py:923
  40.3 3.2 %collective-permute-done.16.refs_1_ = bf16[15,128,128]{2,1,0:T(8,128)(2,1)S(1)} collective-permute-done((bf16[15,128,128]{2,1,0:T(8,128)(2,1)S(1)}, bf16[15,128,128]{2,1,0:T(8,128)(2,1)S(1)}, u32[]{:S(2)}, u32[]{:S(2)}) %collective-permute-start.16) | collective-permute-done | bytes 491552 | tf_op jit(solution)/shard_map/ppermute | solution.py:948
  45.1 3.3 %collective-permute-done.3.refs_0_ = bf16[14,128,128]{2,1,0:T(8,128)(2,1)S(1)} collective-permute-done((bf16[14,128,128]{2,1,0:T(8,128)(2,1)S(1)}, bf16[14,128,128]{2,1,0:T(8,128)(2,1)S(1)}, u32[]{:S(2)}, u32[]{:S(2)}) %collective-permute-start.3) | collective-permute-done | bytes 458784 | tf_op jit(solution)/shard_map/ppermute | solution.py:948
  60.2 3.7 %collective-permute-done.23.refs_1_ = bf16[15,128,128]{2,1,0:T(8,128)(2,1)S(1)} collective-permute-done((bf16[15,128,128]{2,1,0:T(8,128)(2,1)S(1)}, bf16[15,128,128]{2,1,0:T(8,128)(2,1)S(1)}, u32[]{:S(2)}, u32[]{:S(2)}) %collective-permute-start.23) | collective-permute-done | bytes 491552 | tf_op jit(solution)/shard_map/ppermute | solution.py:948
  70.5 3.5 %collective-permute-done.26.refs_1_ = bf16[15,128,128]{2,1,0:T(8,128)(2,1)S(1)} collective-permute-done((bf16[15,128,128]{2,1,0:T(8,128)(2,1)S(1)}, bf16[15,128,128]{2,1,0:T(8,128)(2,1)S(1)}, u32[]{:S(2)}, u32[]{:S(2)}) %collective-permute-start.26) | collective-permute-done | bytes 491552 | tf_op jit(solution)/shard_map/ppermute | solution.py:948
  74.8 4.2 %collective-permute-done.22.refs_0_ = bf16[14,128,128]{2,1,0:T(8,128)(2,1)S(1)} collective-permute-done((bf16[14,128,128]{2,1,0:T(8,128)(2,1)S(1)}, bf16[14,128,128]{2,1,0:T(8,128)(2,1)S(1)}, u32[]{:S(2)}, u32[]{:S(2)}) %collective-permute-start.22) | collective-permute-done | bytes 458784 | tf_op jit(solution)/shard_map/ppermute | solution.py:948
  81.5 3.5 %self_forward.1 = (bf16[3,512,384]{2,1,0:T(8,128)(2,1)S(1)}, f32[4,3,256,128]{3,2,1,0:T(8,128)S(1)}, bf16[512,384]{1,0:T(8,128)(2,1)S(1)}, bf16[128,768]{1,0:T(8...) custom-call(bf16[464,128,128]{2,1,0:T(8,128)(2,1)S(1)} %place_blocks.9.nat, ...), custom_call_target="tpu_custom_call" | custom-call | flops 1 | bytes 1 | tf_op jit(solution)/shard_map/self_forward/pallas_call | solution.py:228
  88.0 3.5 %image_forward.1 = (bf16[1088,384]{1,0:T(8,128)(2,1)S(1)}, bf16[1088,384]{1,0:T(8,128)(2,1)S(1)}) custom-call(bf16[464,128,128]{2,1,0:T(8,128)(2,1)S(1)} %place_blocks.9.nat, bf16[1088,1408]{1,0:T(8,128)(2,1)S(1)} %bitcast.30), custom_call_target="tpu_custom_call" | custom-call | flops 1 | bytes 1 | tf_op jit(solution)/shard_map/image_forward/pallas_call | solution.py:254
  97.3 8.2 %collective-permute-done.31.other = bf16[128,768]{1,0:T(8,128)(2,1)S(1)} collective-permute-done((bf16[128,768]{1,0:T(8,128)(2,1)S(1)}, bf16[128,768]{1,0:T(8,128)(2,1)S(1)}, u32[]{:S(2)}, u32[]{:S(2)}) %collective-permute-start.31) | collective-permute-done | bytes 196640 | tf_op jit(solution)/shard_map/ppermute | solution.py:670
  107.0 3.3 %text_forward.2 = (f32[192,768]{1,0:T(8,128)S(1)}, f32[192,768]{1,0:T(8,128)S(1)}, bf16[192,768]{1,0:T(8,128)(2,1)S(1)}, bf16[192,1536]{1,0:T(8,128)(2,1)S(1)}, ...) custom-call(bf16[464,128,128]{2,1,0:T(8,128)(2,1)S(1)} %place_blocks.9.nat, bf16[512,768]{1,0:T(8,128)(2,1)S(1)} %bitcast.35, ...), custom_call_target="tpu_custom_call" | custom-call | flops 1 | bytes 1 | tf_op jit(solution)/shard_map/text_forward/pallas_call | solution.py:385
  115.2 3.3 %text_forward.3 = (f32[192,768]{1,0:T(8,128)S(1)}, f32[192,768]{1,0:T(8,128)S(1)}, bf16[192,768]{1,0:T(8,128)(2,1)S(1)}, bf16[192,1536]{1,0:T(8,128)(2,1)S(1)}, ...) custom-call(bf16[464,128,128]{2,1,0:T(8,128)(2,1)S(1)} %place_blocks.9.nat, bf16[512,768]{1,0:T(8,128)(2,1)S(1)} %bitcast.36, ...), custom_call_target="tpu_custom_call" | custom-call | flops 1 | bytes 1 | tf_op jit(solution)/shard_map/text_forward/pallas_call | solution.py:385
  120.7 3.7 %feed_backward.3 = (bf16[192,768]{1,0:T(8,128)(2,1)S(1)}, f32[192,768]{1,0:T(8,128)S(1)}, bf16[192,768]{1,0:T(8,128)(2,1)S(1)}, bf16[192,1536]{1,0:T(8,128)(2,1)...) custom-call(bf16[464,128,128]{2,1,0:T(8,128)(2,1)S(1)} %place_blocks.9.nat, ...), custom_call_target="tpu_custom_call" | custom-call | flops 1 | bytes 1 | tf_op jit(solution)/shard_map/feed_backward/pallas_call | solution.py:464
  127.8 4.1 %feed_backward.4 = (bf16[128,768]{1,0:T(8,128)(2,1)S(1)}, f32[128,768]{1,0:T(8,128)S(1)}, bf16[128,768]{1,0:T(8,128)(2,1)S(1)}, bf16[128,1536]{1,0:T(8,128)(2,1)...) custom-call(bf16[464,128,128]{2,1,0:T(8,128)(2,1)S(1)} %place_blocks.9.nat, ...), custom_call_target="tpu_custom_call" | custom-call | flops 1 | bytes 1 | tf_op jit(solution)/shard_map/feed_backward/pallas_call | solution.py:464
  132.6 3.7 %feed_backward.5 = (bf16[192,768]{1,0:T(8,128)(2,1)S(1)}, f32[192,768]{1,0:T(8,128)S(1)}, bf16[192,768]{1,0:T(8,128)(2,1)S(1)}, bf16[192,1536]{1,0:T(8,128)(2,1)...) custom-call(bf16[464,128,128]{2,1,0:T(8,128)(2,1)S(1)} %place_blocks.9.nat, ...), custom_call_target="tpu_custom_call" | custom-call | flops 1 | bytes 1 | tf_op jit(solution)/shard_map/feed_backward/pallas_call | solution.py:464
  146.7 3.7 %grad_blocks.8.refs_4_ = bf16[464,128,128]{2,1,0:T(8,128)(2,1)S(1)} custom-call(s32[464]{0:T(512)S(1)} %get-tuple-element.183.place, bf16[192,768]{1,0:T(8,128)(2,1)S(1)} %get-tuple-element.205.refs_0_, bf16[192,768]{1,0:T(8,128)(2,1)S(1)} %get-tuple-element.206.refs_1_, ...), custom_call_target="tpu_custom_call", output_to_operand_aliasing={{}: (9, {})} | custom-call | flops 1 | bytes 1 | tf_op jit(solution)/shard_map/grad_blocks/pallas_call | solution.py:654
  153.3 4.9 %self_backward.1 = (f32[512,768]{1,0:T(8,128)S(1)}, bf16[512,768]{1,0:T(8,128)(2,1)S(1)}, bf16[512,1152]{1,0:T(8,128)(2,1)S(1)}, bf16[512,768]{1,0:T(8,128)(2,1)S(1)}, f32[2,768]{1,0:T(2,128)S(1)}) custom-call(bf16[464,128,128]{2,1,0:T(8,128)(2,1)S(1)} %place_blocks.9.nat, f32[128,768]{1,0:T(8,128)S(1)} %copy-done.10, ...), custom_call_target="tpu_custom_call" | custom-call | flops 1 | bytes 1 | tf_op jit(solution)/shard_map/self_backward/pallas_call | solution.py:602
  173.9 3.9 %collective-permute-done.45 = bf16[58,128,128]{2,1,0:T(8,128)(2,1)S(1)} collective-permute-done((bf16[58,128,128]{2,1,0:T(8,128)(2,1)S(1)}, bf16[58,128,128]{2,1,0:T(8,128)(2,1)S(1)}, u32[]{:S(2)}, u32[]{:S(2)}) %collective-permute-start.45) | collective-permute-done | bytes 1900576 | tf_op jit(solution)/shard_map/ppermute | solution.py:984
  182.2 5.0 %collective-permute-done.56 = bf16[15,128,128]{2,1,0:T(8,128)(2,1)S(1)} collective-permute-done((bf16[15,128,128]{2,1,0:T(8,128)(2,1)S(1)}, bf16[15,128,128]{2,1,0:T(8,128)(2,1)S(1)}, u32[]{:S(2)}, u32[]{:S(2)}) %collective-permute-start.56) | collective-permute-done | bytes 491552 | tf_op jit(solution)/shard_map/ppermute | solution.py:997
  193.9 3.4 %collective-permute-done.57 = bf16[15,128,128]{2,1,0:T(8,128)(2,1)S(1)} collective-permute-done((bf16[15,128,128]{2,1,0:T(8,128)(2,1)S(1)}, bf16[15,128,128]{2,1,0:T(8,128)(2,1)S(1)}, u32[]{:S(2)}, u32[]{:S(2)}) %collective-permute-start.57) | collective-permute-done | bytes 491552 | tf_op jit(solution)/shard_map/ppermute | solution.py:997
  204.1 3.5 %collective-permute-done.58 = bf16[15,128,128]{2,1,0:T(8,128)(2,1)S(1)} collective-permute-done((bf16[15,128,128]{2,1,0:T(8,128)(2,1)S(1)}, bf16[15,128,128]{2,1,0:T(8,128)(2,1)S(1)}, u32[]{:S(2)}, u32[]{:S(2)}) %collective-permute-start.58) | collective-permute-done | bytes 491552 | tf_op jit(solution)/shard_map/ppermute | solution.py:997
  214.3 3.5 %collective-permute-done.59 = bf16[15,128,128]{2,1,0:T(8,128)(2,1)S(1)} collective-permute-done((bf16[15,128,128]{2,1,0:T(8,128)(2,1)S(1)}, bf16[15,128,128]{2,1,0:T(8,128)(2,1)S(1)}, u32[]{:S(2)}, u32[]{:S(2)}) %collective-permute-start.59) | collective-permute-done | bytes 491552 | tf_op jit(solution)/shard_map/ppermute | solution.py:997
  224.5 3.4 %collective-permute-done.60 = bf16[15,128,128]{2,1,0:T(8,128)(2,1)S(1)} collective-permute-done((bf16[15,128,128]{2,1,0:T(8,128)(2,1)S(1)}, bf16[15,128,128]{2,1,0:T(8,128)(2,1)S(1)}, u32[]{:S(2)}, u32[]{:S(2)}) %collective-permute-start.60) | collective-permute-done | bytes 491552 | tf_op jit(solution)/shard_map/ppermute | solution.py:997
  254.2 32.9 %optimizer.1 = (f32[29,128,128]{2,1,0:T(8,128)}, bf16[29,128,128]{2,1,0:T(8,128)(2,1)}, f32[29,128,128]{2,1,0:T(8,128)}, f32[29,128,128]{2,1,0:T(8,128)}, f32[29...) custom-call(bf16[14,128,128]{2,1,0:T(8,128)(2,1)} %slice.119.refs_0_, ...), custom_call_target="tpu_custom_call" | custom-call | tf_op jit(solution)/shard_map/optimizer/pallas_call | solution.py:1272
  (214 shorter events, 160.2 us)
Async XLA Ops:
  5.5 11.7 %collective-permute-start = (bf16[14,128,128]{2,1,0:T(8,128)(2,1)S(1)}, bf16[14,128,128]{2,1,0:T(8,128)(2,1)}, u32[]{:S(2)}, u32[]{:S(2)}) collective-permute-start(bf16[14,128,128]{2,1,0:T(8,128)(2,1)S(1)} %slice.152), channel_id=1, source_target_pairs={{0,8},{2,6},{8,16},{10,2},{16,24},{18,10},{24,28},{26,18},{28,20},... | collective-permute-start | bytes 1376264 | tf_op jit(solution)/shard_map/ppermute | solution.py:948
  12.2 10.2 %collective-permute-start.9 = (bf16[15,128,128]{2,1,0:T(8,128)(2,1)S(1)}, bf16[15,128,128]{2,1,0:T(8,128)(2,1)S(1)}, u32[]{:S(2)}, u32[]{:S(2)}) collective-permute-start(bf16[15,128,128]{2,1,0:T(8,128)(2,1)S(1)} %collective-permute-done.5.refs_3_), channel_id=1, source_target_pairs={{0,8},{2,6},{8,16},{10,2},{16,24},{18,10},{24,28},{26,18},{28,20},... | collective-permute-start | bytes 1474568 | tf_op jit(solution)/shard_map/ppermute | solution.py:948
  17.2 12.2 %collective-permute-start.1 = (bf16[14,128,128]{2,1,0:T(8,128)(2,1)}, bf16[14,128,128]{2,1,0:T(8,128)(2,1)}, u32[]{:S(2)}, u32[]{:S(2)}) collective-permute-start(bf16[14,128,128]{2,1,0:T(8,128)(2,1)} %collective-permute-done.refs_2_), channel_id=1, source_target_pairs={{0,8},{2,6},{8,16},{10,2},{16,24},{18,10},{24,28},{26,18},{28,20},... | collective-permute-start | bytes 1376264 | tf_op jit(solution)/shard_map/ppermute | solution.py:948
  19.3 20.5 %collective-permute-start.4 = (bf16[29,128,128]{2,1,0:T(8,128)(2,1)S(1)}, bf16[29,128,128]{2,1,0:T(8,128)(2,1)S(1)}, u32[]{:S(2)}, u32[]{:S(2)}) collective-permute-start(bf16[29,128,128]{2,1,0:T(8,128)(2,1)S(1)} %bitcast_convert_fusion.refs_0_), channel_id=1, source_target_pairs={{0,2},{2,0},{4,6},{6,4},{8,10},{10,8},{12,14},{14,12},{16,18},{18,... | collective-permute-start | bytes 2850824 | tf_op jit(solution)/shard_map/ppermute | solution.py:943
  32.6 10.9 %collective-permute-start.16 = (bf16[15,128,128]{2,1,0:T(8,128)(2,1)S(1)}, bf16[15,128,128]{2,1,0:T(8,128)(2,1)S(1)}, u32[]{:S(2)}, u32[]{:S(2)}) collective-permute-start(bf16[15,128,128]{2,1,0:T(8,128)(2,1)S(1)} %collective-permute-done.12.refs_5_), channel_id=1, source_target_pairs={{0,8},{2,6},{8,16},{10,2},{16,24},{18,10},{24,28},{26,18},{28,20},... | collective-permute-start | bytes 1474568 | tf_op jit(solution)/shard_map/ppermute | solution.py:948
  34.7 10.4 %collective-permute-start.7 = (bf16[15,128,128]{2,1,0:T(8,128)(2,1)S(1)}, bf16[15,128,128]{2,1,0:T(8,128)(2,1)S(1)}, u32[]{:S(2)}, u32[]{:S(2)}) collective-permute-start(bf16[15,128,128]{2,1,0:T(8,128)(2,1)S(1)} %collective-permute-done.5.refs_3_), channel_id=1, source_target_pairs={{0,2},{2,0},{4,6},{6,4},{8,10},{10,8},{12,14},{14,12},{16,18},{18,... | collective-permute-start | bytes 1474568 | tf_op jit(solution)/shard_map/ppermute | solution.py:959
  38.2 10.2 %collective-permute-start.3 = (bf16[14,128,128]{2,1,0:T(8,128)(2,1)S(1)}, bf16[14,128,128]{2,1,0:T(8,128)(2,1)S(1)}, u32[]{:S(2)}, u32[]{:S(2)}) collective-permute-start(bf16[14,128,128]{2,1,0:T(8,128)(2,1)S(1)} %collective-permute-done.2.refs_4_), channel_id=1, source_target_pairs={{0,8},{2,6},{8,16},{10,2},{16,24},{18,10},{24,28},{26,18},{28,20},... | collective-permute-start | bytes 1376264 | tf_op jit(solution)/shard_map/ppermute | solution.py:948
  39.8 11.5 %collective-permute-start.11 = (bf16[15,128,128]{2,1,0:T(8,128)(2,1)S(1)}, bf16[15,128,128]{2,1,0:T(8,128)(2,1)S(1)}, u32[]{:S(2)}, u32[]{:S(2)}) collective-permute-start(bf16[15,128,128]{2,1,0:T(8,128)(2,1)S(1)} %collective-permute-done.9.refs_1_), channel_id=1, source_target_pairs={{0,2},{2,0},{4,6},{6,4},{8,10},{10,8},{12,14},{14,12},{16,18},{18,... | collective-permute-start | bytes 1474568 | tf_op jit(solution)/shard_map/ppermute | solution.py:959
  43.5 10.2 %collective-permute-start.19 = (bf16[15,128,128]{2,1,0:T(8,128)(2,1)S(1)}, bf16[15,128,128]{2,1,0:T(8,128)(2,1)S(1)}, u32[]{:S(2)}, u32[]{:S(2)}) collective-permute-start(bf16[15,128,128]{2,1,0:T(8,128)(2,1)S(1)} %collective-permute-done.16.refs_1_), channel_id=1, source_target_pairs={{0,8},{2,6},{8,16},{10,2},{16,24},{18,10},{24,28},{26,18},{28,20},... | collective-permute-start | bytes 1474568 | tf_op jit(solution)/shard_map/ppermute | solution.py:948
  45.1 10.2 %collective-permute-start.14 = (bf16[15,128,128]{2,1,0:T(8,128)(2,1)S(1)}, bf16[15,128,128]{2,1,0:T(8,128)(2,1)S(1)}, u32[]{:S(2)}, u32[]{:S(2)}) collective-permute-start(bf16[15,128,128]{2,1,0:T(8,128)(2,1)S(1)} %collective-permute-done.12.refs_5_), channel_id=1, source_target_pairs={{0,2},{2,0},{4,6},{6,4},{8,10},{10,8},{12,14},{14,12},{16,18},{18,... | collective-permute-start | bytes 1474568 | tf_op jit(solution)/shard_map/ppermute | solution.py:959
  53.7 10.2 %collective-permute-start.23 = (bf16[15,128,128]{2,1,0:T(8,128)(2,1)S(1)}, bf16[15,128,128]{2,1,0:T(8,128)(2,1)S(1)}, u32[]{:S(2)}, u32[]{:S(2)}) collective-permute-start(bf16[15,128,128]{2,1,0:T(8,128)(2,1)S(1)} %collective-permute-done.19.refs_5_), channel_id=1, source_target_pairs={{0,8},{2,6},{8,16},{10,2},{16,24},{18,10},{24,28},{26,18},{28,20},... | collective-permute-start | bytes 1474568 | tf_op jit(solution)/shard_map/ppermute | solution.py:948
  55.3 10.2 %collective-permute-start.21 = (bf16[15,128,128]{2,1,0:T(8,128)(2,1)S(1)}, bf16[15,128,128]{2,1,0:T(8,128)(2,1)S(1)}, u32[]{:S(2)}, u32[]{:S(2)}) collective-permute-start(bf16[15,128,128]{2,1,0:T(8,128)(2,1)S(1)} %collective-permute-done.19.refs_5_), channel_id=1, source_target_pairs={{0,2},{2,0},{4,6},{6,4},{8,10},{10,8},{12,14},{14,12},{16,18},{18,... | collective-permute-start | bytes 1474568 | tf_op jit(solution)/shard_map/ppermute | solution.py:959
  63.9 10.2 %collective-permute-start.26 = (bf16[15,128,128]{2,1,0:T(8,128)(2,1)S(1)}, bf16[15,128,128]{2,1,0:T(8,128)(2,1)S(1)}, u32[]{:S(2)}, u32[]{:S(2)}) collective-permute-start(bf16[15,128,128]{2,1,0:T(8,128)(2,1)S(1)} %collective-permute-done.23.refs_1_), channel_id=1, source_target_pairs={{0,8},{2,6},{8,16},{10,2},{16,24},{18,10},{24,28},{26,18},{28,20},... | collective-permute-start | bytes 1474568 | tf_op jit(solution)/shard_map/ppermute | solution.py:948
  93.0 12.4 %collective-permute-start.30 = (bf16[192,768]{1,0:T(8,128)(2,1)S(1)}, bf16[192,768]{1,0:T(8,128)(2,1)S(1)}, u32[]{:S(2)}, u32[]{:S(2)}) collective-permute-start(bf16[192,768]{1,0:T(8,128)(2,1)S(1)} %get-tuple-element.156.mine), channel_id=1, source_target_pairs={{0,1},{1,0},{2,3},{3,2},{4,5},{5,4},{6,7},{7,6},{8,9},{9,8},{10,11... | collective-permute-start | bytes 884744 | tf_op jit(solution)/shard_map/ppermute | solution.py:670
  110.3 10.4 %collective-permute-start.34 = (bf16[192,768]{1,0:T(8,128)(2,1)S(1)}, bf16[192,768]{1,0:T(8,128)(2,1)S(1)}, u32[]{:S(2)}, u32[]{:S(2)}) collective-permute-start(bf16[192,768]{1,0:T(8,128)(2,1)S(1)} %get-tuple-element.159.mine), channel_id=1, source_target_pairs={{0,1},{1,0},{2,3},{3,2},{4,5},{5,4},{6,7},{7,6},{8,9},{9,8},{10,11... | collective-permute-start | bytes 884744 | tf_op jit(solution)/shard_map/ppermute | solution.py:670
  113.6 14.2 %collective-permute-start.33 = (bf16[128,768]{1,0:T(8,128)(2,1)S(1)}, bf16[128,768]{1,0:T(8,128)(2,1)S(1)}, u32[]{:S(2)}, u32[]{:S(2)}) collective-permute-start(bf16[128,768]{1,0:T(8,128)(2,1)S(1)} %get-tuple-element.164.mine), channel_id=1, source_target_pairs={{0,1},{1,0},{2,3},{3,2},{4,5},{5,4},{6,7},{7,6},{8,9},{9,8},{10,11... | collective-permute-start | bytes 589832 | tf_op jit(solution)/shard_map/ppermute | solution.py:670
  118.5 14.1 %collective-permute-start.35 = (bf16[192,768]{1,0:T(8,128)(2,1)S(1)}, bf16[192,768]{1,0:T(8,128)(2,1)S(1)}, u32[]{:S(2)}, u32[]{:S(2)}) collective-permute-start(bf16[192,768]{1,0:T(8,128)(2,1)S(1)} %get-tuple-element.167.mine), channel_id=1, source_target_pairs={{0,1},{1,0},{2,3},{3,2},{4,5},{5,4},{6,7},{7,6},{8,9},{9,8},{10,11... | collective-permute-start | bytes 884744 | tf_op jit(solution)/shard_map/ppermute | solution.py:670
  125.3 16.5 %collective-permute-start.37 = (bf16[192,768]{1,0:T(8,128)(2,1)S(1)}, bf16[192,768]{1,0:T(8,128)(2,1)S(1)}, u32[]{:S(2)}, u32[]{:S(2)}) collective-permute-start(bf16[192,768]{1,0:T(8,128)(2,1)S(1)} %get-tuple-element.170.refs_4_), channel_id=1, source_target_pairs={{0,1},{1,0},{2,3},{3,2},{4,5},{5,4},{6,7},{7,6},{8,9},{9,8},{10,11... | collective-permute-start | bytes 884744 | tf_op jit(solution)/shard_map/ppermute | solution.py:670
  136.4 16.9 %collective-permute-start.39 = (bf16[192,768]{1,0:T(8,128)(2,1)S(1)}, bf16[192,768]{1,0:T(8,128)(2,1)S(1)}, u32[]{:S(2)}, u32[]{:S(2)}) collective-permute-start(bf16[192,768]{1,0:T(8,128)(2,1)S(1)} %get-tuple-element.186.refs_5_), channel_id=1, source_target_pairs={{0,1},{1,0},{2,3},{3,2},{4,5},{5,4},{6,7},{7,6},{8,9},{9,8},{10,11... | collective-permute-start | bytes 884744 | tf_op jit(solution)/shard_map/ppermute | solution.py:670
  158.3 15.5 %collective-permute-start.44 = (bf16[512,768]{1,0:T(8,128)(2,1)S(1)}, bf16[512,768]{1,0:T(8,128)(2,1)S(1)}, u32[]{:S(2)}, u32[]{:S(2)}) collective-permute-start(bf16[512,768]{1,0:T(8,128)(2,1)S(1)} %get-tuple-element.220), channel_id=1, source_target_pairs={{0,1},{1,0},{2,3},{3,2},{4,5},{5,4},{6,7},{7,6},{8,9},{9,8},{10,11... | collective-permute-start | bytes 2359304 | tf_op jit(solution)/shard_map/ppermute | solution.py:670
  180.1 12.0 %collective-permute-start.49 = (bf16[14,128,128]{2,1,0:T(8,128)(2,1)S(1)}, bf16[14,128,128]{2,1,0:T(8,128)(2,1)S(1)}, u32[]{:S(2)}, u32[]{:S(2)}) collective-permute-start(bf16[14,128,128]{2,1,0:T(8,128)(2,1)S(1)} %add_convert_fusion.13), channel_id=1, source_target_pairs={{0,8},{2,6},{8,16},{10,2},{16,24},{18,10},{24,28},{26,18},{28,20},... | collective-permute-start | bytes 1376264 | tf_op jit(solution)/shard_map/ppermute | solution.py:997
  182.0 27.3 %collective-permute-start.47 = (bf16[58,128,128]{2,1,0:T(8,128)(2,1)S(1)}, bf16[58,128,128]{2,1,0:T(8,128)(2,1)S(1)}, u32[]{:S(2)}, u32[]{:S(2)}) collective-permute-start(bf16[58,128,128]{2,1,0:T(8,128)(2,1)S(1)} %slice.118), channel_id=1, source_target_pairs={{0,2},{2,0},{4,6},{6,4},{8,10},{10,8},{12,14},{14,12},{16,18},{18,... | collective-permute-start | bytes 5701640 | tf_op jit(solution)/shard_map/ppermute | solution.py:984
  209.6 28.5 %collective-permute-start.48 = (bf16[58,128,128]{2,1,0:T(8,128)(2,1)S(1)}, bf16[58,128,128]{2,1,0:T(8,128)(2,1)S(1)}, u32[]{:S(2)}, u32[]{:S(2)}) collective-permute-start(bf16[58,128,128]{2,1,0:T(8,128)(2,1)S(1)} %slice.120), channel_id=1, source_target_pairs={{0,2},{2,0},{4,6},{6,4},{8,10},{10,8},{12,14},{14,12},{16,18},{18,... | collective-permute-start | bytes 5701640 | tf_op jit(solution)/shard_map/ppermute | solution.py:984
  238.3 14.9 %collective-permute-start.62 = (bf16[15,128,128]{2,1,0:T(8,128)(2,1)S(1)}, bf16[15,128,128]{2,1,0:T(8,128)(2,1)S(1)}, u32[]{:S(2)}, u32[]{:S(2)}) collective-permute-start(bf16[15,128,128]{2,1,0:T(8,128)(2,1)S(1)} %add_convert_fusion), channel_id=1, source_target_pairs={{0,8},{2,6},{8,16},{10,2},{16,24},{18,10},{24,28},{26,18},{28,20},... | collective-permute-start | bytes 1474568 | tf_op jit(solution)/shard_map/ppermute | solution.py:997
  (64 other events, 498.7 us)

commit v10 on v9

--- a/solution.py
+++ b/solution.py
@@ -805,12 +805,12 @@
         6 * tokens * width * half,
     )
     buffer, norms = after((buffer, norms))
-    norms = norm_steps.send(norms)
     buffer = grad_blocks(
         buffer, place, plan.self_out, [mixed, self_low], [((0,), (1,), 0, width, 3)],
         2 * tokens * width * half,
     )
     buffer, norms, other_six = after((buffer, norms, other_six))
+    norms = norm_steps.send(norms)
     output_rows = jnp.concatenate(
         [
             out_query.reshape(rows, NQ, width),
@@ -972,7 +972,7 @@
     return table
 
 
-def scatter_ring(packed, slots, chains=2):
+def scatter_ring(packed, beside, slots, chains=2):
     parts = chain_parts(slots, chains)
     held = [None] * chains
     other = None
@@ -982,6 +982,8 @@
             if other is not None:
                 packed, other = lax.optimization_barrier((packed, other))
             other = lax.ppermute(packed[base : base + 2 * slots], "dp", CORE_PAIRS)
+            if step == 1:
+                other, beside = lax.optimization_barrier((other, beside))
         pieces = []
         for number, (first, count) in enumerate(parts):
             start = (RING + step - 1) * slots + first
@@ -991,7 +993,7 @@
                 terms.append(held[number])
             pieces.append(terms)
         if step == RING:
-            return pieces
+            return pieces, beside
         for number, terms in enumerate(pieces):
             summed = sum(term.astype(f32) for term in terms).astype(bf16)
             held[number] = lax.ppermute(summed, "dp", RING_PAIRS)
@@ -1328,7 +1330,7 @@
         place,
     )
     if ring:
-        owned = scatter_ring(packed, slots)
+        owned, norm_total = scatter_ring(packed, norm_total, slots)
     else:
         owned = [[lax.psum_scatter(packed, "dp", scatter_dimension=0, tiled=True)]]
     in_grad = first_grad + (part_six.astype(f32) + other_six.astype(f32))

time: 292 us -> 292 us (level)
    ppermute x4, waiting for transfers between devices: 4.05 us -> 0.34 us  [scatter_ring(): other = lax.ppermute(packed[base:base + 2 * slots], 'dp', CORE_PAIRS)]
    ppermute x12, waiting for transfers between devices: 10.7 us -> 14.1 us  [swap_tensor(): return lax.ppermute(part, 'tensor', [(0, 1), (1, 0)])]
where the time goes in v10:
time: 292 us; the launch traced here: 288 us
  waiting for transfers between devices  99.6 us (34%)
  Pallas kernels  95.9 us (33%)
  starting transfers between devices  72.5 us (25%)
  local copies, waits for them, and re-layouts  10.8 us (4%)
  other arithmetic  7.37 us (3%)
    ppermute x14, waiting for transfers between devices, scatter_ring(): held[number] = lax.ppermute(summed, 'dp', RING_PAIRS)  42 us
    ppermute x14, waiting for transfers between devices, gather_ring(): held = [lax.ppermute(piece, 'dp', RING_PAIRS) for piece in held]  37.3 us
    pallas_call x1, Pallas kernels, optimizer(): pl.pallas_call(functools.partial(optimizer_body, padded, counts), out_sha...  32.9 us
    ppermute x14, starting transfers between devices, gather_ring(): held = [lax.ppermute(piece, 'dp', RING_PAIRS) for piece in held]  26 us
    ppermute x14, starting transfers between devices, scatter_ring(): held[number] = lax.ppermute(summed, 'dp', RING_PAIRS)  23.1 us
    ppermute x12, starting transfers between devices, swap_tensor(): return lax.ppermute(part, 'tensor', [(0, 1), (1, 0)])  16.3 us
    pallas_call x7, Pallas kernels, grad_blocks(): pl.pallas_call(functools.partial(grad_blocks_body, first_block, pairs, le...  15.9 us
    ppermute x12, waiting for transfers between devices, swap_tensor(): return lax.ppermute(part, 'tensor', [(0, 1), (1, 0)])  14.1 us
  transfers between devices with their start and end apart: 63, of which 36 were waited for; matrix products, arithmetic and copies ran while one was open for 4% of the time, Pallas kernels for 19%

profile of v10, /device:TPU:0, one launch (start us, length us, event | category | flops | bytes accessed | tf_op | source)
XLA Modules:
  0.0 288.0 jit_solution(15871182861522311492)
XLA Ops:
  7.2 5.1 %collective-permute-done.5.refs_3_ = bf16[15,128,128]{2,1,0:T(8,128)(2,1)S(1)} collective-permute-done((bf16[15,128,128]{2,1,0:T(8,128)(2,1)S(1)}, bf16[15,128,128]{2,1,0:T(8,128)(2,1)S(1)}, u32[]{:S(2)}, u32[]{:S(2)}) %collective-permute-start.5) | collective-permute-done | bytes 491552 | tf_op jit(solution)/shard_map/ppermute | solution.py:948
  24.5 4.9 %block_indices.1 = (s32[464]{0:T(512)S(1)}, s32[464]{0:T(512)S(1)}) custom-call(s32[1]{0:T(128)} %bitcast.1.device, s32[464]{0:T(512)S(1)} %bitcast.49, s32[16,464]{1,0:T(8,128)S(1)} %copy-done.17, s32[16,464]{1,0:T(8,128)S(1)} %copy-done.18), custom_call_target="tpu_custom_call" | custom-call | tf_op jit(solution)/shard_map/block_indices/pallas_call | solution.py:923
  40.3 3.2 %collective-permute-done.16.refs_1_ = bf16[15,128,128]{2,1,0:T(8,128)(2,1)S(1)} collective-permute-done((bf16[15,128,128]{2,1,0:T(8,128)(2,1)S(1)}, bf16[15,128,128]{2,1,0:T(8,128)(2,1)S(1)}, u32[]{:S(2)}, u32[]{:S(2)}) %collective-permute-start.16) | collective-permute-done | bytes 491552 | tf_op jit(solution)/shard_map/ppermute | solution.py:948
  45.1 3.3 %collective-permute-done.3.refs_0_ = bf16[14,128,128]{2,1,0:T(8,128)(2,1)S(1)} collective-permute-done((bf16[14,128,128]{2,1,0:T(8,128)(2,1)S(1)}, bf16[14,128,128]{2,1,0:T(8,128)(2,1)S(1)}, u32[]{:S(2)}, u32[]{:S(2)}) %collective-permute-start.3) | collective-permute-done | bytes 458784 | tf_op jit(solution)/shard_map/ppermute | solution.py:948
  60.2 3.7 %collective-permute-done.23.refs_1_ = bf16[15,128,128]{2,1,0:T(8,128)(2,1)S(1)} collective-permute-done((bf16[15,128,128]{2,1,0:T(8,128)(2,1)S(1)}, bf16[15,128,128]{2,1,0:T(8,128)(2,1)S(1)}, u32[]{:S(2)}, u32[]{:S(2)}) %collective-permute-start.23) | collective-permute-done | bytes 491552 | tf_op jit(solution)/shard_map/ppermute | solution.py:948
  70.5 3.5 %collective-permute-done.26.refs_1_ = bf16[15,128,128]{2,1,0:T(8,128)(2,1)S(1)} collective-permute-done((bf16[15,128,128]{2,1,0:T(8,128)(2,1)S(1)}, bf16[15,128,128]{2,1,0:T(8,128)(2,1)S(1)}, u32[]{:S(2)}, u32[]{:S(2)}) %collective-permute-start.26) | collective-permute-done | bytes 491552 | tf_op jit(solution)/shard_map/ppermute | solution.py:948
  74.8 4.2 %collective-permute-done.22.refs_0_ = bf16[14,128,128]{2,1,0:T(8,128)(2,1)S(1)} collective-permute-done((bf16[14,128,128]{2,1,0:T(8,128)(2,1)S(1)}, bf16[14,128,128]{2,1,0:T(8,128)(2,1)S(1)}, u32[]{:S(2)}, u32[]{:S(2)}) %collective-permute-start.22) | collective-permute-done | bytes 458784 | tf_op jit(solution)/shard_map/ppermute | solution.py:948
  81.5 3.5 %self_forward.1 = (bf16[3,512,384]{2,1,0:T(8,128)(2,1)S(1)}, f32[4,3,256,128]{3,2,1,0:T(8,128)S(1)}, bf16[512,384]{1,0:T(8,128)(2,1)S(1)}, bf16[128,768]{1,0:T(8...) custom-call(bf16[464,128,128]{2,1,0:T(8,128)(2,1)S(1)} %place_blocks.9.nat, ...), custom_call_target="tpu_custom_call" | custom-call | flops 1 | bytes 1 | tf_op jit(solution)/shard_map/self_forward/pallas_call | solution.py:228
  88.0 3.5 %image_forward.1 = (bf16[1088,384]{1,0:T(8,128)(2,1)S(1)}, bf16[1088,384]{1,0:T(8,128)(2,1)S(1)}) custom-call(bf16[464,128,128]{2,1,0:T(8,128)(2,1)S(1)} %place_blocks.9.nat, bf16[1088,1408]{1,0:T(8,128)(2,1)S(1)} %bitcast.30), custom_call_target="tpu_custom_call" | custom-call | flops 1 | bytes 1 | tf_op jit(solution)/shard_map/image_forward/pallas_call | solution.py:254
  97.3 8.2 %collective-permute-done.31.other = bf16[128,768]{1,0:T(8,128)(2,1)S(1)} collective-permute-done((bf16[128,768]{1,0:T(8,128)(2,1)S(1)}, bf16[128,768]{1,0:T(8,128)(2,1)S(1)}, u32[]{:S(2)}, u32[]{:S(2)}) %collective-permute-start.31) | collective-permute-done | bytes 196640 | tf_op jit(solution)/shard_map/ppermute | solution.py:670
  107.0 3.3 %text_forward.2 = (f32[192,768]{1,0:T(8,128)S(1)}, f32[192,768]{1,0:T(8,128)S(1)}, bf16[192,768]{1,0:T(8,128)(2,1)S(1)}, bf16[192,1536]{1,0:T(8,128)(2,1)S(1)}, ...) custom-call(bf16[464,128,128]{2,1,0:T(8,128)(2,1)S(1)} %place_blocks.9.nat, bf16[512,768]{1,0:T(8,128)(2,1)S(1)} %bitcast.35, ...), custom_call_target="tpu_custom_call" | custom-call | flops 1 | bytes 1 | tf_op jit(solution)/shard_map/text_forward/pallas_call | solution.py:385
  115.2 3.3 %text_forward.3 = (f32[192,768]{1,0:T(8,128)S(1)}, f32[192,768]{1,0:T(8,128)S(1)}, bf16[192,768]{1,0:T(8,128)(2,1)S(1)}, bf16[192,1536]{1,0:T(8,128)(2,1)S(1)}, ...) custom-call(bf16[464,128,128]{2,1,0:T(8,128)(2,1)S(1)} %place_blocks.9.nat, bf16[512,768]{1,0:T(8,128)(2,1)S(1)} %bitcast.36, ...), custom_call_target="tpu_custom_call" | custom-call | flops 1 | bytes 1 | tf_op jit(solution)/shard_map/text_forward/pallas_call | solution.py:385
  120.7 3.7 %feed_backward.3 = (bf16[192,768]{1,0:T(8,128)(2,1)S(1)}, f32[192,768]{1,0:T(8,128)S(1)}, bf16[192,768]{1,0:T(8,128)(2,1)S(1)}, bf16[192,1536]{1,0:T(8,128)(2,1)...) custom-call(bf16[464,128,128]{2,1,0:T(8,128)(2,1)S(1)} %place_blocks.9.nat, ...), custom_call_target="tpu_custom_call" | custom-call | flops 1 | bytes 1 | tf_op jit(solution)/shard_map/feed_backward/pallas_call | solution.py:464
  127.8 4.1 %feed_backward.4 = (bf16[128,768]{1,0:T(8,128)(2,1)S(1)}, f32[128,768]{1,0:T(8,128)S(1)}, bf16[128,768]{1,0:T(8,128)(2,1)S(1)}, bf16[128,1536]{1,0:T(8,128)(2,1)...) custom-call(bf16[464,128,128]{2,1,0:T(8,128)(2,1)S(1)} %place_blocks.9.nat, ...), custom_call_target="tpu_custom_call" | custom-call | flops 1 | bytes 1 | tf_op jit(solution)/shard_map/feed_backward/pallas_call | solution.py:464
  132.6 3.7 %feed_backward.5 = (bf16[192,768]{1,0:T(8,128)(2,1)S(1)}, f32[192,768]{1,0:T(8,128)S(1)}, bf16[192,768]{1,0:T(8,128)(2,1)S(1)}, bf16[192,1536]{1,0:T(8,128)(2,1)...) custom-call(bf16[464,128,128]{2,1,0:T(8,128)(2,1)S(1)} %place_blocks.9.nat, ...), custom_call_target="tpu_custom_call" | custom-call | flops 1 | bytes 1 | tf_op jit(solution)/shard_map/feed_backward/pallas_call | solution.py:464
  146.7 3.7 %grad_blocks.8.refs_4_ = bf16[464,128,128]{2,1,0:T(8,128)(2,1)S(1)} custom-call(s32[464]{0:T(512)S(1)} %get-tuple-element.185.place, bf16[192,768]{1,0:T(8,128)(2,1)S(1)} %get-tuple-element.207.refs_0_, bf16[192,768]{1,0:T(8,128)(2,1)S(1)} %get-tuple-element.208.refs_1_, ...), custom_call_target="tpu_custom_call", output_to_operand_aliasing={{}: (9, {})} | custom-call | flops 1 | bytes 1 | tf_op jit(solution)/shard_map/grad_blocks/pallas_call | solution.py:654
  153.3 4.9 %self_backward.1 = (f32[512,768]{1,0:T(8,128)S(1)}, bf16[512,768]{1,0:T(8,128)(2,1)S(1)}, bf16[512,1152]{1,0:T(8,128)(2,1)S(1)}, bf16[512,768]{1,0:T(8,128)(2,1)S(1)}, f32[2,768]{1,0:T(2,128)S(1)}) custom-call(bf16[464,128,128]{2,1,0:T(8,128)(2,1)S(1)} %place_blocks.9.nat, f32[128,768]{1,0:T(8,128)S(1)} %copy-done.10, ...), custom_call_target="tpu_custom_call" | custom-call | flops 1 | bytes 1 | tf_op jit(solution)/shard_map/self_backward/pallas_call | solution.py:602
  170.0 3.4 %collective-permute-done.43 = bf16[512,768]{1,0:T(8,128)(2,1)S(1)} collective-permute-done((bf16[512,768]{1,0:T(8,128)(2,1)S(1)}, bf16[512,768]{1,0:T(8,128)(2,1)S(1)}, u32[]{:S(2)}, u32[]{:S(2)}) %collective-permute-start.43) | collective-permute-done | bytes 786464 | tf_op jit(solution)/shard_map/ppermute | solution.py:670
  182.8 4.8 %collective-permute-done.56 = bf16[15,128,128]{2,1,0:T(8,128)(2,1)S(1)} collective-permute-done((bf16[15,128,128]{2,1,0:T(8,128)(2,1)S(1)}, bf16[15,128,128]{2,1,0:T(8,128)(2,1)S(1)}, u32[]{:S(2)}, u32[]{:S(2)}) %collective-permute-start.56) | collective-permute-done | bytes 491552 | tf_op jit(solution)/shard_map/ppermute | solution.py:999
  194.4 3.4 %collective-permute-done.57 = bf16[15,128,128]{2,1,0:T(8,128)(2,1)S(1)} collective-permute-done((bf16[15,128,128]{2,1,0:T(8,128)(2,1)S(1)}, bf16[15,128,128]{2,1,0:T(8,128)(2,1)S(1)}, u32[]{:S(2)}, u32[]{:S(2)}) %collective-permute-start.57) | collective-permute-done | bytes 491552 | tf_op jit(solution)/shard_map/ppermute | solution.py:999
  204.6 3.4 %collective-permute-done.58 = bf16[15,128,128]{2,1,0:T(8,128)(2,1)S(1)} collective-permute-done((bf16[15,128,128]{2,1,0:T(8,128)(2,1)S(1)}, bf16[15,128,128]{2,1,0:T(8,128)(2,1)S(1)}, u32[]{:S(2)}, u32[]{:S(2)}) %collective-permute-start.58) | collective-permute-done | bytes 491552 | tf_op jit(solution)/shard_map/ppermute | solution.py:999
  214.8 3.4 %collective-permute-done.59 = bf16[15,128,128]{2,1,0:T(8,128)(2,1)S(1)} collective-permute-done((bf16[15,128,128]{2,1,0:T(8,128)(2,1)S(1)}, bf16[15,128,128]{2,1,0:T(8,128)(2,1)S(1)}, u32[]{:S(2)}, u32[]{:S(2)}) %collective-permute-start.59) | collective-permute-done | bytes 491552 | tf_op jit(solution)/shard_map/ppermute | solution.py:999
  225.0 3.4 %collective-permute-done.60 = bf16[15,128,128]{2,1,0:T(8,128)(2,1)S(1)} collective-permute-done((bf16[15,128,128]{2,1,0:T(8,128)(2,1)S(1)}, bf16[15,128,128]{2,1,0:T(8,128)(2,1)S(1)}, u32[]{:S(2)}, u32[]{:S(2)}) %collective-permute-start.60) | collective-permute-done | bytes 491552 | tf_op jit(solution)/shard_map/ppermute | solution.py:999
  254.6 32.9 %optimizer.1 = (f32[29,128,128]{2,1,0:T(8,128)}, bf16[29,128,128]{2,1,0:T(8,128)(2,1)}, f32[29,128,128]{2,1,0:T(8,128)}, f32[29,128,128]{2,1,0:T(8,128)}, f32[29...) custom-call(bf16[14,128,128]{2,1,0:T(8,128)(2,1)} %slice.119.refs_0_, ...), custom_call_target="tpu_custom_call" | custom-call | tf_op jit(solution)/shard_map/optimizer/pallas_call | solution.py:1274
  (214 shorter events, 161.5 us)
Async XLA Ops:
  5.5 11.7 %collective-permute-start = (bf16[14,128,128]{2,1,0:T(8,128)(2,1)S(1)}, bf16[14,128,128]{2,1,0:T(8,128)(2,1)}, u32[]{:S(2)}, u32[]{:S(2)}) collective-permute-start(bf16[14,128,128]{2,1,0:T(8,128)(2,1)S(1)} %slice.152), channel_id=1, source_target_pairs={{0,8},{2,6},{8,16},{10,2},{16,24},{18,10},{24,28},{26,18},{28,20},... | collective-permute-start | bytes 1376264 | tf_op jit(solution)/shard_map/ppermute | solution.py:948
  12.2 10.2 %collective-permute-start.9 = (bf16[15,128,128]{2,1,0:T(8,128)(2,1)S(1)}, bf16[15,128,128]{2,1,0:T(8,128)(2,1)S(1)}, u32[]{:S(2)}, u32[]{:S(2)}) collective-permute-start(bf16[15,128,128]{2,1,0:T(8,128)(2,1)S(1)} %collective-permute-done.5.refs_3_), channel_id=1, source_target_pairs={{0,8},{2,6},{8,16},{10,2},{16,24},{18,10},{24,28},{26,18},{28,20},... | collective-permute-start | bytes 1474568 | tf_op jit(solution)/shard_map/ppermute | solution.py:948
  17.2 12.2 %collective-permute-start.1 = (bf16[14,128,128]{2,1,0:T(8,128)(2,1)}, bf16[14,128,128]{2,1,0:T(8,128)(2,1)}, u32[]{:S(2)}, u32[]{:S(2)}) collective-permute-start(bf16[14,128,128]{2,1,0:T(8,128)(2,1)} %collective-permute-done.refs_2_), channel_id=1, source_target_pairs={{0,8},{2,6},{8,16},{10,2},{16,24},{18,10},{24,28},{26,18},{28,20},... | collective-permute-start | bytes 1376264 | tf_op jit(solution)/shard_map/ppermute | solution.py:948
  19.3 20.5 %collective-permute-start.4 = (bf16[29,128,128]{2,1,0:T(8,128)(2,1)S(1)}, bf16[29,128,128]{2,1,0:T(8,128)(2,1)S(1)}, u32[]{:S(2)}, u32[]{:S(2)}) collective-permute-start(bf16[29,128,128]{2,1,0:T(8,128)(2,1)S(1)} %bitcast_convert_fusion.refs_0_), channel_id=1, source_target_pairs={{0,2},{2,0},{4,6},{6,4},{8,10},{10,8},{12,14},{14,12},{16,18},{18,... | collective-permute-start | bytes 2850824 | tf_op jit(solution)/shard_map/ppermute | solution.py:943
  22.4 10.2 %collective-permute-start.12 = (bf16[15,128,128]{2,1,0:T(8,128)(2,1)S(1)}, bf16[15,128,128]{2,1,0:T(8,128)(2,1)S(1)}, u32[]{:S(2)}, u32[]{:S(2)}) collective-permute-start(bf16[15,128,128]{2,1,0:T(8,128)(2,1)S(1)} %collective-permute-done.9.refs_1_), channel_id=1, source_target_pairs={{0,8},{2,6},{8,16},{10,2},{16,24},{18,10},{24,28},{26,18},{28,20},... | collective-permute-start | bytes 1474568 | tf_op jit(solution)/shard_map/ppermute | solution.py:948
  32.6 10.9 %collective-permute-start.16 = (bf16[15,128,128]{2,1,0:T(8,128)(2,1)S(1)}, bf16[15,128,128]{2,1,0:T(8,128)(2,1)S(1)}, u32[]{:S(2)}, u32[]{:S(2)}) collective-permute-start(bf16[15,128,128]{2,1,0:T(8,128)(2,1)S(1)} %collective-permute-done.12.refs_5_), channel_id=1, source_target_pairs={{0,8},{2,6},{8,16},{10,2},{16,24},{18,10},{24,28},{26,18},{28,20},... | collective-permute-start | bytes 1474568 | tf_op jit(solution)/shard_map/ppermute | solution.py:948
  34.7 10.4 %collective-permute-start.7 = (bf16[15,128,128]{2,1,0:T(8,128)(2,1)S(1)}, bf16[15,128,128]{2,1,0:T(8,128)(2,1)S(1)}, u32[]{:S(2)}, u32[]{:S(2)}) collective-permute-start(bf16[15,128,128]{2,1,0:T(8,128)(2,1)S(1)} %collective-permute-done.5.refs_3_), channel_id=1, source_target_pairs={{0,2},{2,0},{4,6},{6,4},{8,10},{10,8},{12,14},{14,12},{16,18},{18,... | collective-permute-start | bytes 1474568 | tf_op jit(solution)/shard_map/ppermute | solution.py:959
  38.2 10.2 %collective-permute-start.3 = (bf16[14,128,128]{2,1,0:T(8,128)(2,1)S(1)}, bf16[14,128,128]{2,1,0:T(8,128)(2,1)S(1)}, u32[]{:S(2)}, u32[]{:S(2)}) collective-permute-start(bf16[14,128,128]{2,1,0:T(8,128)(2,1)S(1)} %collective-permute-done.2.refs_4_), channel_id=1, source_target_pairs={{0,8},{2,6},{8,16},{10,2},{16,24},{18,10},{24,28},{26,18},{28,20},... | collective-permute-start | bytes 1376264 | tf_op jit(solution)/shard_map/ppermute | solution.py:948
  39.8 11.5 %collective-permute-start.11 = (bf16[15,128,128]{2,1,0:T(8,128)(2,1)S(1)}, bf16[15,128,128]{2,1,0:T(8,128)(2,1)S(1)}, u32[]{:S(2)}, u32[]{:S(2)}) collective-permute-start(bf16[15,128,128]{2,1,0:T(8,128)(2,1)S(1)} %collective-permute-done.9.refs_1_), channel_id=1, source_target_pairs={{0,2},{2,0},{4,6},{6,4},{8,10},{10,8},{12,14},{14,12},{16,18},{18,... | collective-permute-start | bytes 1474568 | tf_op jit(solution)/shard_map/ppermute | solution.py:959
  43.5 10.2 %collective-permute-start.19 = (bf16[15,128,128]{2,1,0:T(8,128)(2,1)S(1)}, bf16[15,128,128]{2,1,0:T(8,128)(2,1)S(1)}, u32[]{:S(2)}, u32[]{:S(2)}) collective-permute-start(bf16[15,128,128]{2,1,0:T(8,128)(2,1)S(1)} %collective-permute-done.16.refs_1_), channel_id=1, source_target_pairs={{0,8},{2,6},{8,16},{10,2},{16,24},{18,10},{24,28},{26,18},{28,20},... | collective-permute-start | bytes 1474568 | tf_op jit(solution)/shard_map/ppermute | solution.py:948
  45.1 10.2 %collective-permute-start.14 = (bf16[15,128,128]{2,1,0:T(8,128)(2,1)S(1)}, bf16[15,128,128]{2,1,0:T(8,128)(2,1)S(1)}, u32[]{:S(2)}, u32[]{:S(2)}) collective-permute-start(bf16[15,128,128]{2,1,0:T(8,128)(2,1)S(1)} %collective-permute-done.12.refs_5_), channel_id=1, source_target_pairs={{0,2},{2,0},{4,6},{6,4},{8,10},{10,8},{12,14},{14,12},{16,18},{18,... | collective-permute-start | bytes 1474568 | tf_op jit(solution)/shard_map/ppermute | solution.py:959
  53.7 10.2 %collective-permute-start.23 = (bf16[15,128,128]{2,1,0:T(8,128)(2,1)S(1)}, bf16[15,128,128]{2,1,0:T(8,128)(2,1)S(1)}, u32[]{:S(2)}, u32[]{:S(2)}) collective-permute-start(bf16[15,128,128]{2,1,0:T(8,128)(2,1)S(1)} %collective-permute-done.19.refs_5_), channel_id=1, source_target_pairs={{0,8},{2,6},{8,16},{10,2},{16,24},{18,10},{24,28},{26,18},{28,20},... | collective-permute-start | bytes 1474568 | tf_op jit(solution)/shard_map/ppermute | solution.py:948
  55.3 10.2 %collective-permute-start.21 = (bf16[15,128,128]{2,1,0:T(8,128)(2,1)S(1)}, bf16[15,128,128]{2,1,0:T(8,128)(2,1)S(1)}, u32[]{:S(2)}, u32[]{:S(2)}) collective-permute-start(bf16[15,128,128]{2,1,0:T(8,128)(2,1)S(1)} %collective-permute-done.19.refs_5_), channel_id=1, source_target_pairs={{0,2},{2,0},{4,6},{6,4},{8,10},{10,8},{12,14},{14,12},{16,18},{18,... | collective-permute-start | bytes 1474568 | tf_op jit(solution)/shard_map/ppermute | solution.py:959
  93.0 12.4 %collective-permute-start.30 = (bf16[192,768]{1,0:T(8,128)(2,1)S(1)}, bf16[192,768]{1,0:T(8,128)(2,1)S(1)}, u32[]{:S(2)}, u32[]{:S(2)}) collective-permute-start(bf16[192,768]{1,0:T(8,128)(2,1)S(1)} %get-tuple-element.158.mine), channel_id=1, source_target_pairs={{0,1},{1,0},{2,3},{3,2},{4,5},{5,4},{6,7},{7,6},{8,9},{9,8},{10,11... | collective-permute-start | bytes 884744 | tf_op jit(solution)/shard_map/ppermute | solution.py:670
  110.3 10.4 %collective-permute-start.34 = (bf16[192,768]{1,0:T(8,128)(2,1)S(1)}, bf16[192,768]{1,0:T(8,128)(2,1)S(1)}, u32[]{:S(2)}, u32[]{:S(2)}) collective-permute-start(bf16[192,768]{1,0:T(8,128)(2,1)S(1)} %get-tuple-element.161.mine), channel_id=1, source_target_pairs={{0,1},{1,0},{2,3},{3,2},{4,5},{5,4},{6,7},{7,6},{8,9},{9,8},{10,11... | collective-permute-start | bytes 884744 | tf_op jit(solution)/shard_map/ppermute | solution.py:670
  113.6 14.2 %collective-permute-start.33 = (bf16[128,768]{1,0:T(8,128)(2,1)S(1)}, bf16[128,768]{1,0:T(8,128)(2,1)S(1)}, u32[]{:S(2)}, u32[]{:S(2)}) collective-permute-start(bf16[128,768]{1,0:T(8,128)(2,1)S(1)} %get-tuple-element.166.mine), channel_id=1, source_target_pairs={{0,1},{1,0},{2,3},{3,2},{4,5},{5,4},{6,7},{7,6},{8,9},{9,8},{10,11... | collective-permute-start | bytes 589832 | tf_op jit(solution)/shard_map/ppermute | solution.py:670
  118.5 14.1 %collective-permute-start.35 = (bf16[192,768]{1,0:T(8,128)(2,1)S(1)}, bf16[192,768]{1,0:T(8,128)(2,1)S(1)}, u32[]{:S(2)}, u32[]{:S(2)}) collective-permute-start(bf16[192,768]{1,0:T(8,128)(2,1)S(1)} %get-tuple-element.169.mine), channel_id=1, source_target_pairs={{0,1},{1,0},{2,3},{3,2},{4,5},{5,4},{6,7},{7,6},{8,9},{9,8},{10,11... | collective-permute-start | bytes 884744 | tf_op jit(solution)/shard_map/ppermute | solution.py:670
  125.3 16.5 %collective-permute-start.37 = (bf16[192,768]{1,0:T(8,128)(2,1)S(1)}, bf16[192,768]{1,0:T(8,128)(2,1)S(1)}, u32[]{:S(2)}, u32[]{:S(2)}) collective-permute-start(bf16[192,768]{1,0:T(8,128)(2,1)S(1)} %get-tuple-element.172.refs_4_), channel_id=1, source_target_pairs={{0,1},{1,0},{2,3},{3,2},{4,5},{5,4},{6,7},{7,6},{8,9},{9,8},{10,11... | collective-permute-start | bytes 884744 | tf_op jit(solution)/shard_map/ppermute | solution.py:670
  136.4 16.9 %collective-permute-start.39 = (bf16[192,768]{1,0:T(8,128)(2,1)S(1)}, bf16[192,768]{1,0:T(8,128)(2,1)S(1)}, u32[]{:S(2)}, u32[]{:S(2)}) collective-permute-start(bf16[192,768]{1,0:T(8,128)(2,1)S(1)} %get-tuple-element.188.refs_5_), channel_id=1, source_target_pairs={{0,1},{1,0},{2,3},{3,2},{4,5},{5,4},{6,7},{7,6},{8,9},{9,8},{10,11... | collective-permute-start | bytes 884744 | tf_op jit(solution)/shard_map/ppermute | solution.py:670
  158.3 15.1 %collective-permute-start.43 = (bf16[512,768]{1,0:T(8,128)(2,1)S(1)}, bf16[512,768]{1,0:T(8,128)(2,1)S(1)}, u32[]{:S(2)}, u32[]{:S(2)}) collective-permute-start(bf16[512,768]{1,0:T(8,128)(2,1)S(1)} %get-tuple-element.222), channel_id=1, source_target_pairs={{0,1},{1,0},{2,3},{3,2},{4,5},{5,4},{6,7},{7,6},{8,9},{9,8},{10,11... | collective-permute-start | bytes 2359304 | tf_op jit(solution)/shard_map/ppermute | solution.py:670
  180.6 12.0 %collective-permute-start.49 = (bf16[14,128,128]{2,1,0:T(8,128)(2,1)S(1)}, bf16[14,128,128]{2,1,0:T(8,128)(2,1)S(1)}, u32[]{:S(2)}, u32[]{:S(2)}) collective-permute-start(bf16[14,128,128]{2,1,0:T(8,128)(2,1)S(1)} %add_convert_fusion.13), channel_id=1, source_target_pairs={{0,8},{2,6},{8,16},{10,2},{16,24},{18,10},{24,28},{26,18},{28,20},... | collective-permute-start | bytes 1376264 | tf_op jit(solution)/shard_map/ppermute | solution.py:999
  182.6 27.3 %collective-permute-start.47 = (bf16[58,128,128]{2,1,0:T(8,128)(2,1)S(1)}, bf16[58,128,128]{2,1,0:T(8,128)(2,1)S(1)}, u32[]{:S(2)}, u32[]{:S(2)}) collective-permute-start(bf16[58,128,128]{2,1,0:T(8,128)(2,1)S(1)} %slice.118), channel_id=1, source_target_pairs={{0,2},{2,0},{4,6},{6,4},{8,10},{10,8},{12,14},{14,12},{16,18},{18,... | collective-permute-start | bytes 5701640 | tf_op jit(solution)/shard_map/ppermute | solution.py:984
  210.1 28.5 %collective-permute-start.48 = (bf16[58,128,128]{2,1,0:T(8,128)(2,1)S(1)}, bf16[58,128,128]{2,1,0:T(8,128)(2,1)S(1)}, u32[]{:S(2)}, u32[]{:S(2)}) collective-permute-start(bf16[58,128,128]{2,1,0:T(8,128)(2,1)S(1)} %slice.120), channel_id=1, source_target_pairs={{0,2},{2,0},{4,6},{6,4},{8,10},{10,8},{12,14},{14,12},{16,18},{18,... | collective-permute-start | bytes 5701640 | tf_op jit(solution)/shard_map/ppermute | solution.py:984
  238.8 14.9 %collective-permute-start.62 = (bf16[15,128,128]{2,1,0:T(8,128)(2,1)S(1)}, bf16[15,128,128]{2,1,0:T(8,128)(2,1)S(1)}, u32[]{:S(2)}, u32[]{:S(2)}) collective-permute-start(bf16[15,128,128]{2,1,0:T(8,128)(2,1)S(1)} %add_convert_fusion), channel_id=1, source_target_pairs={{0,8},{2,6},{8,16},{10,2},{16,24},{18,10},{24,28},{26,18},{28,20},... | collective-permute-start | bytes 1474568 | tf_op jit(solution)/shard_map/ppermute | solution.py:999
  (64 other events, 481.4 us)
